TPU v7x, 32 devices: a whole 2x2x4 slice. The times are simulated.
32 devices in a mesh: blk: 8 (over z, y), dp: 4 (over x, core).
Axes of the slice: x: 2, y: 2, z: 4, core: 2. Of those that a mesh axis runs over, the one named last changes fastest.
Arguments:
- visual_rows: bfloat16 [4, 256, 4096], P('dp', 'blk'), may hold values from -6 to 6
- value_matrix: bfloat16 [4, 256, 512], P('dp', 'blk'), may hold values from -6 to 6
- key_weight: bfloat16 [4096, 512], replicated, may hold values from -1 to 1
- queries: bfloat16 [4, 1024, 4096], P('dp', 'blk'), may hold values from -1024 to 1024
- output_gradient: bfloat16 [4, 1024, 4096], P('dp', 'blk'), may hold values from -6 to 6
- visual_len: int32 [4], P('dp'), may hold values from 128 to 256, as said below
- frame_end: int32 [4, 8], P('dp'), may hold values from 1 to 2, as said below
Outputs:
- attn_out: bfloat16 [4, 1024, 4096], P('dp', 'blk')
- query_grad: bfloat16 [4, 1024, 4096], P('dp', 'blk')
- value_grad: bfloat16 [4, 256, 512], P('dp', 'blk')
- key_weight_grad: float32 [4096, 512], P(('blk', 'dp'))
Inputs may be any that keep to these rules, and one draw needn't show every extreme that they name: `visual_len`: rows 0 to the count minus one of a sample are live; some sample has 256, another 128. `frame_end`: never falling along the text blocks of a sample, 1 for its first block and 2 for its last.
All inputs are finite; a program needn't handle non-finite values.
Results may differ from a plain program's by a relative error of at most 0.02.
Values may be sent and summed in bfloat16 or wider, within the bound.
No kernel may reach another device: no remote copies, remote signals or barrier semaphores. Data moves between devices by JAX's collectives and lax.ppermute only.
A program may use at most 128 MiB of HBM per device.

v0:
```python
import jax
import jax.numpy as jnp
from jax import lax
from jax.sharding import PartitionSpec as P

HQ = 32
KEY_HEADS = 4
HEAD_SIZE = 128
TILE = 128
HEADS_PER_KEY = 8


NEGATIVE_FILLER = -1e30


def local(visual_rows, value_matrix, key_weight, queries, output_gradient, visual_len, frame_end):
    head_span_width = KEY_HEADS * HEAD_SIZE
    text_row_count = queries.shape[1]
    cycle_size = lax.axis_size("blk")
    cycle_index = lax.axis_index("blk")
    scale = HEAD_SIZE ** (-0.5)
    visual = visual_rows[0]
    key_rows = jnp.dot(visual, key_weight, preferred_element_type=jnp.float32).astype(jnp.bfloat16)
    key_values = jnp.concatenate([key_rows, value_matrix[0]], axis=1)
    all_rows = visual.shape[0] * cycle_size
    query_matrix = queries[0].reshape(text_row_count, KEY_HEADS, HEADS_PER_KEY, HEAD_SIZE)
    gradient_rows = output_gradient[0].reshape(text_row_count, KEY_HEADS, HEADS_PER_KEY, HEAD_SIZE)
    tile_count = text_row_count // TILE
    frame_tiles = lax.dynamic_slice_in_dim(frame_end[0], cycle_index * tile_count, tile_count, 0)
    limits = jnp.minimum(
        visual_len[0], TILE * jnp.repeat(frame_tiles, TILE, total_repeat_length=text_row_count)
    )
    gathered = lax.all_gather(key_values, "blk", axis=0, tiled=True)
    key_portion = gathered[:, :head_span_width].reshape(all_rows, KEY_HEADS, HEAD_SIZE)
    value_portion = gathered[:, head_span_width:].reshape(all_rows, KEY_HEADS, HEAD_SIZE)
    raw_scores = jnp.einsum(
        "tkgd,rkd->kgrt", query_matrix, key_portion, preferred_element_type=jnp.float32
    )
    positions = jnp.arange(all_rows, dtype=jnp.int32)
    live_mask = positions[:, None] < limits[None, :]
    scores = jnp.where(live_mask, raw_scores * scale, NEGATIVE_FILLER)
    row_peak = jnp.max(scores, axis=2, keepdims=True)
    shifted = jnp.where(live_mask, jnp.exp(scores - row_peak), 0.0)
    probs = shifted / jnp.sum(shifted, axis=2, keepdims=True)
    weights = probs.astype(jnp.bfloat16)
    attn_out = jnp.einsum(
        "kgrt,rkd->tkgd", weights, value_portion, preferred_element_type=jnp.float32
    ).astype(jnp.bfloat16)
    grad_delta = jnp.einsum(
        "tkgd,tkgd->kgt", gradient_rows.astype(jnp.float32), attn_out.astype(jnp.float32)
    )
    dprobs = jnp.einsum(
        "tkgd,rkd->kgrt", gradient_rows, value_portion, preferred_element_type=jnp.float32
    )
    dscores = (probs * (dprobs - grad_delta[:, :, None, :]) * scale).astype(jnp.bfloat16)
    query_acc = jnp.einsum(
        "kgrt,rkd->tkgd", dscores, key_portion, preferred_element_type=jnp.float32
    )
    key_grads = jnp.einsum(
        "kgrt,tkgd->rkd", dscores, query_matrix, preferred_element_type=jnp.float32
    )
    value_grads = jnp.einsum(
        "kgrt,tkgd->rkd", weights, gradient_rows, preferred_element_type=jnp.float32
    )
    row_sums = jnp.concatenate(
        [
            key_grads.reshape(all_rows, head_span_width),
            value_grads.reshape(all_rows, head_span_width),
        ],
        axis=1,
    )
    own_sums = lax.psum_scatter(
        row_sums.astype(jnp.bfloat16), "blk", scatter_dimension=0, tiled=True
    ).astype(jnp.float32)
    value_grad = own_sums[:, head_span_width:].astype(jnp.bfloat16)
    key_grad = own_sums[:, :head_span_width].astype(jnp.bfloat16)
    partial_grad = jnp.einsum("rc,rk->ck", visual, key_grad, preferred_element_type=jnp.float32)
    sample_rows = lax.psum_scatter(
        partial_grad.astype(jnp.bfloat16), "blk", scatter_dimension=0, tiled=True
    )
    weight_grad = lax.psum_scatter(sample_rows, "dp", scatter_dimension=0, tiled=True).astype(
        jnp.float32
    )
    return (
        attn_out.reshape(1, text_row_count, HQ * HEAD_SIZE),
        query_acc.astype(jnp.bfloat16).reshape(1, text_row_count, HQ * HEAD_SIZE),
        value_grad[None],
        weight_grad,
    )


def solution(mesh):
    return jax.shard_map(
        local,
        mesh=mesh,
        in_specs=(
            P("dp", "blk", None),
            P("dp", "blk", None),
            P(),
            P("dp", "blk", None),
            P("dp", "blk", None),
            P("dp"),
            P("dp", None),
        ),
        out_specs=(
            P("dp", "blk", None),
            P("dp", "blk", None),
            P("dp", "blk", None),
            P(("blk", "dp"), None),
        ),
        check_vma=False,
    )
```

profile of v0, /device:TPU:0, one launch (start us, length us, event | category | flops | bytes accessed | tf_op | source)
XLA Modules:
  0.0 261.9 jit_solution(16135653474844658226)
XLA Ops:
  8.0 1.2 fusion.26
  9.9 3.0 %convolution_convert_fusion.3 = bf16[32,512]{1,0:T(8,128)(2,1)S(1)} fusion(bf16[4096,512]{1,0:T(8,128)(2,1)} %param.13, bf16[1,32,4096]{2,1,0:T(8,128)(2,1)S(1)} %copy-done), kind=kOutput, calls=%fused_computation.25 | convolution fusion | flops 134234112 | bytes 4489216 | tf_op jit(solution)/shard_map/dot_general | solution.py:23
  12.9 33.0 %all_gather.3 = bf16[256,1024]{1,0:T(8,128)(2,1)S(1)} all-gather(bf16[32,1024]{1,0:T(8,128)(2,1)S(1)} %pad_maximum_fusion.1), channel_id=1, replica_groups=mesh['blk'=8,'dp'=4] {'blk'}, dimensions={0}, use_global_device_ids=true | all-gather | bytes 589824 | tf_op jit(solution)/shard_map/all_gather | solution.py:33
  46.1 0.2 copy.47
  46.3 0.7 copy.60
  46.9 0.1 reshape.96
  47.0 3.6 %fusion.27 = (f32[4,8,128]{2,1,0:T(8,128)S(1)}, f32[4,8,256,128]{3,2,1,0:T(8,128)}) fusion(pred[256,128]{1,0:T(8,128)(4,1)S(1)} %iota_compare_fusion, bf16[256,4,128,1]{0,2,3,1:T(8,128)(2,1)S(1)} %copy.47, bf16[128,4,8,128]{0,3,2,1:T(8,128)(2,1)S(1)} %bitcast.89), kind=kOutput, calls=%fused_computation.42 | convolution fusion | flops 273678592 | bytes 5554176 | tf_op jit(solution)/shard_map/sub | solution.py:43
  50.6 2.7 %fusion.13 = bf16[4,8,256,128]{3,2,1,0:T(8,128)(2,1)S(1)} fusion(f32[4,8,256,128]{3,2,1,0:T(8,128)} %get-tuple-element.39, f32[4,8,128]{2,1,0:T(8,128)S(1)} %get-tuple-element.38), kind=kLoop, calls=%fused_computation.18 | loop fusion | flops 2097152 | bytes 6307840 | tf_op jit(solution)/shard_map/convert_element_type | solution.py:45
  53.3 2.2 bitcast_convert_fusion
  55.5 3.1 %copy.45 = f32[4,8,128,128]{3,1,0,2:T(8,128)} copy(f32[4,8,128,128]{2,3,1,0:T(8,128)} %get-tuple-element.40) | data formatting | bytes 4194304
  58.7 1.4 copy.61
  60.1 1.7 copy.31
  61.8 3.0 %multiply_reduce_fusion = f32[4,8,128]{1,0,2:T(4,128)} fusion(f32[4,8,128,128]{3,1,0,2:T(8,128)} %copy.45, bf16[128,4,8,128]{3,2,1,0:T(8,128)(2,1)S(1)} %bitcast.85), kind=kLoop, calls=%fused_computation.13 | loop fusion | flops 1568768 | bytes 3162112
  64.8 1.0 copy.46
  65.8 2.1 fusion.15
  67.9 3.6 %fusion.4 = bf16[4,8,256,128]{3,2,1,0:T(8,128)(2,1)S(1)} fusion(bf16[128,4,8,128]{0,3,2,1:T(8,128)(2,1)} %copy.31, f32[4,8,128]{2,1,0:T(8,128)S(1)} %copy.46, f32[4,8,256,128]{3,2,1,0:T(8,128)} %get-tuple-element.39, f32[4,8,128]{2,1,0:T(8,128)S(1)} %get-tuple-element.38, bf16[256,4,128,1]{2,1,0,3:T(4,128)(2,1)} %bitcast.93), kind=kOutput, calls=%fused_computation.6 | convolution fusion | flops 273678336 | bytes 7634944 | tf_op jit(solution)/shard_map/tkgd,rkd->kgrt/dot_general | solution.py:52
  71.5 1.3 copy-done.2
  72.8 0.8 fusion.14
  73.6 0.1 copy.32
  73.8 0.1 copy.33
  73.9 0.9 pad_maximum_fusion
  74.9 63.1 %reduce-scatter.6.cloned.1.call-done = bf16[32,1024]{1,0:T(8,128)(2,1)} async-done(((bf16[256,1024]{1,0:T(8,128)(2,1)}), bf16[32,1024]{1,0:T(8,128)(2,1)}) %reduce-scatter.6.cloned.1.call-update) | async-done | bytes 65552 | tf_op jit(solution)/shard_map/reduce_scatter | solution.py:72
  138.0 4.0 %fusion.1 = bf16[4096,512]{0,1:T(8,128)(2,1)} fusion(bf16[1,32,4096]{2,1,0:T(8,128)(2,1)S(1)} %copy-done, bf16[32,1024]{1,0:T(8,128)(2,1)} %reduce-scatter.6.cloned.1.call-done), kind=kOutput, calls=%fused_computation.2 | convolution fusion | flops 136314880 | bytes 4489216 | tf_op jit(solution)/shard_map/rc,rk->ck/dot_general | solution.py:77
  142.0 87.5 %reduce-scatter.8.cloned.1.call-done = bf16[512,512]{0,1:T(8,128)(2,1)} async-done(((bf16[4096,512]{0,1:T(8,128)(2,1)}), bf16[512,512]{0,1:T(8,128)(2,1)}) %reduce-scatter.8.cloned.1.call-update) | async-done | bytes 524304 | tf_op jit(solution)/shard_map/reduce_scatter | solution.py:78
  229.6 2.0 copy.58
  231.6 2.0 convolution_convert_fusion.1
  233.7 1.3 copy.35
  235.0 1.3 copy.34
  236.3 0.6 slice_bitcast_fusion
  236.9 16.6 %reduce-scatter.10.cloned.1.call-done = bf16[128,512]{1,0:T(8,128)(2,1)} async-done(((bf16[512,512]{1,0:T(8,128)(2,1)}), bf16[128,512]{1,0:T(8,128)(2,1)}) %reduce-scatter.10.cloned.1.call-update) | async-done | bytes 131088
  253.5 1.0 copy.59
  254.5 0.8 copy.36
  (31 shorter events, 0.4 us)
Async XLA Ops:
  7.2 2.8 %copy-start = (bf16[1,32,4096]{2,1,0:T(8,128)(2,1)S(1)}, bf16[1,32,4096]{2,1,0:T(8,128)(2,1)}, u32[]{:S(2)}) copy-start(bf16[1,32,4096]{2,1,0:T(8,128)(2,1)} %param.11) | copy-start | bytes 786436
  7.2 5.7 %copy-start.10 = (bf16[1,32,512]{2,1,0:T(8,128)(2,1)S(1)}, bf16[1,32,512]{2,1,0:T(8,128)(2,1)}, u32[]{:S(2)}) copy-start(bf16[1,32,512]{2,1,0:T(8,128)(2,1)} %param.12) | copy-start | bytes 98308
  7.2 39.1 %copy-start.3 = (bf16[1,128,4096]{2,1,0:T(8,128)(2,1)S(1)}, bf16[1,128,4096]{2,1,0:T(8,128)(2,1)}, u32[]{:S(2)}) copy-start(bf16[1,128,4096]{2,1,0:T(8,128)(2,1)} %param.14) | copy-start | bytes 3145732
  7.2 130.8 %reduce-scatter.6.cloned.1.call-start = ((), (), s32[]{:S(2)}) async-start(), calls=%async_computation.3 | async-start | bytes 589824 | tf_op jit(solution)/shard_map/reduce_scatter | solution.py:72
  46.3 4.4 %copy-start.6 = (bf16[256,4,128,1]{0,2,3,1:T(8,128)(2,1)}, bf16[256,4,128,1]{0,2,3,1:T(8,128)(2,1)S(1)}, u32[]{:S(2)}) copy-start(bf16[256,4,128,1]{0,2,3,1:T(8,128)(2,1)S(1)} %copy.47) | copy-start | bytes 786436
  46.9 3.7 %copy-start.4 = (bf16[1,128,4096]{1,2,0:T(8,128)(2,1)}, bf16[1,128,4096]{1,2,0:T(8,128)(2,1)S(1)}, u32[]{:S(2)}) copy-start(bf16[1,128,4096]{1,2,0:T(8,128)(2,1)S(1)} %copy.60) | copy-start | bytes 3145732
  47.0 6.3 %copy-start.8 = (bf16[256,4,128]{2,1,0:T(4,128)(2,1)}, bf16[256,4,128]{2,1,0:T(4,128)(2,1)S(1)}, u32[]{:S(2)}) copy-start(bf16[256,4,128]{2,1,0:T(4,128)(2,1)S(1)} %reshape.96) | copy-start | bytes 786436
  67.9 5.0 %copy-start.5 = (bf16[1,128,4096]{1,2,0:T(8,128)(2,1)S(1)}, bf16[1,128,4096]{1,2,0:T(8,128)(2,1)}, u32[]{:S(2)}) copy-start(bf16[1,128,4096]{1,2,0:T(8,128)(2,1)} %copy-done.4) | copy-start | bytes 3145732
  71.5 1.3 copy-start.2
  74.8 156.8 %copy-start.7 = (bf16[256,4,128,1]{0,2,3,1:T(8,128)(2,1)S(1)}, bf16[256,4,128,1]{0,2,3,1:T(8,128)(2,1)}, u32[]{:S(2)}) copy-start(bf16[256,4,128,1]{0,2,3,1:T(8,128)(2,1)} %copy-done.6) | copy-start | bytes 786436
  74.8 154.7 %reduce-scatter.8.cloned.1.call-start = ((), (), s32[]{:S(2)}) async-start(), calls=%async_computation.4 | async-start | bytes 4718592 | tf_op jit(solution)/shard_map/reduce_scatter | solution.py:78
  142.0 93.0 %copy-start.1 = (bf16[4,128,8,128]{3,1,2,0:T(8,128)(2,1)S(1)}, bf16[4,128,8,128]{3,1,2,0:T(8,128)(2,1)}, u32[]{:S(2)}) copy-start(bf16[4,128,8,128]{3,1,2,0:T(8,128)(2,1)} %get-tuple-element.41) | copy-start | bytes 3145732
  142.0 111.5 %reduce-scatter.10.cloned.1.call-start = ((), (), s32[]{:S(2)}) async-start(), calls=%async_computation.5 | async-start | bytes 655360
  231.6 4.7 %copy-start.9 = (bf16[32,1024]{1,0:T(8,128)(2,1)S(1)}, bf16[32,1024]{1,0:T(8,128)(2,1)}, u32[]{:S(2)}) copy-start(bf16[32,1024]{1,0:T(8,128)(2,1)} %reduce-scatter.6.cloned.1.call-done) | copy-start | bytes 196612
Sparse Core Ops, SparseCore 0:
  74.9 63.0 reduce-scatter.5
  142.1 87.4 reduce-scatter.7
  232.1 21.3 reduce-scatter.9
where the time goes:
time: 262 us
  waiting for transfers between devices  167 us (64%)
  blocking collectives  33 us (13%)
  matrix products  21.2 us (8%)
  local copies, waits for them, and re-layouts  17.1 us (7%)
  between operations  15.4 us (6%)
  other arithmetic  7.82 us (3%)
    reduce_scatter x1, waiting for transfers between devices, local(): lax.psum_scatter(partial_grad.astype(jnp.bfloat16), 'blk', scatter_dimens...  87.5 us
    reduce_scatter x1, waiting for transfers between devices, local(): lax.psum_scatter(row_sums.astype(jnp.bfloat16), 'blk', scatter_dimension=...  63.1 us
    all_gather x1, blocking collectives, local(): gathered = lax.all_gather(key_values, 'blk', axis=0, tiled=True)  33 us
    unnamed x4, waiting for transfers between devices  16.6 us
    unnamed x29, local copies, waits for them, and re-layouts  12.4 us
  transfers between devices with their start and end apart: 3, of which 3 were waited for; matrix products, arithmetic and copies ran while one was open for 2% of the time, Pallas kernels for 0%

commit v1 on v0

v1 whole, which is shorter than its diff:
```python
import functools

import jax
import jax.numpy as jnp
from jax import lax
from jax.experimental import pallas as pl
from jax.experimental.pallas import tpu as pltpu
from jax.sharding import PartitionSpec as P

KEY_HEADS = 4
HEAD_SIZE = 128
TILE = 128
HEADS_PER_KEY = 8
LOG2_E = 1.4426950408889634
NEGATIVE_FILLER = -1e30
F32 = jnp.float32
BF16 = jnp.bfloat16


def dot(a, b, contract=((1,), (0,))):
    return lax.dot_general(a, b, (contract, ((), ())), preferred_element_type=F32)


def swap(x, axis, mask):
    size = lax.axis_size(axis)
    return lax.ppermute(x, axis, [(i, i ^ mask) for i in range(size)])


def attention_kernel(pieces, limit_ref, source_ref, q_ref, g_ref, *refs):
    k_refs, v_refs = refs[:pieces], refs[pieces : 2 * pieces]
    o_ref, qg_ref = refs[2 * pieces : 2 * pieces + 2]
    outs = refs[2 * pieces + 2 :]
    kg_refs, vg_refs = outs[:pieces], outs[pieces : 2 * pieces]
    w_all, ds_all, kg_acc, vg_acc = outs[2 * pieces :]
    j, i = pl.program_id(0), pl.program_id(1)
    columns = pl.ds(pl.multiple_of(j * HEAD_SIZE, HEAD_SIZE), HEAD_SIZE)
    keys = jnp.concatenate([r[:, columns] for r in k_refs], axis=0)
    values = jnp.concatenate([r[:, columns] for r in v_refs], axis=0)
    keys_t, values_t = keys.T, values.T
    rows = k_refs[0].shape[0]
    row = lax.broadcasted_iota(jnp.int32, (rows, TILE), 0)
    limit = limit_ref[i]
    bias = jnp.concatenate(
        [
            jnp.where(row + source_ref[p] * rows < limit, 0.0, NEGATIVE_FILLER)
            for p in range(pieces)
        ],
        axis=0,
    )
    scale = HEAD_SIZE**-0.5
    q_stack, g_stack = [], []
    for h in range(HEADS_PER_KEY):
        span = slice(h * HEAD_SIZE, (h + 1) * HEAD_SIZE)
        q, g = q_ref[:, span], g_ref[:, span]
        q_stack.append(q)
        g_stack.append(g)
        raw = dot(keys, q, ((1,), (1,))) + bias
        dprobs = dot(values, g, ((1,), (1,)))
        peak = jnp.max(raw, axis=0, keepdims=True)
        shifted = jnp.exp2((raw - peak) * (scale * LOG2_E))
        probs = shifted * (1.0 / jnp.sum(shifted, axis=0, keepdims=True))
        weights = probs.astype(BF16)
        terms = probs * dprobs
        delta = jnp.sum(terms, axis=0, keepdims=True)
        dscores = ((terms - probs * delta) * scale).astype(BF16)
        w_all[:, span] = weights
        ds_all[:, span] = dscores
        o_ref[:, span] = dot(values_t, weights).T.astype(BF16)
        qg_ref[:, span] = dot(keys_t, dscores).T.astype(BF16)
    kg = dot(ds_all[...], jnp.concatenate(q_stack, axis=0))
    vg = dot(w_all[...], jnp.concatenate(g_stack, axis=0))

    @pl.when(i == 0)
    def _():
        kg_acc[...] = kg
        vg_acc[...] = vg

    @pl.when(i > 0)
    def _():
        kg_acc[...] += kg
        vg_acc[...] += vg

    @pl.when(i == pl.num_programs(1) - 1)
    def _():
        for p in range(pieces):
            kg_refs[p][...] = kg_acc[p * rows : (p + 1) * rows, :].astype(BF16)
            vg_refs[p][...] = vg_acc[p * rows : (p + 1) * rows, :].astype(BF16)


def attention(limits, sources, queries, gradients, keys, values):
    pieces = len(keys)
    rows, width = keys[0].shape
    text = queries.shape[0]
    all_rows = pieces * rows
    span = HEADS_PER_KEY * HEAD_SIZE
    smem = pl.BlockSpec(memory_space=pltpu.SMEM)
    text_block = pl.BlockSpec((TILE, span), lambda j, i: (i, j))
    whole = pl.BlockSpec((rows, width), lambda j, i: (0, 0))
    head = pl.BlockSpec((rows, HEAD_SIZE), lambda j, i: (0, j))
    wide = jax.ShapeDtypeStruct(queries.shape, BF16)
    narrow = jax.ShapeDtypeStruct((rows, width), BF16)
    out = pl.pallas_call(
        functools.partial(attention_kernel, pieces),
        grid=(KEY_HEADS, text // TILE),
        in_specs=[smem, smem, text_block, text_block] + [whole] * (2 * pieces),
        out_specs=[text_block] * 2 + [head] * (2 * pieces),
        out_shape=[wide] * 2 + [narrow] * (2 * pieces),
        scratch_shapes=[
            pltpu.VMEM((all_rows, span), BF16),
            pltpu.VMEM((all_rows, span), BF16),
            pltpu.VMEM((all_rows, HEAD_SIZE), F32),
            pltpu.VMEM((all_rows, HEAD_SIZE), F32),
        ],
        cost_estimate=pl.CostEstimate(
            flops=12 * text * all_rows * KEY_HEADS * span,
            bytes_accessed=8 * text * KEY_HEADS * span,
            transcendentals=0,
        ),
        compiler_params=pltpu.CompilerParams(vmem_limit_bytes=40 * 1024 * 1024),
        name="attention",
    )(limits, sources, queries, gradients, *keys, *values)
    return out[0], out[1], out[2 : 2 + pieces], out[2 + pieces :]


def weight_kernel(pieces, source_ref, core_ref, visual_ref, *refs):
    kg_refs = refs[:pieces]
    own_ref, other_ref, kg_all = refs[pieces:]
    rows = kg_refs[0].shape[0]
    for p in range(pieces):
        start = pl.multiple_of(source_ref[p] * rows, rows)
        kg_all[pl.ds(start, rows), :] = kg_refs[p][...]
    total = dot(visual_ref[...], kg_all[...], ((0,), (0,)))
    half = total.shape[0] // 2
    first = core_ref[0] == 0
    own_ref[...] = jnp.where(first, total[:half], total[half:])
    other_ref[...] = jnp.where(first, total[half:], total[:half])


def weight_terms(sources, core, visual, key_grads):
    pieces = len(key_grads)
    rows, width = key_grads[0].shape
    vmem = pl.BlockSpec(memory_space=pltpu.VMEM)
    smem = pl.BlockSpec(memory_space=pltpu.SMEM)
    half = jax.ShapeDtypeStruct((visual.shape[1] // 2, width), F32)
    return pl.pallas_call(
        functools.partial(weight_kernel, pieces),
        in_specs=[smem, smem] + [vmem] * (1 + pieces),
        out_specs=[vmem] * 2,
        out_shape=[half] * 2,
        scratch_shapes=[pltpu.VMEM((pieces * rows, width), BF16)],
        compiler_params=pltpu.CompilerParams(vmem_limit_bytes=40 * 1024 * 1024),
        name="weight_terms",
    )(sources, core, visual, *key_grads)


def summed(pieces):
    total = pieces[0].astype(F32)
    for piece in pieces[1:]:
        total = total + piece.astype(F32)
    return total.astype(BF16)


def local(visual_rows, value_matrix, key_weight, queries, output_gradient, visual_len, frame_end):
    blocks, samples = lax.axis_size("blk"), lax.axis_size("dp")
    block, sample = lax.axis_index("blk"), lax.axis_index("dp")
    chips = samples // 2
    chip, core = sample // 2, sample % 2
    visual, value = visual_rows[0], value_matrix[0]
    rows, features = visual.shape
    text = queries.shape[1]
    masks = range(1, blocks)
    sources = jnp.stack([block ^ m for m in range(blocks)]).astype(jnp.int32)

    values = [value] + [swap(value, "blk", m) for m in masks]
    key = dot(visual, key_weight).astype(BF16)
    keys = [key] + [swap(key, "blk", m) for m in masks]

    width = features // (blocks * chips)
    spread = visual.reshape(rows, blocks, chips, width)

    def for_chip(m):
        part = lax.dynamic_index_in_dim(spread, chip ^ m, 2, keepdims=False)
        return part.reshape(rows, blocks * width)

    visual_parts = [for_chip(0)] + [swap(for_chip(m), "dp", 2 * m) for m in range(1, chips)]
    visual_columns = lax.all_to_all(
        jnp.concatenate(visual_parts, axis=0), "blk", split_axis=1, concat_axis=0, tiled=True
    )

    tiles = text // TILE
    frames = lax.dynamic_slice_in_dim(frame_end[0], block * tiles, tiles, 0)
    limits = jnp.minimum(visual_len[0], TILE * frames)
    attn_out, query_grad, key_terms, value_terms = attention(
        limits, sources, queries[0], output_gradient[0], keys, values
    )
    key_grad = summed([key_terms[0]] + [swap(key_terms[m], "blk", m) for m in masks])
    value_grad = summed([value_terms[0]] + [swap(value_terms[m], "blk", m) for m in masks])

    chip_grads = jnp.concatenate(
        [key_grad] + [swap(key_grad, "dp", 2 * m) for m in range(1, chips)], axis=0
    )
    key_grads = [chip_grads] + [swap(chip_grads, "blk", m) for m in masks]
    own, other = weight_terms(sources, core[None].astype(jnp.int32), visual_columns, key_grads)
    weight_grad = own + swap(other, "dp", 1)
    return attn_out[None], query_grad[None], value_grad[None], weight_grad


def solution(mesh):
    return jax.shard_map(
        local,
        mesh=mesh,
        in_specs=(
            P("dp", "blk", None),
            P("dp", "blk", None),
            P(),
            P("dp", "blk", None),
            P("dp", "blk", None),
            P("dp"),
            P("dp", None),
        ),
        out_specs=(
            P("dp", "blk", None),
            P("dp", "blk", None),
            P("dp", "blk", None),
            P(("blk", "dp"), None),
        ),
        check_vma=False,
    )
```

time: 262 us -> 99.3 us (0.38)
  waiting for transfers between devices: 167 us -> 8.13 us
  starting transfers between devices: 0.12 us -> 66.4 us
  blocking collectives: 33 us -> 0 us
  matrix products: 21.2 us -> 3.22 us
  Pallas kernels: 0 us -> 14.3 us
  local copies, waits for them, and re-layouts: 17.1 us -> 2.83 us
  between operations: 15.4 us -> 2.16 us
  other arithmetic: 7.82 us -> 2.05 us
    reduce_scatter x2 -> x0, waiting for transfers between devices: 151 us -> none  [the longest x1 87.5 us: local(): lax.psum_scatter(partial_grad.astype(jnp.bfloat16), 'blk', scatter_dimens...]
    ppermute x0 -> x38, starting transfers between devices: none -> 60.5 us  [swap(): return lax.ppermute(x, axis, [(i, i ^ mask) for i in range(size)])]
    all_gather x1 -> x0, blocking collectives: 33 us -> none  [local(): gathered = lax.all_gather(key_values, 'blk', axis=0, tiled=True)]
    unnamed x4 -> x0, waiting for transfers between devices: 16.6 us -> none
    dot_general x7 -> x1, matrix products: 17.6 us -> 3.22 us  [dot(): lax.dot_general(a, b, (contract, ((), ())), preferred_element_type=F32)]
    pallas_call x0 -> x2, Pallas kernels: none -> 14.3 us  [the longest x1 13.4 us: attention(): pl.pallas_call(functools.partial(attention_kernel, pieces), grid=(KEY_HEA...]
    unnamed x29 -> x13, local copies, waits for them, and re-layouts: 12.4 us -> 0.74 us
    ppermute x0 -> x38, waiting for transfers between devices: none -> 8.12 us  [swap(): return lax.ppermute(x, axis, [(i, i ^ mask) for i in range(size)])]
  transfers between devices with their start and end apart: 3 -> 39, of which waited for: 3 -> 6; matrix products, arithmetic and copies ran while one was open for 2% -> 4% of each run, Pallas kernels for 0% -> 14%
where the time goes in v1:
time: 99.3 us; the launch traced here: 99 us
  starting transfers between devices  66.4 us (67%)
  Pallas kernels  14.3 us (14%)
  waiting for transfers between devices  8.13 us (8%)
  matrix products  3.22 us (3%)
  local copies, waits for them, and re-layouts  2.83 us (3%)
  between operations  2.16 us (2%)
  other arithmetic  2.05 us (2%)
    ppermute x38, starting transfers between devices, swap(): return lax.ppermute(x, axis, [(i, i ^ mask) for i in range(size)])  60.5 us
    pallas_call x1, Pallas kernels, attention(): pl.pallas_call(functools.partial(attention_kernel, pieces), grid=(KEY_HEA...  13.4 us
    ppermute x38, waiting for transfers between devices, swap(): return lax.ppermute(x, axis, [(i, i ^ mask) for i in range(size)])  8.12 us
    all_to_all x1, starting transfers between devices, local(): lax.all_to_all(jnp.concatenate(visual_parts, axis=0), 'blk', split_axis=1...  5.84 us
    dot_general x1, matrix products, dot(): lax.dot_general(a, b, (contract, ((), ())), preferred_element_type=F32)  3.22 us
  transfers between devices with their start and end apart: 39, of which 6 were waited for; matrix products, arithmetic and copies ran while one was open for 4% of the time, Pallas kernels for 14%

profile of v1, /device:TPU:0, one launch (start us, length us, event | category | flops | bytes accessed | tf_op | source)
XLA Modules:
  0.0 99.0 jit_solution(13418889077064937209)
XLA Ops:
  0.7 3.2 %convolution_convert_fusion.refs_0_ = bf16[32,512]{1,0:T(8,128)(2,1)S(1)} fusion(bf16[4096,512]{1,0:T(8,128)(2,1)} %param.9, bf16[1,32,4096]{2,1,0:T(8,128)(2,1)} %param.7), kind=kOutput, calls=%fused_computation | convolution fusion | flops 134234112 | bytes 4489216 | tf_op jit(solution)/shard_map/dot_general | solution.py:21
  3.9 6.0 %collective-permute-start.6 = (bf16[32,512]{1,0:T(8,128)(2,1)S(1)}, bf16[32,512]{1,0:T(8,128)(2,1)S(1)}, u32[]{:S(2)}, u32[]{:S(2)}) collective-permute-start(bf16[32,512]{1,0:T(8,128)(2,1)S(1)} %convolution_convert_fusion.refs_0_), channel_id=1, source_target_pairs={{0,28},{4,24},{8,20},{12,16},{16,12},{20,8},{24,4},{28,0},{1,29},{... | collective-permute-start | bytes 98312 | tf_op jit(solution)/shard_map/ppermute | solution.py:26
  10.9 2.0 %collective-permute-start.3 = (bf16[32,512]{1,0:T(8,128)(2,1)S(1)}, bf16[32,512]{1,0:T(8,128)(2,1)S(1)}, u32[]{:S(2)}, u32[]{:S(2)}) collective-permute-start(bf16[32,512]{1,0:T(8,128)(2,1)S(1)} %convolution_convert_fusion.refs_0_), channel_id=1, source_target_pairs={{0,16},{4,20},{8,24},{12,28},{16,0},{20,4},{24,8},{28,12},{1,17},{... | collective-permute-start | bytes 98312 | tf_op jit(solution)/shard_map/ppermute | solution.py:26
  12.9 2.3 %collective-permute-start.2 = (bf16[32,512]{1,0:T(8,128)(2,1)S(1)}, bf16[32,512]{1,0:T(8,128)(2,1)S(1)}, u32[]{:S(2)}, u32[]{:S(2)}) collective-permute-start(bf16[32,512]{1,0:T(8,128)(2,1)S(1)} %convolution_convert_fusion.refs_0_), channel_id=1, source_target_pairs={{0,12},{4,8},{8,4},{12,0},{16,28},{20,24},{24,20},{28,16},{1,13},{... | collective-permute-start | bytes 98312 | tf_op jit(solution)/shard_map/ppermute | solution.py:26
  15.2 0.8 collective-permute-start.1
  16.4 4.7 %collective-permute-start.13 = (bf16[32,512]{1,0:T(8,128)(2,1)S(1)}, bf16[32,512]{1,0:T(8,128)(2,1)S(1)}, u32[]{:S(2)}, u32[]{:S(2)}) collective-permute-start(bf16[32,512]{1,0:T(8,128)(2,1)S(1)} %bitcast.34), channel_id=1, source_target_pairs={{0,28},{4,24},{8,20},{12,16},{16,12},{20,8},{24,4},{28,0},{1,29},{... | collective-permute-start | bytes 98312 | tf_op jit(solution)/shard_map/ppermute | solution.py:26
  21.9 2.4 %collective-permute-start.10 = (bf16[32,512]{1,0:T(8,128)(2,1)S(1)}, bf16[32,512]{1,0:T(8,128)(2,1)S(1)}, u32[]{:S(2)}, u32[]{:S(2)}) collective-permute-start(bf16[32,512]{1,0:T(8,128)(2,1)S(1)} %bitcast.37), channel_id=1, source_target_pairs={{0,16},{4,20},{8,24},{12,28},{16,0},{20,4},{24,8},{28,12},{1,17},{... | collective-permute-start | bytes 98312 | tf_op jit(solution)/shard_map/ppermute | solution.py:26
  24.4 2.4 %collective-permute-start.9 = (bf16[32,512]{1,0:T(8,128)(2,1)S(1)}, bf16[32,512]{1,0:T(8,128)(2,1)S(1)}, u32[]{:S(2)}, u32[]{:S(2)}) collective-permute-start(bf16[32,512]{1,0:T(8,128)(2,1)S(1)} %bitcast.38), channel_id=1, source_target_pairs={{0,12},{4,8},{8,4},{12,0},{16,28},{20,24},{24,20},{28,16},{1,13},{... | collective-permute-start | bytes 98312 | tf_op jit(solution)/shard_map/ppermute | solution.py:26
  27.9 1.1 %constant_dynamic-slice_fusion = (bf16[32,8,1,256]{3,2,1,0:T(2,128)(2,1)S(1)}, bf16[32,8,256]{2,1,0:T(8,128)(2,1)S(1)}) fusion(bf16[32,8,2,256]{3,2,1,0:T(2,128)(2,1)S(1)} %reshape_squeeze.3, s32[]{:T(128)S(6)} %select_n.24, s32[]{:T(128)S(6)} %select_n.25), kind=kLoop, calls=%fused_computation.9 | loop fusion | bytes 524296 | tf_op jit(solution)/shard_map/jit(dynamic_index_in_dim)/dynamic_slice | solution.py:182
  31.6 1.6 %collective-permute-start.21 = (bf16[32,2048]{1,0:T(8,128)(2,1)}, bf16[32,2048]{1,0:T(8,128)(2,1)S(1)}, u32[]{:S(2)}, u32[]{:S(2)}) collective-permute-start(bf16[32,2048]{1,0:T(8,128)(2,1)} %bitcast.22), channel_id=1, source_target_pairs={{0,2},{1,3},{2,0},{3,1},{4,6},{5,7},{6,4},{7,5},{8,10},{9,11},{10,... | collective-permute-start | bytes 393224 | tf_op jit(solution)/shard_map/ppermute | solution.py:26
  33.3 13.4 %attention.1 = (bf16[128,4096]{1,0:T(8,128)(2,1)}, bf16[128,4096]{1,0:T(8,128)(2,1)}, bf16[32,512]{1,0:T(8,128)(2,1)S(1)}, bf16[32,512]{1,0:T(8,128)(2,1)S(1)}, ...) custom-call(s32[1]{0:T(128)S(6)} %min.3.limit_ref, ...), custom_call_target="tpu_custom_call" | custom-call | flops 1610612736 | bytes 4194304 | tf_op jit(solution)/shard_map/attention/pallas_call | solution.py:102
  46.7 1.5 %collective-permute-start.22 = (bf16[32,512]{1,0:T(8,128)(2,1)S(1)}, bf16[32,512]{1,0:T(8,128)(2,1)S(1)}, u32[]{:S(2)}, u32[]{:S(2)}) collective-permute-start(bf16[32,512]{1,0:T(8,128)(2,1)S(1)} %get-tuple-element.35), channel_id=1, source_target_pairs={{0,4},{4,0},{8,12},{12,8},{16,20},{20,16},{24,28},{28,24},{1,5},{5... | collective-permute-start | bytes 98312 | tf_op jit(solution)/shard_map/ppermute | solution.py:26
  48.2 1.3 %collective-permute-start.23 = (bf16[32,512]{1,0:T(8,128)(2,1)S(1)}, bf16[32,512]{1,0:T(8,128)(2,1)S(1)}, u32[]{:S(2)}, u32[]{:S(2)}) collective-permute-start(bf16[32,512]{1,0:T(8,128)(2,1)S(1)} %get-tuple-element.36), channel_id=1, source_target_pairs={{0,8},{4,12},{8,0},{12,4},{16,24},{20,28},{24,16},{28,20},{1,9},{5... | collective-permute-start | bytes 98312 | tf_op jit(solution)/shard_map/ppermute | solution.py:26
  50.3 2.3 %collective-permute-start.25 = (bf16[32,512]{1,0:T(8,128)(2,1)S(1)}, bf16[32,512]{1,0:T(8,128)(2,1)S(1)}, u32[]{:S(2)}, u32[]{:S(2)}) collective-permute-start(bf16[32,512]{1,0:T(8,128)(2,1)S(1)} %get-tuple-element.38), channel_id=1, source_target_pairs={{0,16},{4,20},{8,24},{12,28},{16,0},{20,4},{24,8},{28,12},{1,17},{... | collective-permute-start | bytes 98312 | tf_op jit(solution)/shard_map/ppermute | solution.py:26
  52.5 1.6 %collective-permute-start.26 = (bf16[32,512]{1,0:T(8,128)(2,1)S(1)}, bf16[32,512]{1,0:T(8,128)(2,1)S(1)}, u32[]{:S(2)}, u32[]{:S(2)}) collective-permute-start(bf16[32,512]{1,0:T(8,128)(2,1)S(1)} %get-tuple-element.39), channel_id=1, source_target_pairs={{0,20},{4,16},{8,28},{12,24},{16,4},{20,0},{24,12},{28,8},{1,21},{... | collective-permute-start | bytes 98312 | tf_op jit(solution)/shard_map/ppermute | solution.py:26
  54.2 3.7 %collective-permute-start.27 = (bf16[32,512]{1,0:T(8,128)(2,1)S(1)}, bf16[32,512]{1,0:T(8,128)(2,1)S(1)}, u32[]{:S(2)}, u32[]{:S(2)}) collective-permute-start(bf16[32,512]{1,0:T(8,128)(2,1)S(1)} %get-tuple-element.40), channel_id=1, source_target_pairs={{0,24},{4,28},{8,16},{12,20},{16,8},{20,12},{24,0},{28,4},{1,25},{... | collective-permute-start | bytes 98312 | tf_op jit(solution)/shard_map/ppermute | solution.py:26
  58.0 0.8 copy.17
  58.8 5.8 %all-to-all-start = ((bf16[64,8,256]{2,0,1:T(8,128)(2,1)}), bf16[64,8,256]{2,0,1:T(8,128)(2,1)S(1)}, u32[]{:S(2)}, u32[]{:S(2)}) async-start(bf16[64,8,256]{2,0,1:T(8,128)(2,1)} %copy.17), calls=%async_computation | async-start | bytes 524288 | tf_op jit(solution)/shard_map/all_to_all | solution.py:186
  65.4 3.4 %collective-permute-done.29 = bf16[32,512]{1,0:T(8,128)(2,1)S(1)} collective-permute-done((bf16[32,512]{1,0:T(8,128)(2,1)S(1)}, bf16[32,512]{1,0:T(8,128)(2,1)S(1)}, u32[]{:S(2)}, u32[]{:S(2)}) %collective-permute-start.29) | collective-permute-done | bytes 32800 | tf_op jit(solution)/shard_map/ppermute | solution.py:26
  68.8 4.6 %collective-permute-start.36 = (bf16[64,512]{1,0:T(8,128)(2,1)S(1)}, bf16[64,512]{1,0:T(8,128)(2,1)S(1)}, u32[]{:S(2)}, u32[]{:S(2)}) collective-permute-start(bf16[64,512]{1,0:T(8,128)(2,1)S(1)} %pad_maximum_fusion.1.refs_0_), channel_id=1, source_target_pairs={{0,28},{4,24},{8,20},{12,16},{16,12},{20,8},{24,4},{28,0},{1,29},{... | collective-permute-start | bytes 196616 | tf_op jit(solution)/shard_map/ppermute | solution.py:26
  74.2 5.1 %collective-permute-start.34 = (bf16[64,512]{1,0:T(8,128)(2,1)S(1)}, bf16[64,512]{1,0:T(8,128)(2,1)S(1)}, u32[]{:S(2)}, u32[]{:S(2)}) collective-permute-start(bf16[64,512]{1,0:T(8,128)(2,1)S(1)} %pad_maximum_fusion.1.refs_0_), channel_id=1, source_target_pairs={{0,20},{4,16},{8,28},{12,24},{16,4},{20,0},{24,12},{28,8},{1,21},{... | collective-permute-start | bytes 196616 | tf_op jit(solution)/shard_map/ppermute | solution.py:26
  79.3 2.5 %collective-permute-start.32 = (bf16[64,512]{1,0:T(8,128)(2,1)S(1)}, bf16[64,512]{1,0:T(8,128)(2,1)S(1)}, u32[]{:S(2)}, u32[]{:S(2)}) collective-permute-start(bf16[64,512]{1,0:T(8,128)(2,1)S(1)} %pad_maximum_fusion.1.refs_0_), channel_id=1, source_target_pairs={{0,12},{4,8},{8,4},{12,0},{16,28},{20,24},{24,20},{28,16},{1,13},{... | collective-permute-start | bytes 196616 | tf_op jit(solution)/shard_map/ppermute | solution.py:26
  82.2 1.3 %collective-permute-start.30 = (bf16[64,512]{1,0:T(8,128)(2,1)S(1)}, bf16[64,512]{1,0:T(8,128)(2,1)S(1)}, u32[]{:S(2)}, u32[]{:S(2)}) collective-permute-start(bf16[64,512]{1,0:T(8,128)(2,1)S(1)} %pad_maximum_fusion.1.refs_0_), channel_id=1, source_target_pairs={{0,4},{4,0},{8,12},{12,8},{16,20},{20,16},{24,28},{28,24},{1,5},{5... | collective-permute-start | bytes 196616 | tf_op jit(solution)/shard_map/ppermute | solution.py:26
  83.5 0.9 collective-permute-done.34.refs_5_
  84.4 0.9 collective-permute-start.16
  85.9 0.9 collective-permute-start.17
  86.8 2.5 %collective-permute-start.18 = (bf16[32,512]{1,0:T(8,128)(2,1)S(1)}, bf16[32,512]{1,0:T(8,128)(2,1)S(1)}, u32[]{:S(2)}, u32[]{:S(2)}) collective-permute-start(bf16[32,512]{1,0:T(8,128)(2,1)S(1)} %get-tuple-element.31), channel_id=1, source_target_pairs={{0,20},{4,16},{8,28},{12,24},{16,4},{20,0},{24,12},{28,8},{1,21},{... | collective-permute-start | bytes 98312 | tf_op jit(solution)/shard_map/ppermute | solution.py:26
  89.4 1.7 %collective-permute-start.19 = (bf16[32,512]{1,0:T(8,128)(2,1)S(1)}, bf16[32,512]{1,0:T(8,128)(2,1)S(1)}, u32[]{:S(2)}, u32[]{:S(2)}) collective-permute-start(bf16[32,512]{1,0:T(8,128)(2,1)S(1)} %get-tuple-element.32), channel_id=1, source_target_pairs={{0,24},{4,28},{8,16},{12,20},{16,8},{20,12},{24,0},{28,4},{1,25},{... | collective-permute-start | bytes 98312 | tf_op jit(solution)/shard_map/ppermute | solution.py:26
  91.0 2.5 %collective-permute-start.20 = (bf16[32,512]{1,0:T(8,128)(2,1)S(1)}, bf16[32,512]{1,0:T(8,128)(2,1)S(1)}, u32[]{:S(2)}, u32[]{:S(2)}) collective-permute-start(bf16[32,512]{1,0:T(8,128)(2,1)S(1)} %get-tuple-element.33), channel_id=1, source_target_pairs={{0,28},{4,24},{8,20},{12,16},{16,12},{20,8},{24,4},{28,0},{1,29},{... | collective-permute-start | bytes 98312 | tf_op jit(solution)/shard_map/ppermute | solution.py:26
  93.6 0.9 weight_terms.1
  95.1 2.6 %collective-permute-done.20 = bf16[32,512]{1,0:T(8,128)(2,1)S(1)} collective-permute-done((bf16[32,512]{1,0:T(8,128)(2,1)S(1)}, bf16[32,512]{1,0:T(8,128)(2,1)S(1)}, u32[]{:S(2)}, u32[]{:S(2)}) %collective-permute-start.20) | collective-permute-done | bytes 32800 | tf_op jit(solution)/shard_map/ppermute | solution.py:26
  98.3 0.7 add.78
  (72 shorter events, 9.5 us)
Async XLA Ops:
  3.9 11.3 %collective-permute-start.6 = (bf16[32,512]{1,0:T(8,128)(2,1)S(1)}, bf16[32,512]{1,0:T(8,128)(2,1)S(1)}, u32[]{:S(2)}, u32[]{:S(2)}) collective-permute-start(bf16[32,512]{1,0:T(8,128)(2,1)S(1)} %convolution_convert_fusion.refs_0_), channel_id=1, source_target_pairs={{0,28},{4,24},{8,20},{12,16},{16,12},{20,8},{24,4},{28,0},{1,29},{... | collective-permute-start | bytes 98312 | tf_op jit(solution)/shard_map/ppermute | solution.py:26
  10.2 6.3 %collective-permute-start.4 = (bf16[32,512]{1,0:T(8,128)(2,1)S(1)}, bf16[32,512]{1,0:T(8,128)(2,1)S(1)}, u32[]{:S(2)}, u32[]{:S(2)}) collective-permute-start(bf16[32,512]{1,0:T(8,128)(2,1)S(1)} %convolution_convert_fusion.refs_0_), channel_id=1, source_target_pairs={{0,20},{4,16},{8,28},{12,24},{16,4},{20,0},{24,12},{28,8},{1,21},{... | collective-permute-start | bytes 98312 | tf_op jit(solution)/shard_map/ppermute | solution.py:26
  10.9 10.2 %collective-permute-start.3 = (bf16[32,512]{1,0:T(8,128)(2,1)S(1)}, bf16[32,512]{1,0:T(8,128)(2,1)S(1)}, u32[]{:S(2)}, u32[]{:S(2)}) collective-permute-start(bf16[32,512]{1,0:T(8,128)(2,1)S(1)} %convolution_convert_fusion.refs_0_), channel_id=1, source_target_pairs={{0,16},{4,20},{8,24},{12,28},{16,0},{20,4},{24,8},{28,12},{1,17},{... | collective-permute-start | bytes 98312 | tf_op jit(solution)/shard_map/ppermute | solution.py:26
  12.9 8.6 %collective-permute-start.2 = (bf16[32,512]{1,0:T(8,128)(2,1)S(1)}, bf16[32,512]{1,0:T(8,128)(2,1)S(1)}, u32[]{:S(2)}, u32[]{:S(2)}) collective-permute-start(bf16[32,512]{1,0:T(8,128)(2,1)S(1)} %convolution_convert_fusion.refs_0_), channel_id=1, source_target_pairs={{0,12},{4,8},{8,4},{12,0},{16,28},{20,24},{24,20},{28,16},{1,13},{... | collective-permute-start | bytes 98312 | tf_op jit(solution)/shard_map/ppermute | solution.py:26
  15.2 6.7 %collective-permute-start.1 = (bf16[32,512]{1,0:T(8,128)(2,1)S(1)}, bf16[32,512]{1,0:T(8,128)(2,1)S(1)}, u32[]{:S(2)}, u32[]{:S(2)}) collective-permute-start(bf16[32,512]{1,0:T(8,128)(2,1)S(1)} %convolution_convert_fusion.refs_0_), channel_id=1, source_target_pairs={{0,8},{4,12},{8,0},{12,4},{16,24},{20,28},{24,16},{28,20},{1,9},{5... | collective-permute-start | bytes 98312 | tf_op jit(solution)/shard_map/ppermute | solution.py:26
  16.0 8.4 %collective-permute-start = (bf16[32,512]{1,0:T(8,128)(2,1)S(1)}, bf16[32,512]{1,0:T(8,128)(2,1)S(1)}, u32[]{:S(2)}, u32[]{:S(2)}) collective-permute-start(bf16[32,512]{1,0:T(8,128)(2,1)S(1)} %convolution_convert_fusion.refs_0_), channel_id=1, source_target_pairs={{0,4},{4,0},{8,12},{12,8},{16,20},{20,16},{24,28},{28,24},{1,5},{5... | collective-permute-start | bytes 98312 | tf_op jit(solution)/shard_map/ppermute | solution.py:26
  16.4 10.3 %collective-permute-start.13 = (bf16[32,512]{1,0:T(8,128)(2,1)S(1)}, bf16[32,512]{1,0:T(8,128)(2,1)S(1)}, u32[]{:S(2)}, u32[]{:S(2)}) collective-permute-start(bf16[32,512]{1,0:T(8,128)(2,1)S(1)} %bitcast.34), channel_id=1, source_target_pairs={{0,28},{4,24},{8,20},{12,16},{16,12},{20,8},{24,4},{28,0},{1,29},{... | collective-permute-start | bytes 98312 | tf_op jit(solution)/shard_map/ppermute | solution.py:26
  21.1 6.4 %collective-permute-start.12 = (bf16[32,512]{1,0:T(8,128)(2,1)S(1)}, bf16[32,512]{1,0:T(8,128)(2,1)S(1)}, u32[]{:S(2)}, u32[]{:S(2)}) collective-permute-start(bf16[32,512]{1,0:T(8,128)(2,1)S(1)} %bitcast.35), channel_id=1, source_target_pairs={{0,24},{4,28},{8,16},{12,20},{16,8},{20,12},{24,0},{28,4},{1,25},{... | collective-permute-start | bytes 98312 | tf_op jit(solution)/shard_map/ppermute | solution.py:26
  21.5 10.1 %collective-permute-start.11 = (bf16[32,512]{1,0:T(8,128)(2,1)S(1)}, bf16[32,512]{1,0:T(8,128)(2,1)S(1)}, u32[]{:S(2)}, u32[]{:S(2)}) collective-permute-start(bf16[32,512]{1,0:T(8,128)(2,1)S(1)} %bitcast.36), channel_id=1, source_target_pairs={{0,20},{4,16},{8,28},{12,24},{16,4},{20,0},{24,12},{28,8},{1,21},{... | collective-permute-start | bytes 98312 | tf_op jit(solution)/shard_map/ppermute | solution.py:26
  21.9 11.3 %collective-permute-start.10 = (bf16[32,512]{1,0:T(8,128)(2,1)S(1)}, bf16[32,512]{1,0:T(8,128)(2,1)S(1)}, u32[]{:S(2)}, u32[]{:S(2)}) collective-permute-start(bf16[32,512]{1,0:T(8,128)(2,1)S(1)} %bitcast.37), channel_id=1, source_target_pairs={{0,16},{4,20},{8,24},{12,28},{16,0},{20,4},{24,8},{28,12},{1,17},{... | collective-permute-start | bytes 98312 | tf_op jit(solution)/shard_map/ppermute | solution.py:26
  24.4 8.9 %collective-permute-start.9 = (bf16[32,512]{1,0:T(8,128)(2,1)S(1)}, bf16[32,512]{1,0:T(8,128)(2,1)S(1)}, u32[]{:S(2)}, u32[]{:S(2)}) collective-permute-start(bf16[32,512]{1,0:T(8,128)(2,1)S(1)} %bitcast.38), channel_id=1, source_target_pairs={{0,12},{4,8},{8,4},{12,0},{16,28},{20,24},{24,20},{28,16},{1,13},{... | collective-permute-start | bytes 98312 | tf_op jit(solution)/shard_map/ppermute | solution.py:26
  26.7 6.5 %collective-permute-start.8 = (bf16[32,512]{1,0:T(8,128)(2,1)S(1)}, bf16[32,512]{1,0:T(8,128)(2,1)S(1)}, u32[]{:S(2)}, u32[]{:S(2)}) collective-permute-start(bf16[32,512]{1,0:T(8,128)(2,1)S(1)} %bitcast.39), channel_id=1, source_target_pairs={{0,8},{4,12},{8,0},{12,4},{16,24},{20,28},{24,16},{28,20},{1,9},{5... | collective-permute-start | bytes 98312 | tf_op jit(solution)/shard_map/ppermute | solution.py:26
  31.6 20.9 %collective-permute-start.21 = (bf16[32,2048]{1,0:T(8,128)(2,1)}, bf16[32,2048]{1,0:T(8,128)(2,1)S(1)}, u32[]{:S(2)}, u32[]{:S(2)}) collective-permute-start(bf16[32,2048]{1,0:T(8,128)(2,1)} %bitcast.22), channel_id=1, source_target_pairs={{0,2},{1,3},{2,0},{3,1},{4,6},{5,7},{6,4},{7,5},{8,10},{9,11},{10,... | collective-permute-start | bytes 393224 | tf_op jit(solution)/shard_map/ppermute | solution.py:26
  46.7 7.5 %collective-permute-start.22 = (bf16[32,512]{1,0:T(8,128)(2,1)S(1)}, bf16[32,512]{1,0:T(8,128)(2,1)S(1)}, u32[]{:S(2)}, u32[]{:S(2)}) collective-permute-start(bf16[32,512]{1,0:T(8,128)(2,1)S(1)} %get-tuple-element.35), channel_id=1, source_target_pairs={{0,4},{4,0},{8,12},{12,8},{16,20},{20,16},{24,28},{28,24},{1,5},{5... | collective-permute-start | bytes 98312 | tf_op jit(solution)/shard_map/ppermute | solution.py:26
  48.2 9.7 %collective-permute-start.23 = (bf16[32,512]{1,0:T(8,128)(2,1)S(1)}, bf16[32,512]{1,0:T(8,128)(2,1)S(1)}, u32[]{:S(2)}, u32[]{:S(2)}) collective-permute-start(bf16[32,512]{1,0:T(8,128)(2,1)S(1)} %get-tuple-element.36), channel_id=1, source_target_pairs={{0,8},{4,12},{8,0},{12,4},{16,24},{20,28},{24,16},{28,20},{1,9},{5... | collective-permute-start | bytes 98312 | tf_op jit(solution)/shard_map/ppermute | solution.py:26
  49.5 15.1 %collective-permute-start.24 = (bf16[32,512]{1,0:T(8,128)(2,1)S(1)}, bf16[32,512]{1,0:T(8,128)(2,1)S(1)}, u32[]{:S(2)}, u32[]{:S(2)}) collective-permute-start(bf16[32,512]{1,0:T(8,128)(2,1)S(1)} %get-tuple-element.37), channel_id=1, source_target_pairs={{0,12},{4,8},{8,4},{12,0},{16,28},{20,24},{24,20},{28,16},{1,13},{... | collective-permute-start | bytes 98312 | tf_op jit(solution)/shard_map/ppermute | solution.py:26
  50.3 14.4 %collective-permute-start.25 = (bf16[32,512]{1,0:T(8,128)(2,1)S(1)}, bf16[32,512]{1,0:T(8,128)(2,1)S(1)}, u32[]{:S(2)}, u32[]{:S(2)}) collective-permute-start(bf16[32,512]{1,0:T(8,128)(2,1)S(1)} %get-tuple-element.38), channel_id=1, source_target_pairs={{0,16},{4,20},{8,24},{12,28},{16,0},{20,4},{24,8},{28,12},{1,17},{... | collective-permute-start | bytes 98312 | tf_op jit(solution)/shard_map/ppermute | solution.py:26
  52.5 12.1 %collective-permute-start.26 = (bf16[32,512]{1,0:T(8,128)(2,1)S(1)}, bf16[32,512]{1,0:T(8,128)(2,1)S(1)}, u32[]{:S(2)}, u32[]{:S(2)}) collective-permute-start(bf16[32,512]{1,0:T(8,128)(2,1)S(1)} %get-tuple-element.39), channel_id=1, source_target_pairs={{0,20},{4,16},{8,28},{12,24},{16,4},{20,0},{24,12},{28,8},{1,21},{... | collective-permute-start | bytes 98312 | tf_op jit(solution)/shard_map/ppermute | solution.py:26
  54.2 10.5 %collective-permute-start.27 = (bf16[32,512]{1,0:T(8,128)(2,1)S(1)}, bf16[32,512]{1,0:T(8,128)(2,1)S(1)}, u32[]{:S(2)}, u32[]{:S(2)}) collective-permute-start(bf16[32,512]{1,0:T(8,128)(2,1)S(1)} %get-tuple-element.40), channel_id=1, source_target_pairs={{0,24},{4,28},{8,16},{12,20},{16,8},{20,12},{24,0},{28,4},{1,25},{... | collective-permute-start | bytes 98312 | tf_op jit(solution)/shard_map/ppermute | solution.py:26
  57.9 6.9 %collective-permute-start.28 = (bf16[32,512]{1,0:T(8,128)(2,1)S(1)}, bf16[32,512]{1,0:T(8,128)(2,1)S(1)}, u32[]{:S(2)}, u32[]{:S(2)}) collective-permute-start(bf16[32,512]{1,0:T(8,128)(2,1)S(1)} %get-tuple-element.41), channel_id=1, source_target_pairs={{0,28},{4,24},{8,20},{12,16},{16,12},{20,8},{24,4},{28,0},{1,29},{... | collective-permute-start | bytes 98312 | tf_op jit(solution)/shard_map/ppermute | solution.py:26
  58.8 34.8 %all-to-all-start = ((bf16[64,8,256]{2,0,1:T(8,128)(2,1)}), bf16[64,8,256]{2,0,1:T(8,128)(2,1)S(1)}, u32[]{:S(2)}, u32[]{:S(2)}) async-start(bf16[64,8,256]{2,0,1:T(8,128)(2,1)} %copy.17), calls=%async_computation | async-start | bytes 524288 | tf_op jit(solution)/shard_map/all_to_all | solution.py:186
  68.8 13.0 %collective-permute-start.36 = (bf16[64,512]{1,0:T(8,128)(2,1)S(1)}, bf16[64,512]{1,0:T(8,128)(2,1)S(1)}, u32[]{:S(2)}, u32[]{:S(2)}) collective-permute-start(bf16[64,512]{1,0:T(8,128)(2,1)S(1)} %pad_maximum_fusion.1.refs_0_), channel_id=1, source_target_pairs={{0,28},{4,24},{8,20},{12,16},{16,12},{20,8},{24,4},{28,0},{1,29},{... | collective-permute-start | bytes 196616 | tf_op jit(solution)/shard_map/ppermute | solution.py:26
  73.4 8.8 %collective-permute-start.35 = (bf16[64,512]{1,0:T(8,128)(2,1)S(1)}, bf16[64,512]{1,0:T(8,128)(2,1)S(1)}, u32[]{:S(2)}, u32[]{:S(2)}) collective-permute-start(bf16[64,512]{1,0:T(8,128)(2,1)S(1)} %pad_maximum_fusion.1.refs_0_), channel_id=1, source_target_pairs={{0,24},{4,28},{8,16},{12,20},{16,8},{20,12},{24,0},{28,4},{1,25},{... | collective-permute-start | bytes 196616 | tf_op jit(solution)/shard_map/ppermute | solution.py:26
  74.2 10.2 %collective-permute-start.34 = (bf16[64,512]{1,0:T(8,128)(2,1)S(1)}, bf16[64,512]{1,0:T(8,128)(2,1)S(1)}, u32[]{:S(2)}, u32[]{:S(2)}) collective-permute-start(bf16[64,512]{1,0:T(8,128)(2,1)S(1)} %pad_maximum_fusion.1.refs_0_), channel_id=1, source_target_pairs={{0,20},{4,16},{8,28},{12,24},{16,4},{20,0},{24,12},{28,8},{1,21},{... | collective-permute-start | bytes 196616 | tf_op jit(solution)/shard_map/ppermute | solution.py:26
  79.3 6.6 %collective-permute-start.33 = (bf16[64,512]{1,0:T(8,128)(2,1)S(1)}, bf16[64,512]{1,0:T(8,128)(2,1)S(1)}, u32[]{:S(2)}, u32[]{:S(2)}) collective-permute-start(bf16[64,512]{1,0:T(8,128)(2,1)S(1)} %pad_maximum_fusion.1.refs_0_), channel_id=1, source_target_pairs={{0,16},{4,20},{8,24},{12,28},{16,0},{20,4},{24,8},{28,12},{1,17},{... | collective-permute-start | bytes 196616 | tf_op jit(solution)/shard_map/ppermute | solution.py:26
  79.3 7.5 %collective-permute-start.32 = (bf16[64,512]{1,0:T(8,128)(2,1)S(1)}, bf16[64,512]{1,0:T(8,128)(2,1)S(1)}, u32[]{:S(2)}, u32[]{:S(2)}) collective-permute-start(bf16[64,512]{1,0:T(8,128)(2,1)S(1)} %pad_maximum_fusion.1.refs_0_), channel_id=1, source_target_pairs={{0,12},{4,8},{8,4},{12,0},{16,28},{20,24},{24,20},{28,16},{1,13},{... | collective-permute-start | bytes 196616 | tf_op jit(solution)/shard_map/ppermute | solution.py:26
  81.8 7.5 %collective-permute-start.31 = (bf16[64,512]{1,0:T(8,128)(2,1)S(1)}, bf16[64,512]{1,0:T(8,128)(2,1)S(1)}, u32[]{:S(2)}, u32[]{:S(2)}) collective-permute-start(bf16[64,512]{1,0:T(8,128)(2,1)S(1)} %pad_maximum_fusion.1.refs_0_), channel_id=1, source_target_pairs={{0,8},{4,12},{8,0},{12,4},{16,24},{20,28},{24,16},{28,20},{1,9},{5... | collective-permute-start | bytes 196616 | tf_op jit(solution)/shard_map/ppermute | solution.py:26
  82.2 8.8 %collective-permute-start.30 = (bf16[64,512]{1,0:T(8,128)(2,1)S(1)}, bf16[64,512]{1,0:T(8,128)(2,1)S(1)}, u32[]{:S(2)}, u32[]{:S(2)}) collective-permute-start(bf16[64,512]{1,0:T(8,128)(2,1)S(1)} %pad_maximum_fusion.1.refs_0_), channel_id=1, source_target_pairs={{0,4},{4,0},{8,12},{12,8},{16,20},{20,16},{24,28},{28,24},{1,5},{5... | collective-permute-start | bytes 196616 | tf_op jit(solution)/shard_map/ppermute | solution.py:26
  84.4 10.0 %collective-permute-start.16 = (bf16[32,512]{1,0:T(8,128)(2,1)S(1)}, bf16[32,512]{1,0:T(8,128)(2,1)S(1)}, u32[]{:S(2)}, u32[]{:S(2)}) collective-permute-start(bf16[32,512]{1,0:T(8,128)(2,1)S(1)} %get-tuple-element.29), channel_id=1, source_target_pairs={{0,12},{4,8},{8,4},{12,0},{16,28},{20,24},{24,20},{28,16},{1,13},{... | collective-permute-start | bytes 98312 | tf_op jit(solution)/shard_map/ppermute | solution.py:26
  85.9 8.6 %collective-permute-start.17 = (bf16[32,512]{1,0:T(8,128)(2,1)S(1)}, bf16[32,512]{1,0:T(8,128)(2,1)S(1)}, u32[]{:S(2)}, u32[]{:S(2)}) collective-permute-start(bf16[32,512]{1,0:T(8,128)(2,1)S(1)} %get-tuple-element.30), channel_id=1, source_target_pairs={{0,16},{4,20},{8,24},{12,28},{16,0},{20,4},{24,8},{28,12},{1,17},{... | collective-permute-start | bytes 98312 | tf_op jit(solution)/shard_map/ppermute | solution.py:26
  86.8 7.7 %collective-permute-start.18 = (bf16[32,512]{1,0:T(8,128)(2,1)S(1)}, bf16[32,512]{1,0:T(8,128)(2,1)S(1)}, u32[]{:S(2)}, u32[]{:S(2)}) collective-permute-start(bf16[32,512]{1,0:T(8,128)(2,1)S(1)} %get-tuple-element.31), channel_id=1, source_target_pairs={{0,20},{4,16},{8,28},{12,24},{16,4},{20,0},{24,12},{28,8},{1,21},{... | collective-permute-start | bytes 98312 | tf_op jit(solution)/shard_map/ppermute | solution.py:26
  91.0 6.6 %collective-permute-start.20 = (bf16[32,512]{1,0:T(8,128)(2,1)S(1)}, bf16[32,512]{1,0:T(8,128)(2,1)S(1)}, u32[]{:S(2)}, u32[]{:S(2)}) collective-permute-start(bf16[32,512]{1,0:T(8,128)(2,1)S(1)} %get-tuple-element.33), channel_id=1, source_target_pairs={{0,28},{4,24},{8,20},{12,16},{16,12},{20,8},{24,4},{28,0},{1,29},{... | collective-permute-start | bytes 98312 | tf_op jit(solution)/shard_map/ppermute | solution.py:26
  (12 other events, 167.2 us)

commit v2 on v1

v2 whole, which is shorter than its diff:
```python
import functools

import jax
import jax.numpy as jnp
from jax import lax
from jax.experimental import pallas as pl
from jax.experimental.pallas import tpu as pltpu
from jax.sharding import PartitionSpec as P

KEY_HEADS = 4
HEAD_SIZE = 128
TILE = 128
HEADS_PER_KEY = 8
LOG2_E = 1.4426950408889634
NEGATIVE_FILLER = -1e30
F32 = jnp.float32
BF16 = jnp.bfloat16


def dot(a, b, contract=((1,), (0,))):
    return lax.dot_general(a, b, (contract, ((), ())), preferred_element_type=F32)


def swap(x, axis, mask):
    size = lax.axis_size(axis)
    return lax.ppermute(x, axis, [(i, i ^ mask) for i in range(size)])


def project_kernel(blocks, chips, chip_ref, visual_ref, slab_ref, weight_ref, value_ref, *refs):
    copies_ref, spread_refs, acc_ref = refs[0], refs[1:-1], refs[-1]
    step = pl.program_id(0)
    part = dot(slab_ref[...], weight_ref[...])

    @pl.when(step == 0)
    def _():
        acc_ref[...] = part
        width = spread_refs[0].shape[2]
        for m in range(chips):
            chip = chip_ref[0] ^ m
            for b in range(blocks):
                if width % HEAD_SIZE == 0:
                    start = pl.multiple_of((b * chips + chip) * width, HEAD_SIZE)
                    spread_refs[m][b] = visual_ref[:, pl.ds(start, width)]
                else:
                    for c in range(chips):

                        @pl.when(chip == c)
                        def _(m=m, b=b, c=c):
                            start = (b * chips + c) * width
                            spread_refs[m][b] = visual_ref[:, start : start + width]

    @pl.when(step > 0)
    def _():
        acc_ref[...] += part

    @pl.when(step == pl.num_programs(0) - 1)
    def _():
        both = jnp.concatenate([acc_ref[...].astype(BF16), value_ref[...]], axis=1)
        for b in range(blocks):
            copies_ref[b] = both


def project(blocks, chips, chip, visual, key_weight, value):
    rows, features = visual.shape
    columns = key_weight.shape[1]
    width = features // (blocks * chips)
    steps = 8
    slab = features // steps
    smem = pl.BlockSpec(memory_space=pltpu.SMEM)

    def whole(shape):
        return pl.BlockSpec(shape, lambda k: (0,) * len(shape))

    copies = (blocks, rows, columns + value.shape[1])
    spread = (blocks, rows, width)
    out = pl.pallas_call(
        functools.partial(project_kernel, blocks, chips),
        grid=(steps,),
        in_specs=[
            smem,
            whole(visual.shape),
            pl.BlockSpec((rows, slab), lambda k: (0, k)),
            pl.BlockSpec((slab, columns), lambda k: (k, 0)),
            whole(value.shape),
        ],
        out_specs=[whole(copies)] + [whole(spread)] * chips,
        out_shape=[jax.ShapeDtypeStruct(copies, BF16)]
        + [jax.ShapeDtypeStruct(spread, BF16)] * chips,
        scratch_shapes=[pltpu.VMEM((rows, columns), F32)],
        cost_estimate=pl.CostEstimate(
            flops=2 * rows * features * columns,
            bytes_accessed=2 * features * columns,
            transcendentals=0,
        ),
        compiler_params=pltpu.CompilerParams(vmem_limit_bytes=32 * 1024 * 1024),
        name="project",
    )(chip, visual, visual, key_weight, value)
    return out[0], out[1:]


def attention_kernel(limit_ref, q_ref, g_ref, k_ref, v_ref, *refs):
    o_ref, qg_ref, kg_ref, vg_ref, w_all, ds_all, kg_acc, vg_acc = refs
    i = pl.program_id(1)
    keys, values = k_ref[...], v_ref[...]
    keys_t, values_t = keys.T, values.T
    pair = 2 * TILE
    row = lax.broadcasted_iota(jnp.int32, (keys.shape[0], pair), 0)
    bias = jnp.where(row < limit_ref[i], 0.0, NEGATIVE_FILLER)
    scale = HEAD_SIZE**-0.5
    q_stack, g_stack = [], []
    for h in range(0, HEADS_PER_KEY, 2):
        first = slice(h * HEAD_SIZE, (h + 1) * HEAD_SIZE)
        second = slice((h + 1) * HEAD_SIZE, (h + 2) * HEAD_SIZE)
        both = slice(h * HEAD_SIZE, (h + 2) * HEAD_SIZE)
        q = jnp.concatenate([q_ref[:, first], q_ref[:, second]], axis=0)
        g = jnp.concatenate([g_ref[:, first], g_ref[:, second]], axis=0)
        q_stack.append(q)
        g_stack.append(g)
        raw = dot(keys, q, ((1,), (1,))) + bias
        dprobs = dot(values, g, ((1,), (1,)))
        peak = jnp.max(raw, axis=0, keepdims=True)
        shifted = jnp.exp2((raw - peak) * (scale * LOG2_E))
        probs = shifted * (1.0 / jnp.sum(shifted, axis=0, keepdims=True))
        weights = probs.astype(BF16)
        terms = probs * dprobs
        delta = jnp.sum(terms, axis=0, keepdims=True)
        dscores = ((terms - probs * delta) * scale).astype(BF16)
        w_all[:, both] = weights
        ds_all[:, both] = dscores
        out = dot(values_t, weights).T.astype(BF16)
        o_ref[:, first] = out[:TILE]
        o_ref[:, second] = out[TILE:]
        grad = dot(keys_t, dscores).T.astype(BF16)
        qg_ref[:, first] = grad[:TILE]
        qg_ref[:, second] = grad[TILE:]
    kg = dot(ds_all[...], jnp.concatenate(q_stack, axis=0))
    vg = dot(w_all[...], jnp.concatenate(g_stack, axis=0))

    @pl.when(i == 0)
    def _():
        kg_acc[...] = kg
        vg_acc[...] = vg

    @pl.when(i > 0)
    def _():
        kg_acc[...] += kg
        vg_acc[...] += vg

    @pl.when(i == pl.num_programs(1) - 1)
    def _():
        kg_ref[...] = kg_acc[...].astype(BF16)
        vg_ref[...] = vg_acc[...].astype(BF16)


def attention(limits, queries, gradients, keys_values):
    all_rows = keys_values.shape[0]
    text = queries.shape[0]
    span = HEADS_PER_KEY * HEAD_SIZE
    smem = pl.BlockSpec(memory_space=pltpu.SMEM)
    text_block = pl.BlockSpec((TILE, span), lambda j, i: (i, j))
    key_block = pl.BlockSpec((all_rows, HEAD_SIZE), lambda j, i: (0, j))
    value_block = pl.BlockSpec((all_rows, HEAD_SIZE), lambda j, i: (0, KEY_HEADS + j))
    wide = jax.ShapeDtypeStruct(queries.shape, BF16)
    narrow = jax.ShapeDtypeStruct((all_rows, KEY_HEADS * HEAD_SIZE), BF16)
    return pl.pallas_call(
        attention_kernel,
        grid=(KEY_HEADS, text // TILE),
        in_specs=[smem, text_block, text_block, key_block, value_block],
        out_specs=[text_block, text_block, key_block, key_block],
        out_shape=[wide, wide, narrow, narrow],
        scratch_shapes=[
            pltpu.VMEM((all_rows, span), BF16),
            pltpu.VMEM((all_rows, span), BF16),
            pltpu.VMEM((all_rows, HEAD_SIZE), F32),
            pltpu.VMEM((all_rows, HEAD_SIZE), F32),
        ],
        cost_estimate=pl.CostEstimate(
            flops=12 * text * all_rows * KEY_HEADS * span,
            bytes_accessed=8 * text * KEY_HEADS * span,
            transcendentals=0,
        ),
        compiler_params=pltpu.CompilerParams(vmem_limit_bytes=40 * 1024 * 1024),
        name="attention",
    )(limits, queries, gradients, keys_values, keys_values)


def weight_kernel(core_ref, visual_ref, kg_ref, own_ref, other_ref):
    total = dot(visual_ref[...], kg_ref[...], ((0,), (0,)))
    half = total.shape[0] // 2
    first = core_ref[0] == 0
    own_ref[...] = jnp.where(first, total[:half], total[half:])
    other_ref[...] = jnp.where(first, total[half:], total[:half])


def weight_terms(core, visual, key_grads):
    vmem = pl.BlockSpec(memory_space=pltpu.VMEM)
    smem = pl.BlockSpec(memory_space=pltpu.SMEM)
    half = jax.ShapeDtypeStruct((visual.shape[1] // 2, key_grads.shape[1]), F32)
    return pl.pallas_call(
        weight_kernel,
        in_specs=[smem, vmem, vmem],
        out_specs=[vmem] * 2,
        out_shape=[half] * 2,
        compiler_params=pltpu.CompilerParams(vmem_limit_bytes=32 * 1024 * 1024),
        name="weight_terms",
    )(core, visual, key_grads)


def exchange(pieces):
    return lax.all_to_all(pieces, "blk", split_axis=0, concat_axis=0, tiled=True)


def reduced(terms, blocks):
    parts = exchange(terms.reshape(blocks, -1, terms.shape[1]))
    return jnp.sum(parts.astype(F32), axis=0).astype(BF16)


def local(visual_rows, value_matrix, key_weight, queries, output_gradient, visual_len, frame_end):
    blocks, samples = lax.axis_size("blk"), lax.axis_size("dp")
    block, sample = lax.axis_index("blk"), lax.axis_index("dp")
    chips = samples // 2
    chip = (sample // 2)[None].astype(jnp.int32)
    core = (sample % 2)[None].astype(jnp.int32)
    text = queries.shape[1]

    copies, spread = project(blocks, chips, chip, visual_rows[0], key_weight, value_matrix[0])
    keys_values = exchange(copies).reshape(-1, copies.shape[2])

    visual_parts = [spread[0]] + [swap(spread[m], "dp", 2 * m) for m in range(1, chips)]
    visual_columns = exchange(jnp.concatenate(visual_parts, axis=1))
    visual_columns = visual_columns.reshape(-1, visual_columns.shape[2])

    tiles = text // TILE
    frames = lax.dynamic_slice_in_dim(frame_end[0], block * tiles, tiles, 0)
    limits = jnp.minimum(visual_len[0], TILE * frames)
    attn_out, query_grad, key_terms, value_terms = attention(
        limits, queries[0], output_gradient[0], keys_values
    )
    key_grad = reduced(key_terms, blocks)
    value_grad = reduced(value_terms, blocks)

    chip_grads = jnp.concatenate(
        [key_grad] + [swap(key_grad, "dp", 2 * m) for m in range(1, chips)], axis=0
    )
    key_grads = exchange(jnp.broadcast_to(chip_grads[None], (blocks, *chip_grads.shape)))
    own, other = weight_terms(core, visual_columns, key_grads.reshape(-1, key_grad.shape[1]))
    weight_grad = own + swap(other, "dp", 1)
    return attn_out[None], query_grad[None], value_grad[None], weight_grad


def solution(mesh):
    return jax.shard_map(
        local,
        mesh=mesh,
        in_specs=(
            P("dp", "blk", None),
            P("dp", "blk", None),
            P(),
            P("dp", "blk", None),
            P("dp", "blk", None),
            P("dp"),
            P("dp", None),
        ),
        out_specs=(
            P("dp", "blk", None),
            P("dp", "blk", None),
            P("dp", "blk", None),
            P(("blk", "dp"), None),
        ),
        check_vma=False,
    )
```

time: 99.3 us -> 94.3 us (0.950)
  starting transfers between devices: 66.4 us -> 21.3 us
  waiting for transfers between devices: 8.13 us -> 34.6 us
  blocking collectives: 0 us -> 17.4 us
  matrix products: 3.22 us -> 0 us
  Pallas kernels: 14.3 us -> 11.7 us
  local copies, waits for them, and re-layouts: 2.83 us -> 3.94 us
    ppermute x38 -> x3, starting transfers between devices: 60.5 us -> 3.11 us  [swap(): return lax.ppermute(x, axis, [(i, i ^ mask) for i in range(size)])]
    all_to_all x1 -> x4, waiting for transfers between devices: 0.01 us -> 28.5 us  [exchange(): lax.all_to_all(pieces, 'blk', split_axis=0, concat_axis=0, tiled=True)]
    all_to_all x0 -> x1, blocking collectives: none -> 17.4 us  [exchange(): lax.all_to_all(pieces, 'blk', split_axis=0, concat_axis=0, tiled=True)]
    all_to_all x1 -> x4, starting transfers between devices: 5.84 us -> 18.1 us  [exchange(): lax.all_to_all(pieces, 'blk', split_axis=0, concat_axis=0, tiled=True)]
    dot_general x1 -> x0, matrix products: 3.22 us -> none  [dot(): lax.dot_general(a, b, (contract, ((), ())), preferred_element_type=F32)]
    unnamed x13 -> x12, local copies, waits for them, and re-layouts: 0.74 us -> 3.9 us
    pallas_call x2 -> x3, Pallas kernels: 14.3 us -> 11.7 us  [the longest x1 8.86 us: attention(): pl.pallas_call(attention_kernel, grid=(KEY_HEADS, text // TILE), in_specs...]
    ppermute x38 -> x3, waiting for transfers between devices: 8.12 us -> 6.07 us  [swap(): return lax.ppermute(x, axis, [(i, i ^ mask) for i in range(size)])]
  transfers between devices with their start and end apart: 39 -> 7, of which waited for: 6 -> 6; matrix products, arithmetic and copies ran while one was open for 4% -> 2% of each run, Pallas kernels for 14% -> 0%
where the time goes in v2:
time: 94.3 us; the launch traced here: 93.6 us
  waiting for transfers between devices  34.6 us (37%)
  starting transfers between devices  21.3 us (23%)
  blocking collectives  17.4 us (18%)
  Pallas kernels  11.7 us (12%)
  local copies, waits for them, and re-layouts  3.94 us (4%)
  other arithmetic  2.75 us (3%)
  between operations  2.02 us (2%)
    all_to_all x4, waiting for transfers between devices, exchange(): lax.all_to_all(pieces, 'blk', split_axis=0, concat_axis=0, tiled=True)  28.5 us
    all_to_all x4, starting transfers between devices, exchange(): lax.all_to_all(pieces, 'blk', split_axis=0, concat_axis=0, tiled=True)  18.1 us
    all_to_all x1, blocking collectives, exchange(): lax.all_to_all(pieces, 'blk', split_axis=0, concat_axis=0, tiled=True)  17.4 us
    pallas_call x1, Pallas kernels, attention(): pl.pallas_call(attention_kernel, grid=(KEY_HEADS, text // TILE), in_specs...  8.86 us
    ppermute x3, waiting for transfers between devices, swap(): return lax.ppermute(x, axis, [(i, i ^ mask) for i in range(size)])  6.07 us
    unnamed x12, local copies, waits for them, and re-layouts  3.9 us
    ppermute x3, starting transfers between devices, swap(): return lax.ppermute(x, axis, [(i, i ^ mask) for i in range(size)])  3.11 us
    pallas_call x1, Pallas kernels, project(): pl.pallas_call(functools.partial(project_kernel, blocks, chips), grid=(st...  2.5 us
  transfers between devices with their start and end apart: 7, of which 6 were waited for; matrix products, arithmetic and copies ran while one was open for 2% of the time, Pallas kernels for 0%

profile of v2, /device:TPU:0, one launch (start us, length us, event | category | flops | bytes accessed | tf_op | source)
XLA Modules:
  0.0 93.6 jit_solution(3961390443822182315)
XLA Ops:
  0.6 0.0 copy-start.5
  0.7 0.0 copy-start
  0.7 2.2 %copy-done = bf16[4096,512]{1,0:T(8,128)(2,1)S(1)} copy-done((bf16[4096,512]{1,0:T(8,128)(2,1)S(1)}, bf16[4096,512]{1,0:T(8,128)(2,1)}, u32[]{:S(2)}) %copy-start) | copy-done | bytes 4194328
  2.8 0.0 copy-start.1
  2.8 0.9 %copy-done.1 = bf16[1,32,4096]{2,1,0:T(8,128)(2,1)S(1)} copy-done((bf16[1,32,4096]{2,1,0:T(8,128)(2,1)S(1)}, bf16[1,32,4096]{2,1,0:T(8,128)(2,1)}, u32[]{:S(2)}) %copy-start.1) | copy-done | bytes 262168
  3.8 0.0 copy-start.2
  3.8 0.8 copy-done.2
  4.6 2.5 %project.1 = (bf16[8,32,1024]{2,1,0:T(8,128)(2,1)}, bf16[8,32,256]{2,1,0:T(8,128)(2,1)S(1)}, bf16[8,32,256]{2,1,0:T(8,128)(2,1)S(1)}) custom-call(s32[1]{0:T(128)} %bitcast.3.chip_ref, bf16[32,4096]{1,0:T(8,128)(2,1)S(1)} %bitcast.16, bf16[32,4096]{1,0:T(8,128)(2,1)S(1)} %bitcast.17, bf16[4096,512]{1,0:T(8,128)(2,1)S(1)} %copy-done, bf16[32,512]{1,0:T(8,128)(2,1)S(1)} %bitcast.21), custom_call_target="tpu_custom_call" | custom-call | flops 134217728 | bytes 4194304 | tf_op jit(solution)/shard_map/project/pallas_call | solution.py:76
  7.1 7.3 %all-to-all-start = ((bf16[8,32,1024]{2,1,0:T(8,128)(2,1)}), bf16[8,32,1024]{2,1,0:T(8,128)(2,1)S(1)}, u32[]{:S(2)}, u32[]{:S(2)}) async-start(bf16[8,32,1024]{2,1,0:T(8,128)(2,1)} %get-tuple-element.13), calls=%async_computation | async-start | bytes 1048576 | tf_op jit(solution)/shard_map/all_to_all | solution.py:210
  15.0 0.0 copy-done.5
  15.0 0.6 fusion
  16.2 12.6 %all-to-all-done = bf16[8,32,1024]{2,1,0:T(8,128)(2,1)S(1)} async-done(((bf16[8,32,1024]{2,1,0:T(8,128)(2,1)}), bf16[8,32,1024]{2,1,0:T(8,128)(2,1)S(1)}, u32[]{:S(2)}, u32[]{:S(2)}) %all-to-all-start) | async-done | bytes 524320 | tf_op jit(solution)/shard_map/all_to_all | solution.py:210
  28.8 0.0 copy-done.3
  28.8 0.0 copy-done.4
  28.8 8.9 %attention.1 = (bf16[128,4096]{1,0:T(8,128)(2,1)}, bf16[128,4096]{1,0:T(8,128)(2,1)}, bf16[256,512]{1,0:T(8,128)(2,1)}, bf16[256,512]{1,0:T(8,128)(2,1)}) custom-call(s32[1]{0:T(128)S(6)} %min.3.limit_ref, bf16[128,4096]{1,0:T(8,128)(2,1)S(1)} %bitcast.22, bf16[128,4096]{1,0:T(8,128)(2,1)S(1)} %bitcast.23, bf16[256,1024]{1,0:T(8,128)(2,1)S(1)} %bitcast.19, ...), custom_call_target="tpu_custom_call" | custom-call | flops 1610612736 | bytes 4194304 | tf_op jit(solution)/shard_map/attention/pallas_call | solution.py:165
  37.7 3.6 %all-to-all-start.3 = ((bf16[8,32,512]{2,1,0:T(8,128)(2,1)}), bf16[8,32,512]{2,1,0:T(8,128)(2,1)S(1)}, u32[]{:S(2)}, u32[]{:S(2)}) async-start(bf16[8,32,512]{2,1,0:T(8,128)(2,1)} %bitcast.13), calls=%async_computation.3 | async-start | bytes 524288 | tf_op jit(solution)/shard_map/all_to_all | solution.py:210
  41.3 1.5 %collective-permute-start = (bf16[8,32,256]{2,1,0:T(8,128)(2,1)S(1)}, bf16[8,32,256]{2,1,0:T(8,128)(2,1)S(1)}, u32[]{:S(2)}, u32[]{:S(2)}) collective-permute-start(bf16[8,32,256]{2,1,0:T(8,128)(2,1)S(1)} %get-tuple-element.18), channel_id=1, source_target_pairs={{0,2},{1,3},{2,0},{3,1},{4,6},{5,7},{6,4},{7,5},{8,10},{9,11},{10,... | collective-permute-start | bytes 393224 | tf_op jit(solution)/shard_map/ppermute | solution.py:26
  42.8 3.6 %collective-permute-done = bf16[8,32,256]{2,1,0:T(8,128)(2,1)S(1)} collective-permute-done((bf16[8,32,256]{2,1,0:T(8,128)(2,1)S(1)}, bf16[8,32,256]{2,1,0:T(8,128)(2,1)S(1)}, u32[]{:S(2)}, u32[]{:S(2)}) %collective-permute-start) | collective-permute-done | bytes 131104 | tf_op jit(solution)/shard_map/ppermute | solution.py:26
  46.5 0.7 pad_maximum_fusion
  47.2 3.2 %all-to-all-done.3 = bf16[8,32,512]{2,1,0:T(8,128)(2,1)S(1)} async-done(((bf16[8,32,512]{2,1,0:T(8,128)(2,1)}), bf16[8,32,512]{2,1,0:T(8,128)(2,1)S(1)}, u32[]{:S(2)}, u32[]{:S(2)}) %all-to-all-start.3) | async-done | bytes 262176 | tf_op jit(solution)/shard_map/all_to_all | solution.py:210
  50.4 3.6 %all-to-all-start.2 = ((bf16[8,64,256]{2,1,0:T(8,128)(2,1)}), bf16[8,64,256]{2,1,0:T(8,128)(2,1)S(1)}, u32[]{:S(2)}, u32[]{:S(2)}) async-start(bf16[8,64,256]{2,1,0:T(8,128)(2,1)} %pad_maximum_fusion), calls=%async_computation.2 | async-start | bytes 524288 | tf_op jit(solution)/shard_map/all_to_all | solution.py:210
  54.1 1.6 %collective-permute-start.1 = (bf16[32,512]{1,0:T(8,128)(2,1)S(1)}, bf16[32,512]{1,0:T(8,128)(2,1)S(1)}, u32[]{:S(2)}, u32[]{:S(2)}) collective-permute-start(bf16[32,512]{1,0:T(8,128)(2,1)S(1)} %reduce_sum.25), channel_id=1, source_target_pairs={{0,2},{1,3},{2,0},{3,1},{4,6},{5,7},{6,4},{7,5},{8,10},{9,11},{10,... | collective-permute-start | bytes 98312 | tf_op jit(solution)/shard_map/ppermute | solution.py:26
  55.6 2.4 %collective-permute-done.1 = bf16[32,512]{1,0:T(8,128)(2,1)S(1)} collective-permute-done((bf16[32,512]{1,0:T(8,128)(2,1)S(1)}, bf16[32,512]{1,0:T(8,128)(2,1)S(1)}, u32[]{:S(2)}, u32[]{:S(2)}) %collective-permute-start.1) | collective-permute-done | bytes 32800 | tf_op jit(solution)/shard_map/ppermute | solution.py:26
  58.0 4.5 %all-to-all-done.2 = bf16[8,64,256]{2,1,0:T(8,128)(2,1)S(1)} async-done(((bf16[8,64,256]{2,1,0:T(8,128)(2,1)}), bf16[8,64,256]{2,1,0:T(8,128)(2,1)S(1)}, u32[]{:S(2)}, u32[]{:S(2)}) %all-to-all-start.2) | async-done | bytes 262176 | tf_op jit(solution)/shard_map/all_to_all | solution.py:210
  62.6 17.4 %all_to_all.25 = bf16[8,64,512]{2,1,0:T(8,128)(2,1)S(1)} all-to-all(bf16[8,64,512]{2,1,0:T(8,128)(2,1)S(1)} %broadcast_in_dim.26), channel_id=1, replica_groups=mesh['blk'=8,'dp'=4] {'blk'}, dimensions={0} | all-to-all | bytes 1048576 | tf_op jit(solution)/shard_map/all_to_all | solution.py:210
  80.0 3.6 %all-to-all-start.1 = ((bf16[8,32,512]{2,1,0:T(8,128)(2,1)}), bf16[8,32,512]{2,1,0:T(8,128)(2,1)S(1)}, u32[]{:S(2)}, u32[]{:S(2)}) async-start(bf16[8,32,512]{2,1,0:T(8,128)(2,1)} %bitcast.9), calls=%async_computation.1 | async-start | bytes 524288 | tf_op jit(solution)/shard_map/all_to_all | solution.py:210
  83.6 0.3 weight_terms.1
  84.0 0.1 collective-permute-start.2
  84.1 8.1 %all-to-all-done.1 = bf16[8,32,512]{2,1,0:T(8,128)(2,1)S(1)} async-done(((bf16[8,32,512]{2,1,0:T(8,128)(2,1)}), bf16[8,32,512]{2,1,0:T(8,128)(2,1)S(1)}, u32[]{:S(2)}, u32[]{:S(2)}) %all-to-all-start.1) | async-done | bytes 262176 | tf_op jit(solution)/shard_map/all_to_all | solution.py:210
  92.2 0.7 reduce_sum.24
  92.8 0.0 collective-permute-done.2
  92.8 0.7 add.13
  (5 shorter events, 0.1 us)
Async XLA Ops:
  0.6 14.4 %copy-start.5 = (s32[1,8]{1,0:T(1,128)S(1)}, s32[1,8]{1,0:T(1,128)}, u32[]{:S(2)}) copy-start(s32[1,8]{1,0:T(1,128)} %param.13) | copy-start | bytes 100
  0.7 2.2 %copy-start = (bf16[4096,512]{1,0:T(8,128)(2,1)S(1)}, bf16[4096,512]{1,0:T(8,128)(2,1)}, u32[]{:S(2)}) copy-start(bf16[4096,512]{1,0:T(8,128)(2,1)} %weight_ref.1) | copy-start | bytes 12582916
  2.8 0.9 %copy-start.1 = (bf16[1,32,4096]{2,1,0:T(8,128)(2,1)S(1)}, bf16[1,32,4096]{2,1,0:T(8,128)(2,1)}, u32[]{:S(2)}) copy-start(bf16[1,32,4096]{2,1,0:T(8,128)(2,1)} %param.7) | copy-start | bytes 786436
  3.8 0.8 copy-start.2
  4.6 24.3 %copy-start.3 = (bf16[1,128,4096]{2,1,0:T(8,128)(2,1)S(1)}, bf16[1,128,4096]{2,1,0:T(8,128)(2,1)}, u32[]{:S(2)}) copy-start(bf16[1,128,4096]{2,1,0:T(8,128)(2,1)} %param.10) | copy-start | bytes 3145732
  4.6 24.3 %copy-start.4 = (bf16[1,128,4096]{2,1,0:T(8,128)(2,1)S(1)}, bf16[1,128,4096]{2,1,0:T(8,128)(2,1)}, u32[]{:S(2)}) copy-start(bf16[1,128,4096]{2,1,0:T(8,128)(2,1)} %param.11) | copy-start | bytes 3145732
  7.1 21.8 %all-to-all-start = ((bf16[8,32,1024]{2,1,0:T(8,128)(2,1)}), bf16[8,32,1024]{2,1,0:T(8,128)(2,1)S(1)}, u32[]{:S(2)}, u32[]{:S(2)}) async-start(bf16[8,32,1024]{2,1,0:T(8,128)(2,1)} %get-tuple-element.13), calls=%async_computation | async-start | bytes 1048576 | tf_op jit(solution)/shard_map/all_to_all | solution.py:210
  37.7 12.7 %all-to-all-start.3 = ((bf16[8,32,512]{2,1,0:T(8,128)(2,1)}), bf16[8,32,512]{2,1,0:T(8,128)(2,1)S(1)}, u32[]{:S(2)}, u32[]{:S(2)}) async-start(bf16[8,32,512]{2,1,0:T(8,128)(2,1)} %bitcast.13), calls=%async_computation.3 | async-start | bytes 524288 | tf_op jit(solution)/shard_map/all_to_all | solution.py:210
  41.3 5.1 %collective-permute-start = (bf16[8,32,256]{2,1,0:T(8,128)(2,1)S(1)}, bf16[8,32,256]{2,1,0:T(8,128)(2,1)S(1)}, u32[]{:S(2)}, u32[]{:S(2)}) collective-permute-start(bf16[8,32,256]{2,1,0:T(8,128)(2,1)S(1)} %get-tuple-element.18), channel_id=1, source_target_pairs={{0,2},{1,3},{2,0},{3,1},{4,6},{5,7},{6,4},{7,5},{8,10},{9,11},{10,... | collective-permute-start | bytes 393224 | tf_op jit(solution)/shard_map/ppermute | solution.py:26
  50.4 12.2 %all-to-all-start.2 = ((bf16[8,64,256]{2,1,0:T(8,128)(2,1)}), bf16[8,64,256]{2,1,0:T(8,128)(2,1)S(1)}, u32[]{:S(2)}, u32[]{:S(2)}) async-start(bf16[8,64,256]{2,1,0:T(8,128)(2,1)} %pad_maximum_fusion), calls=%async_computation.2 | async-start | bytes 524288 | tf_op jit(solution)/shard_map/all_to_all | solution.py:210
  54.1 4.0 %collective-permute-start.1 = (bf16[32,512]{1,0:T(8,128)(2,1)S(1)}, bf16[32,512]{1,0:T(8,128)(2,1)S(1)}, u32[]{:S(2)}, u32[]{:S(2)}) collective-permute-start(bf16[32,512]{1,0:T(8,128)(2,1)S(1)} %reduce_sum.25), channel_id=1, source_target_pairs={{0,2},{1,3},{2,0},{3,1},{4,6},{5,7},{6,4},{7,5},{8,10},{9,11},{10,... | collective-permute-start | bytes 98312 | tf_op jit(solution)/shard_map/ppermute | solution.py:26
  80.0 12.2 %all-to-all-start.1 = ((bf16[8,32,512]{2,1,0:T(8,128)(2,1)}), bf16[8,32,512]{2,1,0:T(8,128)(2,1)S(1)}, u32[]{:S(2)}, u32[]{:S(2)}) async-start(bf16[8,32,512]{2,1,0:T(8,128)(2,1)} %bitcast.9), calls=%async_computation.1 | async-start | bytes 524288 | tf_op jit(solution)/shard_map/all_to_all | solution.py:210
  84.0 8.9 %collective-permute-start.2 = (f32[128,512]{1,0:T(8,128)S(1)}, f32[128,512]{1,0:T(8,128)S(1)}, u32[]{:S(2)}, u32[]{:S(2)}) collective-permute-start(f32[128,512]{1,0:T(8,128)S(1)} %get-tuple-element.21), channel_id=1, source_target_pairs={{0,1},{1,0},{2,3},{3,2},{4,5},{5,4},{6,7},{7,6},{8,9},{9,8},{10,11... | collective-permute-start | bytes 786440 | tf_op jit(solution)/shard_map/ppermute | solution.py:26

commit v3 on v2

v3 whole, which is shorter than its diff:
```python
import functools

import jax
import jax.numpy as jnp
from jax import lax
from jax.experimental import pallas as pl
from jax.experimental.pallas import tpu as pltpu
from jax.sharding import PartitionSpec as P

KEY_HEADS = 4
HEAD_SIZE = 128
TILE = 128
HEADS_PER_KEY = 8
LOG2_E = 1.4426950408889634
NEGATIVE_FILLER = -1e30
F32 = jnp.float32
BF16 = jnp.bfloat16


def dot(a, b, contract=((1,), (0,))):
    return lax.dot_general(a, b, (contract, ((), ())), preferred_element_type=F32)


def spread_kernel(visual_ref, value_ref, out_ref):
    blocks = out_ref.shape[0]
    values = value_ref[...]
    start = values.shape[1]
    width = out_ref.shape[2] - start
    for b in range(blocks):
        out_ref[b, :, :start] = values
        out_ref[b, :, start:] = visual_ref[:, b * width : (b + 1) * width]


def spread(blocks, visual, value):
    rows, features = visual.shape
    vmem = pl.BlockSpec(memory_space=pltpu.VMEM)
    return pl.pallas_call(
        spread_kernel,
        in_specs=[vmem, vmem],
        out_specs=vmem,
        out_shape=jax.ShapeDtypeStruct(
            (blocks, rows, value.shape[1] + features // blocks), BF16
        ),
        name="spread",
    )(visual, value)


def project_kernel(visual_ref, weight_ref, copies_ref, acc_ref):
    step = pl.program_id(0)
    part = dot(visual_ref[...], weight_ref[...])

    @pl.when(step == 0)
    def _():
        acc_ref[...] = part

    @pl.when(step > 0)
    def _():
        acc_ref[...] += part

    @pl.when(step == pl.num_programs(0) - 1)
    def _():
        keys = acc_ref[...].astype(BF16)
        for b in range(copies_ref.shape[0]):
            copies_ref[b] = keys


def project(blocks, visual, key_weight):
    rows, features = visual.shape
    columns = key_weight.shape[1]
    steps = 8
    slab = features // steps
    return pl.pallas_call(
        project_kernel,
        grid=(steps,),
        in_specs=[
            pl.BlockSpec((rows, slab), lambda k: (0, k)),
            pl.BlockSpec((slab, columns), lambda k: (k, 0)),
        ],
        out_specs=pl.BlockSpec((blocks, rows, columns), lambda k: (0, 0, 0)),
        out_shape=jax.ShapeDtypeStruct((blocks, rows, columns), BF16),
        scratch_shapes=[pltpu.VMEM((rows, columns), F32)],
        cost_estimate=pl.CostEstimate(
            flops=2 * rows * features * columns,
            bytes_accessed=2 * features * columns,
            transcendentals=0,
        ),
        name="project",
    )(visual, key_weight)


def attention_kernel(length_ref, frame_ref, q_ref, g_ref, k_ref, v_ref, *refs):
    o_ref, qg_ref, kg_ref, vg_ref, w_all, ds_all, kg_acc, vg_acc = refs
    i = pl.program_id(1)
    tile = lax.axis_index("blk") * pl.num_programs(1) + i
    limit = jnp.minimum(length_ref[0], TILE * frame_ref[0, tile])
    keys, values = k_ref[...], v_ref[...]
    keys_t, values_t = keys.T, values.T
    pair = 2 * TILE
    row = lax.broadcasted_iota(jnp.int32, (keys.shape[0], pair), 0)
    bias = jnp.where(row < limit, 0.0, NEGATIVE_FILLER)
    scale = HEAD_SIZE**-0.5
    q_stack, g_stack = [], []
    for h in range(0, HEADS_PER_KEY, 2):
        first = slice(h * HEAD_SIZE, (h + 1) * HEAD_SIZE)
        second = slice((h + 1) * HEAD_SIZE, (h + 2) * HEAD_SIZE)
        both = slice(h * HEAD_SIZE, (h + 2) * HEAD_SIZE)
        q = jnp.concatenate([q_ref[:, first], q_ref[:, second]], axis=0)
        g = jnp.concatenate([g_ref[:, first], g_ref[:, second]], axis=0)
        q_stack.append(q)
        g_stack.append(g)
        raw = dot(keys, q, ((1,), (1,))) + bias
        dprobs = dot(values, g, ((1,), (1,)))
        peak = jnp.max(raw, axis=0, keepdims=True)
        shifted = jnp.exp2((raw - peak) * (scale * LOG2_E))
        probs = shifted * (1.0 / jnp.sum(shifted, axis=0, keepdims=True))
        weights = probs.astype(BF16)
        terms = probs * dprobs
        delta = jnp.sum(terms, axis=0, keepdims=True)
        dscores = ((terms - probs * delta) * scale).astype(BF16)
        w_all[:, both] = weights
        ds_all[:, both] = dscores
        out = dot(values_t, weights).T.astype(BF16)
        o_ref[:, first] = out[:TILE]
        o_ref[:, second] = out[TILE:]
        grad = dot(keys_t, dscores).T.astype(BF16)
        qg_ref[:, first] = grad[:TILE]
        qg_ref[:, second] = grad[TILE:]
    kg = dot(ds_all[...], jnp.concatenate(q_stack, axis=0))
    vg = dot(w_all[...], jnp.concatenate(g_stack, axis=0))

    @pl.when(i == 0)
    def _():
        kg_acc[...] = kg
        vg_acc[...] = vg

    @pl.when(i > 0)
    def _():
        kg_acc[...] += kg
        vg_acc[...] += vg

    @pl.when(i == pl.num_programs(1) - 1)
    def _():
        kg_ref[...] = kg_acc[...].astype(BF16)
        vg_ref[...] = vg_acc[...].astype(BF16)


def attention(length, frames, queries, gradients, keys, values):
    all_rows = keys.shape[0]
    text = queries.shape[0]
    span = HEADS_PER_KEY * HEAD_SIZE
    smem = pl.BlockSpec(memory_space=pltpu.SMEM)
    text_block = pl.BlockSpec((TILE, span), lambda j, i: (i, j))
    key_block = pl.BlockSpec((all_rows, HEAD_SIZE), lambda j, i: (0, j))
    wide = jax.ShapeDtypeStruct(queries.shape, BF16)
    narrow = jax.ShapeDtypeStruct((all_rows, KEY_HEADS * HEAD_SIZE), BF16)
    return pl.pallas_call(
        attention_kernel,
        grid=(KEY_HEADS, text // TILE),
        in_specs=[smem, smem, text_block, text_block, key_block, key_block],
        out_specs=[text_block, text_block, key_block, key_block],
        out_shape=[wide, wide, narrow, narrow],
        scratch_shapes=[
            pltpu.VMEM((all_rows, span), BF16),
            pltpu.VMEM((all_rows, span), BF16),
            pltpu.VMEM((all_rows, HEAD_SIZE), F32),
            pltpu.VMEM((all_rows, HEAD_SIZE), F32),
        ],
        cost_estimate=pl.CostEstimate(
            flops=12 * text * all_rows * KEY_HEADS * span,
            bytes_accessed=8 * text * KEY_HEADS * span,
            transcendentals=0,
        ),
        compiler_params=pltpu.CompilerParams(vmem_limit_bytes=40 * 1024 * 1024),
        name="attention",
    )(length, frames, queries, gradients, keys, values)


def weight_kernel(visual_ref, kg_ref, out_ref):
    total = dot(visual_ref[...], kg_ref[...], ((0,), (0,)))
    out_ref[...] = total.astype(BF16).reshape(out_ref.shape)


def weight_terms(samples, width, gathered, key_grads):
    rows, columns = key_grads.shape
    skipped = (gathered.shape[1] - width) // width
    return pl.pallas_call(
        weight_kernel,
        grid=(1,),
        in_specs=[
            pl.BlockSpec((rows, width), lambda k: (0, skipped)),
            pl.BlockSpec((rows, columns), lambda k: (0, 0)),
        ],
        out_specs=pl.BlockSpec((samples, width // samples, columns), lambda k: (0, 0, 0)),
        out_shape=jax.ShapeDtypeStruct((samples, width // samples, columns), BF16),
        compiler_params=pltpu.CompilerParams(vmem_limit_bytes=32 * 1024 * 1024),
        name="weight_terms",
    )(gathered, key_grads)


def sum_kernel(parts_ref, copies_ref):
    total = jnp.sum(parts_ref[...].astype(F32), axis=0).astype(BF16)
    for b in range(copies_ref.shape[0]):
        copies_ref[b] = total


def sum_copies(parts):
    vmem = pl.BlockSpec(memory_space=pltpu.VMEM)
    return pl.pallas_call(
        sum_kernel,
        in_specs=[vmem],
        out_specs=vmem,
        out_shape=jax.ShapeDtypeStruct(parts.shape, BF16),
        compiler_params=pltpu.CompilerParams(vmem_limit_bytes=32 * 1024 * 1024),
        name="sum_copies",
    )(parts)


def exchange(pieces, axis="blk"):
    return lax.all_to_all(pieces, axis, split_axis=0, concat_axis=0, tiled=True)


def flat(pieces):
    return pieces.reshape(-1, pieces.shape[-1])


def local(visual_rows, value_matrix, key_weight, queries, output_gradient, visual_len, frame_end):
    blocks, samples = lax.axis_size("blk"), lax.axis_size("dp")
    visual, value = visual_rows[0], value_matrix[0]
    rows, features = visual.shape
    columns = key_weight.shape[1]

    first = spread(blocks, visual, value)
    first, visual = lax.optimization_barrier((first, visual))
    gathered = flat(exchange(first))
    keys = flat(exchange(project(blocks, visual, key_weight)))
    attn_out, query_grad, key_terms, value_terms = attention(
        visual_len, frame_end, queries[0], output_gradient[0], keys, gathered
    )
    key_parts = exchange(key_terms.reshape(blocks, rows, columns))
    key_grads = flat(exchange(sum_copies(key_parts)))
    weight_parts = weight_terms(samples, features // blocks, gathered, key_grads)
    weight_parts, value_terms = lax.optimization_barrier((weight_parts, value_terms))
    weight_grad = jnp.sum(exchange(weight_parts, "dp").astype(F32), axis=0)
    value_parts = exchange(value_terms.reshape(blocks, rows, columns))
    value_grad = jnp.sum(value_parts.astype(F32), axis=0).astype(BF16)
    return attn_out[None], query_grad[None], value_grad[None], weight_grad


def solution(mesh):
    return jax.shard_map(
        local,
        mesh=mesh,
        in_specs=(
            P("dp", "blk", None),
            P("dp", "blk", None),
            P(),
            P("dp", "blk", None),
            P("dp", "blk", None),
            P("dp"),
            P("dp", None),
        ),
        out_specs=(
            P("dp", "blk", None),
            P("dp", "blk", None),
            P("dp", "blk", None),
            P(("blk", "dp"), None),
        ),
        check_vma=False,
    )
```

time: 94.3 us -> 102 us (1.082)
  blocking collectives: 17.4 us -> 51.8 us
  starting transfers between devices: 21.3 us -> 7.17 us
  waiting for transfers between devices: 34.6 us -> 21.4 us
  Pallas kernels: 11.7 us -> 17.7 us
  local copies, waits for them, and re-layouts: 3.94 us -> 0.01 us
  other arithmetic: 2.75 us -> 1.42 us
    all_to_all x1 -> x4, blocking collectives: 17.4 us -> 51.8 us  [exchange(): return lax.all_to_all(pieces, axis, split_axis=0, concat_axis=0, tiled=True)]
    all_to_all x4 -> x2, starting transfers between devices: 18.1 us -> 7.17 us  [exchange(): return lax.all_to_all(pieces, axis, split_axis=0, concat_axis=0, tiled=True)]
    all_to_all x4 -> x2, waiting for transfers between devices: 28.5 us -> 21.4 us  [exchange(): return lax.all_to_all(pieces, axis, split_axis=0, concat_axis=0, tiled=True)]
    ppermute x3 -> x0, waiting for transfers between devices: 6.07 us -> none  [swap(): return lax.ppermute(x, axis, [(i, i ^ mask) for i in range(size)])]
    pallas_call x2 -> x4, Pallas kernels: 2.82 us -> 8.41 us  [the longest x1 6.1 us: project(): pl.pallas_call(project_kernel, grid=(steps,), in_specs=[pl.BlockSpec((row...]
    unnamed x12 -> x6, local copies, waits for them, and re-layouts: 3.9 us -> 0.01 us
    ppermute x3 -> x0, starting transfers between devices: 3.11 us -> none  [swap(): return lax.ppermute(x, axis, [(i, i ^ mask) for i in range(size)])]
  transfers between devices with their start and end apart: 7 -> 2, of which waited for: 6 -> 2; matrix products, arithmetic and copies ran while one was open for 2% -> 1% of each run, Pallas kernels for 0% -> 0%
where the time goes in v3:
time: 102 us; the launch traced here: 101 us
  blocking collectives  51.8 us (51%)
  waiting for transfers between devices  21.4 us (21%)
  Pallas kernels  17.7 us (17%)
  starting transfers between devices  7.17 us (7%)
  other arithmetic  1.42 us (1%)
  between operations  1.33 us (1%)
    all_to_all x4, blocking collectives, exchange(): return lax.all_to_all(pieces, axis, split_axis=0, concat_axis=0, tiled=True)  51.8 us
    all_to_all x2, waiting for transfers between devices, exchange(): return lax.all_to_all(pieces, axis, split_axis=0, concat_axis=0, tiled=True)  21.4 us
    pallas_call x1, Pallas kernels, attention(): pl.pallas_call(attention_kernel, grid=(KEY_HEADS, text // TILE), in_specs...  9.33 us
    all_to_all x2, starting transfers between devices, exchange(): return lax.all_to_all(pieces, axis, split_axis=0, concat_axis=0, tiled=True)  7.17 us
    pallas_call x1, Pallas kernels, project(): pl.pallas_call(project_kernel, grid=(steps,), in_specs=[pl.BlockSpec((row...  6.1 us
  transfers between devices with their start and end apart: 2, of which 2 were waited for; matrix products, arithmetic and copies ran while one was open for 1% of the time, Pallas kernels for 0%

profile of v3, /device:TPU:0, one launch (start us, length us, event | category | flops | bytes accessed | tf_op | source)
XLA Modules:
  0.0 100.9 jit_solution(3225333594759196732)
XLA Ops:
  0.6 0.0 copy-start.2
  0.6 0.0 copy-start.1
  0.7 0.0 copy-start
  0.7 1.9 %spread.1 = bf16[8,32,1024]{2,1,0:T(8,128)(2,1)} custom-call(bf16[32,4096]{1,0:T(8,128)(2,1)} %bitcast.19, bf16[32,512]{1,0:T(8,128)(2,1)} %bitcast.21), custom_call_target="tpu_custom_call" | custom-call | tf_op jit(solution)/shard_map/spread/pallas_call | solution.py:37
  2.6 6.1 %project.1 = bf16[8,32,512]{2,1,0:T(8,128)(2,1)} custom-call(bf16[32,4096]{1,0:T(8,128)(2,1)} %bitcast.20, bf16[4096,512]{1,0:T(8,128)(2,1)} %weight_ref.1), custom_call_target="tpu_custom_call" | custom-call | flops 134217728 | bytes 4194304 | tf_op jit(solution)/shard_map/project/pallas_call | solution.py:72
  8.7 16.2 %all_to_all.30 = bf16[8,32,512]{2,1,0:T(8,128)(2,1)S(1)} all-to-all(bf16[8,32,512]{2,1,0:T(8,128)(2,1)} %project.1), channel_id=1, replica_groups=mesh['blk'=8,'dp'=4] {'blk'}, dimensions={0} | all-to-all | bytes 524288 | tf_op jit(solution)/shard_map/all_to_all | solution.py:219
  24.9 3.6 %all-to-all-start.1 = ((bf16[8,32,1024]{2,1,0:T(8,128)(2,1)}), bf16[8,32,1024]{2,1,0:T(8,128)(2,1)S(1)}, u32[]{:S(2)}, u32[]{:S(2)}) async-start(bf16[8,32,1024]{2,1,0:T(8,128)(2,1)} %spread.1), calls=%async_computation.1 | async-start | bytes 1048576 | tf_op jit(solution)/shard_map/all_to_all | solution.py:219
  29.1 13.5 %all-to-all-done.1 = bf16[8,32,1024]{2,1,0:T(8,128)(2,1)S(1)} async-done(((bf16[8,32,1024]{2,1,0:T(8,128)(2,1)}), bf16[8,32,1024]{2,1,0:T(8,128)(2,1)S(1)}, u32[]{:S(2)}, u32[]{:S(2)}) %all-to-all-start.1) | async-done | bytes 524320 | tf_op jit(solution)/shard_map/all_to_all | solution.py:219
  42.7 0.0 copy-done.2
  42.7 0.0 copy-done.1
  42.7 0.0 copy-done
  42.7 9.3 %attention.1 = (bf16[128,4096]{1,0:T(8,128)(2,1)}, bf16[128,4096]{1,0:T(8,128)(2,1)}, bf16[256,512]{1,0:T(8,128)(2,1)S(1)}, bf16[256,512]{1,0:T(8,128)(2,1)}) custom-call(s32[1]{0:T(128)S(6)} %copy.11.length_ref, s32[1,8]{1,0:T(1,128)S(1)} %copy-done.2, bf16[128,4096]{1,0:T(8,128)(2,1)S(1)} %bitcast.17, bf16[128,4096]{1,0:T(8,128)(2,1)S(1)} %bitcast.18, ...), custom_call_target="tpu_custom_call" | custom-call | flops 1610612736 | bytes 4194304 | tf_op jit(solution)/shard_map/attention/pallas_call | solution.py:156
  52.0 12.3 %all_to_all.31.parts_ref = bf16[8,32,512]{2,1,0:T(8,128)(2,1)S(1)} all-to-all(bf16[8,32,512]{2,1,0:T(8,128)(2,1)S(1)} %bitcast.16), channel_id=1, replica_groups=mesh['blk'=8,'dp'=4] {'blk'}, dimensions={0} | all-to-all | bytes 524288 | tf_op jit(solution)/shard_map/all_to_all | solution.py:219
  64.3 12.0 %all_to_all.32 = bf16[8,32,512]{2,1,0:T(8,128)(2,1)S(1)} all-to-all(bf16[8,32,512]{2,1,0:T(8,128)(2,1)S(1)} %sum_copies.1), channel_id=1, replica_groups=mesh['blk'=8,'dp'=4] {'blk'}, dimensions={0} | all-to-all | bytes 524288 | tf_op jit(solution)/shard_map/all_to_all | solution.py:219
  76.3 0.3 weight_terms.1
  76.6 11.4 %all_to_all.33 = bf16[4,128,512]{2,1,0:T(8,128)(2,1)S(1)} all-to-all(bf16[4,128,512]{2,1,0:T(8,128)(2,1)S(1)} %weight_terms.1), channel_id=1, replica_groups=mesh['blk'=8,'dp'=4] {'dp'}, dimensions={0} | all-to-all | bytes 1048576 | tf_op jit(solution)/shard_map/all_to_all | solution.py:219
  88.0 3.6 %all-to-all-start.4 = ((bf16[8,32,512]{2,1,0:T(8,128)(2,1)}), bf16[8,32,512]{2,1,0:T(8,128)(2,1)S(1)}, u32[]{:S(2)}, u32[]{:S(2)}) async-start(bf16[8,32,512]{2,1,0:T(8,128)(2,1)} %bitcast.10), calls=%async_computation.4 | async-start | bytes 524288 | tf_op jit(solution)/shard_map/all_to_all | solution.py:219
  91.6 0.8 convert_reduce_fusion
  92.4 7.8 %all-to-all-done.4 = bf16[8,32,512]{2,1,0:T(8,128)(2,1)S(1)} async-done(((bf16[8,32,512]{2,1,0:T(8,128)(2,1)}), bf16[8,32,512]{2,1,0:T(8,128)(2,1)S(1)}, u32[]{:S(2)}, u32[]{:S(2)}) %all-to-all-start.4) | async-done | bytes 262176 | tf_op jit(solution)/shard_map/all_to_all | solution.py:219
  100.2 0.7 reduce_sum.21
  (1 shorter events, 0.0 us)
Async XLA Ops:
  0.6 42.0 %copy-start.2 = (s32[1,8]{1,0:T(1,128)S(1)}, s32[1,8]{1,0:T(1,128)}, u32[]{:S(2)}) copy-start(s32[1,8]{1,0:T(1,128)} %frame_ref.1) | copy-start | bytes 100
  0.6 42.0 %copy-start.1 = (bf16[1,128,4096]{2,1,0:T(8,128)(2,1)S(1)}, bf16[1,128,4096]{2,1,0:T(8,128)(2,1)}, u32[]{:S(2)}) copy-start(bf16[1,128,4096]{2,1,0:T(8,128)(2,1)} %param.11) | copy-start | bytes 3145732
  0.7 42.0 %copy-start = (bf16[1,128,4096]{2,1,0:T(8,128)(2,1)S(1)}, bf16[1,128,4096]{2,1,0:T(8,128)(2,1)}, u32[]{:S(2)}) copy-start(bf16[1,128,4096]{2,1,0:T(8,128)(2,1)} %param.10) | copy-start | bytes 3145732
  24.9 17.8 %all-to-all-start.1 = ((bf16[8,32,1024]{2,1,0:T(8,128)(2,1)}), bf16[8,32,1024]{2,1,0:T(8,128)(2,1)S(1)}, u32[]{:S(2)}, u32[]{:S(2)}) async-start(bf16[8,32,1024]{2,1,0:T(8,128)(2,1)} %spread.1), calls=%async_computation.1 | async-start | bytes 1048576 | tf_op jit(solution)/shard_map/all_to_all | solution.py:219
  88.0 12.2 %all-to-all-start.4 = ((bf16[8,32,512]{2,1,0:T(8,128)(2,1)}), bf16[8,32,512]{2,1,0:T(8,128)(2,1)S(1)}, u32[]{:S(2)}, u32[]{:S(2)}) async-start(bf16[8,32,512]{2,1,0:T(8,128)(2,1)} %bitcast.10), calls=%async_computation.4 | async-start | bytes 524288 | tf_op jit(solution)/shard_map/all_to_all | solution.py:219

commit v4 on v3

v4 whole, which is shorter than its diff:
```python
import functools

import jax
import jax.numpy as jnp
from jax import lax
from jax.experimental import pallas as pl
from jax.experimental.pallas import tpu as pltpu
from jax.sharding import PartitionSpec as P

KEY_HEADS = 4
HEAD_SIZE = 128
TILE = 128
HEADS_PER_KEY = 8
LOG2_E = 1.4426950408889634
NEGATIVE_FILLER = -1e30
F32 = jnp.float32
BF16 = jnp.bfloat16
MIB = 1024 * 1024
VMEM = pl.BlockSpec(memory_space=pltpu.VMEM)


def dot(a, b, contract=((1,), (0,))):
    return lax.dot_general(a, b, (contract, ((), ())), preferred_element_type=F32)


def swap(x, axis, mask):
    size = lax.axis_size(axis)
    return lax.ppermute(x, axis, [(i, i ^ mask) for i in range(size)])


def project_kernel(streams, visual_ref, *refs):
    weight_refs, value_ref, out_ref, acc_ref = refs[:streams], *refs[streams:]
    step = pl.program_id(0)
    slab = weight_refs[0].shape[0]
    part = dot(visual_ref[:, :slab], weight_refs[0][...])
    for p in range(1, streams):
        part += dot(visual_ref[:, p * slab : (p + 1) * slab], weight_refs[p][...])

    @pl.when(step == 0)
    def _():
        acc_ref[...] = part

    @pl.when(step > 0)
    def _():
        acc_ref[...] += part

    @pl.when(step == pl.num_programs(0) - 1)
    def _():
        columns = acc_ref.shape[1]
        out_ref[:, :columns] = acc_ref[...].astype(BF16)
        out_ref[:, columns:] = value_ref[...]


def project(visual, key_weight, value):
    rows, features = visual.shape
    columns = key_weight.shape[1]
    steps, streams = 2, 4
    slab = features // (steps * streams)
    out = (rows, columns + value.shape[1])
    return pl.pallas_call(
        functools.partial(project_kernel, streams),
        grid=(steps,),
        in_specs=[pl.BlockSpec((rows, streams * slab), lambda k: (0, k))]
        + [
            pl.BlockSpec((slab, columns), lambda k, p=p: (k * streams + p, 0))
            for p in range(streams)
        ]
        + [pl.BlockSpec(value.shape, lambda k: (0, 0))],
        out_specs=pl.BlockSpec(out, lambda k: (0, 0)),
        out_shape=jax.ShapeDtypeStruct(out, BF16),
        scratch_shapes=[pltpu.VMEM((rows, columns), F32)],
        cost_estimate=pl.CostEstimate(
            flops=2 * rows * features * columns,
            bytes_accessed=2 * features * columns,
            transcendentals=0,
        ),
        name="project",
    )(visual, *[key_weight] * streams, value)


def attention_kernel(pieces, length_ref, frame_ref, q_ref, g_ref, visual_ref, *refs):
    kv_refs, (o_ref, qg_ref) = refs[:pieces], refs[pieces : pieces + 2]
    key_refs, value_refs = refs[pieces + 2 : 2 * pieces + 2], refs[2 * pieces + 2 : 3 * pieces + 2]
    w_all, ds_all, kg_acc, vg_acc = refs[3 * pieces + 2 :]
    j, i = pl.program_id(0), pl.program_id(1)
    block = lax.axis_index("blk")
    limit = jnp.minimum(length_ref[0], TILE * frame_ref[0, block * pl.num_programs(1) + i])
    width = KEY_HEADS * HEAD_SIZE
    head = pl.ds(pl.multiple_of(j * HEAD_SIZE, HEAD_SIZE), HEAD_SIZE)
    value_head = pl.ds(pl.multiple_of(width + j * HEAD_SIZE, HEAD_SIZE), HEAD_SIZE)
    keys = jnp.concatenate([r[:, head] for r in kv_refs], axis=0)
    values = jnp.concatenate([r[:, value_head] for r in kv_refs], axis=0)
    keys_t, values_t = keys.T, values.T
    pair = 2 * TILE
    rows = kv_refs[0].shape[0]
    row = lax.broadcasted_iota(jnp.int32, (rows, pair), 0)
    bias = jnp.concatenate(
        [
            jnp.where(row + (block ^ m) * rows < limit, 0.0, NEGATIVE_FILLER)
            for m in range(pieces)
        ],
        axis=0,
    )
    scale = HEAD_SIZE**-0.5
    q_stack, g_stack = [], []
    for h in range(0, HEADS_PER_KEY, 2):
        first = slice(h * HEAD_SIZE, (h + 1) * HEAD_SIZE)
        second = slice((h + 1) * HEAD_SIZE, (h + 2) * HEAD_SIZE)
        both = slice(h * HEAD_SIZE, (h + 2) * HEAD_SIZE)
        q = jnp.concatenate([q_ref[:, first], q_ref[:, second]], axis=0)
        g = jnp.concatenate([g_ref[:, first], g_ref[:, second]], axis=0)
        q_stack.append(q)
        g_stack.append(g)
        raw = dot(keys, q, ((1,), (1,))) + bias
        dprobs = dot(values, g, ((1,), (1,)))
        peak = jnp.max(raw, axis=0, keepdims=True)
        shifted = jnp.exp2((raw - peak) * (scale * LOG2_E))
        probs = shifted * (1.0 / jnp.sum(shifted, axis=0, keepdims=True))
        weights = probs.astype(BF16)
        terms = probs * dprobs
        delta = jnp.sum(terms, axis=0, keepdims=True)
        dscores = ((terms - probs * delta) * scale).astype(BF16)
        w_all[:, both] = weights
        ds_all[:, both] = dscores
        out = dot(values_t, weights).T.astype(BF16)
        o_ref[:, first] = out[:TILE]
        o_ref[:, second] = out[TILE:]
        grad = dot(keys_t, dscores).T.astype(BF16)
        qg_ref[:, first] = grad[:TILE]
        qg_ref[:, second] = grad[TILE:]
    kg = dot(ds_all[...], jnp.concatenate(q_stack, axis=0))
    vg = dot(w_all[...], jnp.concatenate(g_stack, axis=0))

    @pl.when(i == 0)
    def _():
        kg_acc[...] = kg
        vg_acc[...] = vg

    @pl.when(i > 0)
    def _():
        kg_acc[...] += kg
        vg_acc[...] += vg

    @pl.when(i == pl.num_programs(1) - 1)
    def _():
        for m in range(pieces):
            part = slice(m * rows, (m + 1) * rows)
            key_refs[m][:, head] = kg_acc[part, :].astype(BF16)
            value_refs[m][:, head] = vg_acc[part, :].astype(BF16)

    @pl.when(jnp.logical_and(j == 0, i == 0))
    def _():
        share = visual_ref.shape[1] // pieces
        for m in range(pieces):
            start = pl.multiple_of((block ^ m) * share, HEAD_SIZE)
            key_refs[m][:, width:] = visual_ref[:, pl.ds(start, share)]


def attention(length, frames, queries, gradients, visual, keys_values):
    pieces = len(keys_values)
    rows, both = keys_values[0].shape
    width = both // 2
    text = queries.shape[0]
    all_rows = pieces * rows
    span = HEADS_PER_KEY * HEAD_SIZE
    smem = pl.BlockSpec(memory_space=pltpu.SMEM)
    text_block = pl.BlockSpec((TILE, span), lambda j, i: (i, j))

    def whole(shape):
        return pl.BlockSpec(shape, lambda j, i: (0, 0))

    key_shape, value_shape = (rows, width + visual.shape[1] // pieces), (rows, width)
    wide = jax.ShapeDtypeStruct(queries.shape, BF16)
    out = pl.pallas_call(
        functools.partial(attention_kernel, pieces),
        grid=(KEY_HEADS, text // TILE),
        in_specs=[smem, smem, text_block, text_block, whole(visual.shape)]
        + [whole((rows, both))] * pieces,
        out_specs=[text_block] * 2 + [whole(key_shape)] * pieces + [whole(value_shape)] * pieces,
        out_shape=[wide] * 2
        + [jax.ShapeDtypeStruct(key_shape, BF16)] * pieces
        + [jax.ShapeDtypeStruct(value_shape, BF16)] * pieces,
        scratch_shapes=[
            pltpu.VMEM((all_rows, span), BF16),
            pltpu.VMEM((all_rows, span), BF16),
            pltpu.VMEM((all_rows, HEAD_SIZE), F32),
            pltpu.VMEM((all_rows, HEAD_SIZE), F32),
        ],
        cost_estimate=pl.CostEstimate(
            flops=12 * text * all_rows * KEY_HEADS * span,
            bytes_accessed=8 * text * KEY_HEADS * span,
            transcendentals=0,
        ),
        compiler_params=pltpu.CompilerParams(vmem_limit_bytes=40 * MIB),
        name="attention",
    )(length, frames, queries, gradients, visual, *keys_values)
    return out[0], out[1], out[2 : 2 + pieces], out[2 + pieces :]


def sum_kernel(pieces, *refs):
    part_refs, value_refs, out_refs = (refs[k * pieces : (k + 1) * pieces] for k in range(3))
    width = value_refs[0].shape[1]
    total = part_refs[0][:, :width].astype(F32)
    for ref in part_refs[1:]:
        total += ref[:, :width].astype(F32)
    own = total.astype(BF16)
    for m in range(pieces):
        out_refs[m][:, :width] = own
        out_refs[m][:, width:] = value_refs[m][...]


def sum_terms(parts, value_terms):
    pieces = len(parts)
    rows, width = value_terms[0].shape
    return pl.pallas_call(
        functools.partial(sum_kernel, pieces),
        in_specs=[VMEM] * (2 * pieces),
        out_specs=[VMEM] * pieces,
        out_shape=[jax.ShapeDtypeStruct((rows, 2 * width), BF16)] * pieces,
        compiler_params=pltpu.CompilerParams(vmem_limit_bytes=32 * MIB),
        name="sum_terms",
    )(*parts, *value_terms)


def weight_kernel(pieces, core_ref, *refs):
    part_refs, sum_refs = refs[:pieces], refs[pieces : 2 * pieces]
    value_ref, keep_ref, send_ref = refs[2 * pieces :]
    width = value_ref.shape[1]
    total = sum_refs[0][:, width:].astype(F32)
    for ref in sum_refs[1:]:
        total += ref[:, width:].astype(F32)
    value_ref[...] = total.astype(BF16)
    visual = jnp.concatenate([r[:, width:] for r in part_refs], axis=0)
    key_grad = jnp.concatenate([r[:, :width] for r in sum_refs], axis=0)
    product = dot(visual, key_grad, ((0,), (0,)))
    count, rows, _ = keep_ref.shape
    core = core_ref[0] == 0
    for n in range(count):
        even = product[2 * n * rows : (2 * n + 1) * rows]
        odd = product[(2 * n + 1) * rows : (2 * n + 2) * rows]
        keep_ref[n] = jnp.where(core, even, odd)
        send_ref[n] = jnp.where(core, odd, even).astype(BF16)


def weight_terms(samples, core, parts, sums):
    pieces = len(parts)
    rows, both = sums[0].shape
    width = both // 2
    features = parts[0].shape[1] - width
    half = (samples // 2, features // samples, width)
    return pl.pallas_call(
        functools.partial(weight_kernel, pieces),
        in_specs=[pl.BlockSpec(memory_space=pltpu.SMEM)] + [VMEM] * (2 * pieces),
        out_specs=[VMEM] * 3,
        out_shape=[
            jax.ShapeDtypeStruct((rows, width), BF16),
            jax.ShapeDtypeStruct(half, F32),
            jax.ShapeDtypeStruct(half, BF16),
        ],
        compiler_params=pltpu.CompilerParams(vmem_limit_bytes=32 * MIB),
        name="weight_terms",
    )(core, *parts, *sums)


def halve_kernel(bit_ref, kept_ref, came_ref, keep_ref, send_ref):
    low = bit_ref[0] == 0
    for n in range(keep_ref.shape[0]):
        even = kept_ref[2 * n] + came_ref[2 * n].astype(F32)
        odd = kept_ref[2 * n + 1] + came_ref[2 * n + 1].astype(F32)
        keep_ref[n] = jnp.where(low, even, odd)
        send_ref[n] = jnp.where(low, odd, even).astype(BF16)


def halve(bit, kept, came):
    half = (kept.shape[0] // 2, *kept.shape[1:])
    return pl.pallas_call(
        halve_kernel,
        in_specs=[pl.BlockSpec(memory_space=pltpu.SMEM), VMEM, VMEM],
        out_specs=[VMEM] * 2,
        out_shape=[jax.ShapeDtypeStruct(half, F32), jax.ShapeDtypeStruct(half, BF16)],
        compiler_params=pltpu.CompilerParams(vmem_limit_bytes=32 * MIB),
        name="halve",
    )(bit, kept, came)


def local(visual_rows, value_matrix, key_weight, queries, output_gradient, visual_len, frame_end):
    blocks, samples = lax.axis_size("blk"), lax.axis_size("dp")
    sample = lax.axis_index("dp").astype(jnp.int32)
    visual = visual_rows[0]
    masks = range(1, blocks)

    own = project(visual, key_weight, value_matrix[0])
    keys_values = [own] + [swap(own, "blk", m) for m in masks]
    attn_out, query_grad, key_terms, value_terms = attention(
        visual_len, frame_end, queries[0], output_gradient[0], visual, keys_values
    )
    parts = [key_terms[0]] + [swap(key_terms[m], "blk", m) for m in masks]
    sums = sum_terms(parts, value_terms)
    sums = [sums[0]] + [swap(sums[m], "blk", m) for m in masks]
    value_grad, kept, sent = weight_terms(samples, (sample % 2)[None], parts, sums)
    came, bit = swap(sent, "dp", 1), 1
    while kept.shape[0] > 1:
        kept, sent = halve(((sample >> bit) % 2)[None], kept, came)
        came, bit = swap(sent, "dp", 1 << bit), bit + 1
    weight_grad = kept[0] + came[0].astype(F32)
    return attn_out[None], query_grad[None], value_grad[None], weight_grad


def solution(mesh):
    return jax.shard_map(
        local,
        mesh=mesh,
        in_specs=(
            P("dp", "blk", None),
            P("dp", "blk", None),
            P(),
            P("dp", "blk", None),
            P("dp", "blk", None),
            P("dp"),
            P("dp", None),
        ),
        out_specs=(
            P("dp", "blk", None),
            P("dp", "blk", None),
            P("dp", "blk", None),
            P(("blk", "dp"), None),
        ),
        check_vma=False,
    )
```

time: 102 us -> 73.4 us (0.72)
  blocking collectives: 51.8 us -> 0 us
  starting transfers between devices: 7.17 us -> 36.9 us
  Pallas kernels: 17.7 us -> 13.8 us
  waiting for transfers between devices: 21.4 us -> 19.6 us
    all_to_all x4 -> x0, blocking collectives: 51.8 us -> none  [exchange(): return lax.all_to_all(pieces, axis, split_axis=0, concat_axis=0, tiled=True)]
    ppermute x0 -> x23, starting transfers between devices: none -> 36.9 us  [swap(): return lax.ppermute(x, axis, [(i, i ^ mask) for i in range(size)])]
    all_to_all x2 -> x0, waiting for transfers between devices: 21.4 us -> none  [exchange(): return lax.all_to_all(pieces, axis, split_axis=0, concat_axis=0, tiled=True)]
    ppermute x0 -> x23, waiting for transfers between devices: none -> 19.6 us  [swap(): return lax.ppermute(x, axis, [(i, i ^ mask) for i in range(size)])]
    all_to_all x2 -> x0, starting transfers between devices: 7.17 us -> none  [exchange(): return lax.all_to_all(pieces, axis, split_axis=0, concat_axis=0, tiled=True)]
    pallas_call x5, Pallas kernels: 17.7 us -> 13.8 us  [the longest x1 9.25 us: attention(): pl.pallas_call(functools.partial(attention_kernel, pieces), grid=(KEY_HEA...]
    reduce_sum x2 -> x0, other arithmetic: 1.42 us -> none  [the longest x1 0.77 us: local(): weight_grad = jnp.sum(exchange(weight_parts, 'dp').astype(F32), axis=0)]
  transfers between devices with their start and end apart: 2 -> 23, of which waited for: 2 -> 10; matrix products, arithmetic and copies ran while one was open for 1% -> 0% of each run, Pallas kernels for 0% -> 0%
where the time goes in v4:
time: 73.4 us; the launch traced here: 73.2 us
  starting transfers between devices  36.9 us (50%)
  waiting for transfers between devices  19.6 us (27%)
  Pallas kernels  13.8 us (19%)
  between operations  1.38 us (2%)
  local copies, waits for them, and re-layouts  0.85 us (1%)
  other arithmetic  0.74 us (1%)
    ppermute x23, starting transfers between devices, swap(): return lax.ppermute(x, axis, [(i, i ^ mask) for i in range(size)])  36.9 us
    ppermute x23, waiting for transfers between devices, swap(): return lax.ppermute(x, axis, [(i, i ^ mask) for i in range(size)])  19.6 us
    pallas_call x1, Pallas kernels, attention(): pl.pallas_call(functools.partial(attention_kernel, pieces), grid=(KEY_HEA...  9.25 us
    pallas_call x1, Pallas kernels, project(): pl.pallas_call(functools.partial(project_kernel, streams), grid=(steps,),...  3.51 us
  transfers between devices with their start and end apart: 23, of which 10 were waited for; matrix products, arithmetic and copies ran while one was open for 0% of the time, Pallas kernels for 0%

profile of v4, /device:TPU:0, one launch (start us, length us, event | category | flops | bytes accessed | tf_op | source)
XLA Modules:
  0.0 73.2 jit_solution(3710769972576121084)
XLA Ops:
  0.7 3.5 %project.1.refs_0_ = bf16[32,1024]{1,0:T(8,128)(2,1)} custom-call(bf16[32,4096]{1,0:T(8,128)(2,1)} %bitcast.11, bf16[4096,512]{1,0:T(8,128)(2,1)} %refs_3_.1, bf16[4096,512]{1,0:T(8,128)(2,1)} %refs_3_.1, bf16[4096,512]{1,0:T(8,128)(2,1)} %refs_3_.1, bf16[4096,512]{1,0:T(8,128)(2,1)} %refs_3_.1, bf16[32,512]{1,0:T(8,128)(2,1)} %bitcast.15), custom_call_target="tpu_custom_call" | custom-call | flops 134217728 | bytes 4194304 | tf_op jit(solution)/shard_map/project/pallas_call | solution.py:60
  4.2 6.0 %collective-permute-start.6 = (bf16[32,1024]{1,0:T(8,128)(2,1)}, bf16[32,1024]{1,0:T(8,128)(2,1)S(1)}, u32[]{:S(2)}, u32[]{:S(2)}) collective-permute-start(bf16[32,1024]{1,0:T(8,128)(2,1)} %project.1.refs_0_), channel_id=1, source_target_pairs={{0,28},{4,24},{8,20},{12,16},{16,12},{20,8},{24,4},{28,0},{1,29},{... | collective-permute-start | bytes 196616 | tf_op jit(solution)/shard_map/ppermute | solution.py:28
  10.4 0.7 %collective-permute-start.4 = (bf16[32,1024]{1,0:T(8,128)(2,1)}, bf16[32,1024]{1,0:T(8,128)(2,1)S(1)}, u32[]{:S(2)}, u32[]{:S(2)}) collective-permute-start(bf16[32,1024]{1,0:T(8,128)(2,1)} %project.1.refs_0_), channel_id=1, source_target_pairs={{0,20},{4,16},{8,28},{12,24},{16,4},{20,0},{24,12},{28,8},{1,21},{... | collective-permute-start | bytes 196616 | tf_op jit(solution)/shard_map/ppermute | solution.py:28
  11.1 2.0 %collective-permute-start.3 = (bf16[32,1024]{1,0:T(8,128)(2,1)}, bf16[32,1024]{1,0:T(8,128)(2,1)S(1)}, u32[]{:S(2)}, u32[]{:S(2)}) collective-permute-start(bf16[32,1024]{1,0:T(8,128)(2,1)} %project.1.refs_0_), channel_id=1, source_target_pairs={{0,16},{4,20},{8,24},{12,28},{16,0},{20,4},{24,8},{28,12},{1,17},{... | collective-permute-start | bytes 196616 | tf_op jit(solution)/shard_map/ppermute | solution.py:28
  13.1 2.4 %collective-permute-start.2 = (bf16[32,1024]{1,0:T(8,128)(2,1)}, bf16[32,1024]{1,0:T(8,128)(2,1)S(1)}, u32[]{:S(2)}, u32[]{:S(2)}) collective-permute-start(bf16[32,1024]{1,0:T(8,128)(2,1)} %project.1.refs_0_), channel_id=1, source_target_pairs={{0,12},{4,8},{8,4},{12,0},{16,28},{20,24},{24,20},{28,16},{1,13},{... | collective-permute-start | bytes 196616 | tf_op jit(solution)/shard_map/ppermute | solution.py:28
  15.5 0.8 %collective-permute-start.1 = (bf16[32,1024]{1,0:T(8,128)(2,1)}, bf16[32,1024]{1,0:T(8,128)(2,1)S(1)}, u32[]{:S(2)}, u32[]{:S(2)}) collective-permute-start(bf16[32,1024]{1,0:T(8,128)(2,1)} %project.1.refs_0_), channel_id=1, source_target_pairs={{0,8},{4,12},{8,0},{12,4},{16,24},{20,28},{24,16},{28,20},{1,9},{5... | collective-permute-start | bytes 196616 | tf_op jit(solution)/shard_map/ppermute | solution.py:28
  16.3 0.4 collective-permute-done.5.refs_6_
  16.7 0.5 collective-permute-start
  17.8 2.7 %collective-permute-done.4.refs_5_ = bf16[32,1024]{1,0:T(8,128)(2,1)S(1)} collective-permute-done((bf16[32,1024]{1,0:T(8,128)(2,1)}, bf16[32,1024]{1,0:T(8,128)(2,1)S(1)}, u32[]{:S(2)}, u32[]{:S(2)}) %collective-permute-start.4) | collective-permute-done | bytes 65568 | tf_op jit(solution)/shard_map/ppermute | solution.py:28
  20.4 1.2 %collective-permute-done.3.refs_4_ = bf16[32,1024]{1,0:T(8,128)(2,1)S(1)} collective-permute-done((bf16[32,1024]{1,0:T(8,128)(2,1)}, bf16[32,1024]{1,0:T(8,128)(2,1)S(1)}, u32[]{:S(2)}, u32[]{:S(2)}) %collective-permute-start.3) | collective-permute-done | bytes 65568 | tf_op jit(solution)/shard_map/ppermute | solution.py:28
  21.7 0.4 collective-permute-done.1.refs_2_
  22.1 0.8 %copy-done.1 = bf16[32,1024]{1,0:T(8,128)(2,1)S(1)} copy-done((bf16[32,1024]{1,0:T(8,128)(2,1)S(1)}, bf16[32,1024]{1,0:T(8,128)(2,1)}, u32[]{:S(2)}) %copy-start.1) | copy-done | bytes 65560
  22.9 9.2 %attention.1 = (bf16[128,4096]{1,0:T(8,128)(2,1)}, bf16[128,4096]{1,0:T(8,128)(2,1)}, bf16[32,1024]{1,0:T(8,128)(2,1)S(1)}, bf16[32,1024]{1,0:T(8,128)(2,1)S(1)}...) custom-call(s32[1]{0:T(128)S(6)} %copy.11.length_ref, ...), custom_call_target="tpu_custom_call" | custom-call | flops 1610612736 | bytes 4194304 | tf_op jit(solution)/shard_map/attention/pallas_call | solution.py:174
  32.2 0.6 collective-permute-start.7
  32.8 1.5 %collective-permute-start.8 = (bf16[32,1024]{1,0:T(8,128)(2,1)S(1)}, bf16[32,1024]{1,0:T(8,128)(2,1)S(1)}, u32[]{:S(2)}, u32[]{:S(2)}) collective-permute-start(bf16[32,1024]{1,0:T(8,128)(2,1)S(1)} %get-tuple-element.39), channel_id=1, source_target_pairs={{0,8},{4,12},{8,0},{12,4},{16,24},{20,28},{24,16},{28,20},{1,9},{5... | collective-permute-start | bytes 196616 | tf_op jit(solution)/shard_map/ppermute | solution.py:28
  34.4 1.5 %collective-permute-start.9 = (bf16[32,1024]{1,0:T(8,128)(2,1)S(1)}, bf16[32,1024]{1,0:T(8,128)(2,1)S(1)}, u32[]{:S(2)}, u32[]{:S(2)}) collective-permute-start(bf16[32,1024]{1,0:T(8,128)(2,1)S(1)} %get-tuple-element.40), channel_id=1, source_target_pairs={{0,12},{4,8},{8,4},{12,0},{16,28},{20,24},{24,20},{28,16},{1,13},{... | collective-permute-start | bytes 196616 | tf_op jit(solution)/shard_map/ppermute | solution.py:28
  35.8 3.2 %collective-permute-start.10 = (bf16[32,1024]{1,0:T(8,128)(2,1)S(1)}, bf16[32,1024]{1,0:T(8,128)(2,1)S(1)}, u32[]{:S(2)}, u32[]{:S(2)}) collective-permute-start(bf16[32,1024]{1,0:T(8,128)(2,1)S(1)} %get-tuple-element.41), channel_id=1, source_target_pairs={{0,16},{4,20},{8,24},{12,28},{16,0},{20,4},{24,8},{28,12},{1,17},{... | collective-permute-start | bytes 196616 | tf_op jit(solution)/shard_map/ppermute | solution.py:28
  39.1 3.6 %collective-permute-start.12 = (bf16[32,1024]{1,0:T(8,128)(2,1)S(1)}, bf16[32,1024]{1,0:T(8,128)(2,1)S(1)}, u32[]{:S(2)}, u32[]{:S(2)}) collective-permute-start(bf16[32,1024]{1,0:T(8,128)(2,1)S(1)} %get-tuple-element.43), channel_id=1, source_target_pairs={{0,24},{4,28},{8,16},{12,20},{16,8},{20,12},{24,0},{28,4},{1,25},{... | collective-permute-start | bytes 196616 | tf_op jit(solution)/shard_map/ppermute | solution.py:28
  42.6 1.2 %collective-permute-start.13 = (bf16[32,1024]{1,0:T(8,128)(2,1)S(1)}, bf16[32,1024]{1,0:T(8,128)(2,1)S(1)}, u32[]{:S(2)}, u32[]{:S(2)}) collective-permute-start(bf16[32,1024]{1,0:T(8,128)(2,1)S(1)} %get-tuple-element.44), channel_id=1, source_target_pairs={{0,28},{4,24},{8,20},{12,16},{16,12},{20,8},{24,4},{28,0},{1,29},{... | collective-permute-start | bytes 196616 | tf_op jit(solution)/shard_map/ppermute | solution.py:28
  43.8 3.0 %collective-permute-done.11.refs_5_ = bf16[32,1024]{1,0:T(8,128)(2,1)S(1)} collective-permute-done((bf16[32,1024]{1,0:T(8,128)(2,1)S(1)}, bf16[32,1024]{1,0:T(8,128)(2,1)S(1)}, u32[]{:S(2)}, u32[]{:S(2)}) %collective-permute-start.11) | collective-permute-done | bytes 65568 | tf_op jit(solution)/shard_map/ppermute | solution.py:28
  46.8 3.3 %collective-permute-done.13.refs_7_ = bf16[32,1024]{1,0:T(8,128)(2,1)S(1)} collective-permute-done((bf16[32,1024]{1,0:T(8,128)(2,1)S(1)}, bf16[32,1024]{1,0:T(8,128)(2,1)S(1)}, u32[]{:S(2)}, u32[]{:S(2)}) %collective-permute-start.13) | collective-permute-done | bytes 65568 | tf_op jit(solution)/shard_map/ppermute | solution.py:28
  50.3 3.3 %collective-permute-start.16 = (bf16[32,1024]{1,0:T(8,128)(2,1)S(1)}, bf16[32,1024]{1,0:T(8,128)(2,1)S(1)}, u32[]{:S(2)}, u32[]{:S(2)}) collective-permute-start(bf16[32,1024]{1,0:T(8,128)(2,1)S(1)} %get-tuple-element.56), channel_id=1, source_target_pairs={{0,12},{4,8},{8,4},{12,0},{16,28},{20,24},{24,20},{28,16},{1,13},{... | collective-permute-start | bytes 196616 | tf_op jit(solution)/shard_map/ppermute | solution.py:28
  53.7 2.5 %collective-permute-start.18 = (bf16[32,1024]{1,0:T(8,128)(2,1)S(1)}, bf16[32,1024]{1,0:T(8,128)(2,1)S(1)}, u32[]{:S(2)}, u32[]{:S(2)}) collective-permute-start(bf16[32,1024]{1,0:T(8,128)(2,1)S(1)} %get-tuple-element.58), channel_id=1, source_target_pairs={{0,20},{4,16},{8,28},{12,24},{16,4},{20,0},{24,12},{28,8},{1,21},{... | collective-permute-start | bytes 196616 | tf_op jit(solution)/shard_map/ppermute | solution.py:28
  56.2 1.2 %collective-permute-start.19 = (bf16[32,1024]{1,0:T(8,128)(2,1)S(1)}, bf16[32,1024]{1,0:T(8,128)(2,1)S(1)}, u32[]{:S(2)}, u32[]{:S(2)}) collective-permute-start(bf16[32,1024]{1,0:T(8,128)(2,1)S(1)} %get-tuple-element.59), channel_id=1, source_target_pairs={{0,24},{4,28},{8,16},{12,20},{16,8},{20,12},{24,0},{28,4},{1,25},{... | collective-permute-start | bytes 196616 | tf_op jit(solution)/shard_map/ppermute | solution.py:28
  57.4 4.0 %collective-permute-start.20 = (bf16[32,1024]{1,0:T(8,128)(2,1)S(1)}, bf16[32,1024]{1,0:T(8,128)(2,1)S(1)}, u32[]{:S(2)}, u32[]{:S(2)}) collective-permute-start(bf16[32,1024]{1,0:T(8,128)(2,1)S(1)} %get-tuple-element.60), channel_id=1, source_target_pairs={{0,28},{4,24},{8,20},{12,16},{16,12},{20,8},{24,4},{28,0},{1,29},{... | collective-permute-start | bytes 196616 | tf_op jit(solution)/shard_map/ppermute | solution.py:28
  61.4 1.0 %collective-permute-done.19.refs_14_ = bf16[32,1024]{1,0:T(8,128)(2,1)S(1)} collective-permute-done((bf16[32,1024]{1,0:T(8,128)(2,1)S(1)}, bf16[32,1024]{1,0:T(8,128)(2,1)S(1)}, u32[]{:S(2)}, u32[]{:S(2)}) %collective-permute-start.19) | collective-permute-done | bytes 65568 | tf_op jit(solution)/shard_map/ppermute | solution.py:28
  62.4 2.0 %collective-permute-done.20.refs_15_ = bf16[32,1024]{1,0:T(8,128)(2,1)S(1)} collective-permute-done((bf16[32,1024]{1,0:T(8,128)(2,1)S(1)}, bf16[32,1024]{1,0:T(8,128)(2,1)S(1)}, u32[]{:S(2)}, u32[]{:S(2)}) %collective-permute-start.20) | collective-permute-done | bytes 65568 | tf_op jit(solution)/shard_map/ppermute | solution.py:28
  64.4 0.9 %weight_terms.1 = (bf16[32,512]{1,0:T(8,128)(2,1)}, f32[2,128,512]{2,1,0:T(8,128)S(1)}, bf16[2,128,512]{2,1,0:T(8,128)(2,1)S(1)}) custom-call(s32[1]{0:T(128)} %bitcast.6.core_ref, bf16[32,1024]{1,0:T(8,128)(2,1)S(1)} %get-tuple-element.37.refs_0_, bf16[32,1024]{1,0:T(8,128)(2,1)S(1)} %collective-permute-done.7.refs_1_, ...), custom_call_target="tpu_custom_call" | custom-call | tf_op jit(solution)/shard_map/weight_terms/pallas_call | solution.py:251
  65.3 1.5 %collective-permute-done.21.came_ref = bf16[2,128,512]{2,1,0:T(8,128)(2,1)S(1)} collective-permute-done((bf16[2,128,512]{2,1,0:T(8,128)(2,1)S(1)}, bf16[2,128,512]{2,1,0:T(8,128)(2,1)S(1)}, u32[]{:S(2)}, u32[]{:S(2)}) %collective-permute-start.21) | collective-permute-done | bytes 262176 | tf_op jit(solution)/shard_map/ppermute | solution.py:28
  66.9 1.6 %collective-permute-start.22 = (bf16[1,128,512]{2,1,0:T(8,128)(2,1)S(1)}, bf16[1,128,512]{2,1,0:T(8,128)(2,1)S(1)}, u32[]{:S(2)}, u32[]{:S(2)}) collective-permute-start(bf16[1,128,512]{2,1,0:T(8,128)(2,1)S(1)} %get-tuple-element.65), channel_id=1, source_target_pairs={{0,2},{1,3},{2,0},{3,1},{4,6},{5,7},{6,4},{7,5},{8,10},{9,11},{10,... | collective-permute-start | bytes 393224 | tf_op jit(solution)/shard_map/ppermute | solution.py:28
  68.4 4.0 %collective-permute-done.22 = bf16[1,128,512]{2,1,0:T(8,128)(2,1)S(1)} collective-permute-done((bf16[1,128,512]{2,1,0:T(8,128)(2,1)S(1)}, bf16[1,128,512]{2,1,0:T(8,128)(2,1)S(1)}, u32[]{:S(2)}, u32[]{:S(2)}) %collective-permute-start.22) | collective-permute-done | bytes 131104 | tf_op jit(solution)/shard_map/ppermute | solution.py:28
  72.5 0.7 %add_bitcast_fusion = f32[128,512]{1,0:T(8,128)} fusion(f32[1,128,512]{2,1,0:T(8,128)S(1)} %get-tuple-element.64, bf16[1,128,512]{2,1,0:T(8,128)(2,1)S(1)} %collective-permute-done.22), kind=kLoop, calls=%fused_computation | loop fusion | flops 131072 | bytes 655360 | tf_op jit(solution)/shard_map/add | solution.py:305
  (30 shorter events, 0.6 us)
Async XLA Ops:
  0.6 21.4 %copy-start = (bf16[1,32,4096]{2,1,0:T(8,128)(2,1)S(1)}, bf16[1,32,4096]{2,1,0:T(8,128)(2,1)}, u32[]{:S(2)}) copy-start(bf16[1,32,4096]{2,1,0:T(8,128)(2,1)} %param.7) | copy-start | bytes 786436
  0.6 21.4 %copy-start.2 = (bf16[1,128,4096]{2,1,0:T(8,128)(2,1)S(1)}, bf16[1,128,4096]{2,1,0:T(8,128)(2,1)}, u32[]{:S(2)}) copy-start(bf16[1,128,4096]{2,1,0:T(8,128)(2,1)} %param.10) | copy-start | bytes 3145732
  0.7 21.4 %copy-start.3 = (bf16[1,128,4096]{2,1,0:T(8,128)(2,1)S(1)}, bf16[1,128,4096]{2,1,0:T(8,128)(2,1)}, u32[]{:S(2)}) copy-start(bf16[1,128,4096]{2,1,0:T(8,128)(2,1)} %param.11) | copy-start | bytes 3145732
  0.7 21.4 %copy-start.4 = (s32[1,8]{1,0:T(1,128)S(1)}, s32[1,8]{1,0:T(1,128)}, u32[]{:S(2)}) copy-start(s32[1,8]{1,0:T(1,128)} %frame_ref.1) | copy-start | bytes 100
  4.2 11.3 %collective-permute-start.6 = (bf16[32,1024]{1,0:T(8,128)(2,1)}, bf16[32,1024]{1,0:T(8,128)(2,1)S(1)}, u32[]{:S(2)}, u32[]{:S(2)}) collective-permute-start(bf16[32,1024]{1,0:T(8,128)(2,1)} %project.1.refs_0_), channel_id=1, source_target_pairs={{0,28},{4,24},{8,20},{12,16},{16,12},{20,8},{24,4},{28,0},{1,29},{... | collective-permute-start | bytes 196616 | tf_op jit(solution)/shard_map/ppermute | solution.py:28
  10.2 6.5 %collective-permute-start.5 = (bf16[32,1024]{1,0:T(8,128)(2,1)}, bf16[32,1024]{1,0:T(8,128)(2,1)S(1)}, u32[]{:S(2)}, u32[]{:S(2)}) collective-permute-start(bf16[32,1024]{1,0:T(8,128)(2,1)} %project.1.refs_0_), channel_id=1, source_target_pairs={{0,24},{4,28},{8,16},{12,20},{16,8},{20,12},{24,0},{28,4},{1,25},{... | collective-permute-start | bytes 196616 | tf_op jit(solution)/shard_map/ppermute | solution.py:28
  10.4 10.0 %collective-permute-start.4 = (bf16[32,1024]{1,0:T(8,128)(2,1)}, bf16[32,1024]{1,0:T(8,128)(2,1)S(1)}, u32[]{:S(2)}, u32[]{:S(2)}) collective-permute-start(bf16[32,1024]{1,0:T(8,128)(2,1)} %project.1.refs_0_), channel_id=1, source_target_pairs={{0,20},{4,16},{8,28},{12,24},{16,4},{20,0},{24,12},{28,8},{1,21},{... | collective-permute-start | bytes 196616 | tf_op jit(solution)/shard_map/ppermute | solution.py:28
  11.1 10.5 %collective-permute-start.3 = (bf16[32,1024]{1,0:T(8,128)(2,1)}, bf16[32,1024]{1,0:T(8,128)(2,1)S(1)}, u32[]{:S(2)}, u32[]{:S(2)}) collective-permute-start(bf16[32,1024]{1,0:T(8,128)(2,1)} %project.1.refs_0_), channel_id=1, source_target_pairs={{0,16},{4,20},{8,24},{12,28},{16,0},{20,4},{24,8},{28,12},{1,17},{... | collective-permute-start | bytes 196616 | tf_op jit(solution)/shard_map/ppermute | solution.py:28
  13.1 8.5 %collective-permute-start.2 = (bf16[32,1024]{1,0:T(8,128)(2,1)}, bf16[32,1024]{1,0:T(8,128)(2,1)S(1)}, u32[]{:S(2)}, u32[]{:S(2)}) collective-permute-start(bf16[32,1024]{1,0:T(8,128)(2,1)} %project.1.refs_0_), channel_id=1, source_target_pairs={{0,12},{4,8},{8,4},{12,0},{16,28},{20,24},{24,20},{28,16},{1,13},{... | collective-permute-start | bytes 196616 | tf_op jit(solution)/shard_map/ppermute | solution.py:28
  15.5 6.6 %collective-permute-start.1 = (bf16[32,1024]{1,0:T(8,128)(2,1)}, bf16[32,1024]{1,0:T(8,128)(2,1)S(1)}, u32[]{:S(2)}, u32[]{:S(2)}) collective-permute-start(bf16[32,1024]{1,0:T(8,128)(2,1)} %project.1.refs_0_), channel_id=1, source_target_pairs={{0,8},{4,12},{8,0},{12,4},{16,24},{20,28},{24,16},{28,20},{1,9},{5... | collective-permute-start | bytes 196616 | tf_op jit(solution)/shard_map/ppermute | solution.py:28
  16.7 5.4 %collective-permute-start = (bf16[32,1024]{1,0:T(8,128)(2,1)}, bf16[32,1024]{1,0:T(8,128)(2,1)S(1)}, u32[]{:S(2)}, u32[]{:S(2)}) collective-permute-start(bf16[32,1024]{1,0:T(8,128)(2,1)} %project.1.refs_0_), channel_id=1, source_target_pairs={{0,4},{4,0},{8,12},{12,8},{16,20},{20,16},{24,28},{28,24},{1,5},{5... | collective-permute-start | bytes 196616 | tf_op jit(solution)/shard_map/ppermute | solution.py:28
  22.1 0.8 %copy-start.1 = (bf16[32,1024]{1,0:T(8,128)(2,1)S(1)}, bf16[32,1024]{1,0:T(8,128)(2,1)}, u32[]{:S(2)}) copy-start(bf16[32,1024]{1,0:T(8,128)(2,1)} %project.1.refs_0_) | copy-start | bytes 196612
  32.2 6.9 %collective-permute-start.7 = (bf16[32,1024]{1,0:T(8,128)(2,1)S(1)}, bf16[32,1024]{1,0:T(8,128)(2,1)S(1)}, u32[]{:S(2)}, u32[]{:S(2)}) collective-permute-start(bf16[32,1024]{1,0:T(8,128)(2,1)S(1)} %get-tuple-element.38), channel_id=1, source_target_pairs={{0,4},{4,0},{8,12},{12,8},{16,20},{20,16},{24,28},{28,24},{1,5},{5... | collective-permute-start | bytes 196616 | tf_op jit(solution)/shard_map/ppermute | solution.py:28
  32.8 9.8 %collective-permute-start.8 = (bf16[32,1024]{1,0:T(8,128)(2,1)S(1)}, bf16[32,1024]{1,0:T(8,128)(2,1)S(1)}, u32[]{:S(2)}, u32[]{:S(2)}) collective-permute-start(bf16[32,1024]{1,0:T(8,128)(2,1)S(1)} %get-tuple-element.39), channel_id=1, source_target_pairs={{0,8},{4,12},{8,0},{12,4},{16,24},{20,28},{24,16},{28,20},{1,9},{5... | collective-permute-start | bytes 196616 | tf_op jit(solution)/shard_map/ppermute | solution.py:28
  34.4 9.4 %collective-permute-start.9 = (bf16[32,1024]{1,0:T(8,128)(2,1)S(1)}, bf16[32,1024]{1,0:T(8,128)(2,1)S(1)}, u32[]{:S(2)}, u32[]{:S(2)}) collective-permute-start(bf16[32,1024]{1,0:T(8,128)(2,1)S(1)} %get-tuple-element.40), channel_id=1, source_target_pairs={{0,12},{4,8},{8,4},{12,0},{16,28},{20,24},{24,20},{28,16},{1,13},{... | collective-permute-start | bytes 196616 | tf_op jit(solution)/shard_map/ppermute | solution.py:28
  35.8 8.0 %collective-permute-start.10 = (bf16[32,1024]{1,0:T(8,128)(2,1)S(1)}, bf16[32,1024]{1,0:T(8,128)(2,1)S(1)}, u32[]{:S(2)}, u32[]{:S(2)}) collective-permute-start(bf16[32,1024]{1,0:T(8,128)(2,1)S(1)} %get-tuple-element.41), channel_id=1, source_target_pairs={{0,16},{4,20},{8,24},{12,28},{16,0},{20,4},{24,8},{28,12},{1,17},{... | collective-permute-start | bytes 196616 | tf_op jit(solution)/shard_map/ppermute | solution.py:28
  39.0 7.8 %collective-permute-start.11 = (bf16[32,1024]{1,0:T(8,128)(2,1)S(1)}, bf16[32,1024]{1,0:T(8,128)(2,1)S(1)}, u32[]{:S(2)}, u32[]{:S(2)}) collective-permute-start(bf16[32,1024]{1,0:T(8,128)(2,1)S(1)} %get-tuple-element.42), channel_id=1, source_target_pairs={{0,20},{4,16},{8,28},{12,24},{16,4},{20,0},{24,12},{28,8},{1,21},{... | collective-permute-start | bytes 196616 | tf_op jit(solution)/shard_map/ppermute | solution.py:28
  39.1 7.8 %collective-permute-start.12 = (bf16[32,1024]{1,0:T(8,128)(2,1)S(1)}, bf16[32,1024]{1,0:T(8,128)(2,1)S(1)}, u32[]{:S(2)}, u32[]{:S(2)}) collective-permute-start(bf16[32,1024]{1,0:T(8,128)(2,1)S(1)} %get-tuple-element.43), channel_id=1, source_target_pairs={{0,24},{4,28},{8,16},{12,20},{16,8},{20,12},{24,0},{28,4},{1,25},{... | collective-permute-start | bytes 196616 | tf_op jit(solution)/shard_map/ppermute | solution.py:28
  42.6 7.5 %collective-permute-start.13 = (bf16[32,1024]{1,0:T(8,128)(2,1)S(1)}, bf16[32,1024]{1,0:T(8,128)(2,1)S(1)}, u32[]{:S(2)}, u32[]{:S(2)}) collective-permute-start(bf16[32,1024]{1,0:T(8,128)(2,1)S(1)} %get-tuple-element.44), channel_id=1, source_target_pairs={{0,28},{4,24},{8,20},{12,16},{16,12},{20,8},{24,4},{28,0},{1,29},{... | collective-permute-start | bytes 196616 | tf_op jit(solution)/shard_map/ppermute | solution.py:28
  50.1 6.1 %collective-permute-start.14 = (bf16[32,1024]{1,0:T(8,128)(2,1)S(1)}, bf16[32,1024]{1,0:T(8,128)(2,1)S(1)}, u32[]{:S(2)}, u32[]{:S(2)}) collective-permute-start(bf16[32,1024]{1,0:T(8,128)(2,1)S(1)} %get-tuple-element.54), channel_id=1, source_target_pairs={{0,4},{4,0},{8,12},{12,8},{16,20},{20,16},{24,28},{28,24},{1,5},{5... | collective-permute-start | bytes 196616 | tf_op jit(solution)/shard_map/ppermute | solution.py:28
  50.3 7.1 %collective-permute-start.15 = (bf16[32,1024]{1,0:T(8,128)(2,1)S(1)}, bf16[32,1024]{1,0:T(8,128)(2,1)S(1)}, u32[]{:S(2)}, u32[]{:S(2)}) collective-permute-start(bf16[32,1024]{1,0:T(8,128)(2,1)S(1)} %get-tuple-element.55), channel_id=1, source_target_pairs={{0,8},{4,12},{8,0},{12,4},{16,24},{20,28},{24,16},{28,20},{1,9},{5... | collective-permute-start | bytes 196616 | tf_op jit(solution)/shard_map/ppermute | solution.py:28
  50.3 11.0 %collective-permute-start.16 = (bf16[32,1024]{1,0:T(8,128)(2,1)S(1)}, bf16[32,1024]{1,0:T(8,128)(2,1)S(1)}, u32[]{:S(2)}, u32[]{:S(2)}) collective-permute-start(bf16[32,1024]{1,0:T(8,128)(2,1)S(1)} %get-tuple-element.56), channel_id=1, source_target_pairs={{0,12},{4,8},{8,4},{12,0},{16,28},{20,24},{24,20},{28,16},{1,13},{... | collective-permute-start | bytes 196616 | tf_op jit(solution)/shard_map/ppermute | solution.py:28
  53.7 7.7 %collective-permute-start.17 = (bf16[32,1024]{1,0:T(8,128)(2,1)S(1)}, bf16[32,1024]{1,0:T(8,128)(2,1)S(1)}, u32[]{:S(2)}, u32[]{:S(2)}) collective-permute-start(bf16[32,1024]{1,0:T(8,128)(2,1)S(1)} %get-tuple-element.57), channel_id=1, source_target_pairs={{0,16},{4,20},{8,24},{12,28},{16,0},{20,4},{24,8},{28,12},{1,17},{... | collective-permute-start | bytes 196616 | tf_op jit(solution)/shard_map/ppermute | solution.py:28
  53.7 7.7 %collective-permute-start.18 = (bf16[32,1024]{1,0:T(8,128)(2,1)S(1)}, bf16[32,1024]{1,0:T(8,128)(2,1)S(1)}, u32[]{:S(2)}, u32[]{:S(2)}) collective-permute-start(bf16[32,1024]{1,0:T(8,128)(2,1)S(1)} %get-tuple-element.58), channel_id=1, source_target_pairs={{0,20},{4,16},{8,28},{12,24},{16,4},{20,0},{24,12},{28,8},{1,21},{... | collective-permute-start | bytes 196616 | tf_op jit(solution)/shard_map/ppermute | solution.py:28
  56.2 6.2 %collective-permute-start.19 = (bf16[32,1024]{1,0:T(8,128)(2,1)S(1)}, bf16[32,1024]{1,0:T(8,128)(2,1)S(1)}, u32[]{:S(2)}, u32[]{:S(2)}) collective-permute-start(bf16[32,1024]{1,0:T(8,128)(2,1)S(1)} %get-tuple-element.59), channel_id=1, source_target_pairs={{0,24},{4,28},{8,16},{12,20},{16,8},{20,12},{24,0},{28,4},{1,25},{... | collective-permute-start | bytes 196616 | tf_op jit(solution)/shard_map/ppermute | solution.py:28
  57.4 7.0 %collective-permute-start.20 = (bf16[32,1024]{1,0:T(8,128)(2,1)S(1)}, bf16[32,1024]{1,0:T(8,128)(2,1)S(1)}, u32[]{:S(2)}, u32[]{:S(2)}) collective-permute-start(bf16[32,1024]{1,0:T(8,128)(2,1)S(1)} %get-tuple-element.60), channel_id=1, source_target_pairs={{0,28},{4,24},{8,20},{12,16},{16,12},{20,8},{24,4},{28,0},{1,29},{... | collective-permute-start | bytes 196616 | tf_op jit(solution)/shard_map/ppermute | solution.py:28
  65.3 1.5 %collective-permute-start.21 = (bf16[2,128,512]{2,1,0:T(8,128)(2,1)S(1)}, bf16[2,128,512]{2,1,0:T(8,128)(2,1)S(1)}, u32[]{:S(2)}, u32[]{:S(2)}) collective-permute-start(bf16[2,128,512]{2,1,0:T(8,128)(2,1)S(1)} %get-tuple-element.63), channel_id=1, source_target_pairs={{0,1},{1,0},{2,3},{3,2},{4,5},{5,4},{6,7},{7,6},{8,9},{9,8},{10,11... | collective-permute-start | bytes 786440 | tf_op jit(solution)/shard_map/ppermute | solution.py:28
  66.9 5.6 %collective-permute-start.22 = (bf16[1,128,512]{2,1,0:T(8,128)(2,1)S(1)}, bf16[1,128,512]{2,1,0:T(8,128)(2,1)S(1)}, u32[]{:S(2)}, u32[]{:S(2)}) collective-permute-start(bf16[1,128,512]{2,1,0:T(8,128)(2,1)S(1)} %get-tuple-element.65), channel_id=1, source_target_pairs={{0,2},{1,3},{2,0},{3,1},{4,6},{5,7},{6,4},{7,5},{8,10},{9,11},{10,... | collective-permute-start | bytes 393224 | tf_op jit(solution)/shard_map/ppermute | solution.py:28

commit v5 on v4

v5 whole, which is shorter than its diff:
```python
import functools

import jax
import jax.numpy as jnp
from jax import lax
from jax.experimental import pallas as pl
from jax.experimental.pallas import tpu as pltpu
from jax.sharding import PartitionSpec as P

KEY_HEADS = 4
HEAD_SIZE = 128
TILE = 128
HEADS_PER_KEY = 8
LOG2_E = 1.4426950408889634
NEGATIVE_FILLER = -1e30
F32 = jnp.float32
BF16 = jnp.bfloat16
MIB = 1024 * 1024
VMEM = pl.BlockSpec(memory_space=pltpu.VMEM)


def dot(a, b, contract=((1,), (0,))):
    return lax.dot_general(a, b, (contract, ((), ())), preferred_element_type=F32)


def swap(x, axis, mask):
    size = lax.axis_size(axis)
    return lax.ppermute(x, axis, [(i, i ^ mask) for i in range(size)])


def partner(piece, pieces):
    return (pieces - piece) % pieces


def project_kernel(chunks, weight_hbm, visual_ref, value_ref, out_ref, weight, sems):
    slab = weight.shape[0] // chunks
    copies = []
    for c in range(chunks):
        part = pl.ds(c * slab, slab)
        copies.append(pltpu.make_async_copy(weight_hbm.at[part], weight.at[part], sems.at[c]))
        copies[c].start()
    keys = jnp.zeros((visual_ref.shape[0], weight.shape[1]), F32)
    for c in range(chunks):
        copies[c].wait()
        part = slice(c * slab, (c + 1) * slab)
        keys += dot(visual_ref[:, part], weight[part, :])
    columns = weight.shape[1]
    out_ref[:, :columns] = keys.astype(BF16)
    out_ref[:, columns:] = value_ref[...]


def project(visual, key_weight, value):
    rows, features = visual.shape
    columns = key_weight.shape[1]
    chunks = 16
    return pl.pallas_call(
        functools.partial(project_kernel, chunks),
        in_specs=[pl.BlockSpec(memory_space=pltpu.HBM), VMEM, VMEM],
        out_specs=VMEM,
        out_shape=jax.ShapeDtypeStruct((rows, columns + value.shape[1]), BF16),
        scratch_shapes=[
            pltpu.VMEM(key_weight.shape, BF16),
            pltpu.SemaphoreType.DMA((chunks,)),
        ],
        cost_estimate=pl.CostEstimate(
            flops=2 * rows * features * columns,
            bytes_accessed=2 * features * columns,
            transcendentals=0,
        ),
        name="project",
    )(key_weight, visual, value)


def scores_kernel(pieces, length_ref, frame_ref, q_ref, g_ref, visual_hbm, *refs):
    kv_refs, (w_ref, ds_ref) = refs[:pieces], refs[pieces : pieces + 2]
    key_refs = refs[pieces + 2 : 2 * pieces + 2]
    kg_acc, visual, sem = refs[2 * pieces + 2 :]
    j, i = pl.program_id(0), pl.program_id(1)
    last = jnp.logical_and(j == pl.num_programs(0) - 1, i == pl.num_programs(1) - 1)
    copy = pltpu.make_async_copy(visual_hbm, visual, sem)

    @pl.when(jnp.logical_and(j == 0, i == 0))
    def _():
        copy.start()

    block = lax.axis_index("blk")
    limit = jnp.minimum(length_ref[0], TILE * frame_ref[0, block * pl.num_programs(1) + i])
    width = KEY_HEADS * HEAD_SIZE
    head = pl.ds(pl.multiple_of(j * HEAD_SIZE, HEAD_SIZE), HEAD_SIZE)
    value_head = pl.ds(pl.multiple_of(width + j * HEAD_SIZE, HEAD_SIZE), HEAD_SIZE)
    keys = jnp.concatenate([r[:, head] for r in kv_refs], axis=0)
    values = jnp.concatenate([r[:, value_head] for r in kv_refs], axis=0)
    pair = 2 * TILE
    rows = kv_refs[0].shape[0]
    row = lax.broadcasted_iota(jnp.int32, (rows, pair), 0)
    bias = jnp.concatenate(
        [
            jnp.where(row + (block ^ partner(m, pieces)) * rows < limit, 0.0, NEGATIVE_FILLER)
            for m in range(pieces)
        ],
        axis=0,
    )
    scale = HEAD_SIZE**-0.5
    pairs = HEADS_PER_KEY // 2
    q_stack, raw, dprobs = [], {}, {}

    def stacked(ref, p):
        first = slice(p * pair, p * pair + HEAD_SIZE)
        second = slice(p * pair + HEAD_SIZE, (p + 1) * pair)
        return jnp.concatenate([ref[:, first], ref[:, second]], axis=0)

    def products(p):
        q_stack.append(stacked(q_ref, p))
        raw[p] = dot(keys, q_stack[p], ((1,), (1,)))
        dprobs[p] = dot(values, stacked(g_ref, p), ((1,), (1,)))

    products(0)
    for p in range(pairs):
        if p + 1 < pairs:
            products(p + 1)
        scores = raw.pop(p) + bias
        peak = jnp.max(scores, axis=0, keepdims=True)
        shifted = jnp.exp2((scores - peak) * (scale * LOG2_E))
        probs = shifted * (1.0 / jnp.sum(shifted, axis=0, keepdims=True))
        terms = probs * dprobs.pop(p)
        delta = jnp.sum(terms, axis=0, keepdims=True)
        both = slice(p * pair, (p + 1) * pair)
        w_ref[:, both] = probs.astype(BF16)
        ds_ref[:, both] = ((terms - probs * delta) * scale).astype(BF16)
    kg = dot(ds_ref[...], jnp.concatenate(q_stack, axis=0))

    @pl.when(i == 0)
    def _():
        kg_acc[...] = kg

    @pl.when(i > 0)
    def _():
        kg_acc[...] += kg

    @pl.when(i == pl.num_programs(1) - 1)
    def _():
        for m in range(pieces):
            key_refs[m][:, head] = kg_acc[m * rows : (m + 1) * rows, :].astype(BF16)

    @pl.when(last)
    def _():
        copy.wait()
        share = visual.shape[1] // pieces
        for m in range(pieces):
            start = pl.multiple_of((block ^ partner(m, pieces)) * share, HEAD_SIZE)
            key_refs[m][:, width:] = visual[:, pl.ds(start, share)]


def values_kernel(pieces, g_ref, w_ref, *refs):
    value_refs, vg_acc = refs[:pieces], refs[pieces]
    j, i = pl.program_id(0), pl.program_id(1)
    head = pl.ds(pl.multiple_of(j * HEAD_SIZE, HEAD_SIZE), HEAD_SIZE)
    rows = value_refs[0].shape[0]
    stack = [g_ref[:, h * HEAD_SIZE : (h + 1) * HEAD_SIZE] for h in range(HEADS_PER_KEY)]
    vg = dot(w_ref[...], jnp.concatenate(stack, axis=0))

    @pl.when(i == 0)
    def _():
        vg_acc[...] = vg

    @pl.when(i > 0)
    def _():
        vg_acc[...] += vg

    @pl.when(i == pl.num_programs(1) - 1)
    def _():
        for m in range(pieces):
            value_refs[m][:, head] = vg_acc[m * rows : (m + 1) * rows, :].astype(BF16)


def outputs_kernel(pieces, w_ref, ds_ref, *refs):
    kv_refs, (o_ref, qg_ref) = refs[:pieces], refs[pieces:]
    j = pl.program_id(0)
    width = KEY_HEADS * HEAD_SIZE
    head = pl.ds(pl.multiple_of(j * HEAD_SIZE, HEAD_SIZE), HEAD_SIZE)
    value_head = pl.ds(pl.multiple_of(width + j * HEAD_SIZE, HEAD_SIZE), HEAD_SIZE)
    keys_t = jnp.concatenate([r[:, head] for r in kv_refs], axis=0).T
    values_t = jnp.concatenate([r[:, value_head] for r in kv_refs], axis=0).T
    pair = 2 * TILE
    for p in range(HEADS_PER_KEY // 2):
        first = slice(p * pair, p * pair + HEAD_SIZE)
        second = slice(p * pair + HEAD_SIZE, (p + 1) * pair)
        both = slice(p * pair, (p + 1) * pair)
        out = dot(values_t, w_ref[:, both]).T.astype(BF16)
        grad = dot(keys_t, ds_ref[:, both]).T.astype(BF16)
        o_ref[:, first] = out[:TILE]
        o_ref[:, second] = out[TILE:]
        qg_ref[:, first] = grad[:TILE]
        qg_ref[:, second] = grad[TILE:]


class Attention:
    def __init__(self, queries, pieces, rows):
        self.pieces, self.rows = pieces, rows
        self.text, self.wide = queries.shape
        self.tiles = self.text // TILE
        self.all_rows = pieces * rows
        self.width = KEY_HEADS * HEAD_SIZE
        span = HEADS_PER_KEY * HEAD_SIZE
        tiles = self.tiles
        self.text_block = pl.BlockSpec((TILE, span), lambda j, i: (i, j))
        self.inner_block = pl.BlockSpec((self.all_rows, span), lambda j, i: (0, j * tiles + i))
        self.inner = jax.ShapeDtypeStruct((self.all_rows, tiles * self.wide), BF16)

    def whole(self, columns):
        return pl.BlockSpec((self.rows, columns), lambda j, i: (0, 0))

    def call(self, kernel, products, moved, name, **specs):
        return pl.pallas_call(
            functools.partial(kernel, self.pieces),
            grid=(KEY_HEADS, self.tiles),
            cost_estimate=pl.CostEstimate(
                flops=2 * products * self.text * self.all_rows * self.wide,
                bytes_accessed=2 * moved * self.text * self.wide,
                transcendentals=0,
            ),
            compiler_params=pltpu.CompilerParams(vmem_limit_bytes=32 * MIB),
            name=name,
            **specs,
        )

    def scores(self, length, frames, queries, gradients, visual, keys_values):
        smem = pl.BlockSpec(memory_space=pltpu.SMEM)
        hbm = pl.BlockSpec(memory_space=pltpu.HBM)
        columns = self.width + visual.shape[1] // self.pieces
        piece = jax.ShapeDtypeStruct((self.rows, columns), BF16)
        out = self.call(
            scores_kernel,
            6,
            4,
            "scores",
            in_specs=[smem, smem, self.text_block, self.text_block, hbm]
            + [self.whole(2 * self.width)] * self.pieces,
            out_specs=[self.inner_block] * 2 + [self.whole(columns)] * self.pieces,
            out_shape=[self.inner] * 2 + [piece] * self.pieces,
            scratch_shapes=[
                pltpu.VMEM((self.all_rows, HEAD_SIZE), F32),
                pltpu.VMEM(visual.shape, BF16),
                pltpu.SemaphoreType.DMA,
            ],
        )(length, frames, queries, gradients, visual, *keys_values)
        return out[0], out[1], out[2:]

    def values(self, gradients, weights):
        piece = jax.ShapeDtypeStruct((self.rows, self.width), BF16)
        return self.call(
            values_kernel,
            1,
            2,
            "values",
            in_specs=[self.text_block, self.inner_block],
            out_specs=[self.whole(self.width)] * self.pieces,
            out_shape=[piece] * self.pieces,
            scratch_shapes=[pltpu.VMEM((self.all_rows, HEAD_SIZE), F32)],
        )(gradients, weights)

    def outputs(self, weights, dscores, keys_values):
        return self.call(
            outputs_kernel,
            2,
            4,
            "outputs",
            in_specs=[self.inner_block] * 2 + [self.whole(2 * self.width)] * self.pieces,
            out_specs=[self.text_block] * 2,
            out_shape=[jax.ShapeDtypeStruct((self.text, self.wide), BF16)] * 2,
        )(weights, dscores, *keys_values)


def sum_kernel(pieces, *refs):
    part_refs, value_refs, out_refs = (refs[k * pieces : (k + 1) * pieces] for k in range(3))
    width = value_refs[0].shape[1]
    total = part_refs[0][:, :width].astype(F32)
    for ref in part_refs[1:]:
        total += ref[:, :width].astype(F32)
    own = total.astype(BF16)
    for m in range(pieces):
        out_refs[m][:, :width] = own
        out_refs[m][:, width:] = value_refs[m][...]


def sum_terms(parts, value_terms):
    pieces = len(parts)
    rows, width = value_terms[0].shape
    return pl.pallas_call(
        functools.partial(sum_kernel, pieces),
        in_specs=[VMEM] * (2 * pieces),
        out_specs=[VMEM] * pieces,
        out_shape=[jax.ShapeDtypeStruct((rows, 2 * width), BF16)] * pieces,
        compiler_params=pltpu.CompilerParams(vmem_limit_bytes=32 * MIB),
        name="sum_terms",
    )(*parts, *value_terms)


def weight_kernel(pieces, core_ref, *refs):
    part_refs, sum_refs = refs[:pieces], refs[pieces : 2 * pieces]
    value_ref, keep_ref, send_ref = refs[2 * pieces :]
    width = value_ref.shape[1]
    total = sum_refs[0][:, width:].astype(F32)
    for ref in sum_refs[1:]:
        total += ref[:, width:].astype(F32)
    value_ref[...] = total.astype(BF16)
    visual = jnp.concatenate([r[:, width:] for r in part_refs], axis=0)
    key_grad = jnp.concatenate([r[:, :width] for r in sum_refs], axis=0)
    product = dot(visual, key_grad, ((0,), (0,)))
    count, rows, _ = keep_ref.shape
    core = core_ref[0] == 0
    for n in range(count):
        even = product[2 * n * rows : (2 * n + 1) * rows]
        odd = product[(2 * n + 1) * rows : (2 * n + 2) * rows]
        keep_ref[n] = jnp.where(core, even, odd)
        send_ref[n] = jnp.where(core, odd, even).astype(BF16)


def weight_terms(samples, core, parts, sums):
    pieces = len(parts)
    rows, both = sums[0].shape
    width = both // 2
    features = parts[0].shape[1] - width
    half = (samples // 2, features // samples, width)
    return pl.pallas_call(
        functools.partial(weight_kernel, pieces),
        in_specs=[pl.BlockSpec(memory_space=pltpu.SMEM)] + [VMEM] * (2 * pieces),
        out_specs=[VMEM] * 3,
        out_shape=[
            jax.ShapeDtypeStruct((rows, width), BF16),
            jax.ShapeDtypeStruct(half, F32),
            jax.ShapeDtypeStruct(half, BF16),
        ],
        compiler_params=pltpu.CompilerParams(vmem_limit_bytes=32 * MIB),
        name="weight_terms",
    )(core, *parts, *sums)


def halve_kernel(bit_ref, kept_ref, came_ref, keep_ref, send_ref):
    low = bit_ref[0] == 0
    for n in range(keep_ref.shape[0]):
        even = kept_ref[2 * n] + came_ref[2 * n].astype(F32)
        odd = kept_ref[2 * n + 1] + came_ref[2 * n + 1].astype(F32)
        keep_ref[n] = jnp.where(low, even, odd)
        send_ref[n] = jnp.where(low, odd, even).astype(BF16)


def halve(bit, kept, came):
    half = (kept.shape[0] // 2, *kept.shape[1:])
    return pl.pallas_call(
        halve_kernel,
        in_specs=[pl.BlockSpec(memory_space=pltpu.SMEM), VMEM, VMEM],
        out_specs=[VMEM] * 2,
        out_shape=[jax.ShapeDtypeStruct(half, F32), jax.ShapeDtypeStruct(half, BF16)],
        compiler_params=pltpu.CompilerParams(vmem_limit_bytes=32 * MIB),
        name="halve",
    )(bit, kept, came)


def local(visual_rows, value_matrix, key_weight, queries, output_gradient, visual_len, frame_end):
    blocks, samples = lax.axis_size("blk"), lax.axis_size("dp")
    sample = lax.axis_index("dp").astype(jnp.int32)
    visual = visual_rows[0]

    def from_partners(pieces):
        came = {m: swap(pieces[m], "blk", partner(m, blocks)) for m in reversed(range(1, blocks))}
        return [pieces[0]] + [came[m] for m in range(1, blocks)]

    keys_values = from_partners([project(visual, key_weight, value_matrix[0])] * blocks)
    attention = Attention(queries[0], blocks, visual.shape[0])
    weights, dscores, key_terms = attention.scores(
        visual_len, frame_end, queries[0], output_gradient[0], visual, keys_values
    )
    parts = from_partners(key_terms)
    parts[1], weights = lax.optimization_barrier((parts[1], weights))
    value_terms = attention.values(output_gradient[0], weights)
    sums = from_partners(sum_terms(parts, value_terms))
    sums[1], weights = lax.optimization_barrier((sums[1], weights))
    attn_out, query_grad = attention.outputs(weights, dscores, keys_values)
    value_grad, kept, sent = weight_terms(samples, (sample % 2)[None], parts, sums)
    came, bit = swap(sent, "dp", 1), 1
    while kept.shape[0] > 1:
        kept, sent = halve(((sample >> bit) % 2)[None], kept, came)
        came, bit = swap(sent, "dp", 1 << bit), bit + 1
    came, attn_out, query_grad = lax.optimization_barrier((came, attn_out, query_grad))
    weight_grad = kept[0] + came[0].astype(F32)
    return attn_out[None], query_grad[None], value_grad[None], weight_grad


def solution(mesh):
    return jax.shard_map(
        local,
        mesh=mesh,
        in_specs=(
            P("dp", "blk", None),
            P("dp", "blk", None),
            P(),
            P("dp", "blk", None),
            P("dp", "blk", None),
            P("dp"),
            P("dp", None),
        ),
        out_specs=(
            P("dp", "blk", None),
            P("dp", "blk", None),
            P("dp", "blk", None),
            P(("blk", "dp"), None),
        ),
        check_vma=False,
    )
```

time: 73.4 us -> 83.8 us (1.14)
  local copies, waits for them, and re-layouts: 0.85 us -> 16.6 us
  waiting for transfers between devices: 19.6 us -> 11.8 us
  Pallas kernels: 13.8 us -> 16.2 us
    unnamed x10 -> x68, local copies, waits for them, and re-layouts: 0.85 us -> 16.6 us
    ppermute x23, waiting for transfers between devices: 19.6 us -> 11.8 us  [swap(): return lax.ppermute(x, axis, [(i, i ^ mask) for i in range(size)])]
    pallas_call x2 -> x4, Pallas kernels: 12.8 us -> 14.5 us  [the longest x1 5.87 us: scores(): self.call(scores_kernel, 6, 4, 'scores', in_specs=[smem, smem, self.text_...]
  transfers between devices with their start and end apart: 23 -> 23, of which waited for: 10 -> 10; matrix products, arithmetic and copies ran while one was open for 0% -> 0% of each run, Pallas kernels for 0% -> 5%
where the time goes in v5:
time: 83.8 us; the launch traced here: 83.1 us
  starting transfers between devices  36.2 us (43%)
  local copies, waits for them, and re-layouts  16.6 us (20%)
  Pallas kernels  16.2 us (19%)
  waiting for transfers between devices  11.8 us (14%)
  between operations  1.52 us (2%)
    ppermute x23, starting transfers between devices, swap(): return lax.ppermute(x, axis, [(i, i ^ mask) for i in range(size)])  36.2 us
    unnamed x68, local copies, waits for them, and re-layouts  16.6 us
    ppermute x23, waiting for transfers between devices, swap(): return lax.ppermute(x, axis, [(i, i ^ mask) for i in range(size)])  11.8 us
    pallas_call x1, Pallas kernels, scores(): self.call(scores_kernel, 6, 4, 'scores', in_specs=[smem, smem, self.text_...  5.87 us
    pallas_call x1, Pallas kernels, project(): pl.pallas_call(functools.partial(project_kernel, chunks), in_specs=[pl.Bl...  4.1 us
    pallas_call x1, Pallas kernels, outputs(): self.call(outputs_kernel, 2, 4, 'outputs', in_specs=[self.inner_block] *...  3.07 us
  transfers between devices with their start and end apart: 23, of which 10 were waited for; matrix products, arithmetic and copies ran while one was open for 0% of the time, Pallas kernels for 5%

profile of v5, /device:TPU:0, one launch (start us, length us, event | category | flops | bytes accessed | tf_op | source)
XLA Modules:
  0.0 83.1 jit_solution(2338790477262011040)
XLA Ops:
  0.7 4.1 %project.1.refs_0_ = bf16[32,1024]{1,0:T(8,128)(2,1)} custom-call(bf16[4096,512]{1,0:T(8,128)(2,1)} %weight_hbm.1, bf16[32,4096]{1,0:T(8,128)(2,1)} %bitcast.13, bf16[32,512]{1,0:T(8,128)(2,1)} %bitcast.16), custom_call_target="tpu_custom_call" | custom-call | flops 134217728 | bytes 4194304 | tf_op jit(solution)/shard_map/project/pallas_call | solution.py:56
  4.8 6.1 %collective-permute-start = (bf16[32,1024]{1,0:T(8,128)(2,1)}, bf16[32,1024]{1,0:T(8,128)(2,1)S(1)}, u32[]{:S(2)}, u32[]{:S(2)}) collective-permute-start(bf16[32,1024]{1,0:T(8,128)(2,1)} %project.1.refs_0_), channel_id=1, source_target_pairs={{0,28},{4,24},{8,20},{12,16},{16,12},{20,8},{24,4},{28,0},{1,29},{... | collective-permute-start | bytes 196616 | tf_op jit(solution)/shard_map/ppermute | solution.py:28
  11.8 2.0 %collective-permute-start.3 = (bf16[32,1024]{1,0:T(8,128)(2,1)}, bf16[32,1024]{1,0:T(8,128)(2,1)S(1)}, u32[]{:S(2)}, u32[]{:S(2)}) collective-permute-start(bf16[32,1024]{1,0:T(8,128)(2,1)} %project.1.refs_0_), channel_id=1, source_target_pairs={{0,16},{4,20},{8,24},{12,28},{16,0},{20,4},{24,8},{28,12},{1,17},{... | collective-permute-start | bytes 196616 | tf_op jit(solution)/shard_map/ppermute | solution.py:28
  13.8 2.3 %collective-permute-start.4 = (bf16[32,1024]{1,0:T(8,128)(2,1)}, bf16[32,1024]{1,0:T(8,128)(2,1)S(1)}, u32[]{:S(2)}, u32[]{:S(2)}) collective-permute-start(bf16[32,1024]{1,0:T(8,128)(2,1)} %project.1.refs_0_), channel_id=1, source_target_pairs={{0,12},{4,8},{8,4},{12,0},{16,28},{20,24},{24,20},{28,16},{1,13},{... | collective-permute-start | bytes 196616 | tf_op jit(solution)/shard_map/ppermute | solution.py:28
  18.4 2.8 %collective-permute-done.2.refs_3_ = bf16[32,1024]{1,0:T(8,128)(2,1)S(1)} collective-permute-done((bf16[32,1024]{1,0:T(8,128)(2,1)}, bf16[32,1024]{1,0:T(8,128)(2,1)S(1)}, u32[]{:S(2)}, u32[]{:S(2)}) %collective-permute-start.2) | collective-permute-done | bytes 65568 | tf_op jit(solution)/shard_map/ppermute | solution.py:28
  21.2 1.1 %collective-permute-done.3.refs_4_ = bf16[32,1024]{1,0:T(8,128)(2,1)S(1)} collective-permute-done((bf16[32,1024]{1,0:T(8,128)(2,1)}, bf16[32,1024]{1,0:T(8,128)(2,1)S(1)}, u32[]{:S(2)}, u32[]{:S(2)}) %collective-permute-start.3) | collective-permute-done | bytes 65568 | tf_op jit(solution)/shard_map/ppermute | solution.py:28
  22.8 0.9 %copy-done.3 = bf16[32,1024]{1,0:T(8,128)(2,1)S(1)} copy-done((bf16[32,1024]{1,0:T(8,128)(2,1)S(1)}, bf16[32,1024]{1,0:T(8,128)(2,1)}, u32[]{:S(2)}) %copy-start.3) | copy-done | bytes 65560
  23.6 1.2 %copy-done.32 = bf16[1,128,4096]{2,1,0:T(8,128)(2,1)S(1)} copy-done((bf16[1,128,4096]{2,1,0:T(8,128)(2,1)S(1)}, bf16[1,128,4096]{2,1,0:T(8,128)(2,1)}, u32[]{:S(2)}) %copy-start.32) | copy-done | bytes 1048600
  24.8 5.9 %scores.1 = (bf16[256,4096]{1,0:T(8,128)(2,1)S(1)}, bf16[256,4096]{1,0:T(8,128)(2,1)S(1)}, bf16[32,1024]{1,0:T(8,128)(2,1)S(1)}, bf16[32,1024]{1,0:T(8,128)(2,1)...) custom-call(s32[1]{0:T(128)S(6)} %copy.11.length_ref, ...), custom_call_target="tpu_custom_call" | custom-call | flops 1610612736 | bytes 4194304 | tf_op jit(solution)/shard_map/scores/pallas_call | solution.py:232
  30.8 1.3 %copy-done = bf16[256,4096]{1,0:T(8,128)(2,1)} copy-done((bf16[256,4096]{1,0:T(8,128)(2,1)}, bf16[256,4096]{1,0:T(8,128)(2,1)S(1)}, u32[]{:S(2)}) %copy-start) | copy-done | bytes 2097176
  32.1 4.0 %collective-permute-start.7 = (bf16[32,1024]{1,0:T(8,128)(2,1)S(1)}, bf16[32,1024]{1,0:T(8,128)(2,1)S(1)}, u32[]{:S(2)}, u32[]{:S(2)}) collective-permute-start(bf16[32,1024]{1,0:T(8,128)(2,1)S(1)} %get-tuple-element.45), channel_id=1, source_target_pairs={{0,28},{4,24},{8,20},{12,16},{16,12},{20,8},{24,4},{28,0},{1,29},{... | collective-permute-start | bytes 196616 | tf_op jit(solution)/shard_map/ppermute | solution.py:28
  36.2 2.3 %collective-permute-start.9 = (bf16[32,1024]{1,0:T(8,128)(2,1)S(1)}, bf16[32,1024]{1,0:T(8,128)(2,1)S(1)}, u32[]{:S(2)}, u32[]{:S(2)}) collective-permute-start(bf16[32,1024]{1,0:T(8,128)(2,1)S(1)} %get-tuple-element.49), channel_id=1, source_target_pairs={{0,20},{4,16},{8,28},{12,24},{16,4},{20,0},{24,12},{28,8},{1,21},{... | collective-permute-start | bytes 196616 | tf_op jit(solution)/shard_map/ppermute | solution.py:28
  38.4 1.4 %collective-permute-start.10 = (bf16[32,1024]{1,0:T(8,128)(2,1)S(1)}, bf16[32,1024]{1,0:T(8,128)(2,1)S(1)}, u32[]{:S(2)}, u32[]{:S(2)}) collective-permute-start(bf16[32,1024]{1,0:T(8,128)(2,1)S(1)} %get-tuple-element.50), channel_id=1, source_target_pairs={{0,16},{4,20},{8,24},{12,28},{16,0},{20,4},{24,8},{28,12},{1,17},{... | collective-permute-start | bytes 196616 | tf_op jit(solution)/shard_map/ppermute | solution.py:28
  39.8 1.6 %collective-permute-start.11 = (bf16[32,1024]{1,0:T(8,128)(2,1)S(1)}, bf16[32,1024]{1,0:T(8,128)(2,1)S(1)}, u32[]{:S(2)}, u32[]{:S(2)}) collective-permute-start(bf16[32,1024]{1,0:T(8,128)(2,1)S(1)} %get-tuple-element.51), channel_id=1, source_target_pairs={{0,12},{4,8},{8,4},{12,0},{16,28},{20,24},{24,20},{28,16},{1,13},{... | collective-permute-start | bytes 196616 | tf_op jit(solution)/shard_map/ppermute | solution.py:28
  41.4 1.9 %collective-permute-start.12 = (bf16[32,1024]{1,0:T(8,128)(2,1)S(1)}, bf16[32,1024]{1,0:T(8,128)(2,1)S(1)}, u32[]{:S(2)}, u32[]{:S(2)}) collective-permute-start(bf16[32,1024]{1,0:T(8,128)(2,1)S(1)} %get-tuple-element.52), channel_id=1, source_target_pairs={{0,8},{4,12},{8,0},{12,4},{16,24},{20,28},{24,16},{28,20},{1,9},{5... | collective-permute-start | bytes 196616 | tf_op jit(solution)/shard_map/ppermute | solution.py:28
  43.5 1.4 %values.1 = (bf16[32,512]{1,0:T(8,128)(2,1)S(1)}, bf16[32,512]{1,0:T(8,128)(2,1)S(1)}, bf16[32,512]{1,0:T(8,128)(2,1)S(1)}, bf16[32,512]{1,0:T(8,128)(2,1)S(1)},...) custom-call(bf16[128,4096]{1,0:T(8,128)(2,1)S(1)} %bitcast.12, ...), custom_call_target="tpu_custom_call" | custom-call | flops 268435456 | bytes 2097152 | tf_op jit(solution)/shard_map/values/pallas_call | solution.py:251
  45.0 1.8 %collective-permute-done.9.refs_3_ = bf16[32,1024]{1,0:T(8,128)(2,1)S(1)} collective-permute-done((bf16[32,1024]{1,0:T(8,128)(2,1)S(1)}, bf16[32,1024]{1,0:T(8,128)(2,1)S(1)}, u32[]{:S(2)}, u32[]{:S(2)}) %collective-permute-start.9) | collective-permute-done | bytes 65568 | tf_op jit(solution)/shard_map/ppermute | solution.py:28
  48.9 3.5 %collective-permute-start.14 = (bf16[32,1024]{1,0:T(8,128)(2,1)S(1)}, bf16[32,1024]{1,0:T(8,128)(2,1)S(1)}, u32[]{:S(2)}, u32[]{:S(2)}) collective-permute-start(bf16[32,1024]{1,0:T(8,128)(2,1)S(1)} %get-tuple-element.64), channel_id=1, source_target_pairs={{0,28},{4,24},{8,20},{12,16},{16,12},{20,8},{24,4},{28,0},{1,29},{... | collective-permute-start | bytes 196616 | tf_op jit(solution)/shard_map/ppermute | solution.py:28
  52.8 2.8 %collective-permute-start.16 = (bf16[32,1024]{1,0:T(8,128)(2,1)}, bf16[32,1024]{1,0:T(8,128)(2,1)S(1)}, u32[]{:S(2)}, u32[]{:S(2)}) collective-permute-start(bf16[32,1024]{1,0:T(8,128)(2,1)} %get-tuple-element.67), channel_id=1, source_target_pairs={{0,20},{4,16},{8,28},{12,24},{16,4},{20,0},{24,12},{28,8},{1,21},{... | collective-permute-start | bytes 196616 | tf_op jit(solution)/shard_map/ppermute | solution.py:28
  55.6 0.9 %collective-permute-start.17 = (bf16[32,1024]{1,0:T(8,128)(2,1)S(1)}, bf16[32,1024]{1,0:T(8,128)(2,1)S(1)}, u32[]{:S(2)}, u32[]{:S(2)}) collective-permute-start(bf16[32,1024]{1,0:T(8,128)(2,1)S(1)} %get-tuple-element.68), channel_id=1, source_target_pairs={{0,16},{4,20},{8,24},{12,28},{16,0},{20,4},{24,8},{28,12},{1,17},{... | collective-permute-start | bytes 196616 | tf_op jit(solution)/shard_map/ppermute | solution.py:28
  56.6 1.2 %collective-permute-start.18 = (bf16[32,1024]{1,0:T(8,128)(2,1)S(1)}, bf16[32,1024]{1,0:T(8,128)(2,1)S(1)}, u32[]{:S(2)}, u32[]{:S(2)}) collective-permute-start(bf16[32,1024]{1,0:T(8,128)(2,1)S(1)} %get-tuple-element.69), channel_id=1, source_target_pairs={{0,12},{4,8},{8,4},{12,0},{16,28},{20,24},{24,20},{28,16},{1,13},{... | collective-permute-start | bytes 196616 | tf_op jit(solution)/shard_map/ppermute | solution.py:28
  57.7 1.0 %collective-permute-start.19 = (bf16[32,1024]{1,0:T(8,128)(2,1)S(1)}, bf16[32,1024]{1,0:T(8,128)(2,1)S(1)}, u32[]{:S(2)}, u32[]{:S(2)}) collective-permute-start(bf16[32,1024]{1,0:T(8,128)(2,1)S(1)} %get-tuple-element.70), channel_id=1, source_target_pairs={{0,8},{4,12},{8,0},{12,4},{16,24},{20,28},{24,16},{28,20},{1,9},{5... | collective-permute-start | bytes 196616 | tf_op jit(solution)/shard_map/ppermute | solution.py:28
  59.2 0.9 %collective-permute-start.20 = (bf16[32,1024]{1,0:T(8,128)(2,1)S(1)}, bf16[32,1024]{1,0:T(8,128)(2,1)S(1)}, u32[]{:S(2)}, u32[]{:S(2)}) collective-permute-start(bf16[32,1024]{1,0:T(8,128)(2,1)S(1)} %get-tuple-element.71), channel_id=1, source_target_pairs={{0,4},{4,0},{8,12},{12,8},{16,20},{20,16},{24,28},{28,24},{1,5},{5... | collective-permute-start | bytes 196616 | tf_op jit(solution)/shard_map/ppermute | solution.py:28
  60.1 1.7 %collective-permute-done.16.refs_11_ = bf16[32,1024]{1,0:T(8,128)(2,1)S(1)} collective-permute-done((bf16[32,1024]{1,0:T(8,128)(2,1)}, bf16[32,1024]{1,0:T(8,128)(2,1)S(1)}, u32[]{:S(2)}, u32[]{:S(2)}) %collective-permute-start.16) | collective-permute-done | bytes 65568 | tf_op jit(solution)/shard_map/ppermute | solution.py:28
  64.9 0.8 %copy-done.7 = bf16[32,1024]{1,0:T(8,128)(2,1)S(1)} copy-done((bf16[32,1024]{1,0:T(8,128)(2,1)S(1)}, bf16[32,1024]{1,0:T(8,128)(2,1)}, u32[]{:S(2)}) %copy-start.7) | copy-done | bytes 65560
  65.7 0.8 %copy-done.9 = bf16[32,1024]{1,0:T(8,128)(2,1)S(1)} copy-done((bf16[32,1024]{1,0:T(8,128)(2,1)S(1)}, bf16[32,1024]{1,0:T(8,128)(2,1)}, u32[]{:S(2)}) %copy-start.9) | copy-done | bytes 65560
  66.5 0.8 %copy-done.25 = bf16[32,1024]{1,0:T(8,128)(2,1)S(1)} copy-done((bf16[32,1024]{1,0:T(8,128)(2,1)S(1)}, bf16[32,1024]{1,0:T(8,128)(2,1)}, u32[]{:S(2)}) %copy-start.25) | copy-done | bytes 65560
  69.9 1.0 %weight_terms.1 = (bf16[32,512]{1,0:T(8,128)(2,1)}, f32[2,128,512]{2,1,0:T(8,128)S(1)}, bf16[2,128,512]{2,1,0:T(8,128)(2,1)}) custom-call(s32[1]{0:T(128)} %bitcast.1.core_ref, bf16[32,1024]{1,0:T(8,128)(2,1)S(1)} %get-tuple-element.44.refs_0_, bf16[32,1024]{1,0:T(8,128)(2,1)S(1)} %collective-permute-done.7.refs_1_, ...), custom_call_target="tpu_custom_call" | custom-call | tf_op jit(solution)/shard_map/weight_terms/pallas_call | solution.py:325
  70.9 1.7 %collective-permute-done.21.came_ref = bf16[2,128,512]{2,1,0:T(8,128)(2,1)S(1)} collective-permute-done((bf16[2,128,512]{2,1,0:T(8,128)(2,1)}, bf16[2,128,512]{2,1,0:T(8,128)(2,1)S(1)}, u32[]{:S(2)}, u32[]{:S(2)}) %collective-permute-start.21) | collective-permute-done | bytes 262176 | tf_op jit(solution)/shard_map/ppermute | solution.py:28
  72.7 1.6 %collective-permute-start.22 = (bf16[1,128,512]{2,1,0:T(8,128)(2,1)S(1)}, bf16[1,128,512]{2,1,0:T(8,128)(2,1)S(1)}, u32[]{:S(2)}, u32[]{:S(2)}) collective-permute-start(bf16[1,128,512]{2,1,0:T(8,128)(2,1)S(1)} %get-tuple-element.74), channel_id=1, source_target_pairs={{0,2},{1,3},{2,0},{3,1},{4,6},{5,7},{6,4},{7,5},{8,10},{9,11},{10,... | collective-permute-start | bytes 393224 | tf_op jit(solution)/shard_map/ppermute | solution.py:28
  74.3 1.6 %copy-done.1 = bf16[256,4096]{1,0:T(8,128)(2,1)S(1)} copy-done((bf16[256,4096]{1,0:T(8,128)(2,1)S(1)}, bf16[256,4096]{1,0:T(8,128)(2,1)}, u32[]{:S(2)}) %copy-start.1) | copy-done | bytes 2097176
  79.3 3.1 %outputs.1 = (bf16[128,4096]{1,0:T(8,128)(2,1)}, bf16[128,4096]{1,0:T(8,128)(2,1)}) custom-call(bf16[256,4096]{1,0:T(8,128)(2,1)S(1)} %get-tuple-element.75.w_ref, bf16[256,4096]{1,0:T(8,128)(2,1)S(1)} %copy-done.1, bf16[32,1024]{1,0:T(8,128)(2,1)S(1)} %copy-done.4, bf16[32,1024]{1,0:T(8,128)(2,1)S(1)} %copy-done.11, bf16[32,1024]{1,0:T(8,128)(2,1)S(1)} %copy-done.13, ...), custom_call_target="tpu_custom_call" | custom-call | flops 536870912 | bytes 4194304 | tf_op jit(solution)/shard_map/outputs/pallas_call | solution.py:263
  (90 shorter events, 16.1 us)
Async XLA Ops:
  0.6 22.1 %copy-start.2 = (bf16[1,128,4096]{2,1,0:T(8,128)(2,1)S(1)}, bf16[1,128,4096]{2,1,0:T(8,128)(2,1)}, u32[]{:S(2)}) copy-start(bf16[1,128,4096]{2,1,0:T(8,128)(2,1)} %param.11) | copy-start | bytes 3145732
  0.6 22.1 %copy-start.5 = (bf16[1,32,4096]{2,1,0:T(8,128)(2,1)S(1)}, bf16[1,32,4096]{2,1,0:T(8,128)(2,1)}, u32[]{:S(2)}) copy-start(bf16[1,32,4096]{2,1,0:T(8,128)(2,1)} %param.7) | copy-start | bytes 786436
  0.7 22.1 %copy-start.33 = (s32[1,8]{1,0:T(1,128)S(1)}, s32[1,8]{1,0:T(1,128)}, u32[]{:S(2)}) copy-start(s32[1,8]{1,0:T(1,128)} %frame_ref.1) | copy-start | bytes 100
  4.8 11.4 %collective-permute-start = (bf16[32,1024]{1,0:T(8,128)(2,1)}, bf16[32,1024]{1,0:T(8,128)(2,1)S(1)}, u32[]{:S(2)}, u32[]{:S(2)}) collective-permute-start(bf16[32,1024]{1,0:T(8,128)(2,1)} %project.1.refs_0_), channel_id=1, source_target_pairs={{0,28},{4,24},{8,20},{12,16},{16,12},{20,8},{24,4},{28,0},{1,29},{... | collective-permute-start | bytes 196616 | tf_op jit(solution)/shard_map/ppermute | solution.py:28
  10.8 6.5 %collective-permute-start.1 = (bf16[32,1024]{1,0:T(8,128)(2,1)}, bf16[32,1024]{1,0:T(8,128)(2,1)S(1)}, u32[]{:S(2)}, u32[]{:S(2)}) collective-permute-start(bf16[32,1024]{1,0:T(8,128)(2,1)} %project.1.refs_0_), channel_id=1, source_target_pairs={{0,24},{4,28},{8,16},{12,20},{16,8},{20,12},{24,0},{28,4},{1,25},{... | collective-permute-start | bytes 196616 | tf_op jit(solution)/shard_map/ppermute | solution.py:28
  11.1 10.1 %collective-permute-start.2 = (bf16[32,1024]{1,0:T(8,128)(2,1)}, bf16[32,1024]{1,0:T(8,128)(2,1)S(1)}, u32[]{:S(2)}, u32[]{:S(2)}) collective-permute-start(bf16[32,1024]{1,0:T(8,128)(2,1)} %project.1.refs_0_), channel_id=1, source_target_pairs={{0,20},{4,16},{8,28},{12,24},{16,4},{20,0},{24,12},{28,8},{1,21},{... | collective-permute-start | bytes 196616 | tf_op jit(solution)/shard_map/ppermute | solution.py:28
  11.8 10.5 %collective-permute-start.3 = (bf16[32,1024]{1,0:T(8,128)(2,1)}, bf16[32,1024]{1,0:T(8,128)(2,1)S(1)}, u32[]{:S(2)}, u32[]{:S(2)}) collective-permute-start(bf16[32,1024]{1,0:T(8,128)(2,1)} %project.1.refs_0_), channel_id=1, source_target_pairs={{0,16},{4,20},{8,24},{12,28},{16,0},{20,4},{24,8},{28,12},{1,17},{... | collective-permute-start | bytes 196616 | tf_op jit(solution)/shard_map/ppermute | solution.py:28
  13.8 8.5 %collective-permute-start.4 = (bf16[32,1024]{1,0:T(8,128)(2,1)}, bf16[32,1024]{1,0:T(8,128)(2,1)S(1)}, u32[]{:S(2)}, u32[]{:S(2)}) collective-permute-start(bf16[32,1024]{1,0:T(8,128)(2,1)} %project.1.refs_0_), channel_id=1, source_target_pairs={{0,12},{4,8},{8,4},{12,0},{16,28},{20,24},{24,20},{28,16},{1,13},{... | collective-permute-start | bytes 196616 | tf_op jit(solution)/shard_map/ppermute | solution.py:28
  16.1 14.6 %copy-start.10 = (bf16[32,1024]{1,0:T(8,128)(2,1)}, bf16[32,1024]{1,0:T(8,128)(2,1)S(1)}, u32[]{:S(2)}) copy-start(bf16[32,1024]{1,0:T(8,128)(2,1)S(1)} %collective-permute-done.refs_1_) | copy-start | bytes 196612
  16.1 6.6 %collective-permute-start.5 = (bf16[32,1024]{1,0:T(8,128)(2,1)}, bf16[32,1024]{1,0:T(8,128)(2,1)S(1)}, u32[]{:S(2)}, u32[]{:S(2)}) collective-permute-start(bf16[32,1024]{1,0:T(8,128)(2,1)} %project.1.refs_0_), channel_id=1, source_target_pairs={{0,8},{4,12},{8,0},{12,4},{16,24},{20,28},{24,16},{28,20},{1,9},{5... | collective-permute-start | bytes 196616 | tf_op jit(solution)/shard_map/ppermute | solution.py:28
  17.3 13.4 %copy-start.12 = (bf16[32,1024]{1,0:T(8,128)(2,1)}, bf16[32,1024]{1,0:T(8,128)(2,1)S(1)}, u32[]{:S(2)}) copy-start(bf16[32,1024]{1,0:T(8,128)(2,1)S(1)} %collective-permute-done.1.refs_2_) | copy-start | bytes 196612
  17.3 5.4 %collective-permute-start.6 = (bf16[32,1024]{1,0:T(8,128)(2,1)}, bf16[32,1024]{1,0:T(8,128)(2,1)S(1)}, u32[]{:S(2)}, u32[]{:S(2)}) collective-permute-start(bf16[32,1024]{1,0:T(8,128)(2,1)} %project.1.refs_0_), channel_id=1, source_target_pairs={{0,4},{4,0},{8,12},{12,8},{16,20},{20,16},{24,28},{28,24},{1,5},{5... | collective-permute-start | bytes 196616 | tf_op jit(solution)/shard_map/ppermute | solution.py:28
  32.1 9.3 %collective-permute-start.7 = (bf16[32,1024]{1,0:T(8,128)(2,1)S(1)}, bf16[32,1024]{1,0:T(8,128)(2,1)S(1)}, u32[]{:S(2)}, u32[]{:S(2)}) collective-permute-start(bf16[32,1024]{1,0:T(8,128)(2,1)S(1)} %get-tuple-element.45), channel_id=1, source_target_pairs={{0,28},{4,24},{8,20},{12,16},{16,12},{20,8},{24,4},{28,0},{1,29},{... | collective-permute-start | bytes 196616 | tf_op jit(solution)/shard_map/ppermute | solution.py:28
  36.2 7.2 %collective-permute-start.8 = (bf16[32,1024]{1,0:T(8,128)(2,1)S(1)}, bf16[32,1024]{1,0:T(8,128)(2,1)S(1)}, u32[]{:S(2)}, u32[]{:S(2)}) collective-permute-start(bf16[32,1024]{1,0:T(8,128)(2,1)S(1)} %get-tuple-element.48), channel_id=1, source_target_pairs={{0,24},{4,28},{8,16},{12,20},{16,8},{20,12},{24,0},{28,4},{1,25},{... | collective-permute-start | bytes 196616 | tf_op jit(solution)/shard_map/ppermute | solution.py:28
  36.2 10.6 %collective-permute-start.9 = (bf16[32,1024]{1,0:T(8,128)(2,1)S(1)}, bf16[32,1024]{1,0:T(8,128)(2,1)S(1)}, u32[]{:S(2)}, u32[]{:S(2)}) collective-permute-start(bf16[32,1024]{1,0:T(8,128)(2,1)S(1)} %get-tuple-element.49), channel_id=1, source_target_pairs={{0,20},{4,16},{8,28},{12,24},{16,4},{20,0},{24,12},{28,8},{1,21},{... | collective-permute-start | bytes 196616 | tf_op jit(solution)/shard_map/ppermute | solution.py:28
  38.4 8.3 %collective-permute-start.10 = (bf16[32,1024]{1,0:T(8,128)(2,1)S(1)}, bf16[32,1024]{1,0:T(8,128)(2,1)S(1)}, u32[]{:S(2)}, u32[]{:S(2)}) collective-permute-start(bf16[32,1024]{1,0:T(8,128)(2,1)S(1)} %get-tuple-element.50), channel_id=1, source_target_pairs={{0,16},{4,20},{8,24},{12,28},{16,0},{20,4},{24,8},{28,12},{1,17},{... | collective-permute-start | bytes 196616 | tf_op jit(solution)/shard_map/ppermute | solution.py:28
  39.8 7.0 %collective-permute-start.11 = (bf16[32,1024]{1,0:T(8,128)(2,1)S(1)}, bf16[32,1024]{1,0:T(8,128)(2,1)S(1)}, u32[]{:S(2)}, u32[]{:S(2)}) collective-permute-start(bf16[32,1024]{1,0:T(8,128)(2,1)S(1)} %get-tuple-element.51), channel_id=1, source_target_pairs={{0,12},{4,8},{8,4},{12,0},{16,28},{20,24},{24,20},{28,16},{1,13},{... | collective-permute-start | bytes 196616 | tf_op jit(solution)/shard_map/ppermute | solution.py:28
  41.4 5.3 %collective-permute-start.12 = (bf16[32,1024]{1,0:T(8,128)(2,1)S(1)}, bf16[32,1024]{1,0:T(8,128)(2,1)S(1)}, u32[]{:S(2)}, u32[]{:S(2)}) collective-permute-start(bf16[32,1024]{1,0:T(8,128)(2,1)S(1)} %get-tuple-element.52), channel_id=1, source_target_pairs={{0,8},{4,12},{8,0},{12,4},{16,24},{20,28},{24,16},{28,20},{1,9},{5... | collective-permute-start | bytes 196616 | tf_op jit(solution)/shard_map/ppermute | solution.py:28
  43.3 4.3 %collective-permute-start.13 = (bf16[32,1024]{1,0:T(8,128)(2,1)S(1)}, bf16[32,1024]{1,0:T(8,128)(2,1)S(1)}, u32[]{:S(2)}, u32[]{:S(2)}) collective-permute-start(bf16[32,1024]{1,0:T(8,128)(2,1)S(1)} %get-tuple-element.53), channel_id=1, source_target_pairs={{0,4},{4,0},{8,12},{12,8},{16,20},{20,16},{24,28},{28,24},{1,5},{5... | collective-permute-start | bytes 196616 | tf_op jit(solution)/shard_map/ppermute | solution.py:28
  44.9 29.4 %copy-start.4 = (bf16[32,1024]{1,0:T(8,128)(2,1)S(1)}, bf16[32,1024]{1,0:T(8,128)(2,1)}, u32[]{:S(2)}) copy-start(bf16[32,1024]{1,0:T(8,128)(2,1)} %project.1.refs_0_) | copy-start | bytes 196612
  44.9 29.4 %copy-start.11 = (bf16[32,1024]{1,0:T(8,128)(2,1)S(1)}, bf16[32,1024]{1,0:T(8,128)(2,1)}, u32[]{:S(2)}) copy-start(bf16[32,1024]{1,0:T(8,128)(2,1)} %copy-done.10) | copy-start | bytes 196612
  45.0 29.3 %copy-start.13 = (bf16[32,1024]{1,0:T(8,128)(2,1)S(1)}, bf16[32,1024]{1,0:T(8,128)(2,1)}, u32[]{:S(2)}) copy-start(bf16[32,1024]{1,0:T(8,128)(2,1)} %copy-done.12) | copy-start | bytes 196612
  45.0 29.3 %copy-start.15 = (bf16[32,1024]{1,0:T(8,128)(2,1)S(1)}, bf16[32,1024]{1,0:T(8,128)(2,1)}, u32[]{:S(2)}) copy-start(bf16[32,1024]{1,0:T(8,128)(2,1)} %copy-done.14) | copy-start | bytes 196612
  48.9 8.8 %collective-permute-start.14 = (bf16[32,1024]{1,0:T(8,128)(2,1)S(1)}, bf16[32,1024]{1,0:T(8,128)(2,1)S(1)}, u32[]{:S(2)}, u32[]{:S(2)}) collective-permute-start(bf16[32,1024]{1,0:T(8,128)(2,1)S(1)} %get-tuple-element.64), channel_id=1, source_target_pairs={{0,28},{4,24},{8,20},{12,16},{16,12},{20,8},{24,4},{28,0},{1,29},{... | collective-permute-start | bytes 196616 | tf_op jit(solution)/shard_map/ppermute | solution.py:28
  52.4 6.7 %collective-permute-start.15 = (bf16[32,1024]{1,0:T(8,128)(2,1)S(1)}, bf16[32,1024]{1,0:T(8,128)(2,1)S(1)}, u32[]{:S(2)}, u32[]{:S(2)}) collective-permute-start(bf16[32,1024]{1,0:T(8,128)(2,1)S(1)} %get-tuple-element.66), channel_id=1, source_target_pairs={{0,24},{4,28},{8,16},{12,20},{16,8},{20,12},{24,0},{28,4},{1,25},{... | collective-permute-start | bytes 196616 | tf_op jit(solution)/shard_map/ppermute | solution.py:28
  52.8 8.9 %collective-permute-start.16 = (bf16[32,1024]{1,0:T(8,128)(2,1)}, bf16[32,1024]{1,0:T(8,128)(2,1)S(1)}, u32[]{:S(2)}, u32[]{:S(2)}) collective-permute-start(bf16[32,1024]{1,0:T(8,128)(2,1)} %get-tuple-element.67), channel_id=1, source_target_pairs={{0,20},{4,16},{8,28},{12,24},{16,4},{20,0},{24,12},{28,8},{1,21},{... | collective-permute-start | bytes 196616 | tf_op jit(solution)/shard_map/ppermute | solution.py:28
  55.6 6.7 %collective-permute-start.17 = (bf16[32,1024]{1,0:T(8,128)(2,1)S(1)}, bf16[32,1024]{1,0:T(8,128)(2,1)S(1)}, u32[]{:S(2)}, u32[]{:S(2)}) collective-permute-start(bf16[32,1024]{1,0:T(8,128)(2,1)S(1)} %get-tuple-element.68), channel_id=1, source_target_pairs={{0,16},{4,20},{8,24},{12,28},{16,0},{20,4},{24,8},{28,12},{1,17},{... | collective-permute-start | bytes 196616 | tf_op jit(solution)/shard_map/ppermute | solution.py:28
  56.6 6.4 %collective-permute-start.18 = (bf16[32,1024]{1,0:T(8,128)(2,1)S(1)}, bf16[32,1024]{1,0:T(8,128)(2,1)S(1)}, u32[]{:S(2)}, u32[]{:S(2)}) collective-permute-start(bf16[32,1024]{1,0:T(8,128)(2,1)S(1)} %get-tuple-element.69), channel_id=1, source_target_pairs={{0,12},{4,8},{8,4},{12,0},{16,28},{20,24},{24,20},{28,16},{1,13},{... | collective-permute-start | bytes 196616 | tf_op jit(solution)/shard_map/ppermute | solution.py:28
  57.7 5.9 %collective-permute-start.19 = (bf16[32,1024]{1,0:T(8,128)(2,1)S(1)}, bf16[32,1024]{1,0:T(8,128)(2,1)S(1)}, u32[]{:S(2)}, u32[]{:S(2)}) collective-permute-start(bf16[32,1024]{1,0:T(8,128)(2,1)S(1)} %get-tuple-element.70), channel_id=1, source_target_pairs={{0,8},{4,12},{8,0},{12,4},{16,24},{20,28},{24,16},{28,20},{1,9},{5... | collective-permute-start | bytes 196616 | tf_op jit(solution)/shard_map/ppermute | solution.py:28
  59.2 5.1 %collective-permute-start.20 = (bf16[32,1024]{1,0:T(8,128)(2,1)S(1)}, bf16[32,1024]{1,0:T(8,128)(2,1)S(1)}, u32[]{:S(2)}, u32[]{:S(2)}) collective-permute-start(bf16[32,1024]{1,0:T(8,128)(2,1)S(1)} %get-tuple-element.71), channel_id=1, source_target_pairs={{0,4},{4,0},{8,12},{12,8},{16,20},{20,16},{24,28},{28,24},{1,5},{5... | collective-permute-start | bytes 196616 | tf_op jit(solution)/shard_map/ppermute | solution.py:28
  70.9 1.7 %collective-permute-start.21 = (bf16[2,128,512]{2,1,0:T(8,128)(2,1)}, bf16[2,128,512]{2,1,0:T(8,128)(2,1)S(1)}, u32[]{:S(2)}, u32[]{:S(2)}) collective-permute-start(bf16[2,128,512]{2,1,0:T(8,128)(2,1)} %get-tuple-element.73), channel_id=1, source_target_pairs={{0,1},{1,0},{2,3},{3,2},{4,5},{5,4},{6,7},{7,6},{8,9},{9,8},{10,11... | collective-permute-start | bytes 786440 | tf_op jit(solution)/shard_map/ppermute | solution.py:28
  72.7 9.6 %collective-permute-start.22 = (bf16[1,128,512]{2,1,0:T(8,128)(2,1)S(1)}, bf16[1,128,512]{2,1,0:T(8,128)(2,1)S(1)}, u32[]{:S(2)}, u32[]{:S(2)}) collective-permute-start(bf16[1,128,512]{2,1,0:T(8,128)(2,1)S(1)} %get-tuple-element.74), channel_id=1, source_target_pairs={{0,2},{1,3},{2,0},{3,1},{4,6},{5,7},{6,4},{7,5},{8,10},{9,11},{10,... | collective-permute-start | bytes 393224 | tf_op jit(solution)/shard_map/ppermute | solution.py:28
  (25 other events, 59.8 us)

commit v6 on v5

--- a/solution.py
+++ b/solution.py
@@ -28,53 +28,69 @@
     return lax.ppermute(x, axis, [(i, i ^ mask) for i in range(size)])
 
 
+def in_hbm(x):
+    return pltpu.with_memory_space_constraint(x, pltpu.HBM)
+
+
 def partner(piece, pieces):
     return (pieces - piece) % pieces
 
 
-def project_kernel(chunks, weight_hbm, visual_ref, value_ref, out_ref, weight, sems):
-    slab = weight.shape[0] // chunks
-    copies = []
-    for c in range(chunks):
-        part = pl.ds(c * slab, slab)
-        copies.append(pltpu.make_async_copy(weight_hbm.at[part], weight.at[part], sems.at[c]))
-        copies[c].start()
-    keys = jnp.zeros((visual_ref.shape[0], weight.shape[1]), F32)
-    for c in range(chunks):
-        copies[c].wait()
-        part = slice(c * slab, (c + 1) * slab)
-        keys += dot(visual_ref[:, part], weight[part, :])
-    columns = weight.shape[1]
-    out_ref[:, :columns] = keys.astype(BF16)
-    out_ref[:, columns:] = value_ref[...]
+def project_kernel(streams, visual_ref, *refs):
+    weight_refs, value_ref, out_ref, acc_ref = refs[:streams], *refs[streams:]
+    step = pl.program_id(0)
+    slab = weight_refs[0].shape[0]
+    part = dot(visual_ref[:, :slab], weight_refs[0][...])
+    for p in range(1, streams):
+        part += dot(visual_ref[:, p * slab : (p + 1) * slab], weight_refs[p][...])
+
+    @pl.when(step == 0)
+    def _():
+        acc_ref[...] = part
+
+    @pl.when(step > 0)
+    def _():
+        acc_ref[...] += part
+
+    @pl.when(step == pl.num_programs(0) - 1)
+    def _():
+        columns = acc_ref.shape[1]
+        out_ref[:, :columns] = acc_ref[...].astype(BF16)
+        out_ref[:, columns:] = value_ref[...]
 
 
 def project(visual, key_weight, value):
     rows, features = visual.shape
     columns = key_weight.shape[1]
-    chunks = 16
+    steps, streams = 2, 4
+    slab = features // (steps * streams)
+    out = (rows, columns + value.shape[1])
     return pl.pallas_call(
-        functools.partial(project_kernel, chunks),
-        in_specs=[pl.BlockSpec(memory_space=pltpu.HBM), VMEM, VMEM],
-        out_specs=VMEM,
-        out_shape=jax.ShapeDtypeStruct((rows, columns + value.shape[1]), BF16),
-        scratch_shapes=[
-            pltpu.VMEM(key_weight.shape, BF16),
-            pltpu.SemaphoreType.DMA((chunks,)),
-        ],
+        functools.partial(project_kernel, streams),
+        grid=(steps,),
+        in_specs=[pl.BlockSpec((rows, streams * slab), lambda k: (0, k))]
+        + [
+            pl.BlockSpec((slab, columns), lambda k, p=p: (k * streams + p, 0))
+            for p in range(streams)
+        ]
+        + [pl.BlockSpec(value.shape, lambda k: (0, 0))],
+        out_specs=pl.BlockSpec(out, lambda k: (0, 0)),
+        out_shape=jax.ShapeDtypeStruct(out, BF16),
+        scratch_shapes=[pltpu.VMEM((rows, columns), F32)],
         cost_estimate=pl.CostEstimate(
             flops=2 * rows * features * columns,
             bytes_accessed=2 * features * columns,
             transcendentals=0,
         ),
+        compiler_params=pltpu.CompilerParams(vmem_limit_bytes=32 * MIB),
         name="project",
-    )(key_weight, visual, value)
+    )(in_hbm(visual), *[in_hbm(key_weight)] * streams, in_hbm(value))
 
 
 def scores_kernel(pieces, length_ref, frame_ref, q_ref, g_ref, visual_hbm, *refs):
-    kv_refs, (w_ref, ds_ref) = refs[:pieces], refs[pieces : pieces + 2]
-    key_refs = refs[pieces + 2 : 2 * pieces + 2]
-    kg_acc, visual, sem = refs[2 * pieces + 2 :]
+    kv_refs, (w_ref, ds_ref, kv_ref) = refs[:pieces], refs[pieces : pieces + 3]
+    key_refs = refs[pieces + 3 : 2 * pieces + 3]
+    kg_acc, visual, sem = refs[2 * pieces + 3 :]
     j, i = pl.program_id(0), pl.program_id(1)
     last = jnp.logical_and(j == pl.num_programs(0) - 1, i == pl.num_programs(1) - 1)
     copy = pltpu.make_async_copy(visual_hbm, visual, sem)
@@ -90,6 +106,8 @@
     value_head = pl.ds(pl.multiple_of(width + j * HEAD_SIZE, HEAD_SIZE), HEAD_SIZE)
     keys = jnp.concatenate([r[:, head] for r in kv_refs], axis=0)
     values = jnp.concatenate([r[:, value_head] for r in kv_refs], axis=0)
+    kv_ref[:, :HEAD_SIZE] = keys
+    kv_ref[:, HEAD_SIZE:] = values
     pair = 2 * TILE
     rows = kv_refs[0].shape[0]
     row = lax.broadcasted_iota(jnp.int32, (rows, pair), 0)
@@ -173,14 +191,8 @@
             value_refs[m][:, head] = vg_acc[m * rows : (m + 1) * rows, :].astype(BF16)
 
 
-def outputs_kernel(pieces, w_ref, ds_ref, *refs):
-    kv_refs, (o_ref, qg_ref) = refs[:pieces], refs[pieces:]
-    j = pl.program_id(0)
-    width = KEY_HEADS * HEAD_SIZE
-    head = pl.ds(pl.multiple_of(j * HEAD_SIZE, HEAD_SIZE), HEAD_SIZE)
-    value_head = pl.ds(pl.multiple_of(width + j * HEAD_SIZE, HEAD_SIZE), HEAD_SIZE)
-    keys_t = jnp.concatenate([r[:, head] for r in kv_refs], axis=0).T
-    values_t = jnp.concatenate([r[:, value_head] for r in kv_refs], axis=0).T
+def outputs_kernel(pieces, w_ref, ds_ref, kv_ref, o_ref, qg_ref):
+    keys_t, values_t = kv_ref[:, :HEAD_SIZE].T, kv_ref[:, HEAD_SIZE:].T
     pair = 2 * TILE
     for p in range(HEADS_PER_KEY // 2):
         first = slice(p * pair, p * pair + HEAD_SIZE)
@@ -205,7 +217,8 @@
         tiles = self.tiles
         self.text_block = pl.BlockSpec((TILE, span), lambda j, i: (i, j))
         self.inner_block = pl.BlockSpec((self.all_rows, span), lambda j, i: (0, j * tiles + i))
-        self.inner = jax.ShapeDtypeStruct((self.all_rows, tiles * self.wide), BF16)
+        self.inner = pltpu.HBM((self.all_rows, tiles * self.wide), BF16)
+        self.head_block = pl.BlockSpec((self.all_rows, 2 * HEAD_SIZE), lambda j, i: (0, j))
 
     def whole(self, columns):
         return pl.BlockSpec((self.rows, columns), lambda j, i: (0, 0))
@@ -236,15 +249,19 @@
             "scores",
             in_specs=[smem, smem, self.text_block, self.text_block, hbm]
             + [self.whole(2 * self.width)] * self.pieces,
-            out_specs=[self.inner_block] * 2 + [self.whole(columns)] * self.pieces,
-            out_shape=[self.inner] * 2 + [piece] * self.pieces,
+            out_specs=[self.inner_block] * 2
+            + [self.head_block]
+            + [self.whole(columns)] * self.pieces,
+            out_shape=[self.inner] * 2
+            + [pltpu.HBM((self.all_rows, 2 * self.width), BF16)]
+            + [piece] * self.pieces,
             scratch_shapes=[
                 pltpu.VMEM((self.all_rows, HEAD_SIZE), F32),
                 pltpu.VMEM(visual.shape, BF16),
                 pltpu.SemaphoreType.DMA,
             ],
-        )(length, frames, queries, gradients, visual, *keys_values)
-        return out[0], out[1], out[2:]
+        )(length, frames, queries, gradients, in_hbm(visual), *keys_values)
+        return out[0], out[1], out[2], out[3:]
 
     def values(self, gradients, weights):
         piece = jax.ShapeDtypeStruct((self.rows, self.width), BF16)
@@ -257,7 +274,7 @@
             out_specs=[self.whole(self.width)] * self.pieces,
             out_shape=[piece] * self.pieces,
             scratch_shapes=[pltpu.VMEM((self.all_rows, HEAD_SIZE), F32)],
-        )(gradients, weights)
+        )(in_hbm(gradients), in_hbm(weights))
 
     def outputs(self, weights, dscores, keys_values):
         return self.call(
@@ -265,10 +282,10 @@
             2,
             4,
             "outputs",
-            in_specs=[self.inner_block] * 2 + [self.whole(2 * self.width)] * self.pieces,
+            in_specs=[self.inner_block] * 2 + [self.head_block],
             out_specs=[self.text_block] * 2,
             out_shape=[jax.ShapeDtypeStruct((self.text, self.wide), BF16)] * 2,
-        )(weights, dscores, *keys_values)
+        )(in_hbm(weights), in_hbm(dscores), in_hbm(keys_values))
 
 
 def sum_kernel(pieces, *refs):
@@ -368,7 +385,7 @@
 
     keys_values = from_partners([project(visual, key_weight, value_matrix[0])] * blocks)
     attention = Attention(queries[0], blocks, visual.shape[0])
-    weights, dscores, key_terms = attention.scores(
+    weights, dscores, all_keys_values, key_terms = attention.scores(
         visual_len, frame_end, queries[0], output_gradient[0], visual, keys_values
     )
     parts = from_partners(key_terms)
@@ -376,7 +393,7 @@
     value_terms = attention.values(output_gradient[0], weights)
     sums = from_partners(sum_terms(parts, value_terms))
     sums[1], weights = lax.optimization_barrier((sums[1], weights))
-    attn_out, query_grad = attention.outputs(weights, dscores, keys_values)
+    attn_out, query_grad = attention.outputs(weights, dscores, all_keys_values)
     value_grad, kept, sent = weight_terms(samples, (sample % 2)[None], parts, sums)
     came, bit = swap(sent, "dp", 1), 1
     while kept.shape[0] > 1:

time: 83.8 us -> 68.4 us (0.82)
  local copies, waits for them, and re-layouts: 16.6 us -> 0.01 us
  Pallas kernels: 16.2 us -> 18.8 us
    unnamed x68 -> x6, local copies, waits for them, and re-layouts: 16.6 us -> 0.01 us
    pallas_call x1, Pallas kernels: 3.07 us -> 4.91 us  [outputs(): self.call(outputs_kernel, 2, 4, 'outputs', in_specs=[self.inner_block] *...]
    pallas_call x1, Pallas kernels: 1.42 us -> 3.21 us  [values(): self.call(values_kernel, 1, 2, 'values', in_specs=[self.text_block, self....]
    pallas_call x1, Pallas kernels: 4.1 us -> 2.92 us  [project(): pl.pallas_call(functools.partial(project_kernel, streams), grid=(steps,),...]
    pallas_call x1, Pallas kernels: 5.87 us -> 6.75 us  [scores(): self.call(scores_kernel, 6, 4, 'scores', in_specs=[smem, smem, self.text_...]
  transfers between devices with their start and end apart: 23 -> 23, of which waited for: 10 -> 12; matrix products, arithmetic and copies ran while one was open for 0% -> 0% of each run, Pallas kernels for 5% -> 12%
where the time goes in v6:
time: 68.4 us; the launch traced here: 68.1 us
  starting transfers between devices  36.2 us (53%)
  Pallas kernels  18.8 us (27%)
  waiting for transfers between devices  11 us (16%)
  between operations  1.4 us (2%)
  other arithmetic  0.73 us (1%)
    ppermute x23, starting transfers between devices, swap(): return lax.ppermute(x, axis, [(i, i ^ mask) for i in range(size)])  36.2 us
    ppermute x23, waiting for transfers between devices, swap(): return lax.ppermute(x, axis, [(i, i ^ mask) for i in range(size)])  11 us
    pallas_call x1, Pallas kernels, scores(): self.call(scores_kernel, 6, 4, 'scores', in_specs=[smem, smem, self.text_...  6.75 us
    pallas_call x1, Pallas kernels, outputs(): self.call(outputs_kernel, 2, 4, 'outputs', in_specs=[self.inner_block] *...  4.91 us
    pallas_call x1, Pallas kernels, values(): self.call(values_kernel, 1, 2, 'values', in_specs=[self.text_block, self....  3.21 us
    pallas_call x1, Pallas kernels, project(): pl.pallas_call(functools.partial(project_kernel, streams), grid=(steps,),...  2.92 us
  transfers between devices with their start and end apart: 23, of which 12 were waited for; matrix products, arithmetic and copies ran while one was open for 0% of the time, Pallas kernels for 12%

profile of v6, /device:TPU:0, one launch (start us, length us, event | category | flops | bytes accessed | tf_op | source)
XLA Modules:
  0.0 68.1 jit_solution(14936923826025217342)
XLA Ops:
  0.7 2.9 %project.1.refs_0_ = bf16[32,1024]{1,0:T(8,128)(2,1)S(1)} custom-call(bf16[32,4096]{1,0:T(8,128)(2,1)} %bitcast.14, bf16[4096,512]{1,0:T(8,128)(2,1)} %refs_3_.1, bf16[4096,512]{1,0:T(8,128)(2,1)} %refs_3_.1, bf16[4096,512]{1,0:T(8,128)(2,1)} %refs_3_.1, bf16[4096,512]{1,0:T(8,128)(2,1)} %refs_3_.1, bf16[32,512]{1,0:T(8,128)(2,1)} %bitcast.16), custom_call_target="tpu_custom_call" | custom-call | flops 134217728 | bytes 4194304 | tf_op jit(solution)/shard_map/project/pallas_call | solution.py:68
  3.6 6.1 %collective-permute-start = (bf16[32,1024]{1,0:T(8,128)(2,1)S(1)}, bf16[32,1024]{1,0:T(8,128)(2,1)S(1)}, u32[]{:S(2)}, u32[]{:S(2)}) collective-permute-start(bf16[32,1024]{1,0:T(8,128)(2,1)S(1)} %project.1.refs_0_), channel_id=1, source_target_pairs={{0,28},{4,24},{8,20},{12,16},{16,12},{20,8},{24,4},{28,0},{1,29},{... | collective-permute-start | bytes 196616 | tf_op jit(solution)/shard_map/ppermute | solution.py:28
  9.9 0.7 %collective-permute-start.2 = (bf16[32,1024]{1,0:T(8,128)(2,1)S(1)}, bf16[32,1024]{1,0:T(8,128)(2,1)S(1)}, u32[]{:S(2)}, u32[]{:S(2)}) collective-permute-start(bf16[32,1024]{1,0:T(8,128)(2,1)S(1)} %project.1.refs_0_), channel_id=1, source_target_pairs={{0,20},{4,16},{8,28},{12,24},{16,4},{20,0},{24,12},{28,8},{1,21},{... | collective-permute-start | bytes 196616 | tf_op jit(solution)/shard_map/ppermute | solution.py:28
  10.6 2.0 %collective-permute-start.3 = (bf16[32,1024]{1,0:T(8,128)(2,1)S(1)}, bf16[32,1024]{1,0:T(8,128)(2,1)S(1)}, u32[]{:S(2)}, u32[]{:S(2)}) collective-permute-start(bf16[32,1024]{1,0:T(8,128)(2,1)S(1)} %project.1.refs_0_), channel_id=1, source_target_pairs={{0,16},{4,20},{8,24},{12,28},{16,0},{20,4},{24,8},{28,12},{1,17},{... | collective-permute-start | bytes 196616 | tf_op jit(solution)/shard_map/ppermute | solution.py:28
  12.7 2.3 %collective-permute-start.4 = (bf16[32,1024]{1,0:T(8,128)(2,1)S(1)}, bf16[32,1024]{1,0:T(8,128)(2,1)S(1)}, u32[]{:S(2)}, u32[]{:S(2)}) collective-permute-start(bf16[32,1024]{1,0:T(8,128)(2,1)S(1)} %project.1.refs_0_), channel_id=1, source_target_pairs={{0,12},{4,8},{8,4},{12,0},{16,28},{20,24},{24,20},{28,16},{1,13},{... | collective-permute-start | bytes 196616 | tf_op jit(solution)/shard_map/ppermute | solution.py:28
  15.0 0.8 %collective-permute-start.5 = (bf16[32,1024]{1,0:T(8,128)(2,1)S(1)}, bf16[32,1024]{1,0:T(8,128)(2,1)S(1)}, u32[]{:S(2)}, u32[]{:S(2)}) collective-permute-start(bf16[32,1024]{1,0:T(8,128)(2,1)S(1)} %project.1.refs_0_), channel_id=1, source_target_pairs={{0,8},{4,12},{8,0},{12,4},{16,24},{20,28},{24,16},{28,20},{1,9},{5... | collective-permute-start | bytes 196616 | tf_op jit(solution)/shard_map/ppermute | solution.py:28
  17.0 2.8 %collective-permute-done.2.refs_3_ = bf16[32,1024]{1,0:T(8,128)(2,1)S(1)} collective-permute-done((bf16[32,1024]{1,0:T(8,128)(2,1)S(1)}, bf16[32,1024]{1,0:T(8,128)(2,1)S(1)}, u32[]{:S(2)}, u32[]{:S(2)}) %collective-permute-start.2) | collective-permute-done | bytes 65568 | tf_op jit(solution)/shard_map/ppermute | solution.py:28
  19.8 1.1 %collective-permute-done.3.refs_4_ = bf16[32,1024]{1,0:T(8,128)(2,1)S(1)} collective-permute-done((bf16[32,1024]{1,0:T(8,128)(2,1)S(1)}, bf16[32,1024]{1,0:T(8,128)(2,1)S(1)}, u32[]{:S(2)}, u32[]{:S(2)}) %collective-permute-start.3) | collective-permute-done | bytes 65568 | tf_op jit(solution)/shard_map/ppermute | solution.py:28
  21.3 6.8 %scores.1 = (bf16[256,4096]{1,0:T(8,128)(2,1)}, bf16[256,4096]{1,0:T(8,128)(2,1)}, bf16[256,1024]{1,0:T(8,128)(2,1)}, bf16[32,1024]{1,0:T(8,128)(2,1)S(1)}, bf16...) custom-call(s32[1]{0:T(128)S(6)} %copy.11.length_ref, ...), custom_call_target="tpu_custom_call" | custom-call | flops 1610612736 | bytes 4194304 | tf_op jit(solution)/shard_map/scores/pallas_call | solution.py:245
  28.1 3.9 %collective-permute-start.7 = (bf16[32,1024]{1,0:T(8,128)(2,1)S(1)}, bf16[32,1024]{1,0:T(8,128)(2,1)S(1)}, u32[]{:S(2)}, u32[]{:S(2)}) collective-permute-start(bf16[32,1024]{1,0:T(8,128)(2,1)S(1)} %get-tuple-element.46), channel_id=1, source_target_pairs={{0,28},{4,24},{8,20},{12,16},{16,12},{20,8},{24,4},{28,0},{1,29},{... | collective-permute-start | bytes 196616 | tf_op jit(solution)/shard_map/ppermute | solution.py:28
  32.0 2.2 %collective-permute-start.9 = (bf16[32,1024]{1,0:T(8,128)(2,1)S(1)}, bf16[32,1024]{1,0:T(8,128)(2,1)S(1)}, u32[]{:S(2)}, u32[]{:S(2)}) collective-permute-start(bf16[32,1024]{1,0:T(8,128)(2,1)S(1)} %get-tuple-element.50), channel_id=1, source_target_pairs={{0,20},{4,16},{8,28},{12,24},{16,4},{20,0},{24,12},{28,8},{1,21},{... | collective-permute-start | bytes 196616 | tf_op jit(solution)/shard_map/ppermute | solution.py:28
  34.3 1.6 %collective-permute-start.10 = (bf16[32,1024]{1,0:T(8,128)(2,1)S(1)}, bf16[32,1024]{1,0:T(8,128)(2,1)S(1)}, u32[]{:S(2)}, u32[]{:S(2)}) collective-permute-start(bf16[32,1024]{1,0:T(8,128)(2,1)S(1)} %get-tuple-element.51), channel_id=1, source_target_pairs={{0,16},{4,20},{8,24},{12,28},{16,0},{20,4},{24,8},{28,12},{1,17},{... | collective-permute-start | bytes 196616 | tf_op jit(solution)/shard_map/ppermute | solution.py:28
  35.8 1.4 %collective-permute-start.11 = (bf16[32,1024]{1,0:T(8,128)(2,1)S(1)}, bf16[32,1024]{1,0:T(8,128)(2,1)S(1)}, u32[]{:S(2)}, u32[]{:S(2)}) collective-permute-start(bf16[32,1024]{1,0:T(8,128)(2,1)S(1)} %get-tuple-element.52), channel_id=1, source_target_pairs={{0,12},{4,8},{8,4},{12,0},{16,28},{20,24},{24,20},{28,16},{1,13},{... | collective-permute-start | bytes 196616 | tf_op jit(solution)/shard_map/ppermute | solution.py:28
  37.3 1.2 %collective-permute-start.12 = (bf16[32,1024]{1,0:T(8,128)(2,1)S(1)}, bf16[32,1024]{1,0:T(8,128)(2,1)S(1)}, u32[]{:S(2)}, u32[]{:S(2)}) collective-permute-start(bf16[32,1024]{1,0:T(8,128)(2,1)S(1)} %get-tuple-element.53), channel_id=1, source_target_pairs={{0,8},{4,12},{8,0},{12,4},{16,24},{20,28},{24,16},{28,20},{1,9},{5... | collective-permute-start | bytes 196616 | tf_op jit(solution)/shard_map/ppermute | solution.py:28
  38.8 0.8 %collective-permute-start.13 = (bf16[32,1024]{1,0:T(8,128)(2,1)S(1)}, bf16[32,1024]{1,0:T(8,128)(2,1)S(1)}, u32[]{:S(2)}, u32[]{:S(2)}) collective-permute-start(bf16[32,1024]{1,0:T(8,128)(2,1)S(1)} %get-tuple-element.54), channel_id=1, source_target_pairs={{0,4},{4,0},{8,12},{12,8},{16,20},{20,16},{24,28},{28,24},{1,5},{5... | collective-permute-start | bytes 196616 | tf_op jit(solution)/shard_map/ppermute | solution.py:28
  39.5 3.2 %values.1 = (bf16[32,512]{1,0:T(8,128)(2,1)S(1)}, bf16[32,512]{1,0:T(8,128)(2,1)S(1)}, bf16[32,512]{1,0:T(8,128)(2,1)S(1)}, bf16[32,512]{1,0:T(8,128)(2,1)S(1)},...) custom-call(bf16[128,4096]{1,0:T(8,128)(2,1)} %bitcast.11, ...), custom_call_target="tpu_custom_call" | custom-call | flops 268435456 | bytes 2097152 | tf_op jit(solution)/shard_map/values/pallas_call | solution.py:268
  43.3 4.0 %collective-permute-start.14 = (bf16[32,1024]{1,0:T(8,128)(2,1)S(1)}, bf16[32,1024]{1,0:T(8,128)(2,1)S(1)}, u32[]{:S(2)}, u32[]{:S(2)}) collective-permute-start(bf16[32,1024]{1,0:T(8,128)(2,1)S(1)} %get-tuple-element.65), channel_id=1, source_target_pairs={{0,28},{4,24},{8,20},{12,16},{16,12},{20,8},{24,4},{28,0},{1,29},{... | collective-permute-start | bytes 196616 | tf_op jit(solution)/shard_map/ppermute | solution.py:28
  47.7 2.0 %collective-permute-start.16 = (bf16[32,1024]{1,0:T(8,128)(2,1)S(1)}, bf16[32,1024]{1,0:T(8,128)(2,1)S(1)}, u32[]{:S(2)}, u32[]{:S(2)}) collective-permute-start(bf16[32,1024]{1,0:T(8,128)(2,1)S(1)} %get-tuple-element.68), channel_id=1, source_target_pairs={{0,20},{4,16},{8,28},{12,24},{16,4},{20,0},{24,12},{28,8},{1,21},{... | collective-permute-start | bytes 196616 | tf_op jit(solution)/shard_map/ppermute | solution.py:28
  49.7 1.3 %collective-permute-start.17 = (bf16[32,1024]{1,0:T(8,128)(2,1)S(1)}, bf16[32,1024]{1,0:T(8,128)(2,1)S(1)}, u32[]{:S(2)}, u32[]{:S(2)}) collective-permute-start(bf16[32,1024]{1,0:T(8,128)(2,1)S(1)} %get-tuple-element.69), channel_id=1, source_target_pairs={{0,16},{4,20},{8,24},{12,28},{16,0},{20,4},{24,8},{28,12},{1,17},{... | collective-permute-start | bytes 196616 | tf_op jit(solution)/shard_map/ppermute | solution.py:28
  51.0 1.6 %collective-permute-start.18 = (bf16[32,1024]{1,0:T(8,128)(2,1)S(1)}, bf16[32,1024]{1,0:T(8,128)(2,1)S(1)}, u32[]{:S(2)}, u32[]{:S(2)}) collective-permute-start(bf16[32,1024]{1,0:T(8,128)(2,1)S(1)} %get-tuple-element.70), channel_id=1, source_target_pairs={{0,12},{4,8},{8,4},{12,0},{16,28},{20,24},{24,20},{28,16},{1,13},{... | collective-permute-start | bytes 196616 | tf_op jit(solution)/shard_map/ppermute | solution.py:28
  52.6 0.9 %collective-permute-start.19 = (bf16[32,1024]{1,0:T(8,128)(2,1)S(1)}, bf16[32,1024]{1,0:T(8,128)(2,1)S(1)}, u32[]{:S(2)}, u32[]{:S(2)}) collective-permute-start(bf16[32,1024]{1,0:T(8,128)(2,1)S(1)} %get-tuple-element.71), channel_id=1, source_target_pairs={{0,8},{4,12},{8,0},{12,4},{16,24},{20,28},{24,16},{28,20},{1,9},{5... | collective-permute-start | bytes 196616 | tf_op jit(solution)/shard_map/ppermute | solution.py:28
  53.5 0.6 collective-permute-done.15.refs_10_
  54.2 0.7 %collective-permute-start.20 = (bf16[32,1024]{1,0:T(8,128)(2,1)S(1)}, bf16[32,1024]{1,0:T(8,128)(2,1)S(1)}, u32[]{:S(2)}, u32[]{:S(2)}) collective-permute-start(bf16[32,1024]{1,0:T(8,128)(2,1)S(1)} %get-tuple-element.72), channel_id=1, source_target_pairs={{0,4},{4,0},{8,12},{12,8},{16,20},{20,16},{24,28},{28,24},{1,5},{5... | collective-permute-start | bytes 196616 | tf_op jit(solution)/shard_map/ppermute | solution.py:28
  54.9 1.7 %collective-permute-done.16.refs_11_ = bf16[32,1024]{1,0:T(8,128)(2,1)S(1)} collective-permute-done((bf16[32,1024]{1,0:T(8,128)(2,1)S(1)}, bf16[32,1024]{1,0:T(8,128)(2,1)S(1)}, u32[]{:S(2)}, u32[]{:S(2)}) %collective-permute-start.16) | collective-permute-done | bytes 65568 | tf_op jit(solution)/shard_map/ppermute | solution.py:28
  56.6 0.5 collective-permute-done.17.refs_12_
  57.2 0.6 collective-permute-done.19.refs_14_
  57.7 0.7 collective-permute-done.20.refs_15_
  58.4 0.9 %weight_terms.1 = (bf16[32,512]{1,0:T(8,128)(2,1)}, f32[2,128,512]{2,1,0:T(8,128)S(1)}, bf16[2,128,512]{2,1,0:T(8,128)(2,1)S(1)}) custom-call(s32[1]{0:T(128)} %bitcast.1.core_ref, bf16[32,1024]{1,0:T(8,128)(2,1)S(1)} %get-tuple-element.45.refs_0_, bf16[32,1024]{1,0:T(8,128)(2,1)S(1)} %collective-permute-done.7.refs_1_, ...), custom_call_target="tpu_custom_call" | custom-call | tf_op jit(solution)/shard_map/weight_terms/pallas_call | solution.py:342
  59.3 1.5 %collective-permute-done.21.came_ref = bf16[2,128,512]{2,1,0:T(8,128)(2,1)S(1)} collective-permute-done((bf16[2,128,512]{2,1,0:T(8,128)(2,1)S(1)}, bf16[2,128,512]{2,1,0:T(8,128)(2,1)S(1)}, u32[]{:S(2)}, u32[]{:S(2)}) %collective-permute-start.21) | collective-permute-done | bytes 262176 | tf_op jit(solution)/shard_map/ppermute | solution.py:28
  60.9 1.6 %collective-permute-start.22 = (bf16[1,128,512]{2,1,0:T(8,128)(2,1)S(1)}, bf16[1,128,512]{2,1,0:T(8,128)(2,1)S(1)}, u32[]{:S(2)}, u32[]{:S(2)}) collective-permute-start(bf16[1,128,512]{2,1,0:T(8,128)(2,1)S(1)} %get-tuple-element.75), channel_id=1, source_target_pairs={{0,2},{1,3},{2,0},{3,1},{4,6},{5,7},{6,4},{7,5},{8,10},{9,11},{10,... | collective-permute-start | bytes 393224 | tf_op jit(solution)/shard_map/ppermute | solution.py:28
  62.5 4.9 %outputs.1 = (bf16[128,4096]{1,0:T(8,128)(2,1)}, bf16[128,4096]{1,0:T(8,128)(2,1)}) custom-call(bf16[256,4096]{1,0:T(8,128)(2,1)} %get-tuple-element.76.w_ref, bf16[256,4096]{1,0:T(8,128)(2,1)} %get-tuple-element.77.ds_ref, bf16[256,1024]{1,0:T(8,128)(2,1)} %get-tuple-element.78.kv_ref), custom_call_target="tpu_custom_call" | custom-call | flops 536870912 | bytes 4194304 | tf_op jit(solution)/shard_map/outputs/pallas_call | solution.py:280
  67.4 0.7 %add_bitcast_fusion = f32[128,512]{1,0:T(8,128)} fusion(f32[1,128,512]{2,1,0:T(8,128)S(1)} %get-tuple-element.84, bf16[1,128,512]{2,1,0:T(8,128)(2,1)S(1)} %collective-permute-done.22), kind=kLoop, calls=%fused_computation | loop fusion | flops 131072 | bytes 655360 | tf_op jit(solution)/shard_map/add | solution.py:403
  (28 shorter events, 2.7 us)
Async XLA Ops:
  0.6 20.7 %copy-start = (bf16[1,128,4096]{2,1,0:T(8,128)(2,1)S(1)}, bf16[1,128,4096]{2,1,0:T(8,128)(2,1)}, u32[]{:S(2)}) copy-start(bf16[1,128,4096]{2,1,0:T(8,128)(2,1)} %param.11) | copy-start | bytes 3145732
  0.6 20.7 %copy-start.1 = (bf16[1,128,4096]{2,1,0:T(8,128)(2,1)S(1)}, bf16[1,128,4096]{2,1,0:T(8,128)(2,1)}, u32[]{:S(2)}) copy-start(bf16[1,128,4096]{2,1,0:T(8,128)(2,1)} %param.10) | copy-start | bytes 3145732
  0.7 20.7 %copy-start.2 = (s32[1,8]{1,0:T(1,128)S(1)}, s32[1,8]{1,0:T(1,128)}, u32[]{:S(2)}) copy-start(s32[1,8]{1,0:T(1,128)} %frame_ref.1) | copy-start | bytes 100
  3.6 11.4 %collective-permute-start = (bf16[32,1024]{1,0:T(8,128)(2,1)S(1)}, bf16[32,1024]{1,0:T(8,128)(2,1)S(1)}, u32[]{:S(2)}, u32[]{:S(2)}) collective-permute-start(bf16[32,1024]{1,0:T(8,128)(2,1)S(1)} %project.1.refs_0_), channel_id=1, source_target_pairs={{0,28},{4,24},{8,20},{12,16},{16,12},{20,8},{24,4},{28,0},{1,29},{... | collective-permute-start | bytes 196616 | tf_op jit(solution)/shard_map/ppermute | solution.py:28
  9.7 6.3 %collective-permute-start.1 = (bf16[32,1024]{1,0:T(8,128)(2,1)S(1)}, bf16[32,1024]{1,0:T(8,128)(2,1)S(1)}, u32[]{:S(2)}, u32[]{:S(2)}) collective-permute-start(bf16[32,1024]{1,0:T(8,128)(2,1)S(1)} %project.1.refs_0_), channel_id=1, source_target_pairs={{0,24},{4,28},{8,16},{12,20},{16,8},{20,12},{24,0},{28,4},{1,25},{... | collective-permute-start | bytes 196616 | tf_op jit(solution)/shard_map/ppermute | solution.py:28
  9.9 9.9 %collective-permute-start.2 = (bf16[32,1024]{1,0:T(8,128)(2,1)S(1)}, bf16[32,1024]{1,0:T(8,128)(2,1)S(1)}, u32[]{:S(2)}, u32[]{:S(2)}) collective-permute-start(bf16[32,1024]{1,0:T(8,128)(2,1)S(1)} %project.1.refs_0_), channel_id=1, source_target_pairs={{0,20},{4,16},{8,28},{12,24},{16,4},{20,0},{24,12},{28,8},{1,21},{... | collective-permute-start | bytes 196616 | tf_op jit(solution)/shard_map/ppermute | solution.py:28
  10.6 10.3 %collective-permute-start.3 = (bf16[32,1024]{1,0:T(8,128)(2,1)S(1)}, bf16[32,1024]{1,0:T(8,128)(2,1)S(1)}, u32[]{:S(2)}, u32[]{:S(2)}) collective-permute-start(bf16[32,1024]{1,0:T(8,128)(2,1)S(1)} %project.1.refs_0_), channel_id=1, source_target_pairs={{0,16},{4,20},{8,24},{12,28},{16,0},{20,4},{24,8},{28,12},{1,17},{... | collective-permute-start | bytes 196616 | tf_op jit(solution)/shard_map/ppermute | solution.py:28
  12.7 8.3 %collective-permute-start.4 = (bf16[32,1024]{1,0:T(8,128)(2,1)S(1)}, bf16[32,1024]{1,0:T(8,128)(2,1)S(1)}, u32[]{:S(2)}, u32[]{:S(2)}) collective-permute-start(bf16[32,1024]{1,0:T(8,128)(2,1)S(1)} %project.1.refs_0_), channel_id=1, source_target_pairs={{0,12},{4,8},{8,4},{12,0},{16,28},{20,24},{24,20},{28,16},{1,13},{... | collective-permute-start | bytes 196616 | tf_op jit(solution)/shard_map/ppermute | solution.py:28
  15.0 6.4 %collective-permute-start.5 = (bf16[32,1024]{1,0:T(8,128)(2,1)S(1)}, bf16[32,1024]{1,0:T(8,128)(2,1)S(1)}, u32[]{:S(2)}, u32[]{:S(2)}) collective-permute-start(bf16[32,1024]{1,0:T(8,128)(2,1)S(1)} %project.1.refs_0_), channel_id=1, source_target_pairs={{0,8},{4,12},{8,0},{12,4},{16,24},{20,28},{24,16},{28,20},{1,9},{5... | collective-permute-start | bytes 196616 | tf_op jit(solution)/shard_map/ppermute | solution.py:28
  15.9 5.4 %collective-permute-start.6 = (bf16[32,1024]{1,0:T(8,128)(2,1)S(1)}, bf16[32,1024]{1,0:T(8,128)(2,1)S(1)}, u32[]{:S(2)}, u32[]{:S(2)}) collective-permute-start(bf16[32,1024]{1,0:T(8,128)(2,1)S(1)} %project.1.refs_0_), channel_id=1, source_target_pairs={{0,4},{4,0},{8,12},{12,8},{16,20},{20,16},{24,28},{28,24},{1,5},{5... | collective-permute-start | bytes 196616 | tf_op jit(solution)/shard_map/ppermute | solution.py:28
  28.1 9.2 %collective-permute-start.7 = (bf16[32,1024]{1,0:T(8,128)(2,1)S(1)}, bf16[32,1024]{1,0:T(8,128)(2,1)S(1)}, u32[]{:S(2)}, u32[]{:S(2)}) collective-permute-start(bf16[32,1024]{1,0:T(8,128)(2,1)S(1)} %get-tuple-element.46), channel_id=1, source_target_pairs={{0,28},{4,24},{8,20},{12,16},{16,12},{20,8},{24,4},{28,0},{1,29},{... | collective-permute-start | bytes 196616 | tf_op jit(solution)/shard_map/ppermute | solution.py:28
  32.0 6.8 %collective-permute-start.8 = (bf16[32,1024]{1,0:T(8,128)(2,1)S(1)}, bf16[32,1024]{1,0:T(8,128)(2,1)S(1)}, u32[]{:S(2)}, u32[]{:S(2)}) collective-permute-start(bf16[32,1024]{1,0:T(8,128)(2,1)S(1)} %get-tuple-element.49), channel_id=1, source_target_pairs={{0,24},{4,28},{8,16},{12,20},{16,8},{20,12},{24,0},{28,4},{1,25},{... | collective-permute-start | bytes 196616 | tf_op jit(solution)/shard_map/ppermute | solution.py:28
  32.0 10.7 %collective-permute-start.9 = (bf16[32,1024]{1,0:T(8,128)(2,1)S(1)}, bf16[32,1024]{1,0:T(8,128)(2,1)S(1)}, u32[]{:S(2)}, u32[]{:S(2)}) collective-permute-start(bf16[32,1024]{1,0:T(8,128)(2,1)S(1)} %get-tuple-element.50), channel_id=1, source_target_pairs={{0,20},{4,16},{8,28},{12,24},{16,4},{20,0},{24,12},{28,8},{1,21},{... | collective-permute-start | bytes 196616 | tf_op jit(solution)/shard_map/ppermute | solution.py:28
  34.3 8.5 %collective-permute-start.10 = (bf16[32,1024]{1,0:T(8,128)(2,1)S(1)}, bf16[32,1024]{1,0:T(8,128)(2,1)S(1)}, u32[]{:S(2)}, u32[]{:S(2)}) collective-permute-start(bf16[32,1024]{1,0:T(8,128)(2,1)S(1)} %get-tuple-element.51), channel_id=1, source_target_pairs={{0,16},{4,20},{8,24},{12,28},{16,0},{20,4},{24,8},{28,12},{1,17},{... | collective-permute-start | bytes 196616 | tf_op jit(solution)/shard_map/ppermute | solution.py:28
  35.8 6.9 %collective-permute-start.11 = (bf16[32,1024]{1,0:T(8,128)(2,1)S(1)}, bf16[32,1024]{1,0:T(8,128)(2,1)S(1)}, u32[]{:S(2)}, u32[]{:S(2)}) collective-permute-start(bf16[32,1024]{1,0:T(8,128)(2,1)S(1)} %get-tuple-element.52), channel_id=1, source_target_pairs={{0,12},{4,8},{8,4},{12,0},{16,28},{20,24},{24,20},{28,16},{1,13},{... | collective-permute-start | bytes 196616 | tf_op jit(solution)/shard_map/ppermute | solution.py:28
  37.3 5.5 %collective-permute-start.12 = (bf16[32,1024]{1,0:T(8,128)(2,1)S(1)}, bf16[32,1024]{1,0:T(8,128)(2,1)S(1)}, u32[]{:S(2)}, u32[]{:S(2)}) collective-permute-start(bf16[32,1024]{1,0:T(8,128)(2,1)S(1)} %get-tuple-element.53), channel_id=1, source_target_pairs={{0,8},{4,12},{8,0},{12,4},{16,24},{20,28},{24,16},{28,20},{1,9},{5... | collective-permute-start | bytes 196616 | tf_op jit(solution)/shard_map/ppermute | solution.py:28
  38.8 4.5 %collective-permute-start.13 = (bf16[32,1024]{1,0:T(8,128)(2,1)S(1)}, bf16[32,1024]{1,0:T(8,128)(2,1)S(1)}, u32[]{:S(2)}, u32[]{:S(2)}) collective-permute-start(bf16[32,1024]{1,0:T(8,128)(2,1)S(1)} %get-tuple-element.54), channel_id=1, source_target_pairs={{0,4},{4,0},{8,12},{12,8},{16,20},{20,16},{24,28},{28,24},{1,5},{5... | collective-permute-start | bytes 196616 | tf_op jit(solution)/shard_map/ppermute | solution.py:28
  43.3 9.3 %collective-permute-start.14 = (bf16[32,1024]{1,0:T(8,128)(2,1)S(1)}, bf16[32,1024]{1,0:T(8,128)(2,1)S(1)}, u32[]{:S(2)}, u32[]{:S(2)}) collective-permute-start(bf16[32,1024]{1,0:T(8,128)(2,1)S(1)} %get-tuple-element.65), channel_id=1, source_target_pairs={{0,28},{4,24},{8,20},{12,16},{16,12},{20,8},{24,4},{28,0},{1,29},{... | collective-permute-start | bytes 196616 | tf_op jit(solution)/shard_map/ppermute | solution.py:28
  47.3 6.8 %collective-permute-start.15 = (bf16[32,1024]{1,0:T(8,128)(2,1)S(1)}, bf16[32,1024]{1,0:T(8,128)(2,1)S(1)}, u32[]{:S(2)}, u32[]{:S(2)}) collective-permute-start(bf16[32,1024]{1,0:T(8,128)(2,1)S(1)} %get-tuple-element.67), channel_id=1, source_target_pairs={{0,24},{4,28},{8,16},{12,20},{16,8},{20,12},{24,0},{28,4},{1,25},{... | collective-permute-start | bytes 196616 | tf_op jit(solution)/shard_map/ppermute | solution.py:28
  47.7 8.9 %collective-permute-start.16 = (bf16[32,1024]{1,0:T(8,128)(2,1)S(1)}, bf16[32,1024]{1,0:T(8,128)(2,1)S(1)}, u32[]{:S(2)}, u32[]{:S(2)}) collective-permute-start(bf16[32,1024]{1,0:T(8,128)(2,1)S(1)} %get-tuple-element.68), channel_id=1, source_target_pairs={{0,20},{4,16},{8,28},{12,24},{16,4},{20,0},{24,12},{28,8},{1,21},{... | collective-permute-start | bytes 196616 | tf_op jit(solution)/shard_map/ppermute | solution.py:28
  49.7 7.4 %collective-permute-start.17 = (bf16[32,1024]{1,0:T(8,128)(2,1)S(1)}, bf16[32,1024]{1,0:T(8,128)(2,1)S(1)}, u32[]{:S(2)}, u32[]{:S(2)}) collective-permute-start(bf16[32,1024]{1,0:T(8,128)(2,1)S(1)} %get-tuple-element.69), channel_id=1, source_target_pairs={{0,16},{4,20},{8,24},{12,28},{16,0},{20,4},{24,8},{28,12},{1,17},{... | collective-permute-start | bytes 196616 | tf_op jit(solution)/shard_map/ppermute | solution.py:28
  51.0 6.2 %collective-permute-start.18 = (bf16[32,1024]{1,0:T(8,128)(2,1)S(1)}, bf16[32,1024]{1,0:T(8,128)(2,1)S(1)}, u32[]{:S(2)}, u32[]{:S(2)}) collective-permute-start(bf16[32,1024]{1,0:T(8,128)(2,1)S(1)} %get-tuple-element.70), channel_id=1, source_target_pairs={{0,12},{4,8},{8,4},{12,0},{16,28},{20,24},{24,20},{28,16},{1,13},{... | collective-permute-start | bytes 196616 | tf_op jit(solution)/shard_map/ppermute | solution.py:28
  52.6 5.1 %collective-permute-start.19 = (bf16[32,1024]{1,0:T(8,128)(2,1)S(1)}, bf16[32,1024]{1,0:T(8,128)(2,1)S(1)}, u32[]{:S(2)}, u32[]{:S(2)}) collective-permute-start(bf16[32,1024]{1,0:T(8,128)(2,1)S(1)} %get-tuple-element.71), channel_id=1, source_target_pairs={{0,8},{4,12},{8,0},{12,4},{16,24},{20,28},{24,16},{28,20},{1,9},{5... | collective-permute-start | bytes 196616 | tf_op jit(solution)/shard_map/ppermute | solution.py:28
  54.2 4.3 %collective-permute-start.20 = (bf16[32,1024]{1,0:T(8,128)(2,1)S(1)}, bf16[32,1024]{1,0:T(8,128)(2,1)S(1)}, u32[]{:S(2)}, u32[]{:S(2)}) collective-permute-start(bf16[32,1024]{1,0:T(8,128)(2,1)S(1)} %get-tuple-element.72), channel_id=1, source_target_pairs={{0,4},{4,0},{8,12},{12,8},{16,20},{20,16},{24,28},{28,24},{1,5},{5... | collective-permute-start | bytes 196616 | tf_op jit(solution)/shard_map/ppermute | solution.py:28
  59.3 1.5 %collective-permute-start.21 = (bf16[2,128,512]{2,1,0:T(8,128)(2,1)S(1)}, bf16[2,128,512]{2,1,0:T(8,128)(2,1)S(1)}, u32[]{:S(2)}, u32[]{:S(2)}) collective-permute-start(bf16[2,128,512]{2,1,0:T(8,128)(2,1)S(1)} %get-tuple-element.74), channel_id=1, source_target_pairs={{0,1},{1,0},{2,3},{3,2},{4,5},{5,4},{6,7},{7,6},{8,9},{9,8},{10,11... | collective-permute-start | bytes 786440 | tf_op jit(solution)/shard_map/ppermute | solution.py:28
  60.9 6.5 %collective-permute-start.22 = (bf16[1,128,512]{2,1,0:T(8,128)(2,1)S(1)}, bf16[1,128,512]{2,1,0:T(8,128)(2,1)S(1)}, u32[]{:S(2)}, u32[]{:S(2)}) collective-permute-start(bf16[1,128,512]{2,1,0:T(8,128)(2,1)S(1)} %get-tuple-element.75), channel_id=1, source_target_pairs={{0,2},{1,3},{2,0},{3,1},{4,6},{5,7},{6,4},{7,5},{8,10},{9,11},{10,... | collective-permute-start | bytes 393224 | tf_op jit(solution)/shard_map/ppermute | solution.py:28

commit v7 on v6

--- a/solution.py
+++ b/solution.py
@@ -87,95 +87,89 @@
     )(in_hbm(visual), *[in_hbm(key_weight)] * streams, in_hbm(value))
 
 
+def head_pair(ref, rows, start):
+    first = pl.ds(pl.multiple_of(start, HEAD_SIZE), HEAD_SIZE)
+    second = pl.ds(pl.multiple_of(start + HEAD_SIZE, HEAD_SIZE), HEAD_SIZE)
+    return jnp.concatenate([ref[rows, first], ref[rows, second]], axis=0)
+
+
 def scores_kernel(pieces, length_ref, frame_ref, q_ref, g_ref, visual_hbm, *refs):
-    kv_refs, (w_ref, ds_ref, kv_ref) = refs[:pieces], refs[pieces : pieces + 3]
-    key_refs = refs[pieces + 3 : 2 * pieces + 3]
-    kg_acc, visual, sem = refs[2 * pieces + 3 :]
-    j, i = pl.program_id(0), pl.program_id(1)
-    last = jnp.logical_and(j == pl.num_programs(0) - 1, i == pl.num_programs(1) - 1)
+    kv_refs, (w_ref, ds_ref, k_ref, v_ref) = refs[:pieces], refs[pieces : pieces + 4]
+    key_refs = refs[pieces + 4 : 2 * pieces + 4]
+    kg_acc, bias_ref, visual, sem = refs[2 * pieces + 4 :]
     copy = pltpu.make_async_copy(visual_hbm, visual, sem)
-
-    @pl.when(jnp.logical_and(j == 0, i == 0))
-    def _():
-        copy.start()
-
+    copy.start()
     block = lax.axis_index("blk")
-    limit = jnp.minimum(length_ref[0], TILE * frame_ref[0, block * pl.num_programs(1) + i])
+    tiles = q_ref.shape[0] // TILE
+    rows = kv_refs[0].shape[0]
     width = KEY_HEADS * HEAD_SIZE
-    head = pl.ds(pl.multiple_of(j * HEAD_SIZE, HEAD_SIZE), HEAD_SIZE)
-    value_head = pl.ds(pl.multiple_of(width + j * HEAD_SIZE, HEAD_SIZE), HEAD_SIZE)
-    keys = jnp.concatenate([r[:, head] for r in kv_refs], axis=0)
-    values = jnp.concatenate([r[:, value_head] for r in kv_refs], axis=0)
-    kv_ref[:, :HEAD_SIZE] = keys
-    kv_ref[:, HEAD_SIZE:] = values
     pair = 2 * TILE
-    rows = kv_refs[0].shape[0]
+    pairs = HEADS_PER_KEY // 2
+    span = HEADS_PER_KEY * HEAD_SIZE
+    scale = HEAD_SIZE**-0.5
+    for m in range(pieces):
+        part = slice(m * rows, (m + 1) * rows)
+        k_ref[part, :] = kv_refs[m][:, :width]
+        v_ref[part, :] = kv_refs[m][:, width:]
     row = lax.broadcasted_iota(jnp.int32, (rows, pair), 0)
-    bias = jnp.concatenate(
-        [
-            jnp.where(row + (block ^ partner(m, pieces)) * rows < limit, 0.0, NEGATIVE_FILLER)
-            for m in range(pieces)
-        ],
-        axis=0,
-    )
-    scale = HEAD_SIZE**-0.5
-    pairs = HEADS_PER_KEY // 2
-    q_stack, raw, dprobs = [], {}, {}
-
-    def stacked(ref, p):
-        first = slice(p * pair, p * pair + HEAD_SIZE)
-        second = slice(p * pair + HEAD_SIZE, (p + 1) * pair)
-        return jnp.concatenate([ref[:, first], ref[:, second]], axis=0)
-
-    def products(p):
-        q_stack.append(stacked(q_ref, p))
-        raw[p] = dot(keys, q_stack[p], ((1,), (1,)))
-        dprobs[p] = dot(values, stacked(g_ref, p), ((1,), (1,)))
-
-    products(0)
-    for p in range(pairs):
-        if p + 1 < pairs:
-            products(p + 1)
-        scores = raw.pop(p) + bias
-        peak = jnp.max(scores, axis=0, keepdims=True)
-        shifted = jnp.exp2((scores - peak) * (scale * LOG2_E))
-        probs = shifted * (1.0 / jnp.sum(shifted, axis=0, keepdims=True))
-        terms = probs * dprobs.pop(p)
-        delta = jnp.sum(terms, axis=0, keepdims=True)
-        both = slice(p * pair, (p + 1) * pair)
-        w_ref[:, both] = probs.astype(BF16)
-        ds_ref[:, both] = ((terms - probs * delta) * scale).astype(BF16)
-    kg = dot(ds_ref[...], jnp.concatenate(q_stack, axis=0))
-
-    @pl.when(i == 0)
-    def _():
-        kg_acc[...] = kg
-
-    @pl.when(i > 0)
-    def _():
-        kg_acc[...] += kg
-
-    @pl.when(i == pl.num_programs(1) - 1)
-    def _():
+    for i in range(tiles):
+        text = slice(i * TILE, (i + 1) * TILE)
+        limit = jnp.minimum(length_ref[0], TILE * frame_ref[0, block * tiles + i])
         for m in range(pieces):
-            key_refs[m][:, head] = kg_acc[m * rows : (m + 1) * rows, :].astype(BF16)
-
-    @pl.when(last)
-    def _():
-        copy.wait()
-        share = visual.shape[1] // pieces
-        for m in range(pieces):
-            start = pl.multiple_of((block ^ partner(m, pieces)) * share, HEAD_SIZE)
-            key_refs[m][:, width:] = visual[:, pl.ds(start, share)]
-
-
-def values_kernel(pieces, g_ref, w_ref, *refs):
-    value_refs, vg_acc = refs[:pieces], refs[pieces]
+            live = row + (block ^ partner(m, pieces)) * rows < limit
+            bias_ref[m * rows : (m + 1) * rows, :] = jnp.where(live, 0.0, NEGATIVE_FILLER)
+
+        @pl.loop(0, KEY_HEADS)
+        def _(j, i=i, text=text):
+            head = pl.ds(pl.multiple_of(j * HEAD_SIZE, HEAD_SIZE), HEAD_SIZE)
+            keys, values = k_ref[:, head], v_ref[:, head]
+            q_stack, raw, dprobs = [], {}, {}
+
+            def products(p):
+                start = j * span + p * pair
+                q_stack.append(head_pair(q_ref, text, start))
+                raw[p] = dot(keys, q_stack[p], ((1,), (1,)))
+                dprobs[p] = dot(values, head_pair(g_ref, text, start), ((1,), (1,)))
+
+            products(0)
+            ds_stack = []
+            for p in range(pairs):
+                if p + 1 < pairs:
+                    products(p + 1)
+                scores = raw.pop(p) + bias_ref[...]
+                peak = jnp.max(scores, axis=0, keepdims=True)
+                shifted = jnp.exp2((scores - peak) * (scale * LOG2_E))
+                terms = shifted * dprobs.pop(p)
+                inverse = 1.0 / jnp.sum(shifted, axis=0, keepdims=True)
+                slope = inverse * scale
+                offset = jnp.sum(terms, axis=0, keepdims=True) * inverse * slope
+                start = (i * KEY_HEADS + j) * span + p * pair
+                both = pl.ds(pl.multiple_of(start, HEAD_SIZE), pair)
+                w_ref[:, both] = (shifted * inverse).astype(BF16)
+                ds_stack.append((terms * slope - shifted * offset).astype(BF16))
+                ds_ref[:, both] = ds_stack[p]
+            kg = dot(jnp.concatenate(ds_stack, axis=1), jnp.concatenate(q_stack, axis=0))
+            if i == 0:
+                kg_acc[:, head] = kg
+            else:
+                kg_acc[:, head] += kg
+
+    copy.wait()
+    share = visual.shape[1] // pieces
+    for m in range(pieces):
+        start = pl.multiple_of((block ^ partner(m, pieces)) * share, HEAD_SIZE)
+        key_refs[m][:, :width] = kg_acc[m * rows : (m + 1) * rows, :].astype(BF16)
+        key_refs[m][:, width:] = visual[:, pl.ds(start, share)]
+
+
+def values_kernel(pieces, g_ref, w_ref, v_ref, *refs):
+    o_ref, value_refs, vg_acc = refs[0], refs[1 : 1 + pieces], refs[1 + pieces]
     j, i = pl.program_id(0), pl.program_id(1)
     head = pl.ds(pl.multiple_of(j * HEAD_SIZE, HEAD_SIZE), HEAD_SIZE)
     rows = value_refs[0].shape[0]
     stack = [g_ref[:, h * HEAD_SIZE : (h + 1) * HEAD_SIZE] for h in range(HEADS_PER_KEY)]
     vg = dot(w_ref[...], jnp.concatenate(stack, axis=0))
+    store_rows(o_ref, v_ref[...].T, w_ref)
 
     @pl.when(i == 0)
     def _():
@@ -191,19 +185,16 @@
             value_refs[m][:, head] = vg_acc[m * rows : (m + 1) * rows, :].astype(BF16)
 
 
-def outputs_kernel(pieces, w_ref, ds_ref, kv_ref, o_ref, qg_ref):
-    keys_t, values_t = kv_ref[:, :HEAD_SIZE].T, kv_ref[:, HEAD_SIZE:].T
+def store_rows(out_ref, left, inner_ref):
     pair = 2 * TILE
     for p in range(HEADS_PER_KEY // 2):
-        first = slice(p * pair, p * pair + HEAD_SIZE)
-        second = slice(p * pair + HEAD_SIZE, (p + 1) * pair)
-        both = slice(p * pair, (p + 1) * pair)
-        out = dot(values_t, w_ref[:, both]).T.astype(BF16)
-        grad = dot(keys_t, ds_ref[:, both]).T.astype(BF16)
-        o_ref[:, first] = out[:TILE]
-        o_ref[:, second] = out[TILE:]
-        qg_ref[:, first] = grad[:TILE]
-        qg_ref[:, second] = grad[TILE:]
+        out = dot(left, inner_ref[:, p * pair : (p + 1) * pair]).T.astype(BF16)
+        out_ref[:, p * pair : p * pair + HEAD_SIZE] = out[:TILE]
+        out_ref[:, p * pair + HEAD_SIZE : (p + 1) * pair] = out[TILE:]
+
+
+def queries_kernel(pieces, ds_ref, k_ref, qg_ref):
+    store_rows(qg_ref, k_ref[...].T, ds_ref)
 
 
 class Attention:
@@ -214,19 +205,14 @@
         self.all_rows = pieces * rows
         self.width = KEY_HEADS * HEAD_SIZE
         span = HEADS_PER_KEY * HEAD_SIZE
-        tiles = self.tiles
         self.text_block = pl.BlockSpec((TILE, span), lambda j, i: (i, j))
-        self.inner_block = pl.BlockSpec((self.all_rows, span), lambda j, i: (0, j * tiles + i))
-        self.inner = pltpu.HBM((self.all_rows, tiles * self.wide), BF16)
-        self.head_block = pl.BlockSpec((self.all_rows, 2 * HEAD_SIZE), lambda j, i: (0, j))
-
-    def whole(self, columns):
-        return pl.BlockSpec((self.rows, columns), lambda j, i: (0, 0))
+        self.inner_block = pl.BlockSpec((self.all_rows, span), lambda j, i: (0, i * KEY_HEADS + j))
+        self.head_block = pl.BlockSpec((self.all_rows, HEAD_SIZE), lambda j, i: (0, j))
+        self.inner = jax.ShapeDtypeStruct((self.all_rows, self.tiles * self.wide), BF16)
 
     def call(self, kernel, products, moved, name, **specs):
         return pl.pallas_call(
             functools.partial(kernel, self.pieces),
-            grid=(KEY_HEADS, self.tiles),
             cost_estimate=pl.CostEstimate(
                 flops=2 * products * self.text * self.all_rows * self.wide,
                 bytes_accessed=2 * moved * self.text * self.wide,
@@ -242,50 +228,51 @@
         hbm = pl.BlockSpec(memory_space=pltpu.HBM)
         columns = self.width + visual.shape[1] // self.pieces
         piece = jax.ShapeDtypeStruct((self.rows, columns), BF16)
+        heads = jax.ShapeDtypeStruct((self.all_rows, self.width), BF16)
         out = self.call(
             scores_kernel,
             6,
             4,
             "scores",
-            in_specs=[smem, smem, self.text_block, self.text_block, hbm]
-            + [self.whole(2 * self.width)] * self.pieces,
-            out_specs=[self.inner_block] * 2
-            + [self.head_block]
-            + [self.whole(columns)] * self.pieces,
-            out_shape=[self.inner] * 2
-            + [pltpu.HBM((self.all_rows, 2 * self.width), BF16)]
-            + [piece] * self.pieces,
+            in_specs=[smem, smem, VMEM, VMEM, hbm] + [VMEM] * self.pieces,
+            out_specs=[VMEM] * (4 + self.pieces),
+            out_shape=[self.inner] * 2 + [heads] * 2 + [piece] * self.pieces,
             scratch_shapes=[
-                pltpu.VMEM((self.all_rows, HEAD_SIZE), F32),
+                pltpu.VMEM((self.all_rows, self.width), F32),
+                pltpu.VMEM((self.all_rows, 2 * TILE), F32),
                 pltpu.VMEM(visual.shape, BF16),
                 pltpu.SemaphoreType.DMA,
             ],
         )(length, frames, queries, gradients, in_hbm(visual), *keys_values)
-        return out[0], out[1], out[2], out[3:]
-
-    def values(self, gradients, weights):
+        return out[:4], out[4:]
+
+    def values(self, gradients, weights, values):
         piece = jax.ShapeDtypeStruct((self.rows, self.width), BF16)
-        return self.call(
+        out = self.call(
             values_kernel,
             1,
             2,
             "values",
-            in_specs=[self.text_block, self.inner_block],
-            out_specs=[self.whole(self.width)] * self.pieces,
-            out_shape=[piece] * self.pieces,
+            grid=(KEY_HEADS, self.tiles),
+            in_specs=[self.text_block, self.inner_block, self.head_block],
+            out_specs=[self.text_block]
+            + [pl.BlockSpec((self.rows, self.width), lambda j, i: (0, 0))] * self.pieces,
+            out_shape=[jax.ShapeDtypeStruct((self.text, self.wide), BF16)] + [piece] * self.pieces,
             scratch_shapes=[pltpu.VMEM((self.all_rows, HEAD_SIZE), F32)],
-        )(in_hbm(gradients), in_hbm(weights))
-
-    def outputs(self, weights, dscores, keys_values):
+        )(in_hbm(gradients), weights, values)
+        return out[0], out[1:]
+
+    def queries(self, dscores, keys):
         return self.call(
-            outputs_kernel,
-            2,
-            4,
-            "outputs",
-            in_specs=[self.inner_block] * 2 + [self.head_block],
-            out_specs=[self.text_block] * 2,
-            out_shape=[jax.ShapeDtypeStruct((self.text, self.wide), BF16)] * 2,
-        )(in_hbm(weights), in_hbm(dscores), in_hbm(keys_values))
+            queries_kernel,
+            1,
+            3,
+            "queries",
+            grid=(KEY_HEADS, self.tiles),
+            in_specs=[self.inner_block, self.head_block],
+            out_specs=self.text_block,
+            out_shape=jax.ShapeDtypeStruct((self.text, self.wide), BF16),
+        )(dscores, keys)
 
 
 def sum_kernel(pieces, *refs):
@@ -385,21 +372,22 @@
 
     keys_values = from_partners([project(visual, key_weight, value_matrix[0])] * blocks)
     attention = Attention(queries[0], blocks, visual.shape[0])
-    weights, dscores, all_keys_values, key_terms = attention.scores(
+    inner, key_terms = attention.scores(
         visual_len, frame_end, queries[0], output_gradient[0], visual, keys_values
     )
+    weights, dscores, keys, values = inner
     parts = from_partners(key_terms)
     parts[1], weights = lax.optimization_barrier((parts[1], weights))
-    value_terms = attention.values(output_gradient[0], weights)
+    attn_out, value_terms = attention.values(output_gradient[0], weights, values)
     sums = from_partners(sum_terms(parts, value_terms))
-    sums[1], weights = lax.optimization_barrier((sums[1], weights))
-    attn_out, query_grad = attention.outputs(weights, dscores, all_keys_values)
+    sums[1], dscores = lax.optimization_barrier((sums[1], dscores))
+    query_grad = attention.queries(dscores, keys)
     value_grad, kept, sent = weight_terms(samples, (sample % 2)[None], parts, sums)
     came, bit = swap(sent, "dp", 1), 1
     while kept.shape[0] > 1:
         kept, sent = halve(((sample >> bit) % 2)[None], kept, came)
         came, bit = swap(sent, "dp", 1 << bit), bit + 1
-    came, attn_out, query_grad = lax.optimization_barrier((came, attn_out, query_grad))
+    came, query_grad = lax.optimization_barrier((came, query_grad))
     weight_grad = kept[0] + came[0].astype(F32)
     return attn_out[None], query_grad[None], value_grad[None], weight_grad
 

time: 68.4 us -> 75.8 us (1.11)
  local copies, waits for them, and re-layouts: 0.01 us -> 8.8 us
  Pallas kernels: 18.8 us -> 16.7 us
    unnamed x6 -> x30, local copies, waits for them, and re-layouts: 0.01 us -> 8.8 us
    pallas_call x3, Pallas kernels: 14.9 us -> 12 us  [the longest x1 5.27 us: scores(): self.call(scores_kernel, 6, 4, 'scores', in_specs=[smem, smem, VMEM, VMEM...]
  transfers between devices with their start and end apart: 23 -> 23, of which waited for: 12 -> 10; matrix products, arithmetic and copies ran while one was open for 0% -> 0% of each run, Pallas kernels for 12% -> 9%
where the time goes in v7:
time: 75.8 us; the launch traced here: 75.3 us
  starting transfers between devices  36.7 us (48%)
  Pallas kernels  16.7 us (22%)
  waiting for transfers between devices  11 us (15%)
  local copies, waits for them, and re-layouts  8.8 us (12%)
  between operations  1.39 us (2%)
    ppermute x23, starting transfers between devices, swap(): return lax.ppermute(x, axis, [(i, i ^ mask) for i in range(size)])  36.7 us
    ppermute x23, waiting for transfers between devices, swap(): return lax.ppermute(x, axis, [(i, i ^ mask) for i in range(size)])  11 us
    unnamed x30, local copies, waits for them, and re-layouts  8.8 us
    pallas_call x1, Pallas kernels, scores(): self.call(scores_kernel, 6, 4, 'scores', in_specs=[smem, smem, VMEM, VMEM...  5.27 us
    pallas_call x1, Pallas kernels, values(): self.call(values_kernel, 1, 2, 'values', grid=(KEY_HEADS, self.tiles), in...  4.18 us
    pallas_call x1, Pallas kernels, project(): pl.pallas_call(functools.partial(project_kernel, streams), grid=(steps,),...  2.92 us
    pallas_call x1, Pallas kernels, queries(): self.call(queries_kernel, 1, 3, 'queries', grid=(KEY_HEADS, self.tiles),...  2.56 us
  transfers between devices with their start and end apart: 23, of which 10 were waited for; matrix products, arithmetic and copies ran while one was open for 0% of the time, Pallas kernels for 9%

profile of v7, /device:TPU:0, one launch (start us, length us, event | category | flops | bytes accessed | tf_op | source)
XLA Modules:
  0.0 75.3 jit_solution(13521049031972771057)
XLA Ops:
  0.7 2.9 %project.1.refs_0_ = bf16[32,1024]{1,0:T(8,128)(2,1)S(1)} custom-call(bf16[32,4096]{1,0:T(8,128)(2,1)} %bitcast.15, bf16[4096,512]{1,0:T(8,128)(2,1)} %refs_3_.1, bf16[4096,512]{1,0:T(8,128)(2,1)} %refs_3_.1, bf16[4096,512]{1,0:T(8,128)(2,1)} %refs_3_.1, bf16[4096,512]{1,0:T(8,128)(2,1)} %refs_3_.1, bf16[32,512]{1,0:T(8,128)(2,1)} %bitcast.17), custom_call_target="tpu_custom_call" | custom-call | flops 134217728 | bytes 4194304 | tf_op jit(solution)/shard_map/project/pallas_call | solution.py:68
  3.6 6.1 %collective-permute-start = (bf16[32,1024]{1,0:T(8,128)(2,1)S(1)}, bf16[32,1024]{1,0:T(8,128)(2,1)S(1)}, u32[]{:S(2)}, u32[]{:S(2)}) collective-permute-start(bf16[32,1024]{1,0:T(8,128)(2,1)S(1)} %project.1.refs_0_), channel_id=1, source_target_pairs={{0,28},{4,24},{8,20},{12,16},{16,12},{20,8},{24,4},{28,0},{1,29},{... | collective-permute-start | bytes 196616 | tf_op jit(solution)/shard_map/ppermute | solution.py:28
  9.9 0.7 collective-permute-start.2
  10.6 2.0 %collective-permute-start.3 = (bf16[32,1024]{1,0:T(8,128)(2,1)S(1)}, bf16[32,1024]{1,0:T(8,128)(2,1)S(1)}, u32[]{:S(2)}, u32[]{:S(2)}) collective-permute-start(bf16[32,1024]{1,0:T(8,128)(2,1)S(1)} %project.1.refs_0_), channel_id=1, source_target_pairs={{0,16},{4,20},{8,24},{12,28},{16,0},{20,4},{24,8},{28,12},{1,17},{... | collective-permute-start | bytes 196616 | tf_op jit(solution)/shard_map/ppermute | solution.py:28
  12.7 2.3 %collective-permute-start.4 = (bf16[32,1024]{1,0:T(8,128)(2,1)S(1)}, bf16[32,1024]{1,0:T(8,128)(2,1)S(1)}, u32[]{:S(2)}, u32[]{:S(2)}) collective-permute-start(bf16[32,1024]{1,0:T(8,128)(2,1)S(1)} %project.1.refs_0_), channel_id=1, source_target_pairs={{0,12},{4,8},{8,4},{12,0},{16,28},{20,24},{24,20},{28,16},{1,13},{... | collective-permute-start | bytes 196616 | tf_op jit(solution)/shard_map/ppermute | solution.py:28
  15.0 0.8 %collective-permute-start.5 = (bf16[32,1024]{1,0:T(8,128)(2,1)S(1)}, bf16[32,1024]{1,0:T(8,128)(2,1)S(1)}, u32[]{:S(2)}, u32[]{:S(2)}) collective-permute-start(bf16[32,1024]{1,0:T(8,128)(2,1)S(1)} %project.1.refs_0_), channel_id=1, source_target_pairs={{0,8},{4,12},{8,0},{12,4},{16,24},{20,28},{24,16},{28,20},{1,9},{5... | collective-permute-start | bytes 196616 | tf_op jit(solution)/shard_map/ppermute | solution.py:28
  17.0 2.8 %collective-permute-done.2.refs_3_ = bf16[32,1024]{1,0:T(8,128)(2,1)S(1)} collective-permute-done((bf16[32,1024]{1,0:T(8,128)(2,1)S(1)}, bf16[32,1024]{1,0:T(8,128)(2,1)S(1)}, u32[]{:S(2)}, u32[]{:S(2)}) %collective-permute-start.2) | collective-permute-done | bytes 65568 | tf_op jit(solution)/shard_map/ppermute | solution.py:28
  19.8 1.1 %collective-permute-done.3.refs_4_ = bf16[32,1024]{1,0:T(8,128)(2,1)S(1)} collective-permute-done((bf16[32,1024]{1,0:T(8,128)(2,1)S(1)}, bf16[32,1024]{1,0:T(8,128)(2,1)S(1)}, u32[]{:S(2)}, u32[]{:S(2)}) %collective-permute-start.3) | collective-permute-done | bytes 65568 | tf_op jit(solution)/shard_map/ppermute | solution.py:28
  21.3 5.3 %scores.1 = (bf16[256,4096]{1,0:T(8,128)(2,1)S(1)}, bf16[256,4096]{1,0:T(8,128)(2,1)S(1)}, bf16[256,512]{1,0:T(8,128)(2,1)S(1)}, bf16[256,512]{1,0:T(8,128)(2,1)...) custom-call(s32[1]{0:T(128)S(6)} %copy.11.length_ref, ...), custom_call_target="tpu_custom_call" | custom-call | flops 1610612736 | bytes 4194304 | tf_op jit(solution)/shard_map/scores/pallas_call | solution.py:232
  26.6 3.9 %collective-permute-start.7 = (bf16[32,1024]{1,0:T(8,128)(2,1)S(1)}, bf16[32,1024]{1,0:T(8,128)(2,1)S(1)}, u32[]{:S(2)}, u32[]{:S(2)}) collective-permute-start(bf16[32,1024]{1,0:T(8,128)(2,1)S(1)} %get-tuple-element.44), channel_id=1, source_target_pairs={{0,28},{4,24},{8,20},{12,16},{16,12},{20,8},{24,4},{28,0},{1,29},{... | collective-permute-start | bytes 196616 | tf_op jit(solution)/shard_map/ppermute | solution.py:28
  30.5 1.5 %collective-permute-start.11 = (bf16[32,1024]{1,0:T(8,128)(2,1)S(1)}, bf16[32,1024]{1,0:T(8,128)(2,1)S(1)}, u32[]{:S(2)}, u32[]{:S(2)}) collective-permute-start(bf16[32,1024]{1,0:T(8,128)(2,1)S(1)} %get-tuple-element.54), channel_id=1, source_target_pairs={{0,12},{4,8},{8,4},{12,0},{16,28},{20,24},{24,20},{28,16},{1,13},{... | collective-permute-start | bytes 196616 | tf_op jit(solution)/shard_map/ppermute | solution.py:28
  32.0 1.1 %collective-permute-start.12 = (bf16[32,1024]{1,0:T(8,128)(2,1)S(1)}, bf16[32,1024]{1,0:T(8,128)(2,1)S(1)}, u32[]{:S(2)}, u32[]{:S(2)}) collective-permute-start(bf16[32,1024]{1,0:T(8,128)(2,1)S(1)} %get-tuple-element.55), channel_id=1, source_target_pairs={{0,8},{4,12},{8,0},{12,4},{16,24},{20,28},{24,16},{28,20},{1,9},{5... | collective-permute-start | bytes 196616 | tf_op jit(solution)/shard_map/ppermute | solution.py:28
  33.0 0.9 %collective-permute-start.13 = (bf16[32,1024]{1,0:T(8,128)(2,1)S(1)}, bf16[32,1024]{1,0:T(8,128)(2,1)S(1)}, u32[]{:S(2)}, u32[]{:S(2)}) collective-permute-start(bf16[32,1024]{1,0:T(8,128)(2,1)S(1)} %get-tuple-element.56), channel_id=1, source_target_pairs={{0,4},{4,0},{8,12},{12,8},{16,20},{20,16},{24,28},{28,24},{1,5},{5... | collective-permute-start | bytes 196616 | tf_op jit(solution)/shard_map/ppermute | solution.py:28
  34.0 3.5 %collective-permute-start.8 = (bf16[32,1024]{1,0:T(8,128)(2,1)S(1)}, bf16[32,1024]{1,0:T(8,128)(2,1)S(1)}, u32[]{:S(2)}, u32[]{:S(2)}) collective-permute-start(bf16[32,1024]{1,0:T(8,128)(2,1)S(1)} %get-tuple-element.51), channel_id=1, source_target_pairs={{0,24},{4,28},{8,16},{12,20},{16,8},{20,12},{24,0},{28,4},{1,25},{... | collective-permute-start | bytes 196616 | tf_op jit(solution)/shard_map/ppermute | solution.py:28
  38.0 4.2 %values.1 = (bf16[128,4096]{1,0:T(8,128)(2,1)}, bf16[32,512]{1,0:T(8,128)(2,1)S(1)}, bf16[32,512]{1,0:T(8,128)(2,1)S(1)}, bf16[32,512]{1,0:T(8,128)(2,1)S(1)}, b...) custom-call(bf16[128,4096]{1,0:T(8,128)(2,1)} %bitcast.11, ...), custom_call_target="tpu_custom_call" | custom-call | flops 268435456 | bytes 2097152 | tf_op jit(solution)/shard_map/values/pallas_call | solution.py:251
  42.2 1.4 %collective-permute-done.9.refs_3_ = bf16[32,1024]{1,0:T(8,128)(2,1)S(1)} collective-permute-done((bf16[32,1024]{1,0:T(8,128)(2,1)S(1)}, bf16[32,1024]{1,0:T(8,128)(2,1)S(1)}, u32[]{:S(2)}, u32[]{:S(2)}) %collective-permute-start.9) | collective-permute-done | bytes 65568 | tf_op jit(solution)/shard_map/ppermute | solution.py:28
  44.4 2.1 %collective-permute-start.14 = (bf16[32,1024]{1,0:T(8,128)(2,1)S(1)}, bf16[32,1024]{1,0:T(8,128)(2,1)S(1)}, u32[]{:S(2)}, u32[]{:S(2)}) collective-permute-start(bf16[32,1024]{1,0:T(8,128)(2,1)S(1)} %get-tuple-element.66), channel_id=1, source_target_pairs={{0,28},{4,24},{8,20},{12,16},{16,12},{20,8},{24,4},{28,0},{1,29},{... | collective-permute-start | bytes 196616 | tf_op jit(solution)/shard_map/ppermute | solution.py:28
  46.5 3.2 %collective-permute-start.15 = (bf16[32,1024]{1,0:T(8,128)(2,1)S(1)}, bf16[32,1024]{1,0:T(8,128)(2,1)S(1)}, u32[]{:S(2)}, u32[]{:S(2)}) collective-permute-start(bf16[32,1024]{1,0:T(8,128)(2,1)S(1)} %get-tuple-element.69), channel_id=1, source_target_pairs={{0,24},{4,28},{8,16},{12,20},{16,8},{20,12},{24,0},{28,4},{1,25},{... | collective-permute-start | bytes 196616 | tf_op jit(solution)/shard_map/ppermute | solution.py:28
  49.7 2.3 %collective-permute-start.17 = (bf16[32,1024]{1,0:T(8,128)(2,1)}, bf16[32,1024]{1,0:T(8,128)(2,1)S(1)}, u32[]{:S(2)}, u32[]{:S(2)}) collective-permute-start(bf16[32,1024]{1,0:T(8,128)(2,1)} %get-tuple-element.71), channel_id=1, source_target_pairs={{0,16},{4,20},{8,24},{12,28},{16,0},{20,4},{24,8},{28,12},{1,17},{... | collective-permute-start | bytes 196616 | tf_op jit(solution)/shard_map/ppermute | solution.py:28
  52.0 3.5 %collective-permute-start.19 = (bf16[32,1024]{1,0:T(8,128)(2,1)S(1)}, bf16[32,1024]{1,0:T(8,128)(2,1)S(1)}, u32[]{:S(2)}, u32[]{:S(2)}) collective-permute-start(bf16[32,1024]{1,0:T(8,128)(2,1)S(1)} %get-tuple-element.73), channel_id=1, source_target_pairs={{0,8},{4,12},{8,0},{12,4},{16,24},{20,28},{24,16},{28,20},{1,9},{5... | collective-permute-start | bytes 196616 | tf_op jit(solution)/shard_map/ppermute | solution.py:28
  59.1 1.3 %collective-permute-done.20.refs_15_ = bf16[32,1024]{1,0:T(8,128)(2,1)S(1)} collective-permute-done((bf16[32,1024]{1,0:T(8,128)(2,1)S(1)}, bf16[32,1024]{1,0:T(8,128)(2,1)S(1)}, u32[]{:S(2)}, u32[]{:S(2)}) %collective-permute-start.20) | collective-permute-done | bytes 65568 | tf_op jit(solution)/shard_map/ppermute | solution.py:28
  61.1 0.8 %copy-done.2 = bf16[32,1024]{1,0:T(8,128)(2,1)S(1)} copy-done((bf16[32,1024]{1,0:T(8,128)(2,1)S(1)}, bf16[32,1024]{1,0:T(8,128)(2,1)}, u32[]{:S(2)}) %copy-start.2) | copy-done | bytes 65560
  61.9 0.8 %copy-done.4 = bf16[32,1024]{1,0:T(8,128)(2,1)S(1)} copy-done((bf16[32,1024]{1,0:T(8,128)(2,1)S(1)}, bf16[32,1024]{1,0:T(8,128)(2,1)}, u32[]{:S(2)}) %copy-start.4) | copy-done | bytes 65560
  62.8 0.8 %copy-done.6 = bf16[32,1024]{1,0:T(8,128)(2,1)S(1)} copy-done((bf16[32,1024]{1,0:T(8,128)(2,1)S(1)}, bf16[32,1024]{1,0:T(8,128)(2,1)}, u32[]{:S(2)}) %copy-start.6) | copy-done | bytes 65560
  63.6 0.8 %copy-done.8 = bf16[32,1024]{1,0:T(8,128)(2,1)S(1)} copy-done((bf16[32,1024]{1,0:T(8,128)(2,1)S(1)}, bf16[32,1024]{1,0:T(8,128)(2,1)}, u32[]{:S(2)}) %copy-start.8) | copy-done | bytes 65560
  64.4 0.8 %copy-done.10 = bf16[32,1024]{1,0:T(8,128)(2,1)S(1)} copy-done((bf16[32,1024]{1,0:T(8,128)(2,1)S(1)}, bf16[32,1024]{1,0:T(8,128)(2,1)}, u32[]{:S(2)}) %copy-start.10) | copy-done | bytes 65560
  65.3 0.8 %copy-done.12 = bf16[32,1024]{1,0:T(8,128)(2,1)S(1)} copy-done((bf16[32,1024]{1,0:T(8,128)(2,1)S(1)}, bf16[32,1024]{1,0:T(8,128)(2,1)}, u32[]{:S(2)}) %copy-start.12) | copy-done | bytes 65560
  66.1 1.0 %weight_terms.1 = (bf16[32,512]{1,0:T(8,128)(2,1)}, f32[2,128,512]{2,1,0:T(8,128)S(1)}, bf16[2,128,512]{2,1,0:T(8,128)(2,1)}) custom-call(s32[1]{0:T(128)} %bitcast.6.core_ref, bf16[32,1024]{1,0:T(8,128)(2,1)S(1)} %get-tuple-element.49.refs_0_, bf16[32,1024]{1,0:T(8,128)(2,1)S(1)} %collective-permute-done.7.refs_1_, ...), custom_call_target="tpu_custom_call" | custom-call | tf_op jit(solution)/shard_map/weight_terms/pallas_call | solution.py:329
  67.2 1.7 %collective-permute-done.21.came_ref = bf16[2,128,512]{2,1,0:T(8,128)(2,1)S(1)} collective-permute-done((bf16[2,128,512]{2,1,0:T(8,128)(2,1)}, bf16[2,128,512]{2,1,0:T(8,128)(2,1)S(1)}, u32[]{:S(2)}, u32[]{:S(2)}) %collective-permute-start.21) | collective-permute-done | bytes 262176 | tf_op jit(solution)/shard_map/ppermute | solution.py:28
  69.0 1.6 %collective-permute-start.22 = (bf16[1,128,512]{2,1,0:T(8,128)(2,1)S(1)}, bf16[1,128,512]{2,1,0:T(8,128)(2,1)S(1)}, u32[]{:S(2)}, u32[]{:S(2)}) collective-permute-start(bf16[1,128,512]{2,1,0:T(8,128)(2,1)S(1)} %get-tuple-element.77), channel_id=1, source_target_pairs={{0,2},{1,3},{2,0},{3,1},{4,6},{5,7},{6,4},{7,5},{8,10},{9,11},{10,... | collective-permute-start | bytes 393224 | tf_op jit(solution)/shard_map/ppermute | solution.py:28
  70.5 2.6 %queries.1 = bf16[128,4096]{1,0:T(8,128)(2,1)} custom-call(bf16[256,4096]{1,0:T(8,128)(2,1)S(1)} %get-tuple-element.78.ds_ref, bf16[256,512]{1,0:T(8,128)(2,1)S(1)} %get-tuple-element.79.k_ref), custom_call_target="tpu_custom_call" | custom-call | flops 268435456 | bytes 3145728 | tf_op jit(solution)/shard_map/queries/pallas_call | solution.py:266
  73.1 1.5 %collective-permute-done.22 = bf16[1,128,512]{2,1,0:T(8,128)(2,1)S(1)} collective-permute-done((bf16[1,128,512]{2,1,0:T(8,128)(2,1)S(1)}, bf16[1,128,512]{2,1,0:T(8,128)(2,1)S(1)}, u32[]{:S(2)}, u32[]{:S(2)}) %collective-permute-start.22) | collective-permute-done | bytes 131104 | tf_op jit(solution)/shard_map/ppermute | solution.py:28
  (52 shorter events, 7.6 us)
Async XLA Ops:
  0.6 20.7 %copy-start = (bf16[1,128,4096]{2,1,0:T(8,128)(2,1)S(1)}, bf16[1,128,4096]{2,1,0:T(8,128)(2,1)}, u32[]{:S(2)}) copy-start(bf16[1,128,4096]{2,1,0:T(8,128)(2,1)} %param.11) | copy-start | bytes 3145732
  0.6 20.7 %copy-start.13 = (bf16[1,128,4096]{2,1,0:T(8,128)(2,1)S(1)}, bf16[1,128,4096]{2,1,0:T(8,128)(2,1)}, u32[]{:S(2)}) copy-start(bf16[1,128,4096]{2,1,0:T(8,128)(2,1)} %param.10) | copy-start | bytes 3145732
  0.7 20.7 %copy-start.14 = (s32[1,8]{1,0:T(1,128)S(1)}, s32[1,8]{1,0:T(1,128)}, u32[]{:S(2)}) copy-start(s32[1,8]{1,0:T(1,128)} %frame_ref.1) | copy-start | bytes 100
  3.6 11.4 %collective-permute-start = (bf16[32,1024]{1,0:T(8,128)(2,1)S(1)}, bf16[32,1024]{1,0:T(8,128)(2,1)S(1)}, u32[]{:S(2)}, u32[]{:S(2)}) collective-permute-start(bf16[32,1024]{1,0:T(8,128)(2,1)S(1)} %project.1.refs_0_), channel_id=1, source_target_pairs={{0,28},{4,24},{8,20},{12,16},{16,12},{20,8},{24,4},{28,0},{1,29},{... | collective-permute-start | bytes 196616 | tf_op jit(solution)/shard_map/ppermute | solution.py:28
  9.7 6.3 %collective-permute-start.1 = (bf16[32,1024]{1,0:T(8,128)(2,1)S(1)}, bf16[32,1024]{1,0:T(8,128)(2,1)S(1)}, u32[]{:S(2)}, u32[]{:S(2)}) collective-permute-start(bf16[32,1024]{1,0:T(8,128)(2,1)S(1)} %project.1.refs_0_), channel_id=1, source_target_pairs={{0,24},{4,28},{8,16},{12,20},{16,8},{20,12},{24,0},{28,4},{1,25},{... | collective-permute-start | bytes 196616 | tf_op jit(solution)/shard_map/ppermute | solution.py:28
  9.9 9.9 %collective-permute-start.2 = (bf16[32,1024]{1,0:T(8,128)(2,1)S(1)}, bf16[32,1024]{1,0:T(8,128)(2,1)S(1)}, u32[]{:S(2)}, u32[]{:S(2)}) collective-permute-start(bf16[32,1024]{1,0:T(8,128)(2,1)S(1)} %project.1.refs_0_), channel_id=1, source_target_pairs={{0,20},{4,16},{8,28},{12,24},{16,4},{20,0},{24,12},{28,8},{1,21},{... | collective-permute-start | bytes 196616 | tf_op jit(solution)/shard_map/ppermute | solution.py:28
  10.6 10.3 %collective-permute-start.3 = (bf16[32,1024]{1,0:T(8,128)(2,1)S(1)}, bf16[32,1024]{1,0:T(8,128)(2,1)S(1)}, u32[]{:S(2)}, u32[]{:S(2)}) collective-permute-start(bf16[32,1024]{1,0:T(8,128)(2,1)S(1)} %project.1.refs_0_), channel_id=1, source_target_pairs={{0,16},{4,20},{8,24},{12,28},{16,0},{20,4},{24,8},{28,12},{1,17},{... | collective-permute-start | bytes 196616 | tf_op jit(solution)/shard_map/ppermute | solution.py:28
  12.7 8.3 %collective-permute-start.4 = (bf16[32,1024]{1,0:T(8,128)(2,1)S(1)}, bf16[32,1024]{1,0:T(8,128)(2,1)S(1)}, u32[]{:S(2)}, u32[]{:S(2)}) collective-permute-start(bf16[32,1024]{1,0:T(8,128)(2,1)S(1)} %project.1.refs_0_), channel_id=1, source_target_pairs={{0,12},{4,8},{8,4},{12,0},{16,28},{20,24},{24,20},{28,16},{1,13},{... | collective-permute-start | bytes 196616 | tf_op jit(solution)/shard_map/ppermute | solution.py:28
  15.0 6.4 %collective-permute-start.5 = (bf16[32,1024]{1,0:T(8,128)(2,1)S(1)}, bf16[32,1024]{1,0:T(8,128)(2,1)S(1)}, u32[]{:S(2)}, u32[]{:S(2)}) collective-permute-start(bf16[32,1024]{1,0:T(8,128)(2,1)S(1)} %project.1.refs_0_), channel_id=1, source_target_pairs={{0,8},{4,12},{8,0},{12,4},{16,24},{20,28},{24,16},{28,20},{1,9},{5... | collective-permute-start | bytes 196616 | tf_op jit(solution)/shard_map/ppermute | solution.py:28
  15.9 5.4 %collective-permute-start.6 = (bf16[32,1024]{1,0:T(8,128)(2,1)S(1)}, bf16[32,1024]{1,0:T(8,128)(2,1)S(1)}, u32[]{:S(2)}, u32[]{:S(2)}) collective-permute-start(bf16[32,1024]{1,0:T(8,128)(2,1)S(1)} %project.1.refs_0_), channel_id=1, source_target_pairs={{0,4},{4,0},{8,12},{12,8},{16,20},{20,16},{24,28},{28,24},{1,5},{5... | collective-permute-start | bytes 196616 | tf_op jit(solution)/shard_map/ppermute | solution.py:28
  26.6 7.4 %collective-permute-start.7 = (bf16[32,1024]{1,0:T(8,128)(2,1)S(1)}, bf16[32,1024]{1,0:T(8,128)(2,1)S(1)}, u32[]{:S(2)}, u32[]{:S(2)}) collective-permute-start(bf16[32,1024]{1,0:T(8,128)(2,1)S(1)} %get-tuple-element.44), channel_id=1, source_target_pairs={{0,28},{4,24},{8,20},{12,16},{16,12},{20,8},{24,4},{28,0},{1,29},{... | collective-permute-start | bytes 196616 | tf_op jit(solution)/shard_map/ppermute | solution.py:28
  30.5 7.1 %collective-permute-start.10 = (bf16[32,1024]{1,0:T(8,128)(2,1)S(1)}, bf16[32,1024]{1,0:T(8,128)(2,1)S(1)}, u32[]{:S(2)}, u32[]{:S(2)}) collective-permute-start(bf16[32,1024]{1,0:T(8,128)(2,1)S(1)} %get-tuple-element.53), channel_id=1, source_target_pairs={{0,16},{4,20},{8,24},{12,28},{16,0},{20,4},{24,8},{28,12},{1,17},{... | collective-permute-start | bytes 196616 | tf_op jit(solution)/shard_map/ppermute | solution.py:28
  30.5 11.7 %collective-permute-start.11 = (bf16[32,1024]{1,0:T(8,128)(2,1)S(1)}, bf16[32,1024]{1,0:T(8,128)(2,1)S(1)}, u32[]{:S(2)}, u32[]{:S(2)}) collective-permute-start(bf16[32,1024]{1,0:T(8,128)(2,1)S(1)} %get-tuple-element.54), channel_id=1, source_target_pairs={{0,12},{4,8},{8,4},{12,0},{16,28},{20,24},{24,20},{28,16},{1,13},{... | collective-permute-start | bytes 196616 | tf_op jit(solution)/shard_map/ppermute | solution.py:28
  32.0 10.3 %collective-permute-start.12 = (bf16[32,1024]{1,0:T(8,128)(2,1)S(1)}, bf16[32,1024]{1,0:T(8,128)(2,1)S(1)}, u32[]{:S(2)}, u32[]{:S(2)}) collective-permute-start(bf16[32,1024]{1,0:T(8,128)(2,1)S(1)} %get-tuple-element.55), channel_id=1, source_target_pairs={{0,8},{4,12},{8,0},{12,4},{16,24},{20,28},{24,16},{28,20},{1,9},{5... | collective-permute-start | bytes 196616 | tf_op jit(solution)/shard_map/ppermute | solution.py:28
  33.0 9.2 %collective-permute-start.13 = (bf16[32,1024]{1,0:T(8,128)(2,1)S(1)}, bf16[32,1024]{1,0:T(8,128)(2,1)S(1)}, u32[]{:S(2)}, u32[]{:S(2)}) collective-permute-start(bf16[32,1024]{1,0:T(8,128)(2,1)S(1)} %get-tuple-element.56), channel_id=1, source_target_pairs={{0,4},{4,0},{8,12},{12,8},{16,20},{20,16},{24,28},{28,24},{1,5},{5... | collective-permute-start | bytes 196616 | tf_op jit(solution)/shard_map/ppermute | solution.py:28
  34.0 8.2 %collective-permute-start.8 = (bf16[32,1024]{1,0:T(8,128)(2,1)S(1)}, bf16[32,1024]{1,0:T(8,128)(2,1)S(1)}, u32[]{:S(2)}, u32[]{:S(2)}) collective-permute-start(bf16[32,1024]{1,0:T(8,128)(2,1)S(1)} %get-tuple-element.51), channel_id=1, source_target_pairs={{0,24},{4,28},{8,16},{12,20},{16,8},{20,12},{24,0},{28,4},{1,25},{... | collective-permute-start | bytes 196616 | tf_op jit(solution)/shard_map/ppermute | solution.py:28
  37.6 6.1 %collective-permute-start.9 = (bf16[32,1024]{1,0:T(8,128)(2,1)S(1)}, bf16[32,1024]{1,0:T(8,128)(2,1)S(1)}, u32[]{:S(2)}, u32[]{:S(2)}) collective-permute-start(bf16[32,1024]{1,0:T(8,128)(2,1)S(1)} %get-tuple-element.52), channel_id=1, source_target_pairs={{0,20},{4,16},{8,28},{12,24},{16,4},{20,0},{24,12},{28,8},{1,21},{... | collective-permute-start | bytes 196616 | tf_op jit(solution)/shard_map/ppermute | solution.py:28
  44.4 7.7 %collective-permute-start.14 = (bf16[32,1024]{1,0:T(8,128)(2,1)S(1)}, bf16[32,1024]{1,0:T(8,128)(2,1)S(1)}, u32[]{:S(2)}, u32[]{:S(2)}) collective-permute-start(bf16[32,1024]{1,0:T(8,128)(2,1)S(1)} %get-tuple-element.66), channel_id=1, source_target_pairs={{0,28},{4,24},{8,20},{12,16},{16,12},{20,8},{24,4},{28,0},{1,29},{... | collective-permute-start | bytes 196616 | tf_op jit(solution)/shard_map/ppermute | solution.py:28
  46.5 9.1 %collective-permute-start.15 = (bf16[32,1024]{1,0:T(8,128)(2,1)S(1)}, bf16[32,1024]{1,0:T(8,128)(2,1)S(1)}, u32[]{:S(2)}, u32[]{:S(2)}) collective-permute-start(bf16[32,1024]{1,0:T(8,128)(2,1)S(1)} %get-tuple-element.69), channel_id=1, source_target_pairs={{0,24},{4,28},{8,16},{12,20},{16,8},{20,12},{24,0},{28,4},{1,25},{... | collective-permute-start | bytes 196616 | tf_op jit(solution)/shard_map/ppermute | solution.py:28
  49.7 6.5 %collective-permute-start.16 = (bf16[32,1024]{1,0:T(8,128)(2,1)}, bf16[32,1024]{1,0:T(8,128)(2,1)S(1)}, u32[]{:S(2)}, u32[]{:S(2)}) collective-permute-start(bf16[32,1024]{1,0:T(8,128)(2,1)} %get-tuple-element.70), channel_id=1, source_target_pairs={{0,20},{4,16},{8,28},{12,24},{16,4},{20,0},{24,12},{28,8},{1,21},{... | collective-permute-start | bytes 196616 | tf_op jit(solution)/shard_map/ppermute | solution.py:28
  49.7 7.1 %collective-permute-start.17 = (bf16[32,1024]{1,0:T(8,128)(2,1)}, bf16[32,1024]{1,0:T(8,128)(2,1)S(1)}, u32[]{:S(2)}, u32[]{:S(2)}) collective-permute-start(bf16[32,1024]{1,0:T(8,128)(2,1)} %get-tuple-element.71), channel_id=1, source_target_pairs={{0,16},{4,20},{8,24},{12,28},{16,0},{20,4},{24,8},{28,12},{1,17},{... | collective-permute-start | bytes 196616 | tf_op jit(solution)/shard_map/ppermute | solution.py:28
  52.0 5.8 %collective-permute-start.18 = (bf16[32,1024]{1,0:T(8,128)(2,1)S(1)}, bf16[32,1024]{1,0:T(8,128)(2,1)S(1)}, u32[]{:S(2)}, u32[]{:S(2)}) collective-permute-start(bf16[32,1024]{1,0:T(8,128)(2,1)S(1)} %get-tuple-element.72), channel_id=1, source_target_pairs={{0,12},{4,8},{8,4},{12,0},{16,28},{20,24},{24,20},{28,16},{1,13},{... | collective-permute-start | bytes 196616 | tf_op jit(solution)/shard_map/ppermute | solution.py:28
  52.0 6.5 %collective-permute-start.19 = (bf16[32,1024]{1,0:T(8,128)(2,1)S(1)}, bf16[32,1024]{1,0:T(8,128)(2,1)S(1)}, u32[]{:S(2)}, u32[]{:S(2)}) collective-permute-start(bf16[32,1024]{1,0:T(8,128)(2,1)S(1)} %get-tuple-element.73), channel_id=1, source_target_pairs={{0,8},{4,12},{8,0},{12,4},{16,24},{20,28},{24,16},{28,20},{1,9},{5... | collective-permute-start | bytes 196616 | tf_op jit(solution)/shard_map/ppermute | solution.py:28
  56.2 4.3 %collective-permute-start.20 = (bf16[32,1024]{1,0:T(8,128)(2,1)S(1)}, bf16[32,1024]{1,0:T(8,128)(2,1)S(1)}, u32[]{:S(2)}, u32[]{:S(2)}) collective-permute-start(bf16[32,1024]{1,0:T(8,128)(2,1)S(1)} %get-tuple-element.74), channel_id=1, source_target_pairs={{0,4},{4,0},{8,12},{12,8},{16,20},{20,16},{24,28},{28,24},{1,5},{5... | collective-permute-start | bytes 196616 | tf_op jit(solution)/shard_map/ppermute | solution.py:28
  61.1 0.8 %copy-start.2 = (bf16[32,1024]{1,0:T(8,128)(2,1)S(1)}, bf16[32,1024]{1,0:T(8,128)(2,1)}, u32[]{:S(2)}) copy-start(bf16[32,1024]{1,0:T(8,128)(2,1)} %copy-done.1) | copy-start | bytes 196612
  61.9 0.8 %copy-start.4 = (bf16[32,1024]{1,0:T(8,128)(2,1)S(1)}, bf16[32,1024]{1,0:T(8,128)(2,1)}, u32[]{:S(2)}) copy-start(bf16[32,1024]{1,0:T(8,128)(2,1)} %copy-done.3) | copy-start | bytes 196612
  62.8 0.8 %copy-start.6 = (bf16[32,1024]{1,0:T(8,128)(2,1)S(1)}, bf16[32,1024]{1,0:T(8,128)(2,1)}, u32[]{:S(2)}) copy-start(bf16[32,1024]{1,0:T(8,128)(2,1)} %copy-done.5) | copy-start | bytes 196612
  63.6 0.8 %copy-start.8 = (bf16[32,1024]{1,0:T(8,128)(2,1)S(1)}, bf16[32,1024]{1,0:T(8,128)(2,1)}, u32[]{:S(2)}) copy-start(bf16[32,1024]{1,0:T(8,128)(2,1)} %copy-done.7) | copy-start | bytes 196612
  64.4 0.8 %copy-start.10 = (bf16[32,1024]{1,0:T(8,128)(2,1)S(1)}, bf16[32,1024]{1,0:T(8,128)(2,1)}, u32[]{:S(2)}) copy-start(bf16[32,1024]{1,0:T(8,128)(2,1)} %copy-done.9) | copy-start | bytes 196612
  65.3 0.8 %copy-start.12 = (bf16[32,1024]{1,0:T(8,128)(2,1)S(1)}, bf16[32,1024]{1,0:T(8,128)(2,1)}, u32[]{:S(2)}) copy-start(bf16[32,1024]{1,0:T(8,128)(2,1)} %copy-done.11) | copy-start | bytes 196612
  67.2 1.7 %collective-permute-start.21 = (bf16[2,128,512]{2,1,0:T(8,128)(2,1)}, bf16[2,128,512]{2,1,0:T(8,128)(2,1)S(1)}, u32[]{:S(2)}, u32[]{:S(2)}) collective-permute-start(bf16[2,128,512]{2,1,0:T(8,128)(2,1)} %get-tuple-element.76), channel_id=1, source_target_pairs={{0,1},{1,0},{2,3},{3,2},{4,5},{5,4},{6,7},{7,6},{8,9},{9,8},{10,11... | collective-permute-start | bytes 786440 | tf_op jit(solution)/shard_map/ppermute | solution.py:28
  69.0 5.6 %collective-permute-start.22 = (bf16[1,128,512]{2,1,0:T(8,128)(2,1)S(1)}, bf16[1,128,512]{2,1,0:T(8,128)(2,1)S(1)}, u32[]{:S(2)}, u32[]{:S(2)}) collective-permute-start(bf16[1,128,512]{2,1,0:T(8,128)(2,1)S(1)} %get-tuple-element.77), channel_id=1, source_target_pairs={{0,2},{1,3},{2,0},{3,1},{4,6},{5,7},{6,4},{7,5},{8,10},{9,11},{10,... | collective-permute-start | bytes 393224 | tf_op jit(solution)/shard_map/ppermute | solution.py:28
  (6 other events, 3.8 us)

commit v8 on v7

--- a/solution.py
+++ b/solution.py
@@ -34,6 +34,11 @@
 
 def partner(piece, pieces):
     return (pieces - piece) % pieces
+
+
+def term_order(pieces):
+    order = [partner(p, pieces) for p in range(pieces)]
+    return order[:2] + order[-2:] + order[2:-2] if pieces > 4 else order
 
 
 def project_kernel(streams, visual_ref, *refs):
@@ -94,9 +99,9 @@
 
 
 def scores_kernel(pieces, length_ref, frame_ref, q_ref, g_ref, visual_hbm, *refs):
-    kv_refs, (w_ref, ds_ref, k_ref, v_ref) = refs[:pieces], refs[pieces : pieces + 4]
-    key_refs = refs[pieces + 4 : 2 * pieces + 4]
-    kg_acc, bias_ref, visual, sem = refs[2 * pieces + 4 :]
+    kv_refs, (w_ref, again_ref, ds_ref, k_ref, v_ref) = refs[:pieces], refs[pieces : pieces + 5]
+    key_refs = refs[pieces + 5 : 2 * pieces + 5]
+    kg_acc, bias_ref, visual, sem = refs[2 * pieces + 5 :]
     copy = pltpu.make_async_copy(visual_hbm, visual, sem)
     copy.start()
     block = lax.axis_index("blk")
@@ -145,7 +150,9 @@
                 offset = jnp.sum(terms, axis=0, keepdims=True) * inverse * slope
                 start = (i * KEY_HEADS + j) * span + p * pair
                 both = pl.ds(pl.multiple_of(start, HEAD_SIZE), pair)
-                w_ref[:, both] = (shifted * inverse).astype(BF16)
+                weights = (shifted * inverse).astype(BF16)
+                w_ref[:, both] = weights
+                again_ref[:, both] = weights
                 ds_stack.append((terms * slope - shifted * offset).astype(BF16))
                 ds_ref[:, both] = ds_stack[p]
             kg = dot(jnp.concatenate(ds_stack, axis=1), jnp.concatenate(q_stack, axis=0))
@@ -156,20 +163,20 @@
 
     copy.wait()
     share = visual.shape[1] // pieces
-    for m in range(pieces):
-        start = pl.multiple_of((block ^ partner(m, pieces)) * share, HEAD_SIZE)
-        key_refs[m][:, :width] = kg_acc[m * rows : (m + 1) * rows, :].astype(BF16)
-        key_refs[m][:, width:] = visual[:, pl.ds(start, share)]
-
-
-def values_kernel(pieces, g_ref, w_ref, v_ref, *refs):
-    o_ref, value_refs, vg_acc = refs[0], refs[1 : 1 + pieces], refs[1 + pieces]
+    for ref, other in zip(key_refs, term_order(pieces)):
+        start = pl.multiple_of((block ^ other) * share, HEAD_SIZE)
+        first = partner(other, pieces) * rows
+        ref[:, :width] = kg_acc[first : first + rows, :].astype(BF16)
+        ref[:, width:] = visual[:, pl.ds(start, share)]
+
+
+def values_kernel(pieces, g_ref, w_ref, *refs):
+    value_refs, vg_acc = refs[:pieces], refs[pieces]
     j, i = pl.program_id(0), pl.program_id(1)
     head = pl.ds(pl.multiple_of(j * HEAD_SIZE, HEAD_SIZE), HEAD_SIZE)
     rows = value_refs[0].shape[0]
     stack = [g_ref[:, h * HEAD_SIZE : (h + 1) * HEAD_SIZE] for h in range(HEADS_PER_KEY)]
     vg = dot(w_ref[...], jnp.concatenate(stack, axis=0))
-    store_rows(o_ref, v_ref[...].T, w_ref)
 
     @pl.when(i == 0)
     def _():
@@ -193,8 +200,8 @@
         out_ref[:, p * pair + HEAD_SIZE : (p + 1) * pair] = out[TILE:]
 
 
-def queries_kernel(pieces, ds_ref, k_ref, qg_ref):
-    store_rows(qg_ref, k_ref[...].T, ds_ref)
+def rows_kernel(pieces, inner_ref, head_ref, out_ref):
+    store_rows(out_ref, head_ref[...].T, inner_ref)
 
 
 class Attention:
@@ -235,8 +242,8 @@
             4,
             "scores",
             in_specs=[smem, smem, VMEM, VMEM, hbm] + [VMEM] * self.pieces,
-            out_specs=[VMEM] * (4 + self.pieces),
-            out_shape=[self.inner] * 2 + [heads] * 2 + [piece] * self.pieces,
+            out_specs=[VMEM] * (5 + self.pieces),
+            out_shape=[self.inner] * 3 + [heads] * 2 + [piece] * self.pieces,
             scratch_shapes=[
                 pltpu.VMEM((self.all_rows, self.width), F32),
                 pltpu.VMEM((self.all_rows, 2 * TILE), F32),
@@ -244,44 +251,46 @@
                 pltpu.SemaphoreType.DMA,
             ],
         )(length, frames, queries, gradients, in_hbm(visual), *keys_values)
-        return out[:4], out[4:]
-
-    def values(self, gradients, weights, values):
+        return out[:5], out[5:]
+
+    def values(self, gradients, weights):
         piece = jax.ShapeDtypeStruct((self.rows, self.width), BF16)
-        out = self.call(
+        return self.call(
             values_kernel,
             1,
             2,
             "values",
             grid=(KEY_HEADS, self.tiles),
-            in_specs=[self.text_block, self.inner_block, self.head_block],
-            out_specs=[self.text_block]
-            + [pl.BlockSpec((self.rows, self.width), lambda j, i: (0, 0))] * self.pieces,
-            out_shape=[jax.ShapeDtypeStruct((self.text, self.wide), BF16)] + [piece] * self.pieces,
+            in_specs=[self.text_block, self.inner_block],
+            out_specs=[pl.BlockSpec((self.rows, self.width), lambda j, i: (0, 0))] * self.pieces,
+            out_shape=[piece] * self.pieces,
             scratch_shapes=[pltpu.VMEM((self.all_rows, HEAD_SIZE), F32)],
-        )(in_hbm(gradients), weights, values)
-        return out[0], out[1:]
-
-    def queries(self, dscores, keys):
+        )(in_hbm(gradients), weights)
+
+    def over_rows(self, inner, heads, name):
         return self.call(
-            queries_kernel,
+            rows_kernel,
             1,
             3,
-            "queries",
+            name,
             grid=(KEY_HEADS, self.tiles),
             in_specs=[self.inner_block, self.head_block],
             out_specs=self.text_block,
             out_shape=jax.ShapeDtypeStruct((self.text, self.wide), BF16),
-        )(dscores, keys)
+        )(inner, heads)
 
 
 def sum_kernel(pieces, *refs):
-    part_refs, value_refs, out_refs = (refs[k * pieces : (k + 1) * pieces] for k in range(3))
-    width = value_refs[0].shape[1]
+    part_refs, value_refs = refs[:pieces], refs[pieces : 2 * pieces]
+    visual_ref, out_refs = refs[2 * pieces], refs[2 * pieces + 1 :]
+    rows, width = value_refs[0].shape
     total = part_refs[0][:, :width].astype(F32)
     for ref in part_refs[1:]:
         total += ref[:, :width].astype(F32)
     own = total.astype(BF16)
+    for ref, other in zip(part_refs, term_order(pieces)):
+        first = partner(other, pieces) * rows
+        visual_ref[first : first + rows, :] = ref[:, width:]
     for m in range(pieces):
         out_refs[m][:, :width] = own
         out_refs[m][:, width:] = value_refs[m][...]
@@ -290,27 +299,42 @@
 def sum_terms(parts, value_terms):
     pieces = len(parts)
     rows, width = value_terms[0].shape
-    return pl.pallas_call(
+    visual = (pieces * rows, parts[0].shape[1] - width)
+    out = pl.pallas_call(
         functools.partial(sum_kernel, pieces),
         in_specs=[VMEM] * (2 * pieces),
-        out_specs=[VMEM] * pieces,
-        out_shape=[jax.ShapeDtypeStruct((rows, 2 * width), BF16)] * pieces,
+        out_specs=[VMEM] * (1 + pieces),
+        out_shape=[jax.ShapeDtypeStruct(visual, BF16)]
+        + [jax.ShapeDtypeStruct((rows, 2 * width), BF16)] * pieces,
         compiler_params=pltpu.CompilerParams(vmem_limit_bytes=32 * MIB),
         name="sum_terms",
     )(*parts, *value_terms)
-
-
-def weight_kernel(pieces, core_ref, *refs):
-    part_refs, sum_refs = refs[:pieces], refs[pieces : 2 * pieces]
-    value_ref, keep_ref, send_ref = refs[2 * pieces :]
+    return out[0], out[1:]
+
+
+def turn_kernel(in_ref, out_ref):
+    out_ref[...] = in_ref[...].T
+
+
+def turn(x):
+    return pl.pallas_call(
+        turn_kernel,
+        in_specs=[VMEM],
+        out_specs=VMEM,
+        out_shape=jax.ShapeDtypeStruct(x.shape[::-1], x.dtype),
+        compiler_params=pltpu.CompilerParams(vmem_limit_bytes=32 * MIB),
+        name="turn",
+    )(x)
+
+
+def weight_kernel(pieces, core_ref, visual_ref, *refs):
+    sum_refs, (value_ref, keep_ref, send_ref) = refs[:pieces], refs[pieces:]
     width = value_ref.shape[1]
     total = sum_refs[0][:, width:].astype(F32)
     for ref in sum_refs[1:]:
         total += ref[:, width:].astype(F32)
     value_ref[...] = total.astype(BF16)
-    visual = jnp.concatenate([r[:, width:] for r in part_refs], axis=0)
-    key_grad = jnp.concatenate([r[:, :width] for r in sum_refs], axis=0)
-    product = dot(visual, key_grad, ((0,), (0,)))
+    product = dot(visual_ref[...], jnp.concatenate([r[:, :width] for r in sum_refs], axis=0))
     count, rows, _ = keep_ref.shape
     core = core_ref[0] == 0
     for n in range(count):
@@ -320,15 +344,14 @@
         send_ref[n] = jnp.where(core, odd, even).astype(BF16)
 
 
-def weight_terms(samples, core, parts, sums):
-    pieces = len(parts)
+def weight_terms(samples, core, visual, sums):
+    pieces = len(sums)
     rows, both = sums[0].shape
     width = both // 2
-    features = parts[0].shape[1] - width
-    half = (samples // 2, features // samples, width)
+    half = (samples // 2, visual.shape[0] // samples, width)
     return pl.pallas_call(
         functools.partial(weight_kernel, pieces),
-        in_specs=[pl.BlockSpec(memory_space=pltpu.SMEM)] + [VMEM] * (2 * pieces),
+        in_specs=[pl.BlockSpec(memory_space=pltpu.SMEM)] + [VMEM] * (1 + pieces),
         out_specs=[VMEM] * 3,
         out_shape=[
             jax.ShapeDtypeStruct((rows, width), BF16),
@@ -337,7 +360,7 @@
         ],
         compiler_params=pltpu.CompilerParams(vmem_limit_bytes=32 * MIB),
         name="weight_terms",
-    )(core, *parts, *sums)
+    )(core, visual, *sums)
 
 
 def halve_kernel(bit_ref, kept_ref, came_ref, keep_ref, send_ref):
@@ -366,23 +389,31 @@
     sample = lax.axis_index("dp").astype(jnp.int32)
     visual = visual_rows[0]
 
-    def from_partners(pieces):
-        came = {m: swap(pieces[m], "blk", partner(m, blocks)) for m in reversed(range(1, blocks))}
-        return [pieces[0]] + [came[m] for m in range(1, blocks)]
+    order = [partner(p, blocks) for p in range(blocks)]
+
+    def from_partners(pieces, order=order):
+        came = {p: swap(pieces[p], "blk", order[p]) for p in reversed(range(1, blocks))}
+        return [pieces[0]] + [came[p] for p in range(1, blocks)]
 
     keys_values = from_partners([project(visual, key_weight, value_matrix[0])] * blocks)
     attention = Attention(queries[0], blocks, visual.shape[0])
     inner, key_terms = attention.scores(
         visual_len, frame_end, queries[0], output_gradient[0], visual, keys_values
     )
-    weights, dscores, keys, values = inner
-    parts = from_partners(key_terms)
+    weights, again, dscores, keys, values = inner
+    parts = from_partners(key_terms, term_order(blocks))
     parts[1], weights = lax.optimization_barrier((parts[1], weights))
-    attn_out, value_terms = attention.values(output_gradient[0], weights, values)
-    sums = from_partners(sum_terms(parts, value_terms))
-    sums[1], dscores = lax.optimization_barrier((sums[1], dscores))
-    query_grad = attention.queries(dscores, keys)
-    value_grad, kept, sent = weight_terms(samples, (sample % 2)[None], parts, sums)
+    value_terms = attention.values(output_gradient[0], weights)
+    visual_columns, sums = sum_terms(parts, value_terms)
+    sums = from_partners(sums)
+    sums[1], again, dscores, visual_columns = lax.optimization_barrier(
+        (sums[1], again, dscores, visual_columns)
+    )
+    visual_columns = turn(visual_columns)
+    attn_out = attention.over_rows(again, values, "output")
+    visual_columns, attn_out = lax.optimization_barrier((visual_columns, attn_out))
+    query_grad = attention.over_rows(dscores, keys, "query_grad")
+    value_grad, kept, sent = weight_terms(samples, (sample % 2)[None], visual_columns, sums)
     came, bit = swap(sent, "dp", 1), 1
     while kept.shape[0] > 1:
         kept, sent = halve(((sample >> bit) % 2)[None], kept, came)

time: 75.8 us -> 67.7 us (0.89)
  local copies, waits for them, and re-layouts: 8.8 us -> 1.6 us
  Pallas kernels: 16.7 us -> 18.3 us
  waiting for transfers between devices: 11 us -> 9.48 us
  starting transfers between devices: 36.7 us -> 35.9 us
    unnamed x30 -> x10, local copies, waits for them, and re-layouts: 8.8 us -> 1.6 us
    pallas_call x1 -> x3, Pallas kernels: 2.56 us -> 5.23 us  [the longest x2 5.12 us: over_rows(): self.call(rows_kernel, 1, 3, name, grid=(KEY_HEADS, self.tiles), in_specs...]
    ppermute x23, waiting for transfers between devices: 11 us -> 9.48 us  [swap(): return lax.ppermute(x, axis, [(i, i ^ mask) for i in range(size)])]
    pallas_call x1, Pallas kernels: 4.18 us -> 2.86 us  [values(): self.call(values_kernel, 1, 2, 'values', grid=(KEY_HEADS, self.tiles), in...]
  transfers between devices with their start and end apart: 23 -> 23, of which waited for: 10 -> 10; matrix products, arithmetic and copies ran while one was open for 0% -> 0% of each run, Pallas kernels for 9% -> 12%
where the time goes in v8:
time: 67.7 us; the launch traced here: 67.5 us
  starting transfers between devices  35.9 us (53%)
  Pallas kernels  18.3 us (27%)
  waiting for transfers between devices  9.48 us (14%)
  local copies, waits for them, and re-layouts  1.6 us (2%)
  between operations  1.42 us (2%)
  other arithmetic  0.73 us (1%)
    ppermute x23, starting transfers between devices, swap(): return lax.ppermute(x, axis, [(i, i ^ mask) for i in range(size)])  35.9 us
    ppermute x23, waiting for transfers between devices, swap(): return lax.ppermute(x, axis, [(i, i ^ mask) for i in range(size)])  9.48 us
    pallas_call x1, Pallas kernels, scores(): self.call(scores_kernel, 6, 4, 'scores', in_specs=[smem, smem, VMEM, VMEM...  5.52 us
    pallas_call x2, Pallas kernels, over_rows(): self.call(rows_kernel, 1, 3, name, grid=(KEY_HEADS, self.tiles), in_specs...  5.12 us
    pallas_call x1, Pallas kernels, project(): pl.pallas_call(functools.partial(project_kernel, streams), grid=(steps,),...  2.92 us
    pallas_call x1, Pallas kernels, values(): self.call(values_kernel, 1, 2, 'values', grid=(KEY_HEADS, self.tiles), in...  2.86 us
    unnamed x10, local copies, waits for them, and re-layouts  1.6 us
  transfers between devices with their start and end apart: 23, of which 10 were waited for; matrix products, arithmetic and copies ran while one was open for 0% of the time, Pallas kernels for 12%

profile of v8, /device:TPU:0, one launch (start us, length us, event | category | flops | bytes accessed | tf_op | source)
XLA Modules:
  0.0 67.5 jit_solution(12730009449179747101)
XLA Ops:
  0.7 2.9 %project.1.refs_0_ = bf16[32,1024]{1,0:T(8,128)(2,1)S(1)} custom-call(bf16[32,4096]{1,0:T(8,128)(2,1)} %bitcast.16, bf16[4096,512]{1,0:T(8,128)(2,1)} %refs_3_.1, bf16[4096,512]{1,0:T(8,128)(2,1)} %refs_3_.1, bf16[4096,512]{1,0:T(8,128)(2,1)} %refs_3_.1, bf16[4096,512]{1,0:T(8,128)(2,1)} %refs_3_.1, bf16[32,512]{1,0:T(8,128)(2,1)} %bitcast.18), custom_call_target="tpu_custom_call" | custom-call | flops 134217728 | bytes 4194304 | tf_op jit(solution)/shard_map/project/pallas_call | solution.py:73
  3.6 6.1 %collective-permute-start = (bf16[32,1024]{1,0:T(8,128)(2,1)S(1)}, bf16[32,1024]{1,0:T(8,128)(2,1)S(1)}, u32[]{:S(2)}, u32[]{:S(2)}) collective-permute-start(bf16[32,1024]{1,0:T(8,128)(2,1)S(1)} %project.1.refs_0_), channel_id=1, source_target_pairs={{0,28},{4,24},{8,20},{12,16},{16,12},{20,8},{24,4},{28,0},{1,29},{... | collective-permute-start | bytes 196616 | tf_op jit(solution)/shard_map/ppermute | solution.py:28
  9.9 0.7 %collective-permute-start.2 = (bf16[32,1024]{1,0:T(8,128)(2,1)S(1)}, bf16[32,1024]{1,0:T(8,128)(2,1)S(1)}, u32[]{:S(2)}, u32[]{:S(2)}) collective-permute-start(bf16[32,1024]{1,0:T(8,128)(2,1)S(1)} %project.1.refs_0_), channel_id=1, source_target_pairs={{0,20},{4,16},{8,28},{12,24},{16,4},{20,0},{24,12},{28,8},{1,21},{... | collective-permute-start | bytes 196616 | tf_op jit(solution)/shard_map/ppermute | solution.py:28
  10.6 2.0 %collective-permute-start.3 = (bf16[32,1024]{1,0:T(8,128)(2,1)S(1)}, bf16[32,1024]{1,0:T(8,128)(2,1)S(1)}, u32[]{:S(2)}, u32[]{:S(2)}) collective-permute-start(bf16[32,1024]{1,0:T(8,128)(2,1)S(1)} %project.1.refs_0_), channel_id=1, source_target_pairs={{0,16},{4,20},{8,24},{12,28},{16,0},{20,4},{24,8},{28,12},{1,17},{... | collective-permute-start | bytes 196616 | tf_op jit(solution)/shard_map/ppermute | solution.py:28
  12.7 2.3 %collective-permute-start.4 = (bf16[32,1024]{1,0:T(8,128)(2,1)S(1)}, bf16[32,1024]{1,0:T(8,128)(2,1)S(1)}, u32[]{:S(2)}, u32[]{:S(2)}) collective-permute-start(bf16[32,1024]{1,0:T(8,128)(2,1)S(1)} %project.1.refs_0_), channel_id=1, source_target_pairs={{0,12},{4,8},{8,4},{12,0},{16,28},{20,24},{24,20},{28,16},{1,13},{... | collective-permute-start | bytes 196616 | tf_op jit(solution)/shard_map/ppermute | solution.py:28
  15.0 0.8 %collective-permute-start.5 = (bf16[32,1024]{1,0:T(8,128)(2,1)S(1)}, bf16[32,1024]{1,0:T(8,128)(2,1)S(1)}, u32[]{:S(2)}, u32[]{:S(2)}) collective-permute-start(bf16[32,1024]{1,0:T(8,128)(2,1)S(1)} %project.1.refs_0_), channel_id=1, source_target_pairs={{0,8},{4,12},{8,0},{12,4},{16,24},{20,28},{24,16},{28,20},{1,9},{5... | collective-permute-start | bytes 196616 | tf_op jit(solution)/shard_map/ppermute | solution.py:28
  17.0 2.8 %collective-permute-done.2.refs_3_ = bf16[32,1024]{1,0:T(8,128)(2,1)S(1)} collective-permute-done((bf16[32,1024]{1,0:T(8,128)(2,1)S(1)}, bf16[32,1024]{1,0:T(8,128)(2,1)S(1)}, u32[]{:S(2)}, u32[]{:S(2)}) %collective-permute-start.2) | collective-permute-done | bytes 65568 | tf_op jit(solution)/shard_map/ppermute | solution.py:28
  19.8 1.1 %collective-permute-done.3.refs_4_ = bf16[32,1024]{1,0:T(8,128)(2,1)S(1)} collective-permute-done((bf16[32,1024]{1,0:T(8,128)(2,1)S(1)}, bf16[32,1024]{1,0:T(8,128)(2,1)S(1)}, u32[]{:S(2)}, u32[]{:S(2)}) %collective-permute-start.3) | collective-permute-done | bytes 65568 | tf_op jit(solution)/shard_map/ppermute | solution.py:28
  21.3 5.5 %scores.1 = (bf16[256,4096]{1,0:T(8,128)(2,1)S(1)}, bf16[256,4096]{1,0:T(8,128)(2,1)S(1)}, bf16[256,4096]{1,0:T(8,128)(2,1)S(1)}, bf16[256,512]{1,0:T(8,128)(2,1...) custom-call(s32[1]{0:T(128)S(6)} %copy.11.length_ref, ...), custom_call_target="tpu_custom_call" | custom-call | flops 1610612736 | bytes 4194304 | tf_op jit(solution)/shard_map/scores/pallas_call | solution.py:239
  26.9 3.9 %collective-permute-start.7 = (bf16[32,1024]{1,0:T(8,128)(2,1)S(1)}, bf16[32,1024]{1,0:T(8,128)(2,1)S(1)}, u32[]{:S(2)}, u32[]{:S(2)}) collective-permute-start(bf16[32,1024]{1,0:T(8,128)(2,1)S(1)} %get-tuple-element.50), channel_id=1, source_target_pairs={{0,28},{4,24},{8,20},{12,16},{16,12},{20,8},{24,4},{28,0},{1,29},{... | collective-permute-start | bytes 196616 | tf_op jit(solution)/shard_map/ppermute | solution.py:28
  30.8 2.2 %collective-permute-start.11 = (bf16[32,1024]{1,0:T(8,128)(2,1)S(1)}, bf16[32,1024]{1,0:T(8,128)(2,1)S(1)}, u32[]{:S(2)}, u32[]{:S(2)}) collective-permute-start(bf16[32,1024]{1,0:T(8,128)(2,1)S(1)} %get-tuple-element.56), channel_id=1, source_target_pairs={{0,20},{4,16},{8,28},{12,24},{16,4},{20,0},{24,12},{28,8},{1,21},{... | collective-permute-start | bytes 196616 | tf_op jit(solution)/shard_map/ppermute | solution.py:28
  33.0 1.6 %collective-permute-start.12 = (bf16[32,1024]{1,0:T(8,128)(2,1)S(1)}, bf16[32,1024]{1,0:T(8,128)(2,1)S(1)}, u32[]{:S(2)}, u32[]{:S(2)}) collective-permute-start(bf16[32,1024]{1,0:T(8,128)(2,1)S(1)} %get-tuple-element.57), channel_id=1, source_target_pairs={{0,16},{4,20},{8,24},{12,28},{16,0},{20,4},{24,8},{28,12},{1,17},{... | collective-permute-start | bytes 196616 | tf_op jit(solution)/shard_map/ppermute | solution.py:28
  34.6 1.4 %collective-permute-start.13 = (bf16[32,1024]{1,0:T(8,128)(2,1)S(1)}, bf16[32,1024]{1,0:T(8,128)(2,1)S(1)}, u32[]{:S(2)}, u32[]{:S(2)}) collective-permute-start(bf16[32,1024]{1,0:T(8,128)(2,1)S(1)} %get-tuple-element.58), channel_id=1, source_target_pairs={{0,12},{4,8},{8,4},{12,0},{16,28},{20,24},{24,20},{28,16},{1,13},{... | collective-permute-start | bytes 196616 | tf_op jit(solution)/shard_map/ppermute | solution.py:28
  36.0 1.2 %collective-permute-start.8 = (bf16[32,1024]{1,0:T(8,128)(2,1)S(1)}, bf16[32,1024]{1,0:T(8,128)(2,1)S(1)}, u32[]{:S(2)}, u32[]{:S(2)}) collective-permute-start(bf16[32,1024]{1,0:T(8,128)(2,1)S(1)} %get-tuple-element.53), channel_id=1, source_target_pairs={{0,8},{4,12},{8,0},{12,4},{16,24},{20,28},{24,16},{28,20},{1,9},{5... | collective-permute-start | bytes 196616 | tf_op jit(solution)/shard_map/ppermute | solution.py:28
  37.5 0.8 %collective-permute-start.9 = (bf16[32,1024]{1,0:T(8,128)(2,1)S(1)}, bf16[32,1024]{1,0:T(8,128)(2,1)S(1)}, u32[]{:S(2)}, u32[]{:S(2)}) collective-permute-start(bf16[32,1024]{1,0:T(8,128)(2,1)S(1)} %get-tuple-element.54), channel_id=1, source_target_pairs={{0,4},{4,0},{8,12},{12,8},{16,20},{20,16},{24,28},{28,24},{1,5},{5... | collective-permute-start | bytes 196616 | tf_op jit(solution)/shard_map/ppermute | solution.py:28
  38.3 2.9 %values.1 = (bf16[32,512]{1,0:T(8,128)(2,1)S(1)}, bf16[32,512]{1,0:T(8,128)(2,1)S(1)}, bf16[32,512]{1,0:T(8,128)(2,1)S(1)}, bf16[32,512]{1,0:T(8,128)(2,1)S(1)},...) custom-call(bf16[128,4096]{1,0:T(8,128)(2,1)} %bitcast.11, ...), custom_call_target="tpu_custom_call" | custom-call | flops 268435456 | bytes 2097152 | tf_op jit(solution)/shard_map/values/pallas_call | solution.py:258
  41.5 0.5 collective-permute-done.9.refs_3_
  42.0 0.7 %sum_terms.1 = (bf16[256,512]{1,0:T(8,128)(2,1)S(1)}, bf16[32,1024]{1,0:T(8,128)(2,1)S(1)}, bf16[32,1024]{1,0:T(8,128)(2,1)S(1)}, bf16[32,1024]{1,0:T(8,128)(2,1...) custom-call(bf16[32,1024]{1,0:T(8,128)(2,1)S(1)} %get-tuple-element., ...), custom_call_target="tpu_custom_call" | custom-call | tf_op jit(solution)/shard_map/sum_terms/pallas_call | solution.py:303
  42.7 4.0 %collective-permute-start.14 = (bf16[32,1024]{1,0:T(8,128)(2,1)S(1)}, bf16[32,1024]{1,0:T(8,128)(2,1)S(1)}, u32[]{:S(2)}, u32[]{:S(2)}) collective-permute-start(bf16[32,1024]{1,0:T(8,128)(2,1)S(1)} %get-tuple-element.68), channel_id=1, source_target_pairs={{0,28},{4,24},{8,20},{12,16},{16,12},{20,8},{24,4},{28,0},{1,29},{... | collective-permute-start | bytes 196616 | tf_op jit(solution)/shard_map/ppermute | solution.py:28
  47.1 2.1 %collective-permute-start.16 = (bf16[32,1024]{1,0:T(8,128)(2,1)}, bf16[32,1024]{1,0:T(8,128)(2,1)S(1)}, u32[]{:S(2)}, u32[]{:S(2)}) collective-permute-start(bf16[32,1024]{1,0:T(8,128)(2,1)} %get-tuple-element.80), channel_id=1, source_target_pairs={{0,20},{4,16},{8,28},{12,24},{16,4},{20,0},{24,12},{28,8},{1,21},{... | collective-permute-start | bytes 196616 | tf_op jit(solution)/shard_map/ppermute | solution.py:28
  49.2 1.2 %collective-permute-start.17 = (bf16[32,1024]{1,0:T(8,128)(2,1)}, bf16[32,1024]{1,0:T(8,128)(2,1)S(1)}, u32[]{:S(2)}, u32[]{:S(2)}) collective-permute-start(bf16[32,1024]{1,0:T(8,128)(2,1)} %get-tuple-element.81), channel_id=1, source_target_pairs={{0,16},{4,20},{8,24},{12,28},{16,0},{20,4},{24,8},{28,12},{1,17},{... | collective-permute-start | bytes 196616 | tf_op jit(solution)/shard_map/ppermute | solution.py:28
  50.4 1.6 %collective-permute-start.18 = (bf16[32,1024]{1,0:T(8,128)(2,1)}, bf16[32,1024]{1,0:T(8,128)(2,1)S(1)}, u32[]{:S(2)}, u32[]{:S(2)}) collective-permute-start(bf16[32,1024]{1,0:T(8,128)(2,1)} %get-tuple-element.82), channel_id=1, source_target_pairs={{0,12},{4,8},{8,4},{12,0},{16,28},{20,24},{24,20},{28,16},{1,13},{... | collective-permute-start | bytes 196616 | tf_op jit(solution)/shard_map/ppermute | solution.py:28
  52.0 0.9 %collective-permute-start.19 = (bf16[32,1024]{1,0:T(8,128)(2,1)S(1)}, bf16[32,1024]{1,0:T(8,128)(2,1)S(1)}, u32[]{:S(2)}, u32[]{:S(2)}) collective-permute-start(bf16[32,1024]{1,0:T(8,128)(2,1)S(1)} %get-tuple-element.83), channel_id=1, source_target_pairs={{0,8},{4,12},{8,0},{12,4},{16,24},{20,28},{24,16},{28,20},{1,9},{5... | collective-permute-start | bytes 196616 | tf_op jit(solution)/shard_map/ppermute | solution.py:28
  52.9 0.6 collective-permute-done.15.refs_2_
  54.2 1.6 %copy-done.1 = bf16[256,4096]{1,0:T(8,128)(2,1)S(1)} copy-done((bf16[256,4096]{1,0:T(8,128)(2,1)S(1)}, bf16[256,4096]{1,0:T(8,128)(2,1)}, u32[]{:S(2)}) %copy-start.1) | copy-done | bytes 2097176
  55.7 2.6 %output.1 = bf16[128,4096]{1,0:T(8,128)(2,1)} custom-call(bf16[256,4096]{1,0:T(8,128)(2,1)S(1)} %copy-done.1, bf16[256,512]{1,0:T(8,128)(2,1)S(1)} %get-tuple-element.74.head_ref), custom_call_target="tpu_custom_call" | custom-call | flops 268435456 | bytes 3145728 | tf_op jit(solution)/shard_map/output/pallas_call | solution.py:271
  58.3 1.0 %weight_terms.1 = (bf16[32,512]{1,0:T(8,128)(2,1)}, f32[2,128,512]{2,1,0:T(8,128)S(1)}, bf16[2,128,512]{2,1,0:T(8,128)(2,1)}) custom-call(s32[1]{0:T(128)} %bitcast.6.core_ref, bf16[512,256]{1,0:T(8,128)(2,1)S(1)} %turn.1.visual_ref, bf16[32,1024]{1,0:T(8,128)(2,1)S(1)} %get-tuple-element.77.refs_0_, bf16[32,1024]{1,0:T(8,128)(2,1)S(1)} %collective-permute-done.14.refs_1_, ...), custom_call_target="tpu_custom_call" | custom-call | tf_op jit(solution)/shard_map/weight_terms/pallas_call | solution.py:352
  59.3 1.7 %collective-permute-done.21.came_ref = bf16[2,128,512]{2,1,0:T(8,128)(2,1)S(1)} collective-permute-done((bf16[2,128,512]{2,1,0:T(8,128)(2,1)}, bf16[2,128,512]{2,1,0:T(8,128)(2,1)S(1)}, u32[]{:S(2)}, u32[]{:S(2)}) %collective-permute-start.21) | collective-permute-done | bytes 262176 | tf_op jit(solution)/shard_map/ppermute | solution.py:28
  61.2 1.5 %collective-permute-start.22 = (bf16[1,128,512]{2,1,0:T(8,128)(2,1)S(1)}, bf16[1,128,512]{2,1,0:T(8,128)(2,1)S(1)}, u32[]{:S(2)}, u32[]{:S(2)}) collective-permute-start(bf16[1,128,512]{2,1,0:T(8,128)(2,1)S(1)} %get-tuple-element.87), channel_id=1, source_target_pairs={{0,2},{1,3},{2,0},{3,1},{4,6},{5,7},{6,4},{7,5},{8,10},{9,11},{10,... | collective-permute-start | bytes 393224 | tf_op jit(solution)/shard_map/ppermute | solution.py:28
  62.7 2.6 %query_grad.1 = bf16[128,4096]{1,0:T(8,128)(2,1)} custom-call(bf16[256,4096]{1,0:T(8,128)(2,1)S(1)} %get-tuple-element.88.inner_ref, bf16[256,512]{1,0:T(8,128)(2,1)S(1)} %get-tuple-element.89.head_ref), custom_call_target="tpu_custom_call" | custom-call | flops 268435456 | bytes 3145728 | tf_op jit(solution)/shard_map/query_grad/pallas_call | solution.py:271
  65.2 1.5 %collective-permute-done.22 = bf16[1,128,512]{2,1,0:T(8,128)(2,1)S(1)} collective-permute-done((bf16[1,128,512]{2,1,0:T(8,128)(2,1)S(1)}, bf16[1,128,512]{2,1,0:T(8,128)(2,1)S(1)}, u32[]{:S(2)}, u32[]{:S(2)}) %collective-permute-start.22) | collective-permute-done | bytes 131104 | tf_op jit(solution)/shard_map/ppermute | solution.py:28
  66.8 0.7 %add_bitcast_fusion = f32[128,512]{1,0:T(8,128)} fusion(f32[1,128,512]{2,1,0:T(8,128)S(1)} %get-tuple-element.92, bf16[1,128,512]{2,1,0:T(8,128)(2,1)S(1)} %collective-permute-done.22), kind=kLoop, calls=%fused_computation | loop fusion | flops 131072 | bytes 655360 | tf_op jit(solution)/shard_map/add | solution.py:422
  (34 shorter events, 3.1 us)
Async XLA Ops:
  0.6 20.7 %copy-start.2 = (bf16[1,128,4096]{2,1,0:T(8,128)(2,1)S(1)}, bf16[1,128,4096]{2,1,0:T(8,128)(2,1)}, u32[]{:S(2)}) copy-start(bf16[1,128,4096]{2,1,0:T(8,128)(2,1)} %param.11) | copy-start | bytes 3145732
  0.6 20.7 %copy-start.3 = (bf16[1,128,4096]{2,1,0:T(8,128)(2,1)S(1)}, bf16[1,128,4096]{2,1,0:T(8,128)(2,1)}, u32[]{:S(2)}) copy-start(bf16[1,128,4096]{2,1,0:T(8,128)(2,1)} %param.10) | copy-start | bytes 3145732
  0.7 20.7 %copy-start.4 = (s32[1,8]{1,0:T(1,128)S(1)}, s32[1,8]{1,0:T(1,128)}, u32[]{:S(2)}) copy-start(s32[1,8]{1,0:T(1,128)} %frame_ref.1) | copy-start | bytes 100
  3.6 11.4 %collective-permute-start = (bf16[32,1024]{1,0:T(8,128)(2,1)S(1)}, bf16[32,1024]{1,0:T(8,128)(2,1)S(1)}, u32[]{:S(2)}, u32[]{:S(2)}) collective-permute-start(bf16[32,1024]{1,0:T(8,128)(2,1)S(1)} %project.1.refs_0_), channel_id=1, source_target_pairs={{0,28},{4,24},{8,20},{12,16},{16,12},{20,8},{24,4},{28,0},{1,29},{... | collective-permute-start | bytes 196616 | tf_op jit(solution)/shard_map/ppermute | solution.py:28
  9.7 6.3 %collective-permute-start.1 = (bf16[32,1024]{1,0:T(8,128)(2,1)S(1)}, bf16[32,1024]{1,0:T(8,128)(2,1)S(1)}, u32[]{:S(2)}, u32[]{:S(2)}) collective-permute-start(bf16[32,1024]{1,0:T(8,128)(2,1)S(1)} %project.1.refs_0_), channel_id=1, source_target_pairs={{0,24},{4,28},{8,16},{12,20},{16,8},{20,12},{24,0},{28,4},{1,25},{... | collective-permute-start | bytes 196616 | tf_op jit(solution)/shard_map/ppermute | solution.py:28
  9.9 9.9 %collective-permute-start.2 = (bf16[32,1024]{1,0:T(8,128)(2,1)S(1)}, bf16[32,1024]{1,0:T(8,128)(2,1)S(1)}, u32[]{:S(2)}, u32[]{:S(2)}) collective-permute-start(bf16[32,1024]{1,0:T(8,128)(2,1)S(1)} %project.1.refs_0_), channel_id=1, source_target_pairs={{0,20},{4,16},{8,28},{12,24},{16,4},{20,0},{24,12},{28,8},{1,21},{... | collective-permute-start | bytes 196616 | tf_op jit(solution)/shard_map/ppermute | solution.py:28
  10.6 10.3 %collective-permute-start.3 = (bf16[32,1024]{1,0:T(8,128)(2,1)S(1)}, bf16[32,1024]{1,0:T(8,128)(2,1)S(1)}, u32[]{:S(2)}, u32[]{:S(2)}) collective-permute-start(bf16[32,1024]{1,0:T(8,128)(2,1)S(1)} %project.1.refs_0_), channel_id=1, source_target_pairs={{0,16},{4,20},{8,24},{12,28},{16,0},{20,4},{24,8},{28,12},{1,17},{... | collective-permute-start | bytes 196616 | tf_op jit(solution)/shard_map/ppermute | solution.py:28
  12.7 8.3 %collective-permute-start.4 = (bf16[32,1024]{1,0:T(8,128)(2,1)S(1)}, bf16[32,1024]{1,0:T(8,128)(2,1)S(1)}, u32[]{:S(2)}, u32[]{:S(2)}) collective-permute-start(bf16[32,1024]{1,0:T(8,128)(2,1)S(1)} %project.1.refs_0_), channel_id=1, source_target_pairs={{0,12},{4,8},{8,4},{12,0},{16,28},{20,24},{24,20},{28,16},{1,13},{... | collective-permute-start | bytes 196616 | tf_op jit(solution)/shard_map/ppermute | solution.py:28
  15.0 6.4 %collective-permute-start.5 = (bf16[32,1024]{1,0:T(8,128)(2,1)S(1)}, bf16[32,1024]{1,0:T(8,128)(2,1)S(1)}, u32[]{:S(2)}, u32[]{:S(2)}) collective-permute-start(bf16[32,1024]{1,0:T(8,128)(2,1)S(1)} %project.1.refs_0_), channel_id=1, source_target_pairs={{0,8},{4,12},{8,0},{12,4},{16,24},{20,28},{24,16},{28,20},{1,9},{5... | collective-permute-start | bytes 196616 | tf_op jit(solution)/shard_map/ppermute | solution.py:28
  15.9 5.4 %collective-permute-start.6 = (bf16[32,1024]{1,0:T(8,128)(2,1)S(1)}, bf16[32,1024]{1,0:T(8,128)(2,1)S(1)}, u32[]{:S(2)}, u32[]{:S(2)}) collective-permute-start(bf16[32,1024]{1,0:T(8,128)(2,1)S(1)} %project.1.refs_0_), channel_id=1, source_target_pairs={{0,4},{4,0},{8,12},{12,8},{16,20},{20,16},{24,28},{28,24},{1,5},{5... | collective-permute-start | bytes 196616 | tf_op jit(solution)/shard_map/ppermute | solution.py:28
  26.9 14.3 %copy-start = (bf16[256,4096]{1,0:T(8,128)(2,1)}, bf16[256,4096]{1,0:T(8,128)(2,1)S(1)}, u32[]{:S(2)}) copy-start(bf16[256,4096]{1,0:T(8,128)(2,1)S(1)} %get-tuple-element.73.inner_ref) | copy-start | bytes 6291460
  26.9 9.2 %collective-permute-start.7 = (bf16[32,1024]{1,0:T(8,128)(2,1)S(1)}, bf16[32,1024]{1,0:T(8,128)(2,1)S(1)}, u32[]{:S(2)}, u32[]{:S(2)}) collective-permute-start(bf16[32,1024]{1,0:T(8,128)(2,1)S(1)} %get-tuple-element.50), channel_id=1, source_target_pairs={{0,28},{4,24},{8,20},{12,16},{16,12},{20,8},{24,4},{28,0},{1,29},{... | collective-permute-start | bytes 196616 | tf_op jit(solution)/shard_map/ppermute | solution.py:28
  30.7 6.8 %collective-permute-start.10 = (bf16[32,1024]{1,0:T(8,128)(2,1)S(1)}, bf16[32,1024]{1,0:T(8,128)(2,1)S(1)}, u32[]{:S(2)}, u32[]{:S(2)}) collective-permute-start(bf16[32,1024]{1,0:T(8,128)(2,1)S(1)} %get-tuple-element.55), channel_id=1, source_target_pairs={{0,24},{4,28},{8,16},{12,20},{16,8},{20,12},{24,0},{28,4},{1,25},{... | collective-permute-start | bytes 196616 | tf_op jit(solution)/shard_map/ppermute | solution.py:28
  30.8 10.6 %collective-permute-start.11 = (bf16[32,1024]{1,0:T(8,128)(2,1)S(1)}, bf16[32,1024]{1,0:T(8,128)(2,1)S(1)}, u32[]{:S(2)}, u32[]{:S(2)}) collective-permute-start(bf16[32,1024]{1,0:T(8,128)(2,1)S(1)} %get-tuple-element.56), channel_id=1, source_target_pairs={{0,20},{4,16},{8,28},{12,24},{16,4},{20,0},{24,12},{28,8},{1,21},{... | collective-permute-start | bytes 196616 | tf_op jit(solution)/shard_map/ppermute | solution.py:28
  33.0 8.4 %collective-permute-start.12 = (bf16[32,1024]{1,0:T(8,128)(2,1)S(1)}, bf16[32,1024]{1,0:T(8,128)(2,1)S(1)}, u32[]{:S(2)}, u32[]{:S(2)}) collective-permute-start(bf16[32,1024]{1,0:T(8,128)(2,1)S(1)} %get-tuple-element.57), channel_id=1, source_target_pairs={{0,16},{4,20},{8,24},{12,28},{16,0},{20,4},{24,8},{28,12},{1,17},{... | collective-permute-start | bytes 196616 | tf_op jit(solution)/shard_map/ppermute | solution.py:28
  34.6 6.9 %collective-permute-start.13 = (bf16[32,1024]{1,0:T(8,128)(2,1)S(1)}, bf16[32,1024]{1,0:T(8,128)(2,1)S(1)}, u32[]{:S(2)}, u32[]{:S(2)}) collective-permute-start(bf16[32,1024]{1,0:T(8,128)(2,1)S(1)} %get-tuple-element.58), channel_id=1, source_target_pairs={{0,12},{4,8},{8,4},{12,0},{16,28},{20,24},{24,20},{28,16},{1,13},{... | collective-permute-start | bytes 196616 | tf_op jit(solution)/shard_map/ppermute | solution.py:28
  36.0 5.4 %collective-permute-start.8 = (bf16[32,1024]{1,0:T(8,128)(2,1)S(1)}, bf16[32,1024]{1,0:T(8,128)(2,1)S(1)}, u32[]{:S(2)}, u32[]{:S(2)}) collective-permute-start(bf16[32,1024]{1,0:T(8,128)(2,1)S(1)} %get-tuple-element.53), channel_id=1, source_target_pairs={{0,8},{4,12},{8,0},{12,4},{16,24},{20,28},{24,16},{28,20},{1,9},{5... | collective-permute-start | bytes 196616 | tf_op jit(solution)/shard_map/ppermute | solution.py:28
  37.5 4.5 %collective-permute-start.9 = (bf16[32,1024]{1,0:T(8,128)(2,1)S(1)}, bf16[32,1024]{1,0:T(8,128)(2,1)S(1)}, u32[]{:S(2)}, u32[]{:S(2)}) collective-permute-start(bf16[32,1024]{1,0:T(8,128)(2,1)S(1)} %get-tuple-element.54), channel_id=1, source_target_pairs={{0,4},{4,0},{8,12},{12,8},{16,20},{20,16},{24,28},{28,24},{1,5},{5... | collective-permute-start | bytes 196616 | tf_op jit(solution)/shard_map/ppermute | solution.py:28
  42.7 9.3 %collective-permute-start.14 = (bf16[32,1024]{1,0:T(8,128)(2,1)S(1)}, bf16[32,1024]{1,0:T(8,128)(2,1)S(1)}, u32[]{:S(2)}, u32[]{:S(2)}) collective-permute-start(bf16[32,1024]{1,0:T(8,128)(2,1)S(1)} %get-tuple-element.68), channel_id=1, source_target_pairs={{0,28},{4,24},{8,20},{12,16},{16,12},{20,8},{24,4},{28,0},{1,29},{... | collective-permute-start | bytes 196616 | tf_op jit(solution)/shard_map/ppermute | solution.py:28
  46.7 6.8 %collective-permute-start.15 = (bf16[32,1024]{1,0:T(8,128)(2,1)S(1)}, bf16[32,1024]{1,0:T(8,128)(2,1)S(1)}, u32[]{:S(2)}, u32[]{:S(2)}) collective-permute-start(bf16[32,1024]{1,0:T(8,128)(2,1)S(1)} %get-tuple-element.79), channel_id=1, source_target_pairs={{0,24},{4,28},{8,16},{12,20},{16,8},{20,12},{24,0},{28,4},{1,25},{... | collective-permute-start | bytes 196616 | tf_op jit(solution)/shard_map/ppermute | solution.py:28
  47.1 11.2 %collective-permute-start.16 = (bf16[32,1024]{1,0:T(8,128)(2,1)}, bf16[32,1024]{1,0:T(8,128)(2,1)S(1)}, u32[]{:S(2)}, u32[]{:S(2)}) collective-permute-start(bf16[32,1024]{1,0:T(8,128)(2,1)} %get-tuple-element.80), channel_id=1, source_target_pairs={{0,20},{4,16},{8,28},{12,24},{16,4},{20,0},{24,12},{28,8},{1,21},{... | collective-permute-start | bytes 196616 | tf_op jit(solution)/shard_map/ppermute | solution.py:28
  49.2 9.1 %collective-permute-start.17 = (bf16[32,1024]{1,0:T(8,128)(2,1)}, bf16[32,1024]{1,0:T(8,128)(2,1)S(1)}, u32[]{:S(2)}, u32[]{:S(2)}) collective-permute-start(bf16[32,1024]{1,0:T(8,128)(2,1)} %get-tuple-element.81), channel_id=1, source_target_pairs={{0,16},{4,20},{8,24},{12,28},{16,0},{20,4},{24,8},{28,12},{1,17},{... | collective-permute-start | bytes 196616 | tf_op jit(solution)/shard_map/ppermute | solution.py:28
  50.4 7.9 %collective-permute-start.18 = (bf16[32,1024]{1,0:T(8,128)(2,1)}, bf16[32,1024]{1,0:T(8,128)(2,1)S(1)}, u32[]{:S(2)}, u32[]{:S(2)}) collective-permute-start(bf16[32,1024]{1,0:T(8,128)(2,1)} %get-tuple-element.82), channel_id=1, source_target_pairs={{0,12},{4,8},{8,4},{12,0},{16,28},{20,24},{24,20},{28,16},{1,13},{... | collective-permute-start | bytes 196616 | tf_op jit(solution)/shard_map/ppermute | solution.py:28
  52.0 6.3 %collective-permute-start.19 = (bf16[32,1024]{1,0:T(8,128)(2,1)S(1)}, bf16[32,1024]{1,0:T(8,128)(2,1)S(1)}, u32[]{:S(2)}, u32[]{:S(2)}) collective-permute-start(bf16[32,1024]{1,0:T(8,128)(2,1)S(1)} %get-tuple-element.83), channel_id=1, source_target_pairs={{0,8},{4,12},{8,0},{12,4},{16,24},{20,28},{24,16},{28,20},{1,9},{5... | collective-permute-start | bytes 196616 | tf_op jit(solution)/shard_map/ppermute | solution.py:28
  53.5 4.8 %collective-permute-start.20 = (bf16[32,1024]{1,0:T(8,128)(2,1)S(1)}, bf16[32,1024]{1,0:T(8,128)(2,1)S(1)}, u32[]{:S(2)}, u32[]{:S(2)}) collective-permute-start(bf16[32,1024]{1,0:T(8,128)(2,1)S(1)} %get-tuple-element.84), channel_id=1, source_target_pairs={{0,4},{4,0},{8,12},{12,8},{16,20},{20,16},{24,28},{28,24},{1,5},{5... | collective-permute-start | bytes 196616 | tf_op jit(solution)/shard_map/ppermute | solution.py:28
  54.2 1.6 %copy-start.1 = (bf16[256,4096]{1,0:T(8,128)(2,1)S(1)}, bf16[256,4096]{1,0:T(8,128)(2,1)}, u32[]{:S(2)}) copy-start(bf16[256,4096]{1,0:T(8,128)(2,1)} %copy-done) | copy-start | bytes 6291460
  59.3 1.7 %collective-permute-start.21 = (bf16[2,128,512]{2,1,0:T(8,128)(2,1)}, bf16[2,128,512]{2,1,0:T(8,128)(2,1)S(1)}, u32[]{:S(2)}, u32[]{:S(2)}) collective-permute-start(bf16[2,128,512]{2,1,0:T(8,128)(2,1)} %get-tuple-element.86), channel_id=1, source_target_pairs={{0,1},{1,0},{2,3},{3,2},{4,5},{5,4},{6,7},{7,6},{8,9},{9,8},{10,11... | collective-permute-start | bytes 786440 | tf_op jit(solution)/shard_map/ppermute | solution.py:28
  61.2 5.6 %collective-permute-start.22 = (bf16[1,128,512]{2,1,0:T(8,128)(2,1)S(1)}, bf16[1,128,512]{2,1,0:T(8,128)(2,1)S(1)}, u32[]{:S(2)}, u32[]{:S(2)}) collective-permute-start(bf16[1,128,512]{2,1,0:T(8,128)(2,1)S(1)} %get-tuple-element.87), channel_id=1, source_target_pairs={{0,2},{1,3},{2,0},{3,1},{4,6},{5,7},{6,4},{7,5},{8,10},{9,11},{10,... | collective-permute-start | bytes 393224 | tf_op jit(solution)/shard_map/ppermute | solution.py:28

commit v9 on v8

v9 whole, which is shorter than its diff:
```python
import functools

import jax
import jax.numpy as jnp
from jax import lax
from jax.experimental import pallas as pl
from jax.experimental.pallas import tpu as pltpu
from jax.sharding import PartitionSpec as P

KEY_HEADS = 4
HEAD_SIZE = 128
TILE = 128
HEADS_PER_KEY = 8
LOG2_E = 1.4426950408889634
NEGATIVE_FILLER = -1e30
F32 = jnp.float32
BF16 = jnp.bfloat16
MIB = 1024 * 1024
VMEM = pl.BlockSpec(memory_space=pltpu.VMEM)


def dot(a, b, contract=((1,), (0,))):
    return lax.dot_general(a, b, (contract, ((), ())), preferred_element_type=F32)


def swap(x, axis, mask):
    size = lax.axis_size(axis)
    return lax.ppermute(x, axis, [(i, i ^ mask) for i in range(size)])


def in_hbm(x):
    return pltpu.with_memory_space_constraint(x, pltpu.HBM)


def gather(own, near=None):
    blocks = lax.axis_size("blk")
    half = blocks // 2
    masks = range(half - 1, 0, -1)
    pieces = {half: swap(own, "blk", half)}
    pieces.update({m: swap(near[m - 1] if near else own, "blk", m) for m in masks})
    pieces.update({m + half: swap(pieces[half], "blk", m) for m in masks})
    pieces[0] = own
    return [pieces[m] for m in range(blocks)]


def near_exchange(pieces):
    return [swap(piece, "blk", m) for m, piece in enumerate(pieces, 1)]


def project_kernel(streams, visual_ref, *refs):
    weight_refs, value_ref = refs[:streams], refs[streams]
    out_ref, own_ref, near_refs = refs[streams + 1], refs[streams + 2], refs[streams + 3 : -1]
    acc_ref = refs[-1]
    step = pl.program_id(0)
    slab = weight_refs[0].shape[0]
    part = 0.0
    for p in range(streams):
        start = pl.multiple_of((step * streams + p) * slab, HEAD_SIZE)
        part += dot(visual_ref[:, pl.ds(start, slab)], weight_refs[p][...])

    @pl.when(step == 0)
    def _():
        acc_ref[...] = part
        block = lax.axis_index("blk")
        half = len(near_refs) + 1
        rows, width = visual_ref.shape[0], own_ref.shape[1]
        for m, ref in enumerate((own_ref, *near_refs)):
            for side in range(2):
                start = pl.multiple_of((block ^ (m + side * half)) * width, HEAD_SIZE)
                ref[side * rows : (side + 1) * rows, :] = visual_ref[:, pl.ds(start, width)]

    @pl.when(step > 0)
    def _():
        acc_ref[...] += part

    @pl.when(step == pl.num_programs(0) - 1)
    def _():
        columns = acc_ref.shape[1]
        out_ref[:, :columns] = acc_ref[...].astype(BF16)
        out_ref[:, columns:] = value_ref[...]


def project(blocks, visual, key_weight, value):
    rows, features = visual.shape
    columns = key_weight.shape[1]
    steps, streams = 2, 4
    slab = features // (steps * streams)
    out = (rows, columns + value.shape[1])
    both = (2 * rows, features // blocks)
    half = blocks // 2

    def whole(shape):
        return pl.BlockSpec(shape, lambda k: (0, 0))

    out = pl.pallas_call(
        functools.partial(project_kernel, streams),
        grid=(steps,),
        in_specs=[whole(visual.shape)]
        + [
            pl.BlockSpec((slab, columns), lambda k, p=p: (k * streams + p, 0))
            for p in range(streams)
        ]
        + [whole(value.shape)],
        out_specs=[whole(out)] + [whole(both)] * half,
        out_shape=[jax.ShapeDtypeStruct(out, BF16)] + [jax.ShapeDtypeStruct(both, BF16)] * half,
        scratch_shapes=[pltpu.VMEM((rows, columns), F32)],
        cost_estimate=pl.CostEstimate(
            flops=2 * rows * features * columns,
            bytes_accessed=2 * features * columns,
            transcendentals=0,
        ),
        compiler_params=pltpu.CompilerParams(vmem_limit_bytes=32 * MIB),
        name="project",
    )(in_hbm(visual), *[in_hbm(key_weight)] * streams, in_hbm(value))
    return out[0], out[1], out[2:]


def head_pair(ref, rows, start):
    first = pl.ds(pl.multiple_of(start, HEAD_SIZE), HEAD_SIZE)
    second = pl.ds(pl.multiple_of(start + HEAD_SIZE, HEAD_SIZE), HEAD_SIZE)
    return jnp.concatenate([ref[rows, first], ref[rows, second]], axis=0)


def store_sides(own_ref, near_refs, terms, columns):
    half = len(near_refs) + 1
    rows = own_ref.shape[0] // 2
    for m, ref in enumerate((own_ref, *near_refs)):
        for side in range(2):
            first = (m + side * half) * rows
            part = terms[first : first + rows, :].astype(ref.dtype)
            ref[side * rows : (side + 1) * rows, columns] = part


def scores_kernel(pieces, length_ref, frame_ref, q_ref, g_ref, *refs):
    kv_refs, (w_ref, again_ref, ds_ref, k_ref, v_ref) = refs[:pieces], refs[pieces : pieces + 5]
    own_ref, near_refs, (kg_acc, bias_ref) = refs[pieces + 5], refs[pieces + 6 : -2], refs[-2:]
    block = lax.axis_index("blk")
    tiles = q_ref.shape[0] // TILE
    rows = kv_refs[0].shape[0]
    width = KEY_HEADS * HEAD_SIZE
    pair = 2 * TILE
    pairs = HEADS_PER_KEY // 2
    span = HEADS_PER_KEY * HEAD_SIZE
    scale = HEAD_SIZE**-0.5
    for m in range(pieces):
        part = slice(m * rows, (m + 1) * rows)
        k_ref[part, :] = kv_refs[m][:, :width]
        v_ref[part, :] = kv_refs[m][:, width:]
    row = lax.broadcasted_iota(jnp.int32, (rows, pair), 0)
    for i in range(tiles):
        text = slice(i * TILE, (i + 1) * TILE)
        limit = jnp.minimum(length_ref[0], TILE * frame_ref[0, block * tiles + i])
        for m in range(pieces):
            live = row + (block ^ m) * rows < limit
            bias_ref[m * rows : (m + 1) * rows, :] = jnp.where(live, 0.0, NEGATIVE_FILLER)

        @pl.loop(0, KEY_HEADS)
        def _(j, i=i, text=text):
            head = pl.ds(pl.multiple_of(j * HEAD_SIZE, HEAD_SIZE), HEAD_SIZE)
            keys, values = k_ref[:, head], v_ref[:, head]
            q_stack, raw, dprobs = [], {}, {}

            def products(p):
                start = j * span + p * pair
                q_stack.append(head_pair(q_ref, text, start))
                raw[p] = dot(keys, q_stack[p], ((1,), (1,)))
                dprobs[p] = dot(values, head_pair(g_ref, text, start), ((1,), (1,)))

            products(0)
            ds_stack = []
            for p in range(pairs):
                if p + 1 < pairs:
                    products(p + 1)
                scores = raw.pop(p) + bias_ref[...]
                peak = jnp.max(scores, axis=0, keepdims=True)
                shifted = jnp.exp2((scores - peak) * (scale * LOG2_E))
                terms = shifted * dprobs.pop(p)
                inverse = 1.0 / jnp.sum(shifted, axis=0, keepdims=True)
                slope = inverse * scale
                offset = jnp.sum(terms, axis=0, keepdims=True) * inverse * slope
                start = (i * KEY_HEADS + j) * span + p * pair
                both = pl.ds(pl.multiple_of(start, HEAD_SIZE), pair)
                weights = (shifted * inverse).astype(BF16)
                w_ref[:, both] = weights
                again_ref[:, both] = weights
                ds_stack.append((terms * slope - shifted * offset).astype(BF16))
                ds_ref[:, both] = ds_stack[p]
            kg = dot(jnp.concatenate(ds_stack, axis=1), jnp.concatenate(q_stack, axis=0))
            if i == 0:
                kg_acc[:, head] = kg
            else:
                kg_acc[:, head] += kg

    store_sides(own_ref, near_refs, kg_acc, slice(None))


def values_kernel(pieces, g_ref, w_ref, own_ref, *refs):
    near_refs, vg_acc = refs[:-1], refs[-1]
    j, i = pl.program_id(0), pl.program_id(1)
    head = pl.ds(pl.multiple_of(j * HEAD_SIZE, HEAD_SIZE), HEAD_SIZE)
    stack = [g_ref[:, h * HEAD_SIZE : (h + 1) * HEAD_SIZE] for h in range(HEADS_PER_KEY)]
    vg = dot(w_ref[...], jnp.concatenate(stack, axis=0))

    @pl.when(i == 0)
    def _():
        vg_acc[...] = vg

    @pl.when(i > 0)
    def _():
        vg_acc[...] += vg

    @pl.when(i == pl.num_programs(1) - 1)
    def _():
        store_sides(own_ref, near_refs, vg_acc, head)


def store_rows(out_ref, left, inner_ref):
    pair = 2 * TILE
    for p in range(HEADS_PER_KEY // 2):
        out = dot(left, inner_ref[:, p * pair : (p + 1) * pair]).T.astype(BF16)
        out_ref[:, p * pair : p * pair + HEAD_SIZE] = out[:TILE]
        out_ref[:, p * pair + HEAD_SIZE : (p + 1) * pair] = out[TILE:]


def rows_kernel(pieces, inner_ref, head_ref, out_ref):
    store_rows(out_ref, head_ref[...].T, inner_ref)


class Attention:
    def __init__(self, queries, pieces, rows):
        self.pieces, self.rows = pieces, rows
        self.text, self.wide = queries.shape
        self.tiles = self.text // TILE
        self.all_rows = pieces * rows
        self.width = KEY_HEADS * HEAD_SIZE
        span = HEADS_PER_KEY * HEAD_SIZE
        self.text_block = pl.BlockSpec((TILE, span), lambda j, i: (i, j))
        self.inner_block = pl.BlockSpec((self.all_rows, span), lambda j, i: (0, i * KEY_HEADS + j))
        self.head_block = pl.BlockSpec((self.all_rows, HEAD_SIZE), lambda j, i: (0, j))
        self.inner = jax.ShapeDtypeStruct((self.all_rows, self.tiles * self.wide), BF16)
        self.sides = (2 * rows, self.width)
        self.terms = [jax.ShapeDtypeStruct(self.sides, F32)]
        self.terms += [jax.ShapeDtypeStruct(self.sides, BF16)] * (pieces // 2 - 1)

    def call(self, kernel, products, moved, name, **specs):
        return pl.pallas_call(
            functools.partial(kernel, self.pieces),
            cost_estimate=pl.CostEstimate(
                flops=2 * products * self.text * self.all_rows * self.wide,
                bytes_accessed=2 * moved * self.text * self.wide,
                transcendentals=0,
            ),
            compiler_params=pltpu.CompilerParams(vmem_limit_bytes=32 * MIB),
            name=name,
            **specs,
        )

    def scores(self, length, frames, queries, gradients, keys_values):
        smem = pl.BlockSpec(memory_space=pltpu.SMEM)
        heads = jax.ShapeDtypeStruct((self.all_rows, self.width), BF16)
        out = self.call(
            scores_kernel,
            6,
            4,
            "scores",
            in_specs=[smem, smem, VMEM, VMEM] + [VMEM] * self.pieces,
            out_specs=[VMEM] * (5 + len(self.terms)),
            out_shape=[self.inner] * 3 + [heads] * 2 + self.terms,
            scratch_shapes=[
                pltpu.VMEM((self.all_rows, self.width), F32),
                pltpu.VMEM((self.all_rows, 2 * TILE), F32),
            ],
        )(length, frames, queries, gradients, *keys_values)
        return out[:5], out[5], out[6:]

    def values(self, gradients, weights):
        out = self.call(
            values_kernel,
            1,
            2,
            "values",
            grid=(KEY_HEADS, self.tiles),
            in_specs=[self.text_block, self.inner_block],
            out_specs=[pl.BlockSpec(self.sides, lambda j, i: (0, 0))] * len(self.terms),
            out_shape=self.terms,
            scratch_shapes=[pltpu.VMEM((self.all_rows, HEAD_SIZE), F32)],
        )(in_hbm(gradients), weights)
        return out[0], out[1:]

    def over_rows(self, inner, heads, name):
        return self.call(
            rows_kernel,
            1,
            3,
            name,
            grid=(KEY_HEADS, self.tiles),
            in_specs=[self.inner_block, self.head_block],
            out_specs=self.text_block,
            out_shape=jax.ShapeDtypeStruct((self.text, self.wide), BF16),
        )(inner, heads)


def in_vmem(kernel, name, out_shape, *arrays):
    return pl.pallas_call(
        kernel,
        in_specs=[VMEM] * len(arrays),
        out_specs=[VMEM] * len(out_shape),
        out_shape=[jax.ShapeDtypeStruct(*shape) for shape in out_shape],
        compiler_params=pltpu.CompilerParams(vmem_limit_bytes=32 * MIB),
        name=name,
    )(*arrays)


def sum_kernel(own_ref, *refs):
    came_refs, (near_ref, far_ref) = refs[:-2], refs[-2:]
    rows = near_ref.shape[0]
    for ref, part in ((near_ref, slice(0, rows)), (far_ref, slice(rows, 2 * rows))):
        total = own_ref[part, :]
        for came_ref in came_refs:
            total += came_ref[part, :].astype(F32)
        ref[...] = total.astype(ref.dtype)


def near_sums(own, came, name):
    half = (own.shape[0] // 2, own.shape[1])
    return in_vmem(sum_kernel, name, [(half, F32), (half, BF16)], own, *came)


def add_kernel(near_ref, far_ref, *refs):
    value_refs, (own_ref, again_ref), near_refs = (
        refs[: len(refs) // 2 - 1],
        refs[len(refs) // 2 - 1 : len(refs) // 2 + 1],
        refs[len(refs) // 2 + 1 :],
    )
    rows = own_ref.shape[0]
    total = (near_ref[...] + far_ref[...].astype(F32)).astype(BF16)
    own_ref[...] = total
    again_ref[...] = total
    for ref, value_ref in zip(near_refs, value_refs):
        ref[:rows, :] = total
        ref[rows:, :] = value_ref[...]


def add_far(near, far, values):
    rows, width = far.shape
    more = [((rows + v.shape[0], width), BF16) for v in values]
    out = in_vmem(add_kernel, "key_grad", [(far.shape, BF16)] * 2 + more, near, far, *values)
    return out[0], out[1], out[2:]


def add_value_kernel(near_ref, far_ref, out_ref):
    out_ref[...] = (near_ref[...] + far_ref[...].astype(F32)).astype(BF16)


def pack_kernel(*refs):
    in_refs, (near_ref, far_ref) = refs[:-2], refs[-2:]
    rows = in_refs[0].shape[0] // 2
    for m, ref in enumerate(in_refs):
        near_ref[m * rows : (m + 1) * rows, :] = ref[:rows, :]
        far_ref[m * rows : (m + 1) * rows, :] = ref[rows:, :]


def pack(own, came):
    half = ((1 + len(came)) * own.shape[0] // 2, own.shape[1])
    return in_vmem(pack_kernel, "pack_visual", [(half, BF16)] * 2, own, *came)


def turn_kernel(near_ref, far_ref, out_ref):
    out_ref[...] = jnp.concatenate([near_ref[...], far_ref[...]], axis=0).T


def turn(near, far):
    shape = (near.shape[1], 2 * near.shape[0])
    return in_vmem(turn_kernel, "turn_visual", [(shape, BF16)], near, far)[0]


def weight_kernel(order, core_ref, visual_ref, value_ref, *refs):
    pieces = len(order)
    kg_refs = [refs[order.index(m)] for m in range(pieces)]
    keep_ref, send_ref, near_ref, far_ref = refs[pieces:]
    rows = near_ref.shape[0]
    product = dot(visual_ref[...], jnp.concatenate([r[:rows, :] for r in kg_refs], axis=0))
    count, share, _ = keep_ref.shape
    core = core_ref[0] == 0
    for n in range(count):
        even = product[2 * n * share : (2 * n + 1) * share]
        odd = product[(2 * n + 1) * share : (2 * n + 2) * share]
        keep_ref[n] = jnp.where(core, even, odd)
        send_ref[n] = jnp.where(core, odd, even).astype(BF16)
    for side, ref in enumerate((near_ref, far_ref)):
        total = value_ref[side * rows : (side + 1) * rows, :]
        for kg_ref in kg_refs[1 : pieces // 2]:
            total += kg_ref[(1 + side) * rows : (2 + side) * rows, :].astype(F32)
        ref[...] = total.astype(ref.dtype)


def weight_terms(samples, core, visual, value_own, key_grads):
    rows, width = key_grads[0].shape
    half = (samples // 2, visual.shape[0] // samples, width)
    middle = len(key_grads) // 2
    order = [0, *range(middle - 1, 0, -1), *range(middle + 1, 2 * middle), middle]
    return pl.pallas_call(
        functools.partial(weight_kernel, order),
        in_specs=[pl.BlockSpec(memory_space=pltpu.SMEM)] + [VMEM] * (2 + len(key_grads)),
        out_specs=[VMEM] * 4,
        out_shape=[
            jax.ShapeDtypeStruct(half, F32),
            jax.ShapeDtypeStruct(half, BF16),
            jax.ShapeDtypeStruct((rows, width), F32),
            jax.ShapeDtypeStruct((rows, width), BF16),
        ],
        compiler_params=pltpu.CompilerParams(vmem_limit_bytes=32 * MIB),
        name="weight_terms",
    )(core, visual, value_own, *[key_grads[m] for m in order])


def halve_kernel(bit_ref, kept_ref, came_ref, keep_ref, send_ref):
    low = bit_ref[0] == 0
    for n in range(keep_ref.shape[0]):
        even = kept_ref[2 * n] + came_ref[2 * n].astype(F32)
        odd = kept_ref[2 * n + 1] + came_ref[2 * n + 1].astype(F32)
        keep_ref[n] = jnp.where(low, even, odd)
        send_ref[n] = jnp.where(low, odd, even).astype(BF16)


def halve(bit, kept, came):
    half = (kept.shape[0] // 2, *kept.shape[1:])
    return pl.pallas_call(
        halve_kernel,
        in_specs=[pl.BlockSpec(memory_space=pltpu.SMEM), VMEM, VMEM],
        out_specs=[VMEM] * 2,
        out_shape=[jax.ShapeDtypeStruct(half, F32), jax.ShapeDtypeStruct(half, BF16)],
        compiler_params=pltpu.CompilerParams(vmem_limit_bytes=32 * MIB),
        name="halve",
    )(bit, kept, came)


def local(visual_rows, value_matrix, key_weight, queries, output_gradient, visual_len, frame_end):
    tie = lax.optimization_barrier
    blocks, samples = lax.axis_size("blk"), lax.axis_size("dp")
    sample = lax.axis_index("dp").astype(jnp.int32)
    visual, half = visual_rows[0], blocks // 2

    own, visual_own, visual_near = project(blocks, visual, key_weight, value_matrix[0])
    keys_values = gather(own)
    keys_values[1], *visual_near = tie((keys_values[1], *visual_near))
    visual_near = near_exchange(visual_near)
    attention = Attention(queries[0], blocks, visual.shape[0])
    inner, key_own, key_near = attention.scores(
        visual_len, frame_end, queries[0], output_gradient[0], keys_values
    )
    weights, again, dscores, keys, values = inner
    key_near, visual_near = tie((key_near, visual_near))

    key_near = near_exchange(key_near)
    value_own, value_near = attention.values(output_gradient[0], weights)
    value_own, visual_own, visual_near = tie((value_own, visual_own, visual_near))
    visual_near, visual_far = pack(visual_own, visual_near)
    visual_far = swap(visual_far, "blk", half)
    key_own, value_own = tie((key_own, value_own))
    key_sum, key_far = near_sums(key_own, key_near, "key_sums")
    key_far = swap(key_far, "blk", half)
    key_grad, key_again, near = add_far(key_sum, key_far, value_near)
    key_grads = gather(key_grad, near)
    key_grads[0] = key_again
    visual_columns = turn(visual_near, visual_far)
    attn_out = attention.over_rows(in_hbm(again), values, "output")
    visual_columns, attn_out, dscores = tie((visual_columns, attn_out, dscores))
    kept, sent, value_sum, value_far = weight_terms(
        samples, (sample % 2)[None], visual_columns, value_own, key_grads
    )
    value_far = swap(value_far, "blk", half)
    query_grad = attention.over_rows(dscores, keys, "query_grad")
    came, bit = swap(sent, "dp", 1), 1
    while kept.shape[0] > 1:
        kept, sent = halve(((sample >> bit) % 2)[None], kept, came)
        came, bit = swap(sent, "dp", 1 << bit), bit + 1
    value_far, query_grad = tie((value_far, query_grad))
    shape = [(value_far.shape, BF16)]
    value_grad = in_vmem(add_value_kernel, "value_grad", shape, value_sum, value_far)[0]
    came, query_grad, value_grad = tie((came, query_grad, value_grad))
    weight_grad = kept[0] + came[0].astype(F32)
    return attn_out[None], query_grad[None], value_grad[None], weight_grad


def solution(mesh):
    return jax.shard_map(
        local,
        mesh=mesh,
        in_specs=(
            P("dp", "blk", None),
            P("dp", "blk", None),
            P(),
            P("dp", "blk", None),
            P("dp", "blk", None),
            P("dp"),
            P("dp", None),
        ),
        out_specs=(
            P("dp", "blk", None),
            P("dp", "blk", None),
            P("dp", "blk", None),
            P(("blk", "dp"), None),
        ),
        check_vma=False,
    )
```

time: 67.7 us -> 73.3 us (1.083)
  local copies, waits for them, and re-layouts: 1.6 us -> 4.85 us
  Pallas kernels: 18.3 us -> 20.6 us
  waiting for transfers between devices: 9.48 us -> 7.73 us
  starting transfers between devices: 35.9 us -> 37.3 us
    unnamed x10 -> x26, local copies, waits for them, and re-layouts: 1.6 us -> 4.85 us
    ppermute x23 -> x25, waiting for transfers between devices: 9.48 us -> 7.73 us  [swap(): return lax.ppermute(x, axis, [(i, i ^ mask) for i in range(size)])]
    pallas_call x2, Pallas kernels: 5.12 us -> 6.74 us  [over_rows(): self.call(rows_kernel, 1, 3, name, grid=(KEY_HEADS, self.tiles), in_specs...]
    ppermute x23 -> x25, starting transfers between devices: 35.9 us -> 37.3 us  [swap(): return lax.ppermute(x, axis, [(i, i ^ mask) for i in range(size)])]
    pallas_call x3 -> x6, Pallas kernels: 1.85 us -> 2.5 us  [the longest x5 1.5 us: in_vmem(): pl.pallas_call(kernel, in_specs=[VMEM] * len(arrays), out_specs=[VMEM] *...]
  transfers between devices with their start and end apart: 23 -> 25, of which waited for: 10 -> 5; matrix products, arithmetic and copies ran while one was open for 0% -> 0% of each run, Pallas kernels for 12% -> 23%
where the time goes in v9:
time: 73.3 us; the launch traced here: 72.8 us
  starting transfers between devices  37.3 us (51%)
  Pallas kernels  20.6 us (28%)
  waiting for transfers between devices  7.73 us (11%)
  local copies, waits for them, and re-layouts  4.85 us (7%)
  between operations  1.49 us (2%)
    ppermute x25, starting transfers between devices, swap(): return lax.ppermute(x, axis, [(i, i ^ mask) for i in range(size)])  37.3 us
    ppermute x25, waiting for transfers between devices, swap(): return lax.ppermute(x, axis, [(i, i ^ mask) for i in range(size)])  7.73 us
    pallas_call x2, Pallas kernels, over_rows(): self.call(rows_kernel, 1, 3, name, grid=(KEY_HEADS, self.tiles), in_specs...  6.74 us
    pallas_call x1, Pallas kernels, scores(): self.call(scores_kernel, 6, 4, 'scores', in_specs=[smem, smem, VMEM, VMEM...  5.48 us
    unnamed x26, local copies, waits for them, and re-layouts  4.85 us
    pallas_call x1, Pallas kernels, project(): pl.pallas_call(functools.partial(project_kernel, streams), grid=(steps,),...  2.98 us
    pallas_call x1, Pallas kernels, values(): self.call(values_kernel, 1, 2, 'values', grid=(KEY_HEADS, self.tiles), in...  2.86 us
    pallas_call x5, Pallas kernels, in_vmem(): pl.pallas_call(kernel, in_specs=[VMEM] * len(arrays), out_specs=[VMEM] *...  1.5 us
  transfers between devices with their start and end apart: 25, of which 5 were waited for; matrix products, arithmetic and copies ran while one was open for 0% of the time, Pallas kernels for 23%

profile of v9, /device:TPU:0, one launch (start us, length us, event | category | flops | bytes accessed | tf_op | source)
XLA Modules:
  0.0 72.8 jit_solution(4990976831922677034)
XLA Ops:
  0.7 3.0 %project.1 = (bf16[32,1024]{1,0:T(8,128)(2,1)S(1)}, bf16[64,512]{1,0:T(8,128)(2,1)S(1)}, bf16[64,512]{1,0:T(8,128)(2,1)S(1)}, bf16[64,512]{1,0:T(8,128)(2,1)S(1)}, bf16[64,512]{1,0:T(8,128)(2,1)S(1)}) custom-call(bf16[32,4096]{1,0:T(8,128)(2,1)} %bitcast.16, bf16[4096,512]{1,0:T(8,128)(2,1)} %refs_3_.1, bf16[4096,512]{1,0:T(8,128)(2,1)} %refs_3_.1, ...), custom_call_target="tpu_custom_call" | custom-call | flops 134217728 | bytes 4194304 | tf_op jit(solution)/shard_map/project/pallas_call | solution.py:95
  3.7 4.1 %collective-permute-start.3 = (bf16[32,1024]{1,0:T(8,128)(2,1)S(1)}, bf16[32,1024]{1,0:T(8,128)(2,1)S(1)}, u32[]{:S(2)}, u32[]{:S(2)}) collective-permute-start(bf16[32,1024]{1,0:T(8,128)(2,1)S(1)} %get-tuple-element.62.refs_0_), channel_id=1, source_target_pairs={{0,16},{4,20},{8,24},{12,28},{16,0},{20,4},{24,8},{28,12},{1,17},{... | collective-permute-start | bytes 196616 | tf_op jit(solution)/shard_map/ppermute | solution.py:28
  7.8 1.5 %collective-permute-start = (bf16[32,1024]{1,0:T(8,128)(2,1)S(1)}, bf16[32,1024]{1,0:T(8,128)(2,1)S(1)}, u32[]{:S(2)}, u32[]{:S(2)}) collective-permute-start(bf16[32,1024]{1,0:T(8,128)(2,1)S(1)} %get-tuple-element.62.refs_0_), channel_id=1, source_target_pairs={{0,4},{4,0},{8,12},{12,8},{16,20},{20,16},{24,28},{28,24},{1,5},{5... | collective-permute-start | bytes 196616 | tf_op jit(solution)/shard_map/ppermute | solution.py:28
  9.3 1.6 %collective-permute-start.1 = (bf16[32,1024]{1,0:T(8,128)(2,1)S(1)}, bf16[32,1024]{1,0:T(8,128)(2,1)S(1)}, u32[]{:S(2)}, u32[]{:S(2)}) collective-permute-start(bf16[32,1024]{1,0:T(8,128)(2,1)S(1)} %get-tuple-element.62.refs_0_), channel_id=1, source_target_pairs={{0,8},{4,12},{8,0},{12,4},{16,24},{20,28},{24,16},{28,20},{1,9},{5... | collective-permute-start | bytes 196616 | tf_op jit(solution)/shard_map/ppermute | solution.py:28
  11.2 1.5 %collective-permute-start.4 = (bf16[32,1024]{1,0:T(8,128)(2,1)S(1)}, bf16[32,1024]{1,0:T(8,128)(2,1)S(1)}, u32[]{:S(2)}, u32[]{:S(2)}) collective-permute-start(bf16[32,1024]{1,0:T(8,128)(2,1)S(1)} %collective-permute-done.3.refs_4_), channel_id=1, source_target_pairs={{0,4},{4,0},{8,12},{12,8},{16,20},{20,16},{24,28},{28,24},{1,5},{5... | collective-permute-start | bytes 196616 | tf_op jit(solution)/shard_map/ppermute | solution.py:28
  12.8 1.6 %collective-permute-start.5 = (bf16[32,1024]{1,0:T(8,128)(2,1)S(1)}, bf16[32,1024]{1,0:T(8,128)(2,1)S(1)}, u32[]{:S(2)}, u32[]{:S(2)}) collective-permute-start(bf16[32,1024]{1,0:T(8,128)(2,1)S(1)} %collective-permute-done.3.refs_4_), channel_id=1, source_target_pairs={{0,8},{4,12},{8,0},{12,4},{16,24},{20,28},{24,16},{28,20},{1,9},{5... | collective-permute-start | bytes 196616 | tf_op jit(solution)/shard_map/ppermute | solution.py:28
  14.3 1.0 %collective-permute-start.6 = (bf16[32,1024]{1,0:T(8,128)(2,1)S(1)}, bf16[32,1024]{1,0:T(8,128)(2,1)S(1)}, u32[]{:S(2)}, u32[]{:S(2)}) collective-permute-start(bf16[32,1024]{1,0:T(8,128)(2,1)S(1)} %collective-permute-done.3.refs_4_), channel_id=1, source_target_pairs={{0,12},{4,8},{8,4},{12,0},{16,28},{20,24},{24,20},{28,16},{1,13},{... | collective-permute-start | bytes 196616 | tf_op jit(solution)/shard_map/ppermute | solution.py:28
  16.0 1.0 %collective-permute-start.7 = (bf16[64,512]{1,0:T(8,128)(2,1)S(1)}, bf16[64,512]{1,0:T(8,128)(2,1)S(1)}, u32[]{:S(2)}, u32[]{:S(2)}) collective-permute-start(bf16[64,512]{1,0:T(8,128)(2,1)S(1)} %get-tuple-element.73), channel_id=1, source_target_pairs={{0,4},{4,0},{8,12},{12,8},{16,20},{20,16},{24,28},{28,24},{1,5},{5... | collective-permute-start | bytes 196616 | tf_op jit(solution)/shard_map/ppermute | solution.py:28
  17.0 1.6 %collective-permute-start.8 = (bf16[64,512]{1,0:T(8,128)(2,1)S(1)}, bf16[64,512]{1,0:T(8,128)(2,1)S(1)}, u32[]{:S(2)}, u32[]{:S(2)}) collective-permute-start(bf16[64,512]{1,0:T(8,128)(2,1)S(1)} %get-tuple-element.74), channel_id=1, source_target_pairs={{0,8},{4,12},{8,0},{12,4},{16,24},{20,28},{24,16},{28,20},{1,9},{5... | collective-permute-start | bytes 196616 | tf_op jit(solution)/shard_map/ppermute | solution.py:28
  18.6 1.0 %collective-permute-start.9 = (bf16[64,512]{1,0:T(8,128)(2,1)S(1)}, bf16[64,512]{1,0:T(8,128)(2,1)S(1)}, u32[]{:S(2)}, u32[]{:S(2)}) collective-permute-start(bf16[64,512]{1,0:T(8,128)(2,1)S(1)} %get-tuple-element.75), channel_id=1, source_target_pairs={{0,12},{4,8},{8,4},{12,0},{16,28},{20,24},{24,20},{28,16},{1,13},{... | collective-permute-start | bytes 196616 | tf_op jit(solution)/shard_map/ppermute | solution.py:28
  19.7 5.5 %scores.1 = (bf16[256,4096]{1,0:T(8,128)(2,1)S(1)}, bf16[256,4096]{1,0:T(8,128)(2,1)S(1)}, bf16[256,4096]{1,0:T(8,128)(2,1)S(1)}, bf16[256,512]{1,0:T(8,128)(2,1...) custom-call(s32[1]{0:T(128)S(6)} %copy.11.length_ref, ...), custom_call_target="tpu_custom_call" | custom-call | flops 1610612736 | bytes 4194304 | tf_op jit(solution)/shard_map/scores/pallas_call | solution.py:261
  25.2 0.9 %collective-permute-start.11 = (bf16[64,512]{1,0:T(8,128)(2,1)S(1)}, bf16[64,512]{1,0:T(8,128)(2,1)S(1)}, u32[]{:S(2)}, u32[]{:S(2)}) collective-permute-start(bf16[64,512]{1,0:T(8,128)(2,1)S(1)} %get-tuple-element.94), channel_id=1, source_target_pairs={{0,4},{4,0},{8,12},{12,8},{16,20},{20,16},{24,28},{28,24},{1,5},{5... | collective-permute-start | bytes 196616 | tf_op jit(solution)/shard_map/ppermute | solution.py:28
  26.1 1.6 %collective-permute-start.12 = (bf16[64,512]{1,0:T(8,128)(2,1)S(1)}, bf16[64,512]{1,0:T(8,128)(2,1)S(1)}, u32[]{:S(2)}, u32[]{:S(2)}) collective-permute-start(bf16[64,512]{1,0:T(8,128)(2,1)S(1)} %get-tuple-element.95), channel_id=1, source_target_pairs={{0,8},{4,12},{8,0},{12,4},{16,24},{20,28},{24,16},{28,20},{1,9},{5... | collective-permute-start | bytes 196616 | tf_op jit(solution)/shard_map/ppermute | solution.py:28
  27.7 1.1 %collective-permute-start.13 = (bf16[64,512]{1,0:T(8,128)(2,1)S(1)}, bf16[64,512]{1,0:T(8,128)(2,1)S(1)}, u32[]{:S(2)}, u32[]{:S(2)}) collective-permute-start(bf16[64,512]{1,0:T(8,128)(2,1)S(1)} %get-tuple-element.96), channel_id=1, source_target_pairs={{0,12},{4,8},{8,4},{12,0},{16,28},{20,24},{24,20},{28,16},{1,13},{... | collective-permute-start | bytes 196616 | tf_op jit(solution)/shard_map/ppermute | solution.py:28
  28.8 2.9 %values.1 = (f32[64,512]{1,0:T(8,128)S(1)}, bf16[64,512]{1,0:T(8,128)(2,1)S(1)}, bf16[64,512]{1,0:T(8,128)(2,1)S(1)}, bf16[64,512]{1,0:T(8,128)(2,1)S(1)}) custom-call(bf16[128,4096]{1,0:T(8,128)(2,1)} %bitcast.11, bf16[256,4096]{1,0:T(8,128)(2,1)S(1)} %get-tuple-element.67.w_ref), custom_call_target="tpu_custom_call" | custom-call | flops 268435456 | bytes 2097152 | tf_op jit(solution)/shard_map/values/pallas_call | solution.py:277
  31.7 2.5 %collective-permute-start.10 = (bf16[128,512]{1,0:T(8,128)(2,1)S(1)}, bf16[128,512]{1,0:T(8,128)(2,1)S(1)}, u32[]{:S(2)}, u32[]{:S(2)}) collective-permute-start(bf16[128,512]{1,0:T(8,128)(2,1)S(1)} %get-tuple-element.84), channel_id=1, source_target_pairs={{0,16},{4,20},{8,24},{12,28},{16,0},{20,4},{24,8},{28,12},{1,17},{... | collective-permute-start | bytes 393224 | tf_op jit(solution)/shard_map/ppermute | solution.py:28
  34.3 1.9 %collective-permute-start.14 = (bf16[32,512]{1,0:T(8,128)(2,1)S(1)}, bf16[32,512]{1,0:T(8,128)(2,1)S(1)}, u32[]{:S(2)}, u32[]{:S(2)}) collective-permute-start(bf16[32,512]{1,0:T(8,128)(2,1)S(1)} %get-tuple-element.98), channel_id=1, source_target_pairs={{0,16},{4,20},{8,24},{12,28},{16,0},{20,4},{24,8},{28,12},{1,17},{... | collective-permute-start | bytes 98312 | tf_op jit(solution)/shard_map/ppermute | solution.py:28
  36.1 3.6 %collective-permute-done.14.far_ref = bf16[32,512]{1,0:T(8,128)(2,1)S(1)} collective-permute-done((bf16[32,512]{1,0:T(8,128)(2,1)S(1)}, bf16[32,512]{1,0:T(8,128)(2,1)S(1)}, u32[]{:S(2)}, u32[]{:S(2)}) %collective-permute-start.14) | collective-permute-done | bytes 32800 | tf_op jit(solution)/shard_map/ppermute | solution.py:28
  40.5 1.4 %collective-permute-start.18 = (bf16[32,512]{1,0:T(8,128)(2,1)S(1)}, bf16[32,512]{1,0:T(8,128)(2,1)S(1)}, u32[]{:S(2)}, u32[]{:S(2)}) collective-permute-start(bf16[32,512]{1,0:T(8,128)(2,1)S(1)} %get-tuple-element.106), channel_id=1, source_target_pairs={{0,16},{4,20},{8,24},{12,28},{16,0},{20,4},{24,8},{28,12},{1,17},{... | collective-permute-start | bytes 98312 | tf_op jit(solution)/shard_map/ppermute | solution.py:28
  41.9 3.4 %collective-permute-start.15 = (bf16[96,512]{1,0:T(8,128)(2,1)}, bf16[96,512]{1,0:T(8,128)(2,1)S(1)}, u32[]{:S(2)}, u32[]{:S(2)}) collective-permute-start(bf16[96,512]{1,0:T(8,128)(2,1)} %get-tuple-element.103), channel_id=1, source_target_pairs={{0,12},{4,8},{8,4},{12,0},{16,28},{20,24},{24,20},{28,16},{1,13},{... | collective-permute-start | bytes 294920 | tf_op jit(solution)/shard_map/ppermute | solution.py:28
  46.0 1.4 %collective-permute-start.19 = (bf16[32,512]{1,0:T(8,128)(2,1)S(1)}, bf16[32,512]{1,0:T(8,128)(2,1)S(1)}, u32[]{:S(2)}, u32[]{:S(2)}) collective-permute-start(bf16[32,512]{1,0:T(8,128)(2,1)S(1)} %collective-permute-done.18.refs_7_), channel_id=1, source_target_pairs={{0,4},{4,0},{8,12},{12,8},{16,20},{20,16},{24,28},{28,24},{1,5},{5... | collective-permute-start | bytes 98312 | tf_op jit(solution)/shard_map/ppermute | solution.py:28
  47.4 2.0 %collective-permute-start.20 = (bf16[32,512]{1,0:T(8,128)(2,1)S(1)}, bf16[32,512]{1,0:T(8,128)(2,1)S(1)}, u32[]{:S(2)}, u32[]{:S(2)}) collective-permute-start(bf16[32,512]{1,0:T(8,128)(2,1)S(1)} %collective-permute-done.18.refs_7_), channel_id=1, source_target_pairs={{0,8},{4,12},{8,0},{12,4},{16,24},{20,28},{24,16},{28,20},{1,9},{5... | collective-permute-start | bytes 98312 | tf_op jit(solution)/shard_map/ppermute | solution.py:28
  49.4 1.1 %collective-permute-done.19.refs_4_ = bf16[32,512]{1,0:T(8,128)(2,1)S(1)} collective-permute-done((bf16[32,512]{1,0:T(8,128)(2,1)S(1)}, bf16[32,512]{1,0:T(8,128)(2,1)S(1)}, u32[]{:S(2)}, u32[]{:S(2)}) %collective-permute-start.19) | collective-permute-done | bytes 32800 | tf_op jit(solution)/shard_map/ppermute | solution.py:28
  50.5 2.3 %collective-permute-start.21 = (bf16[32,512]{1,0:T(8,128)(2,1)S(1)}, bf16[32,512]{1,0:T(8,128)(2,1)S(1)}, u32[]{:S(2)}, u32[]{:S(2)}) collective-permute-start(bf16[32,512]{1,0:T(8,128)(2,1)S(1)} %collective-permute-done.18.refs_7_), channel_id=1, source_target_pairs={{0,12},{4,8},{8,4},{12,0},{16,28},{20,24},{24,20},{28,16},{1,13},{... | collective-permute-start | bytes 98312 | tf_op jit(solution)/shard_map/ppermute | solution.py:28
  52.8 4.2 %output.1 = bf16[128,4096]{1,0:T(8,128)(2,1)} custom-call(bf16[256,4096]{1,0:T(8,128)(2,1)} %copy-done, bf16[256,512]{1,0:T(8,128)(2,1)S(1)} %get-tuple-element.86.head_ref), custom_call_target="tpu_custom_call" | custom-call | flops 268435456 | bytes 3145728 | tf_op jit(solution)/shard_map/output/pallas_call | solution.py:291
  59.1 0.8 %copy-done.5 = bf16[32,512]{1,0:T(8,128)(2,1)S(1)} copy-done((bf16[32,512]{1,0:T(8,128)(2,1)S(1)}, bf16[32,512]{1,0:T(8,128)(2,1)}, u32[]{:S(2)}) %copy-start.5) | copy-done | bytes 32792
  61.4 1.0 %weight_terms.1 = (f32[2,128,512]{2,1,0:T(8,128)S(1)}, bf16[2,128,512]{2,1,0:T(8,128)(2,1)}, f32[32,512]{1,0:T(8,128)S(1)}, bf16[32,512]{1,0:T(8,128)(2,1)S(1)}) custom-call(s32[1]{0:T(128)} %bitcast.6.core_ref, bf16[512,256]{1,0:T(8,128)(2,1)S(1)} %turn_visual.1.visual_ref, f32[64,512]{1,0:T(8,128)S(1)} %get-tuple-element.92.value_ref, ...), custom_call_target="tpu_custom_call" | custom-call | tf_op jit(solution)/shard_map/weight_terms/pallas_call | solution.py:402
  63.0 1.7 %collective-permute-done.22.came_ref = bf16[2,128,512]{2,1,0:T(8,128)(2,1)S(1)} collective-permute-done((bf16[2,128,512]{2,1,0:T(8,128)(2,1)}, bf16[2,128,512]{2,1,0:T(8,128)(2,1)S(1)}, u32[]{:S(2)}, u32[]{:S(2)}) %collective-permute-start.22) | collective-permute-done | bytes 262176 | tf_op jit(solution)/shard_map/ppermute | solution.py:28
  64.8 1.6 %collective-permute-start.23 = (bf16[1,128,512]{2,1,0:T(8,128)(2,1)S(1)}, bf16[1,128,512]{2,1,0:T(8,128)(2,1)S(1)}, u32[]{:S(2)}, u32[]{:S(2)}) collective-permute-start(bf16[1,128,512]{2,1,0:T(8,128)(2,1)S(1)} %get-tuple-element.109), channel_id=1, source_target_pairs={{0,2},{1,3},{2,0},{3,1},{4,6},{5,7},{6,4},{7,5},{8,10},{9,11},{10,... | collective-permute-start | bytes 393224 | tf_op jit(solution)/shard_map/ppermute | solution.py:28
  66.4 1.4 %collective-permute-start.24 = (bf16[32,512]{1,0:T(8,128)(2,1)}, bf16[32,512]{1,0:T(8,128)(2,1)S(1)}, u32[]{:S(2)}, u32[]{:S(2)}) collective-permute-start(bf16[32,512]{1,0:T(8,128)(2,1)} %copy-done.11), channel_id=1, source_target_pairs={{0,16},{4,20},{8,24},{12,28},{16,0},{20,4},{24,8},{28,12},{1,17},{... | collective-permute-start | bytes 98312 | tf_op jit(solution)/shard_map/ppermute | solution.py:28
  67.8 2.6 %query_grad.1 = bf16[128,4096]{1,0:T(8,128)(2,1)} custom-call(bf16[256,4096]{1,0:T(8,128)(2,1)S(1)} %get-tuple-element.111.inner_ref, bf16[256,512]{1,0:T(8,128)(2,1)S(1)} %get-tuple-element.112.head_ref), custom_call_target="tpu_custom_call" | custom-call | flops 268435456 | bytes 3145728 | tf_op jit(solution)/shard_map/query_grad/pallas_call | solution.py:291
  70.3 1.1 %collective-permute-done.24.far_ref = bf16[32,512]{1,0:T(8,128)(2,1)S(1)} collective-permute-done((bf16[32,512]{1,0:T(8,128)(2,1)}, bf16[32,512]{1,0:T(8,128)(2,1)S(1)}, u32[]{:S(2)}, u32[]{:S(2)}) %collective-permute-start.24) | collective-permute-done | bytes 32800 | tf_op jit(solution)/shard_map/ppermute | solution.py:28
  (57 shorter events, 7.6 us)
Async XLA Ops:
  0.6 19.1 %copy-start.1 = (bf16[1,128,4096]{2,1,0:T(8,128)(2,1)S(1)}, bf16[1,128,4096]{2,1,0:T(8,128)(2,1)}, u32[]{:S(2)}) copy-start(bf16[1,128,4096]{2,1,0:T(8,128)(2,1)} %param.11) | copy-start | bytes 3145732
  0.6 19.1 %copy-start.10 = (bf16[1,128,4096]{2,1,0:T(8,128)(2,1)S(1)}, bf16[1,128,4096]{2,1,0:T(8,128)(2,1)}, u32[]{:S(2)}) copy-start(bf16[1,128,4096]{2,1,0:T(8,128)(2,1)} %param.10) | copy-start | bytes 3145732
  0.7 19.1 %copy-start.12 = (s32[1,8]{1,0:T(1,128)S(1)}, s32[1,8]{1,0:T(1,128)}, u32[]{:S(2)}) copy-start(s32[1,8]{1,0:T(1,128)} %frame_ref.1) | copy-start | bytes 100
  3.7 7.6 %collective-permute-start.3 = (bf16[32,1024]{1,0:T(8,128)(2,1)S(1)}, bf16[32,1024]{1,0:T(8,128)(2,1)S(1)}, u32[]{:S(2)}, u32[]{:S(2)}) collective-permute-start(bf16[32,1024]{1,0:T(8,128)(2,1)S(1)} %get-tuple-element.62.refs_0_), channel_id=1, source_target_pairs={{0,16},{4,20},{8,24},{12,28},{16,0},{20,4},{24,8},{28,12},{1,17},{... | collective-permute-start | bytes 196616 | tf_op jit(solution)/shard_map/ppermute | solution.py:28
  7.8 6.6 %collective-permute-start = (bf16[32,1024]{1,0:T(8,128)(2,1)S(1)}, bf16[32,1024]{1,0:T(8,128)(2,1)S(1)}, u32[]{:S(2)}, u32[]{:S(2)}) collective-permute-start(bf16[32,1024]{1,0:T(8,128)(2,1)S(1)} %get-tuple-element.62.refs_0_), channel_id=1, source_target_pairs={{0,4},{4,0},{8,12},{12,8},{16,20},{20,16},{24,28},{28,24},{1,5},{5... | collective-permute-start | bytes 196616 | tf_op jit(solution)/shard_map/ppermute | solution.py:28
  9.3 6.7 %collective-permute-start.1 = (bf16[32,1024]{1,0:T(8,128)(2,1)S(1)}, bf16[32,1024]{1,0:T(8,128)(2,1)S(1)}, u32[]{:S(2)}, u32[]{:S(2)}) collective-permute-start(bf16[32,1024]{1,0:T(8,128)(2,1)S(1)} %get-tuple-element.62.refs_0_), channel_id=1, source_target_pairs={{0,8},{4,12},{8,0},{12,4},{16,24},{20,28},{24,16},{28,20},{1,9},{5... | collective-permute-start | bytes 196616 | tf_op jit(solution)/shard_map/ppermute | solution.py:28
  10.9 6.1 %collective-permute-start.2 = (bf16[32,1024]{1,0:T(8,128)(2,1)S(1)}, bf16[32,1024]{1,0:T(8,128)(2,1)S(1)}, u32[]{:S(2)}, u32[]{:S(2)}) collective-permute-start(bf16[32,1024]{1,0:T(8,128)(2,1)S(1)} %get-tuple-element.62.refs_0_), channel_id=1, source_target_pairs={{0,12},{4,8},{8,4},{12,0},{16,28},{20,24},{24,20},{28,16},{1,13},{... | collective-permute-start | bytes 196616 | tf_op jit(solution)/shard_map/ppermute | solution.py:28
  11.2 7.3 %collective-permute-start.4 = (bf16[32,1024]{1,0:T(8,128)(2,1)S(1)}, bf16[32,1024]{1,0:T(8,128)(2,1)S(1)}, u32[]{:S(2)}, u32[]{:S(2)}) collective-permute-start(bf16[32,1024]{1,0:T(8,128)(2,1)S(1)} %collective-permute-done.3.refs_4_), channel_id=1, source_target_pairs={{0,4},{4,0},{8,12},{12,8},{16,20},{20,16},{24,28},{28,24},{1,5},{5... | collective-permute-start | bytes 196616 | tf_op jit(solution)/shard_map/ppermute | solution.py:28
  12.8 6.8 %collective-permute-start.5 = (bf16[32,1024]{1,0:T(8,128)(2,1)S(1)}, bf16[32,1024]{1,0:T(8,128)(2,1)S(1)}, u32[]{:S(2)}, u32[]{:S(2)}) collective-permute-start(bf16[32,1024]{1,0:T(8,128)(2,1)S(1)} %collective-permute-done.3.refs_4_), channel_id=1, source_target_pairs={{0,8},{4,12},{8,0},{12,4},{16,24},{20,28},{24,16},{28,20},{1,9},{5... | collective-permute-start | bytes 196616 | tf_op jit(solution)/shard_map/ppermute | solution.py:28
  14.3 5.4 %collective-permute-start.6 = (bf16[32,1024]{1,0:T(8,128)(2,1)S(1)}, bf16[32,1024]{1,0:T(8,128)(2,1)S(1)}, u32[]{:S(2)}, u32[]{:S(2)}) collective-permute-start(bf16[32,1024]{1,0:T(8,128)(2,1)S(1)} %collective-permute-done.3.refs_4_), channel_id=1, source_target_pairs={{0,12},{4,8},{8,4},{12,0},{16,28},{20,24},{24,20},{28,16},{1,13},{... | collective-permute-start | bytes 196616 | tf_op jit(solution)/shard_map/ppermute | solution.py:28
  16.0 9.2 %collective-permute-start.7 = (bf16[64,512]{1,0:T(8,128)(2,1)S(1)}, bf16[64,512]{1,0:T(8,128)(2,1)S(1)}, u32[]{:S(2)}, u32[]{:S(2)}) collective-permute-start(bf16[64,512]{1,0:T(8,128)(2,1)S(1)} %get-tuple-element.73), channel_id=1, source_target_pairs={{0,4},{4,0},{8,12},{12,8},{16,20},{20,16},{24,28},{28,24},{1,5},{5... | collective-permute-start | bytes 196616 | tf_op jit(solution)/shard_map/ppermute | solution.py:28
  17.0 8.2 %collective-permute-start.8 = (bf16[64,512]{1,0:T(8,128)(2,1)S(1)}, bf16[64,512]{1,0:T(8,128)(2,1)S(1)}, u32[]{:S(2)}, u32[]{:S(2)}) collective-permute-start(bf16[64,512]{1,0:T(8,128)(2,1)S(1)} %get-tuple-element.74), channel_id=1, source_target_pairs={{0,8},{4,12},{8,0},{12,4},{16,24},{20,28},{24,16},{28,20},{1,9},{5... | collective-permute-start | bytes 196616 | tf_op jit(solution)/shard_map/ppermute | solution.py:28
  18.6 6.7 %collective-permute-start.9 = (bf16[64,512]{1,0:T(8,128)(2,1)S(1)}, bf16[64,512]{1,0:T(8,128)(2,1)S(1)}, u32[]{:S(2)}, u32[]{:S(2)}) collective-permute-start(bf16[64,512]{1,0:T(8,128)(2,1)S(1)} %get-tuple-element.75), channel_id=1, source_target_pairs={{0,12},{4,8},{8,4},{12,0},{16,28},{20,24},{24,20},{28,16},{1,13},{... | collective-permute-start | bytes 196616 | tf_op jit(solution)/shard_map/ppermute | solution.py:28
  25.2 6.5 %copy-start = (bf16[256,4096]{1,0:T(8,128)(2,1)}, bf16[256,4096]{1,0:T(8,128)(2,1)S(1)}, u32[]{:S(2)}) copy-start(bf16[256,4096]{1,0:T(8,128)(2,1)S(1)} %get-tuple-element.85.inner_ref) | copy-start | bytes 6291460
  25.2 9.0 %collective-permute-start.11 = (bf16[64,512]{1,0:T(8,128)(2,1)S(1)}, bf16[64,512]{1,0:T(8,128)(2,1)S(1)}, u32[]{:S(2)}, u32[]{:S(2)}) collective-permute-start(bf16[64,512]{1,0:T(8,128)(2,1)S(1)} %get-tuple-element.94), channel_id=1, source_target_pairs={{0,4},{4,0},{8,12},{12,8},{16,20},{20,16},{24,28},{28,24},{1,5},{5... | collective-permute-start | bytes 196616 | tf_op jit(solution)/shard_map/ppermute | solution.py:28
  26.1 8.1 %collective-permute-start.12 = (bf16[64,512]{1,0:T(8,128)(2,1)S(1)}, bf16[64,512]{1,0:T(8,128)(2,1)S(1)}, u32[]{:S(2)}, u32[]{:S(2)}) collective-permute-start(bf16[64,512]{1,0:T(8,128)(2,1)S(1)} %get-tuple-element.95), channel_id=1, source_target_pairs={{0,8},{4,12},{8,0},{12,4},{16,24},{20,28},{24,16},{28,20},{1,9},{5... | collective-permute-start | bytes 196616 | tf_op jit(solution)/shard_map/ppermute | solution.py:28
  27.7 6.5 %collective-permute-start.13 = (bf16[64,512]{1,0:T(8,128)(2,1)S(1)}, bf16[64,512]{1,0:T(8,128)(2,1)S(1)}, u32[]{:S(2)}, u32[]{:S(2)}) collective-permute-start(bf16[64,512]{1,0:T(8,128)(2,1)S(1)} %get-tuple-element.96), channel_id=1, source_target_pairs={{0,12},{4,8},{8,4},{12,0},{16,28},{20,24},{24,20},{28,16},{1,13},{... | collective-permute-start | bytes 196616 | tf_op jit(solution)/shard_map/ppermute | solution.py:28
  31.7 15.7 %collective-permute-start.10 = (bf16[128,512]{1,0:T(8,128)(2,1)S(1)}, bf16[128,512]{1,0:T(8,128)(2,1)S(1)}, u32[]{:S(2)}, u32[]{:S(2)}) collective-permute-start(bf16[128,512]{1,0:T(8,128)(2,1)S(1)} %get-tuple-element.84), channel_id=1, source_target_pairs={{0,16},{4,20},{8,24},{12,28},{16,0},{20,4},{24,8},{28,12},{1,17},{... | collective-permute-start | bytes 393224 | tf_op jit(solution)/shard_map/ppermute | solution.py:28
  34.3 5.5 %collective-permute-start.14 = (bf16[32,512]{1,0:T(8,128)(2,1)S(1)}, bf16[32,512]{1,0:T(8,128)(2,1)S(1)}, u32[]{:S(2)}, u32[]{:S(2)}) collective-permute-start(bf16[32,512]{1,0:T(8,128)(2,1)S(1)} %get-tuple-element.98), channel_id=1, source_target_pairs={{0,16},{4,20},{8,24},{12,28},{16,0},{20,4},{24,8},{28,12},{1,17},{... | collective-permute-start | bytes 98312 | tf_op jit(solution)/shard_map/ppermute | solution.py:28
  40.5 5.5 %collective-permute-start.18 = (bf16[32,512]{1,0:T(8,128)(2,1)S(1)}, bf16[32,512]{1,0:T(8,128)(2,1)S(1)}, u32[]{:S(2)}, u32[]{:S(2)}) collective-permute-start(bf16[32,512]{1,0:T(8,128)(2,1)S(1)} %get-tuple-element.106), channel_id=1, source_target_pairs={{0,16},{4,20},{8,24},{12,28},{16,0},{20,4},{24,8},{28,12},{1,17},{... | collective-permute-start | bytes 98312 | tf_op jit(solution)/shard_map/ppermute | solution.py:28
  41.9 16.4 %collective-permute-start.15 = (bf16[96,512]{1,0:T(8,128)(2,1)}, bf16[96,512]{1,0:T(8,128)(2,1)S(1)}, u32[]{:S(2)}, u32[]{:S(2)}) collective-permute-start(bf16[96,512]{1,0:T(8,128)(2,1)} %get-tuple-element.103), channel_id=1, source_target_pairs={{0,12},{4,8},{8,4},{12,0},{16,28},{20,24},{24,20},{28,16},{1,13},{... | collective-permute-start | bytes 294920 | tf_op jit(solution)/shard_map/ppermute | solution.py:28
  45.3 13.0 %collective-permute-start.16 = (bf16[96,512]{1,0:T(8,128)(2,1)}, bf16[96,512]{1,0:T(8,128)(2,1)S(1)}, u32[]{:S(2)}, u32[]{:S(2)}) collective-permute-start(bf16[96,512]{1,0:T(8,128)(2,1)} %get-tuple-element.104), channel_id=1, source_target_pairs={{0,8},{4,12},{8,0},{12,4},{16,24},{20,28},{24,16},{28,20},{1,9},{5... | collective-permute-start | bytes 294920 | tf_op jit(solution)/shard_map/ppermute | solution.py:28
  45.3 13.0 %collective-permute-start.17 = (bf16[96,512]{1,0:T(8,128)(2,1)}, bf16[96,512]{1,0:T(8,128)(2,1)S(1)}, u32[]{:S(2)}, u32[]{:S(2)}) collective-permute-start(bf16[96,512]{1,0:T(8,128)(2,1)} %get-tuple-element.105), channel_id=1, source_target_pairs={{0,4},{4,0},{8,12},{12,8},{16,20},{20,16},{24,28},{28,24},{1,5},{5... | collective-permute-start | bytes 294920 | tf_op jit(solution)/shard_map/ppermute | solution.py:28
  46.0 12.4 %copy-start.2 = (bf16[32,512]{1,0:T(8,128)(2,1)}, bf16[32,512]{1,0:T(8,128)(2,1)S(1)}, u32[]{:S(2)}) copy-start(bf16[32,512]{1,0:T(8,128)(2,1)S(1)} %collective-permute-done.18.refs_7_) | copy-start | bytes 98308
  46.0 4.6 %collective-permute-start.19 = (bf16[32,512]{1,0:T(8,128)(2,1)S(1)}, bf16[32,512]{1,0:T(8,128)(2,1)S(1)}, u32[]{:S(2)}, u32[]{:S(2)}) collective-permute-start(bf16[32,512]{1,0:T(8,128)(2,1)S(1)} %collective-permute-done.18.refs_7_), channel_id=1, source_target_pairs={{0,4},{4,0},{8,12},{12,8},{16,20},{20,16},{24,28},{28,24},{1,5},{5... | collective-permute-start | bytes 98312 | tf_op jit(solution)/shard_map/ppermute | solution.py:28
  47.4 9.7 %collective-permute-start.20 = (bf16[32,512]{1,0:T(8,128)(2,1)S(1)}, bf16[32,512]{1,0:T(8,128)(2,1)S(1)}, u32[]{:S(2)}, u32[]{:S(2)}) collective-permute-start(bf16[32,512]{1,0:T(8,128)(2,1)S(1)} %collective-permute-done.18.refs_7_), channel_id=1, source_target_pairs={{0,8},{4,12},{8,0},{12,4},{16,24},{20,28},{24,16},{28,20},{1,9},{5... | collective-permute-start | bytes 98312 | tf_op jit(solution)/shard_map/ppermute | solution.py:28
  50.5 7.8 %copy-start.4 = (bf16[32,512]{1,0:T(8,128)(2,1)}, bf16[32,512]{1,0:T(8,128)(2,1)S(1)}, u32[]{:S(2)}) copy-start(bf16[32,512]{1,0:T(8,128)(2,1)S(1)} %collective-permute-done.19.refs_4_) | copy-start | bytes 98308
  50.5 7.2 %collective-permute-start.21 = (bf16[32,512]{1,0:T(8,128)(2,1)S(1)}, bf16[32,512]{1,0:T(8,128)(2,1)S(1)}, u32[]{:S(2)}, u32[]{:S(2)}) collective-permute-start(bf16[32,512]{1,0:T(8,128)(2,1)S(1)} %collective-permute-done.18.refs_7_), channel_id=1, source_target_pairs={{0,12},{4,8},{8,4},{12,0},{16,28},{20,24},{24,20},{28,16},{1,13},{... | collective-permute-start | bytes 98312 | tf_op jit(solution)/shard_map/ppermute | solution.py:28
  58.3 0.8 %copy-start.3 = (bf16[32,512]{1,0:T(8,128)(2,1)S(1)}, bf16[32,512]{1,0:T(8,128)(2,1)}, u32[]{:S(2)}) copy-start(bf16[32,512]{1,0:T(8,128)(2,1)} %copy-done.2) | copy-start | bytes 98308
  63.0 1.7 %collective-permute-start.22 = (bf16[2,128,512]{2,1,0:T(8,128)(2,1)}, bf16[2,128,512]{2,1,0:T(8,128)(2,1)S(1)}, u32[]{:S(2)}, u32[]{:S(2)}) collective-permute-start(bf16[2,128,512]{2,1,0:T(8,128)(2,1)} %get-tuple-element.108), channel_id=1, source_target_pairs={{0,1},{1,0},{2,3},{3,2},{4,5},{5,4},{6,7},{7,6},{8,9},{9,8},{10,11... | collective-permute-start | bytes 786440 | tf_op jit(solution)/shard_map/ppermute | solution.py:28
  64.8 7.2 %collective-permute-start.23 = (bf16[1,128,512]{2,1,0:T(8,128)(2,1)S(1)}, bf16[1,128,512]{2,1,0:T(8,128)(2,1)S(1)}, u32[]{:S(2)}, u32[]{:S(2)}) collective-permute-start(bf16[1,128,512]{2,1,0:T(8,128)(2,1)S(1)} %get-tuple-element.109), channel_id=1, source_target_pairs={{0,2},{1,3},{2,0},{3,1},{4,6},{5,7},{6,4},{7,5},{8,10},{9,11},{10,... | collective-permute-start | bytes 393224 | tf_op jit(solution)/shard_map/ppermute | solution.py:28
  66.4 5.0 %collective-permute-start.24 = (bf16[32,512]{1,0:T(8,128)(2,1)}, bf16[32,512]{1,0:T(8,128)(2,1)S(1)}, u32[]{:S(2)}, u32[]{:S(2)}) collective-permute-start(bf16[32,512]{1,0:T(8,128)(2,1)} %copy-done.11), channel_id=1, source_target_pairs={{0,16},{4,20},{8,24},{12,28},{16,0},{20,4},{24,8},{28,12},{1,17},{... | collective-permute-start | bytes 98312 | tf_op jit(solution)/shard_map/ppermute | solution.py:28
  (6 other events, 4.1 us)

commit v10 on v9

--- a/solution.py
+++ b/solution.py
@@ -64,10 +64,15 @@
         block = lax.axis_index("blk")
         half = len(near_refs) + 1
         rows, width = visual_ref.shape[0], own_ref.shape[1]
-        for m, ref in enumerate((own_ref, *near_refs)):
+        for m in range(half):
             for side in range(2):
                 start = pl.multiple_of((block ^ (m + side * half)) * width, HEAD_SIZE)
-                ref[side * rows : (side + 1) * rows, :] = visual_ref[:, pl.ds(start, width)]
+                columns = visual_ref[:, pl.ds(start, width)]
+                if m == 0:
+                    own_ref[side * rows : (side + 1) * rows, :] = columns
+                else:
+                    first = out_ref.shape[1] + side * width
+                    near_refs[m - 1][:, first : first + width] = columns
 
     @pl.when(step > 0)
     def _():
@@ -76,8 +81,10 @@
     @pl.when(step == pl.num_programs(0) - 1)
     def _():
         columns = acc_ref.shape[1]
-        out_ref[:, :columns] = acc_ref[...].astype(BF16)
-        out_ref[:, columns:] = value_ref[...]
+        keys = acc_ref[...].astype(BF16)
+        for ref in (out_ref, *near_refs):
+            ref[:, :columns] = keys
+            ref[:, columns : out_ref.shape[1]] = value_ref[...]
 
 
 def project(blocks, visual, key_weight, value):
@@ -85,9 +92,9 @@
     columns = key_weight.shape[1]
     steps, streams = 2, 4
     slab = features // (steps * streams)
+    width = features // blocks
     out = (rows, columns + value.shape[1])
-    both = (2 * rows, features // blocks)
-    half = blocks // 2
+    shapes = [out, (2 * rows, width)] + [(rows, out[1] + 2 * width)] * (blocks // 2 - 1)
 
     def whole(shape):
         return pl.BlockSpec(shape, lambda k: (0, 0))
@@ -101,8 +108,8 @@
             for p in range(streams)
         ]
         + [whole(value.shape)],
-        out_specs=[whole(out)] + [whole(both)] * half,
-        out_shape=[jax.ShapeDtypeStruct(out, BF16)] + [jax.ShapeDtypeStruct(both, BF16)] * half,
+        out_specs=[whole(shape) for shape in shapes],
+        out_shape=[jax.ShapeDtypeStruct(shape, BF16) for shape in shapes],
         scratch_shapes=[pltpu.VMEM((rows, columns), F32)],
         cost_estimate=pl.CostEstimate(
             flops=2 * rows * features * columns,
@@ -145,7 +152,7 @@
     for m in range(pieces):
         part = slice(m * rows, (m + 1) * rows)
         k_ref[part, :] = kv_refs[m][:, :width]
-        v_ref[part, :] = kv_refs[m][:, width:]
+        v_ref[part, :] = kv_refs[m][:, width : 2 * width]
     row = lax.broadcasted_iota(jnp.int32, (rows, pair), 0)
     for i in range(tiles):
         text = slice(i * TILE, (i + 1) * TILE)
@@ -242,12 +249,12 @@
         self.terms = [jax.ShapeDtypeStruct(self.sides, F32)]
         self.terms += [jax.ShapeDtypeStruct(self.sides, BF16)] * (pieces // 2 - 1)
 
-    def call(self, kernel, products, moved, name, **specs):
+    def call(self, kernel, share, name, **specs):
         return pl.pallas_call(
             functools.partial(kernel, self.pieces),
             cost_estimate=pl.CostEstimate(
-                flops=2 * products * self.text * self.all_rows * self.wide,
-                bytes_accessed=2 * moved * self.text * self.wide,
+                flops=int(share * 12 * self.text * self.all_rows * self.wide),
+                bytes_accessed=int(share * 8 * self.text * self.wide),
                 transcendentals=0,
             ),
             compiler_params=pltpu.CompilerParams(vmem_limit_bytes=32 * MIB),
@@ -260,8 +267,7 @@
         heads = jax.ShapeDtypeStruct((self.all_rows, self.width), BF16)
         out = self.call(
             scores_kernel,
-            6,
-            4,
+            1.0,
             "scores",
             in_specs=[smem, smem, VMEM, VMEM] + [VMEM] * self.pieces,
             out_specs=[VMEM] * (5 + len(self.terms)),
@@ -276,8 +282,7 @@
     def values(self, gradients, weights):
         out = self.call(
             values_kernel,
-            1,
-            2,
+            0.03,
             "values",
             grid=(KEY_HEADS, self.tiles),
             in_specs=[self.text_block, self.inner_block],
@@ -290,8 +295,7 @@
     def over_rows(self, inner, heads, name):
         return self.call(
             rows_kernel,
-            1,
-            3,
+            0.03,
             name,
             grid=(KEY_HEADS, self.tiles),
             in_specs=[self.inner_block, self.head_block],
@@ -352,12 +356,14 @@
     out_ref[...] = (near_ref[...] + far_ref[...].astype(F32)).astype(BF16)
 
 
-def pack_kernel(*refs):
-    in_refs, (near_ref, far_ref) = refs[:-2], refs[-2:]
-    rows = in_refs[0].shape[0] // 2
-    for m, ref in enumerate(in_refs):
-        near_ref[m * rows : (m + 1) * rows, :] = ref[:rows, :]
-        far_ref[m * rows : (m + 1) * rows, :] = ref[rows:, :]
+def pack_kernel(own_ref, *refs):
+    came_refs, out_refs = refs[:-2], refs[-2:]
+    rows, width = own_ref.shape[0] // 2, own_ref.shape[1]
+    for side, ref in enumerate(out_refs):
+        ref[:rows, :] = own_ref[side * rows : (side + 1) * rows, :]
+        for m, came_ref in enumerate(came_refs, 1):
+            first = came_ref.shape[1] - (2 - side) * width
+            ref[m * rows : (m + 1) * rows, :] = came_ref[:, first : first + width]
 
 
 def pack(own, came):
@@ -441,22 +447,20 @@
     sample = lax.axis_index("dp").astype(jnp.int32)
     visual, half = visual_rows[0], blocks // 2
 
-    own, visual_own, visual_near = project(blocks, visual, key_weight, value_matrix[0])
-    keys_values = gather(own)
-    keys_values[1], *visual_near = tie((keys_values[1], *visual_near))
-    visual_near = near_exchange(visual_near)
+    own, visual_own, near = project(blocks, visual, key_weight, value_matrix[0])
+    keys_values = gather(own, near)
+    keys_values[half + 1], visual_own = tie((keys_values[half + 1], visual_own))
+    visual_near, visual_far = pack(visual_own, keys_values[1:half])
+    visual_far = swap(visual_far, "blk", half)
     attention = Attention(queries[0], blocks, visual.shape[0])
     inner, key_own, key_near = attention.scores(
         visual_len, frame_end, queries[0], output_gradient[0], keys_values
     )
     weights, again, dscores, keys, values = inner
-    key_near, visual_near = tie((key_near, visual_near))
+    key_near, visual_far = tie((key_near, visual_far))
 
     key_near = near_exchange(key_near)
     value_own, value_near = attention.values(output_gradient[0], weights)
-    value_own, visual_own, visual_near = tie((value_own, visual_own, visual_near))
-    visual_near, visual_far = pack(visual_own, visual_near)
-    visual_far = swap(visual_far, "blk", half)
     key_own, value_own = tie((key_own, value_own))
     key_sum, key_far = near_sums(key_own, key_near, "key_sums")
     key_far = swap(key_far, "blk", half)
@@ -464,7 +468,7 @@
     key_grads = gather(key_grad, near)
     key_grads[0] = key_again
     visual_columns = turn(visual_near, visual_far)
-    attn_out = attention.over_rows(in_hbm(again), values, "output")
+    attn_out = attention.over_rows(again, values, "output")
     visual_columns, attn_out, dscores = tie((visual_columns, attn_out, dscores))
     kept, sent, value_sum, value_far = weight_terms(
         samples, (sample % 2)[None], visual_columns, value_own, key_grads

time: 73.3 us -> 74.9 us (1.022)
  waiting for transfers between devices: 7.73 us -> 13.6 us
  starting transfers between devices: 37.3 us -> 33 us
  local copies, waits for them, and re-layouts: 4.85 us -> 6.63 us
  Pallas kernels: 20.6 us -> 19 us
    ppermute x25 -> x22, waiting for transfers between devices: 7.73 us -> 13.6 us  [swap(): return lax.ppermute(x, axis, [(i, i ^ mask) for i in range(size)])]
    ppermute x25 -> x22, starting transfers between devices: 37.3 us -> 33 us  [swap(): return lax.ppermute(x, axis, [(i, i ^ mask) for i in range(size)])]
    unnamed x26, local copies, waits for them, and re-layouts: 4.85 us -> 6.63 us
    pallas_call x4, Pallas kernels: 15.1 us -> 13.5 us  [the longest x1 5.48 us: scores(): self.call(scores_kernel, 1.0, 'scores', in_specs=[smem, smem, VMEM, VMEM]...]
  transfers between devices with their start and end apart: 25 -> 22, of which waited for: 5 -> 7; matrix products, arithmetic and copies ran while one was open for 0% -> 0% of each run, Pallas kernels for 23% -> 19%
where the time goes in v10:
time: 74.9 us; the launch traced here: 74.5 us
  starting transfers between devices  33 us (44%)
  Pallas kernels  19 us (25%)
  waiting for transfers between devices  13.6 us (18%)
  local copies, waits for them, and re-layouts  6.63 us (9%)
  between operations  1.48 us (2%)
    ppermute x22, starting transfers between devices, swap(): return lax.ppermute(x, axis, [(i, i ^ mask) for i in range(size)])  33 us
    ppermute x22, waiting for transfers between devices, swap(): return lax.ppermute(x, axis, [(i, i ^ mask) for i in range(size)])  13.6 us
    unnamed x26, local copies, waits for them, and re-layouts  6.63 us
    pallas_call x1, Pallas kernels, scores(): self.call(scores_kernel, 1.0, 'scores', in_specs=[smem, smem, VMEM, VMEM]...  5.48 us
    pallas_call x2, Pallas kernels, over_rows(): self.call(rows_kernel, 0.03, name, grid=(KEY_HEADS, self.tiles), in_specs...  5.12 us
    pallas_call x1, Pallas kernels, project(): pl.pallas_call(functools.partial(project_kernel, streams), grid=(steps,),...  3 us
    pallas_call x1, Pallas kernels, values(): self.call(values_kernel, 0.03, 'values', grid=(KEY_HEADS, self.tiles), in...  2.85 us
    pallas_call x5, Pallas kernels, in_vmem(): pl.pallas_call(kernel, in_specs=[VMEM] * len(arrays), out_specs=[VMEM] *...  1.52 us
  transfers between devices with their start and end apart: 22, of which 7 were waited for; matrix products, arithmetic and copies ran while one was open for 0% of the time, Pallas kernels for 19%

profile of v10, /device:TPU:0, one launch (start us, length us, event | category | flops | bytes accessed | tf_op | source)
XLA Modules:
  0.0 74.5 jit_solution(18172488183648924601)
XLA Ops:
  0.7 3.0 %project.1 = (bf16[32,1024]{1,0:T(8,128)(2,1)S(1)}, bf16[64,512]{1,0:T(8,128)(2,1)S(1)}, bf16[32,2048]{1,0:T(8,128)(2,1)S(1)}, bf16[32,2048]{1,0:T(8,128)(2,1)S(1)}, bf16[32,2048]{1,0:T(8,128)(2,1)S(1)}) custom-call(bf16[32,4096]{1,0:T(8,128)(2,1)} %bitcast.16, bf16[4096,512]{1,0:T(8,128)(2,1)} %refs_3_.1, bf16[4096,512]{1,0:T(8,128)(2,1)} %refs_3_.1, ...), custom_call_target="tpu_custom_call" | custom-call | flops 134217728 | bytes 4194304 | tf_op jit(solution)/shard_map/project/pallas_call | solution.py:102
  3.7 4.1 %collective-permute-start = (bf16[32,1024]{1,0:T(8,128)(2,1)S(1)}, bf16[32,1024]{1,0:T(8,128)(2,1)S(1)}, u32[]{:S(2)}, u32[]{:S(2)}) collective-permute-start(bf16[32,1024]{1,0:T(8,128)(2,1)S(1)} %get-tuple-element.53.refs_0_), channel_id=1, source_target_pairs={{0,16},{4,20},{8,24},{12,28},{16,0},{20,4},{24,8},{28,12},{1,17},{... | collective-permute-start | bytes 196616 | tf_op jit(solution)/shard_map/ppermute | solution.py:28
  7.8 1.5 %collective-permute-start.2 = (bf16[32,2048]{1,0:T(8,128)(2,1)S(1)}, bf16[32,2048]{1,0:T(8,128)(2,1)S(1)}, u32[]{:S(2)}, u32[]{:S(2)}) collective-permute-start(bf16[32,2048]{1,0:T(8,128)(2,1)S(1)} %get-tuple-element.56), channel_id=1, source_target_pairs={{0,4},{4,0},{8,12},{12,8},{16,20},{20,16},{24,28},{28,24},{1,5},{5... | collective-permute-start | bytes 393224 | tf_op jit(solution)/shard_map/ppermute | solution.py:28
  9.3 1.6 %collective-permute-start.3 = (bf16[32,2048]{1,0:T(8,128)(2,1)S(1)}, bf16[32,2048]{1,0:T(8,128)(2,1)S(1)}, u32[]{:S(2)}, u32[]{:S(2)}) collective-permute-start(bf16[32,2048]{1,0:T(8,128)(2,1)S(1)} %get-tuple-element.57), channel_id=1, source_target_pairs={{0,8},{4,12},{8,0},{12,4},{16,24},{20,28},{24,16},{28,20},{1,9},{5... | collective-permute-start | bytes 393224 | tf_op jit(solution)/shard_map/ppermute | solution.py:28
  11.3 1.5 %collective-permute-start.1 = (bf16[32,1024]{1,0:T(8,128)(2,1)S(1)}, bf16[32,1024]{1,0:T(8,128)(2,1)S(1)}, u32[]{:S(2)}, u32[]{:S(2)}) collective-permute-start(bf16[32,1024]{1,0:T(8,128)(2,1)S(1)} %collective-permute-done.refs_4_), channel_id=1, source_target_pairs={{0,4},{4,0},{8,12},{12,8},{16,20},{20,16},{24,28},{28,24},{1,5},{5... | collective-permute-start | bytes 196616 | tf_op jit(solution)/shard_map/ppermute | solution.py:28
  12.8 1.5 %collective-permute-start.6 = (bf16[32,1024]{1,0:T(8,128)(2,1)S(1)}, bf16[32,1024]{1,0:T(8,128)(2,1)S(1)}, u32[]{:S(2)}, u32[]{:S(2)}) collective-permute-start(bf16[32,1024]{1,0:T(8,128)(2,1)S(1)} %collective-permute-done.refs_4_), channel_id=1, source_target_pairs={{0,12},{4,8},{8,4},{12,0},{16,28},{20,24},{24,20},{28,16},{1,13},{... | collective-permute-start | bytes 196616 | tf_op jit(solution)/shard_map/ppermute | solution.py:28
  14.3 4.6 %collective-permute-done.1.refs_5_ = bf16[32,1024]{1,0:T(8,128)(2,1)S(1)} collective-permute-done((bf16[32,1024]{1,0:T(8,128)(2,1)S(1)}, bf16[32,1024]{1,0:T(8,128)(2,1)S(1)}, u32[]{:S(2)}, u32[]{:S(2)}) %collective-permute-start.1) | collective-permute-done | bytes 65568 | tf_op jit(solution)/shard_map/ppermute | solution.py:28
  18.9 1.4 %collective-permute-start.5 = (bf16[32,1024]{1,0:T(8,128)(2,1)S(1)}, bf16[32,1024]{1,0:T(8,128)(2,1)S(1)}, u32[]{:S(2)}, u32[]{:S(2)}) collective-permute-start(bf16[32,1024]{1,0:T(8,128)(2,1)S(1)} %collective-permute-done.refs_4_), channel_id=1, source_target_pairs={{0,8},{4,12},{8,0},{12,4},{16,24},{20,28},{24,16},{28,20},{1,9},{5... | collective-permute-start | bytes 196616 | tf_op jit(solution)/shard_map/ppermute | solution.py:28
  21.0 2.2 %collective-permute-start.7 = (bf16[128,512]{1,0:T(8,128)(2,1)S(1)}, bf16[128,512]{1,0:T(8,128)(2,1)S(1)}, u32[]{:S(2)}, u32[]{:S(2)}) collective-permute-start(bf16[128,512]{1,0:T(8,128)(2,1)S(1)} %get-tuple-element.64), channel_id=1, source_target_pairs={{0,16},{4,20},{8,24},{12,28},{16,0},{20,4},{24,8},{28,12},{1,17},{... | collective-permute-start | bytes 393224 | tf_op jit(solution)/shard_map/ppermute | solution.py:28
  23.3 5.5 %scores.1 = (bf16[256,4096]{1,0:T(8,128)(2,1)S(1)}, bf16[256,4096]{1,0:T(8,128)(2,1)S(1)}, bf16[256,4096]{1,0:T(8,128)(2,1)S(1)}, bf16[256,512]{1,0:T(8,128)(2,1...) custom-call(s32[1]{0:T(128)S(6)} %copy.11.length_ref, ...), custom_call_target="tpu_custom_call" | custom-call | flops 1610612736 | bytes 4194304 | tf_op jit(solution)/shard_map/scores/pallas_call | solution.py:268
  28.8 1.6 %collective-permute-start.8 = (bf16[64,512]{1,0:T(8,128)(2,1)S(1)}, bf16[64,512]{1,0:T(8,128)(2,1)S(1)}, u32[]{:S(2)}, u32[]{:S(2)}) collective-permute-start(bf16[64,512]{1,0:T(8,128)(2,1)S(1)} %get-tuple-element.76), channel_id=1, source_target_pairs={{0,4},{4,0},{8,12},{12,8},{16,20},{20,16},{24,28},{28,24},{1,5},{5... | collective-permute-start | bytes 196616 | tf_op jit(solution)/shard_map/ppermute | solution.py:28
  30.6 1.7 %collective-permute-start.10 = (bf16[64,512]{1,0:T(8,128)(2,1)S(1)}, bf16[64,512]{1,0:T(8,128)(2,1)S(1)}, u32[]{:S(2)}, u32[]{:S(2)}) collective-permute-start(bf16[64,512]{1,0:T(8,128)(2,1)S(1)} %get-tuple-element.78), channel_id=1, source_target_pairs={{0,12},{4,8},{8,4},{12,0},{16,28},{20,24},{24,20},{28,16},{1,13},{... | collective-permute-start | bytes 196616 | tf_op jit(solution)/shard_map/ppermute | solution.py:28
  32.3 2.9 %values.1 = (f32[64,512]{1,0:T(8,128)S(1)}, bf16[64,512]{1,0:T(8,128)(2,1)S(1)}, bf16[64,512]{1,0:T(8,128)(2,1)S(1)}, bf16[64,512]{1,0:T(8,128)(2,1)S(1)}) custom-call(bf16[128,4096]{1,0:T(8,128)(2,1)} %bitcast.11, bf16[256,4096]{1,0:T(8,128)(2,1)S(1)} %get-tuple-element.72.w_ref), custom_call_target="tpu_custom_call" | custom-call | flops 48318384 | bytes 125829 | tf_op jit(solution)/shard_map/values/pallas_call | solution.py:283
  35.8 4.5 %collective-permute-start.11 = (bf16[32,512]{1,0:T(8,128)(2,1)S(1)}, bf16[32,512]{1,0:T(8,128)(2,1)S(1)}, u32[]{:S(2)}, u32[]{:S(2)}) collective-permute-start(bf16[32,512]{1,0:T(8,128)(2,1)S(1)} %get-tuple-element.80), channel_id=1, source_target_pairs={{0,16},{4,20},{8,24},{12,28},{16,0},{20,4},{24,8},{28,12},{1,17},{... | collective-permute-start | bytes 98312 | tf_op jit(solution)/shard_map/ppermute | solution.py:28
  40.4 2.3 %collective-permute-done.11.far_ref = bf16[32,512]{1,0:T(8,128)(2,1)S(1)} collective-permute-done((bf16[32,512]{1,0:T(8,128)(2,1)S(1)}, bf16[32,512]{1,0:T(8,128)(2,1)S(1)}, u32[]{:S(2)}, u32[]{:S(2)}) %collective-permute-start.11) | collective-permute-done | bytes 32800 | tf_op jit(solution)/shard_map/ppermute | solution.py:28
  43.4 2.5 %collective-permute-start.15 = (bf16[32,512]{1,0:T(8,128)(2,1)S(1)}, bf16[32,512]{1,0:T(8,128)(2,1)S(1)}, u32[]{:S(2)}, u32[]{:S(2)}) collective-permute-start(bf16[32,512]{1,0:T(8,128)(2,1)S(1)} %get-tuple-element.88), channel_id=1, source_target_pairs={{0,16},{4,20},{8,24},{12,28},{16,0},{20,4},{24,8},{28,12},{1,17},{... | collective-permute-start | bytes 98312 | tf_op jit(solution)/shard_map/ppermute | solution.py:28
  45.9 1.8 %collective-permute-start.12 = (bf16[96,512]{1,0:T(8,128)(2,1)}, bf16[96,512]{1,0:T(8,128)(2,1)S(1)}, u32[]{:S(2)}, u32[]{:S(2)}) collective-permute-start(bf16[96,512]{1,0:T(8,128)(2,1)} %get-tuple-element.85), channel_id=1, source_target_pairs={{0,12},{4,8},{8,4},{12,0},{16,28},{20,24},{24,20},{28,16},{1,13},{... | collective-permute-start | bytes 294920 | tf_op jit(solution)/shard_map/ppermute | solution.py:28
  47.7 1.7 %collective-permute-start.14 = (bf16[96,512]{1,0:T(8,128)(2,1)}, bf16[96,512]{1,0:T(8,128)(2,1)S(1)}, u32[]{:S(2)}, u32[]{:S(2)}) collective-permute-start(bf16[96,512]{1,0:T(8,128)(2,1)} %get-tuple-element.87), channel_id=1, source_target_pairs={{0,4},{4,0},{8,12},{12,8},{16,20},{20,16},{24,28},{28,24},{1,5},{5... | collective-permute-start | bytes 294920 | tf_op jit(solution)/shard_map/ppermute | solution.py:28
  49.4 1.8 %collective-permute-start.18 = (bf16[32,512]{1,0:T(8,128)(2,1)S(1)}, bf16[32,512]{1,0:T(8,128)(2,1)S(1)}, u32[]{:S(2)}, u32[]{:S(2)}) collective-permute-start(bf16[32,512]{1,0:T(8,128)(2,1)S(1)} %collective-permute-done.15.refs_7_), channel_id=1, source_target_pairs={{0,12},{4,8},{8,4},{12,0},{16,28},{20,24},{24,20},{28,16},{1,13},{... | collective-permute-start | bytes 98312 | tf_op jit(solution)/shard_map/ppermute | solution.py:28
  51.2 3.1 %collective-permute-done.18.refs_6_ = bf16[32,512]{1,0:T(8,128)(2,1)S(1)} collective-permute-done((bf16[32,512]{1,0:T(8,128)(2,1)S(1)}, bf16[32,512]{1,0:T(8,128)(2,1)S(1)}, u32[]{:S(2)}, u32[]{:S(2)}) %collective-permute-start.18) | collective-permute-done | bytes 32800 | tf_op jit(solution)/shard_map/ppermute | solution.py:28
  54.6 1.6 %copy-done.1 = bf16[256,4096]{1,0:T(8,128)(2,1)S(1)} copy-done((bf16[256,4096]{1,0:T(8,128)(2,1)S(1)}, bf16[256,4096]{1,0:T(8,128)(2,1)}, u32[]{:S(2)}) %copy-start.1) | copy-done | bytes 2097176
  56.2 2.6 %output.1 = bf16[128,4096]{1,0:T(8,128)(2,1)} custom-call(bf16[256,4096]{1,0:T(8,128)(2,1)S(1)} %copy-done.1, bf16[256,512]{1,0:T(8,128)(2,1)S(1)} %get-tuple-element.67.head_ref), custom_call_target="tpu_custom_call" | custom-call | flops 48318384 | bytes 125829 | tf_op jit(solution)/shard_map/output/pallas_call | solution.py:296
  60.8 0.9 %copy-done.4 = bf16[96,512]{1,0:T(8,128)(2,1)S(1)} copy-done((bf16[96,512]{1,0:T(8,128)(2,1)S(1)}, bf16[96,512]{1,0:T(8,128)(2,1)}, u32[]{:S(2)}) %copy-start.4) | copy-done | bytes 98328
  61.7 0.8 %copy-done.6 = bf16[32,512]{1,0:T(8,128)(2,1)S(1)} copy-done((bf16[32,512]{1,0:T(8,128)(2,1)S(1)}, bf16[32,512]{1,0:T(8,128)(2,1)}, u32[]{:S(2)}) %copy-start.6) | copy-done | bytes 32792
  62.4 0.8 %copy-done.8 = bf16[32,512]{1,0:T(8,128)(2,1)S(1)} copy-done((bf16[32,512]{1,0:T(8,128)(2,1)S(1)}, bf16[32,512]{1,0:T(8,128)(2,1)}, u32[]{:S(2)}) %copy-start.8) | copy-done | bytes 32792
  63.2 0.8 %copy-done.10 = bf16[32,512]{1,0:T(8,128)(2,1)S(1)} copy-done((bf16[32,512]{1,0:T(8,128)(2,1)S(1)}, bf16[32,512]{1,0:T(8,128)(2,1)}, u32[]{:S(2)}) %copy-start.10) | copy-done | bytes 32792
  63.9 1.0 %weight_terms.1 = (f32[2,128,512]{2,1,0:T(8,128)S(1)}, bf16[2,128,512]{2,1,0:T(8,128)(2,1)}, f32[32,512]{1,0:T(8,128)S(1)}, bf16[32,512]{1,0:T(8,128)(2,1)S(1)}) custom-call(s32[1]{0:T(128)} %bitcast.6.core_ref, bf16[512,256]{1,0:T(8,128)(2,1)S(1)} %turn_visual.1.visual_ref, f32[64,512]{1,0:T(8,128)S(1)} %get-tuple-element.74.value_ref, ...), custom_call_target="tpu_custom_call" | custom-call | tf_op jit(solution)/shard_map/weight_terms/pallas_call | solution.py:408
  64.9 1.7 %collective-permute-done.19.came_ref = bf16[2,128,512]{2,1,0:T(8,128)(2,1)S(1)} collective-permute-done((bf16[2,128,512]{2,1,0:T(8,128)(2,1)}, bf16[2,128,512]{2,1,0:T(8,128)(2,1)S(1)}, u32[]{:S(2)}, u32[]{:S(2)}) %collective-permute-start.19) | collective-permute-done | bytes 262176 | tf_op jit(solution)/shard_map/ppermute | solution.py:28
  66.7 1.6 %collective-permute-start.20 = (bf16[1,128,512]{2,1,0:T(8,128)(2,1)S(1)}, bf16[1,128,512]{2,1,0:T(8,128)(2,1)S(1)}, u32[]{:S(2)}, u32[]{:S(2)}) collective-permute-start(bf16[1,128,512]{2,1,0:T(8,128)(2,1)S(1)} %get-tuple-element.91), channel_id=1, source_target_pairs={{0,2},{1,3},{2,0},{3,1},{4,6},{5,7},{6,4},{7,5},{8,10},{9,11},{10,... | collective-permute-start | bytes 393224 | tf_op jit(solution)/shard_map/ppermute | solution.py:28
  68.3 1.1 %collective-permute-start.21 = (bf16[32,512]{1,0:T(8,128)(2,1)S(1)}, bf16[32,512]{1,0:T(8,128)(2,1)S(1)}, u32[]{:S(2)}, u32[]{:S(2)}) collective-permute-start(bf16[32,512]{1,0:T(8,128)(2,1)S(1)} %get-tuple-element.92), channel_id=1, source_target_pairs={{0,16},{4,20},{8,24},{12,28},{16,0},{20,4},{24,8},{28,12},{1,17},{... | collective-permute-start | bytes 98312 | tf_op jit(solution)/shard_map/ppermute | solution.py:28
  69.4 2.6 %query_grad.1 = bf16[128,4096]{1,0:T(8,128)(2,1)} custom-call(bf16[256,4096]{1,0:T(8,128)(2,1)S(1)} %get-tuple-element.93.inner_ref, bf16[256,512]{1,0:T(8,128)(2,1)S(1)} %get-tuple-element.94.head_ref), custom_call_target="tpu_custom_call" | custom-call | flops 48318384 | bytes 125829 | tf_op jit(solution)/shard_map/query_grad/pallas_call | solution.py:296
  71.9 1.2 %collective-permute-done.21.far_ref = bf16[32,512]{1,0:T(8,128)(2,1)S(1)} collective-permute-done((bf16[32,512]{1,0:T(8,128)(2,1)S(1)}, bf16[32,512]{1,0:T(8,128)(2,1)S(1)}, u32[]{:S(2)}, u32[]{:S(2)}) %collective-permute-start.21) | collective-permute-done | bytes 32800 | tf_op jit(solution)/shard_map/ppermute | solution.py:28
  (51 shorter events, 5.9 us)
Async XLA Ops:
  0.6 22.6 %copy-start.2 = (bf16[1,128,4096]{2,1,0:T(8,128)(2,1)S(1)}, bf16[1,128,4096]{2,1,0:T(8,128)(2,1)}, u32[]{:S(2)}) copy-start(bf16[1,128,4096]{2,1,0:T(8,128)(2,1)} %param.11) | copy-start | bytes 3145732
  0.6 22.6 %copy-start.11 = (bf16[1,128,4096]{2,1,0:T(8,128)(2,1)S(1)}, bf16[1,128,4096]{2,1,0:T(8,128)(2,1)}, u32[]{:S(2)}) copy-start(bf16[1,128,4096]{2,1,0:T(8,128)(2,1)} %param.10) | copy-start | bytes 3145732
  0.7 22.6 %copy-start.12 = (s32[1,8]{1,0:T(1,128)S(1)}, s32[1,8]{1,0:T(1,128)}, u32[]{:S(2)}) copy-start(s32[1,8]{1,0:T(1,128)} %frame_ref.1) | copy-start | bytes 100
  3.7 7.6 %collective-permute-start = (bf16[32,1024]{1,0:T(8,128)(2,1)S(1)}, bf16[32,1024]{1,0:T(8,128)(2,1)S(1)}, u32[]{:S(2)}, u32[]{:S(2)}) collective-permute-start(bf16[32,1024]{1,0:T(8,128)(2,1)S(1)} %get-tuple-element.53.refs_0_), channel_id=1, source_target_pairs={{0,16},{4,20},{8,24},{12,28},{16,0},{20,4},{24,8},{28,12},{1,17},{... | collective-permute-start | bytes 196616 | tf_op jit(solution)/shard_map/ppermute | solution.py:28
  7.8 13.2 %collective-permute-start.2 = (bf16[32,2048]{1,0:T(8,128)(2,1)S(1)}, bf16[32,2048]{1,0:T(8,128)(2,1)S(1)}, u32[]{:S(2)}, u32[]{:S(2)}) collective-permute-start(bf16[32,2048]{1,0:T(8,128)(2,1)S(1)} %get-tuple-element.56), channel_id=1, source_target_pairs={{0,4},{4,0},{8,12},{12,8},{16,20},{20,16},{24,28},{28,24},{1,5},{5... | collective-permute-start | bytes 393224 | tf_op jit(solution)/shard_map/ppermute | solution.py:28
  9.3 11.7 %collective-permute-start.3 = (bf16[32,2048]{1,0:T(8,128)(2,1)S(1)}, bf16[32,2048]{1,0:T(8,128)(2,1)S(1)}, u32[]{:S(2)}, u32[]{:S(2)}) collective-permute-start(bf16[32,2048]{1,0:T(8,128)(2,1)S(1)} %get-tuple-element.57), channel_id=1, source_target_pairs={{0,8},{4,12},{8,0},{12,4},{16,24},{20,28},{24,16},{28,20},{1,9},{5... | collective-permute-start | bytes 393224 | tf_op jit(solution)/shard_map/ppermute | solution.py:28
  10.9 10.1 %collective-permute-start.4 = (bf16[32,2048]{1,0:T(8,128)(2,1)S(1)}, bf16[32,2048]{1,0:T(8,128)(2,1)S(1)}, u32[]{:S(2)}, u32[]{:S(2)}) collective-permute-start(bf16[32,2048]{1,0:T(8,128)(2,1)S(1)} %get-tuple-element.58), channel_id=1, source_target_pairs={{0,12},{4,8},{8,4},{12,0},{16,28},{20,24},{24,20},{28,16},{1,13},{... | collective-permute-start | bytes 393224 | tf_op jit(solution)/shard_map/ppermute | solution.py:28
  11.3 7.6 %collective-permute-start.1 = (bf16[32,1024]{1,0:T(8,128)(2,1)S(1)}, bf16[32,1024]{1,0:T(8,128)(2,1)S(1)}, u32[]{:S(2)}, u32[]{:S(2)}) collective-permute-start(bf16[32,1024]{1,0:T(8,128)(2,1)S(1)} %collective-permute-done.refs_4_), channel_id=1, source_target_pairs={{0,4},{4,0},{8,12},{12,8},{16,20},{20,16},{24,28},{28,24},{1,5},{5... | collective-permute-start | bytes 196616 | tf_op jit(solution)/shard_map/ppermute | solution.py:28
  12.8 10.4 %collective-permute-start.6 = (bf16[32,1024]{1,0:T(8,128)(2,1)S(1)}, bf16[32,1024]{1,0:T(8,128)(2,1)S(1)}, u32[]{:S(2)}, u32[]{:S(2)}) collective-permute-start(bf16[32,1024]{1,0:T(8,128)(2,1)S(1)} %collective-permute-done.refs_4_), channel_id=1, source_target_pairs={{0,12},{4,8},{8,4},{12,0},{16,28},{20,24},{24,20},{28,16},{1,13},{... | collective-permute-start | bytes 196616 | tf_op jit(solution)/shard_map/ppermute | solution.py:28
  18.9 4.3 %collective-permute-start.5 = (bf16[32,1024]{1,0:T(8,128)(2,1)S(1)}, bf16[32,1024]{1,0:T(8,128)(2,1)S(1)}, u32[]{:S(2)}, u32[]{:S(2)}) collective-permute-start(bf16[32,1024]{1,0:T(8,128)(2,1)S(1)} %collective-permute-done.refs_4_), channel_id=1, source_target_pairs={{0,8},{4,12},{8,0},{12,4},{16,24},{20,28},{24,16},{28,20},{1,9},{5... | collective-permute-start | bytes 196616 | tf_op jit(solution)/shard_map/ppermute | solution.py:28
  21.0 7.7 %collective-permute-start.7 = (bf16[128,512]{1,0:T(8,128)(2,1)S(1)}, bf16[128,512]{1,0:T(8,128)(2,1)S(1)}, u32[]{:S(2)}, u32[]{:S(2)}) collective-permute-start(bf16[128,512]{1,0:T(8,128)(2,1)S(1)} %get-tuple-element.64), channel_id=1, source_target_pairs={{0,16},{4,20},{8,24},{12,28},{16,0},{20,4},{24,8},{28,12},{1,17},{... | collective-permute-start | bytes 393224 | tf_op jit(solution)/shard_map/ppermute | solution.py:28
  28.7 6.4 %copy-start = (bf16[256,4096]{1,0:T(8,128)(2,1)}, bf16[256,4096]{1,0:T(8,128)(2,1)S(1)}, u32[]{:S(2)}) copy-start(bf16[256,4096]{1,0:T(8,128)(2,1)S(1)} %get-tuple-element.66.inner_ref) | copy-start | bytes 6291460
  28.8 6.4 %collective-permute-start.8 = (bf16[64,512]{1,0:T(8,128)(2,1)S(1)}, bf16[64,512]{1,0:T(8,128)(2,1)S(1)}, u32[]{:S(2)}, u32[]{:S(2)}) collective-permute-start(bf16[64,512]{1,0:T(8,128)(2,1)S(1)} %get-tuple-element.76), channel_id=1, source_target_pairs={{0,4},{4,0},{8,12},{12,8},{16,20},{20,16},{24,28},{28,24},{1,5},{5... | collective-permute-start | bytes 196616 | tf_op jit(solution)/shard_map/ppermute | solution.py:28
  30.4 4.8 %collective-permute-start.9 = (bf16[64,512]{1,0:T(8,128)(2,1)S(1)}, bf16[64,512]{1,0:T(8,128)(2,1)S(1)}, u32[]{:S(2)}, u32[]{:S(2)}) collective-permute-start(bf16[64,512]{1,0:T(8,128)(2,1)S(1)} %get-tuple-element.77), channel_id=1, source_target_pairs={{0,8},{4,12},{8,0},{12,4},{16,24},{20,28},{24,16},{28,20},{1,9},{5... | collective-permute-start | bytes 196616 | tf_op jit(solution)/shard_map/ppermute | solution.py:28
  30.6 5.2 %collective-permute-start.10 = (bf16[64,512]{1,0:T(8,128)(2,1)S(1)}, bf16[64,512]{1,0:T(8,128)(2,1)S(1)}, u32[]{:S(2)}, u32[]{:S(2)}) collective-permute-start(bf16[64,512]{1,0:T(8,128)(2,1)S(1)} %get-tuple-element.78), channel_id=1, source_target_pairs={{0,12},{4,8},{8,4},{12,0},{16,28},{20,24},{24,20},{28,16},{1,13},{... | collective-permute-start | bytes 196616 | tf_op jit(solution)/shard_map/ppermute | solution.py:28
  35.8 6.8 %collective-permute-start.11 = (bf16[32,512]{1,0:T(8,128)(2,1)S(1)}, bf16[32,512]{1,0:T(8,128)(2,1)S(1)}, u32[]{:S(2)}, u32[]{:S(2)}) collective-permute-start(bf16[32,512]{1,0:T(8,128)(2,1)S(1)} %get-tuple-element.80), channel_id=1, source_target_pairs={{0,16},{4,20},{8,24},{12,28},{16,0},{20,4},{24,8},{28,12},{1,17},{... | collective-permute-start | bytes 98312 | tf_op jit(solution)/shard_map/ppermute | solution.py:28
  43.4 6.0 %collective-permute-start.15 = (bf16[32,512]{1,0:T(8,128)(2,1)S(1)}, bf16[32,512]{1,0:T(8,128)(2,1)S(1)}, u32[]{:S(2)}, u32[]{:S(2)}) collective-permute-start(bf16[32,512]{1,0:T(8,128)(2,1)S(1)} %get-tuple-element.88), channel_id=1, source_target_pairs={{0,16},{4,20},{8,24},{12,28},{16,0},{20,4},{24,8},{28,12},{1,17},{... | collective-permute-start | bytes 98312 | tf_op jit(solution)/shard_map/ppermute | solution.py:28
  45.9 14.2 %collective-permute-start.12 = (bf16[96,512]{1,0:T(8,128)(2,1)}, bf16[96,512]{1,0:T(8,128)(2,1)S(1)}, u32[]{:S(2)}, u32[]{:S(2)}) collective-permute-start(bf16[96,512]{1,0:T(8,128)(2,1)} %get-tuple-element.85), channel_id=1, source_target_pairs={{0,12},{4,8},{8,4},{12,0},{16,28},{20,24},{24,20},{28,16},{1,13},{... | collective-permute-start | bytes 294920 | tf_op jit(solution)/shard_map/ppermute | solution.py:28
  47.7 12.4 %collective-permute-start.13 = (bf16[96,512]{1,0:T(8,128)(2,1)}, bf16[96,512]{1,0:T(8,128)(2,1)S(1)}, u32[]{:S(2)}, u32[]{:S(2)}) collective-permute-start(bf16[96,512]{1,0:T(8,128)(2,1)} %get-tuple-element.86), channel_id=1, source_target_pairs={{0,8},{4,12},{8,0},{12,4},{16,24},{20,28},{24,16},{28,20},{1,9},{5... | collective-permute-start | bytes 294920 | tf_op jit(solution)/shard_map/ppermute | solution.py:28
  47.7 12.4 %collective-permute-start.14 = (bf16[96,512]{1,0:T(8,128)(2,1)}, bf16[96,512]{1,0:T(8,128)(2,1)S(1)}, u32[]{:S(2)}, u32[]{:S(2)}) collective-permute-start(bf16[96,512]{1,0:T(8,128)(2,1)} %get-tuple-element.87), channel_id=1, source_target_pairs={{0,4},{4,0},{8,12},{12,8},{16,20},{20,16},{24,28},{28,24},{1,5},{5... | collective-permute-start | bytes 294920 | tf_op jit(solution)/shard_map/ppermute | solution.py:28
  49.4 4.8 %collective-permute-start.18 = (bf16[32,512]{1,0:T(8,128)(2,1)S(1)}, bf16[32,512]{1,0:T(8,128)(2,1)S(1)}, u32[]{:S(2)}, u32[]{:S(2)}) collective-permute-start(bf16[32,512]{1,0:T(8,128)(2,1)S(1)} %collective-permute-done.15.refs_7_), channel_id=1, source_target_pairs={{0,12},{4,8},{8,4},{12,0},{16,28},{20,24},{24,20},{28,16},{1,13},{... | collective-permute-start | bytes 98312 | tf_op jit(solution)/shard_map/ppermute | solution.py:28
  51.2 7.7 %collective-permute-start.17 = (bf16[32,512]{1,0:T(8,128)(2,1)S(1)}, bf16[32,512]{1,0:T(8,128)(2,1)S(1)}, u32[]{:S(2)}, u32[]{:S(2)}) collective-permute-start(bf16[32,512]{1,0:T(8,128)(2,1)S(1)} %collective-permute-done.15.refs_7_), channel_id=1, source_target_pairs={{0,8},{4,12},{8,0},{12,4},{16,24},{20,28},{24,16},{28,20},{1,9},{5... | collective-permute-start | bytes 98312 | tf_op jit(solution)/shard_map/ppermute | solution.py:28
  54.2 6.5 %copy-start.5 = (bf16[32,512]{1,0:T(8,128)(2,1)}, bf16[32,512]{1,0:T(8,128)(2,1)S(1)}, u32[]{:S(2)}) copy-start(bf16[32,512]{1,0:T(8,128)(2,1)S(1)} %collective-permute-done.18.refs_6_) | copy-start | bytes 98308
  54.2 5.3 %collective-permute-start.16 = (bf16[32,512]{1,0:T(8,128)(2,1)S(1)}, bf16[32,512]{1,0:T(8,128)(2,1)S(1)}, u32[]{:S(2)}, u32[]{:S(2)}) collective-permute-start(bf16[32,512]{1,0:T(8,128)(2,1)S(1)} %collective-permute-done.15.refs_7_), channel_id=1, source_target_pairs={{0,4},{4,0},{8,12},{12,8},{16,20},{20,16},{24,28},{28,24},{1,5},{5... | collective-permute-start | bytes 98312 | tf_op jit(solution)/shard_map/ppermute | solution.py:28
  54.6 1.6 %copy-start.1 = (bf16[256,4096]{1,0:T(8,128)(2,1)S(1)}, bf16[256,4096]{1,0:T(8,128)(2,1)}, u32[]{:S(2)}) copy-start(bf16[256,4096]{1,0:T(8,128)(2,1)} %copy-done) | copy-start | bytes 6291460
  60.8 0.9 %copy-start.4 = (bf16[96,512]{1,0:T(8,128)(2,1)S(1)}, bf16[96,512]{1,0:T(8,128)(2,1)}, u32[]{:S(2)}) copy-start(bf16[96,512]{1,0:T(8,128)(2,1)} %copy-done.3) | copy-start | bytes 294916
  61.7 0.8 %copy-start.6 = (bf16[32,512]{1,0:T(8,128)(2,1)S(1)}, bf16[32,512]{1,0:T(8,128)(2,1)}, u32[]{:S(2)}) copy-start(bf16[32,512]{1,0:T(8,128)(2,1)} %copy-done.5) | copy-start | bytes 98308
  62.4 0.8 %copy-start.8 = (bf16[32,512]{1,0:T(8,128)(2,1)S(1)}, bf16[32,512]{1,0:T(8,128)(2,1)}, u32[]{:S(2)}) copy-start(bf16[32,512]{1,0:T(8,128)(2,1)} %copy-done.7) | copy-start | bytes 98308
  63.2 0.8 %copy-start.10 = (bf16[32,512]{1,0:T(8,128)(2,1)S(1)}, bf16[32,512]{1,0:T(8,128)(2,1)}, u32[]{:S(2)}) copy-start(bf16[32,512]{1,0:T(8,128)(2,1)} %copy-done.9) | copy-start | bytes 98308
  64.9 1.7 %collective-permute-start.19 = (bf16[2,128,512]{2,1,0:T(8,128)(2,1)}, bf16[2,128,512]{2,1,0:T(8,128)(2,1)S(1)}, u32[]{:S(2)}, u32[]{:S(2)}) collective-permute-start(bf16[2,128,512]{2,1,0:T(8,128)(2,1)} %get-tuple-element.90), channel_id=1, source_target_pairs={{0,1},{1,0},{2,3},{3,2},{4,5},{5,4},{6,7},{7,6},{8,9},{9,8},{10,11... | collective-permute-start | bytes 786440 | tf_op jit(solution)/shard_map/ppermute | solution.py:28
  66.7 7.0 %collective-permute-start.20 = (bf16[1,128,512]{2,1,0:T(8,128)(2,1)S(1)}, bf16[1,128,512]{2,1,0:T(8,128)(2,1)S(1)}, u32[]{:S(2)}, u32[]{:S(2)}) collective-permute-start(bf16[1,128,512]{2,1,0:T(8,128)(2,1)S(1)} %get-tuple-element.91), channel_id=1, source_target_pairs={{0,2},{1,3},{2,0},{3,1},{4,6},{5,7},{6,4},{7,5},{8,10},{9,11},{10,... | collective-permute-start | bytes 393224 | tf_op jit(solution)/shard_map/ppermute | solution.py:28
  68.3 4.8 %collective-permute-start.21 = (bf16[32,512]{1,0:T(8,128)(2,1)S(1)}, bf16[32,512]{1,0:T(8,128)(2,1)S(1)}, u32[]{:S(2)}, u32[]{:S(2)}) collective-permute-start(bf16[32,512]{1,0:T(8,128)(2,1)S(1)} %get-tuple-element.92), channel_id=1, source_target_pairs={{0,16},{4,20},{8,24},{12,28},{16,0},{20,4},{24,8},{28,12},{1,17},{... | collective-permute-start | bytes 98312 | tf_op jit(solution)/shard_map/ppermute | solution.py:28
  (3 other events, 1.9 us)

commit v11 on v10

--- a/solution.py
+++ b/solution.py
@@ -32,14 +32,15 @@
     return pltpu.with_memory_space_constraint(x, pltpu.HBM)
 
 
-def gather(own, near=None):
+def gather(own, near=None, onward=None):
     blocks = lax.axis_size("blk")
     half = blocks // 2
     masks = range(half - 1, 0, -1)
-    pieces = {half: swap(own, "blk", half)}
+    far = swap(own, "blk", half)
+    pieces = {0: own, half: far}
     pieces.update({m: swap(near[m - 1] if near else own, "blk", m) for m in masks})
-    pieces.update({m + half: swap(pieces[half], "blk", m) for m in masks})
-    pieces[0] = own
+    sent = onward(far) if onward else [far] * (half - 1)
+    pieces.update({m + half: swap(sent[m - 1], "blk", m) for m in masks})
     return [pieces[m] for m in range(blocks)]
 
 
@@ -49,8 +50,7 @@
 
 def project_kernel(streams, visual_ref, *refs):
     weight_refs, value_ref = refs[:streams], refs[streams]
-    out_ref, own_ref, near_refs = refs[streams + 1], refs[streams + 2], refs[streams + 3 : -1]
-    acc_ref = refs[-1]
+    out_ref, near_ref, far_ref, acc_ref = refs[streams + 1 :]
     step = pl.program_id(0)
     slab = weight_refs[0].shape[0]
     part = 0.0
@@ -62,17 +62,12 @@
     def _():
         acc_ref[...] = part
         block = lax.axis_index("blk")
-        half = len(near_refs) + 1
-        rows, width = visual_ref.shape[0], own_ref.shape[1]
-        for m in range(half):
-            for side in range(2):
+        rows, width = visual_ref.shape[0], near_ref.shape[1]
+        half = near_ref.shape[0] // rows
+        for side, ref in enumerate((near_ref, far_ref)):
+            for m in range(half):
                 start = pl.multiple_of((block ^ (m + side * half)) * width, HEAD_SIZE)
-                columns = visual_ref[:, pl.ds(start, width)]
-                if m == 0:
-                    own_ref[side * rows : (side + 1) * rows, :] = columns
-                else:
-                    first = out_ref.shape[1] + side * width
-                    near_refs[m - 1][:, first : first + width] = columns
+                ref[m * rows : (m + 1) * rows, :] = visual_ref[:, pl.ds(start, width)]
 
     @pl.when(step > 0)
     def _():
@@ -81,10 +76,8 @@
     @pl.when(step == pl.num_programs(0) - 1)
     def _():
         columns = acc_ref.shape[1]
-        keys = acc_ref[...].astype(BF16)
-        for ref in (out_ref, *near_refs):
-            ref[:, :columns] = keys
-            ref[:, columns : out_ref.shape[1]] = value_ref[...]
+        out_ref[:, :columns] = acc_ref[...].astype(BF16)
+        out_ref[:, columns:] = value_ref[...]
 
 
 def project(blocks, visual, key_weight, value):
@@ -92,9 +85,8 @@
     columns = key_weight.shape[1]
     steps, streams = 2, 4
     slab = features // (steps * streams)
-    width = features // blocks
     out = (rows, columns + value.shape[1])
-    shapes = [out, (2 * rows, width)] + [(rows, out[1] + 2 * width)] * (blocks // 2 - 1)
+    half = (blocks // 2 * rows, features // blocks)
 
     def whole(shape):
         return pl.BlockSpec(shape, lambda k: (0, 0))
@@ -108,8 +100,8 @@
             for p in range(streams)
         ]
         + [whole(value.shape)],
-        out_specs=[whole(shape) for shape in shapes],
-        out_shape=[jax.ShapeDtypeStruct(shape, BF16) for shape in shapes],
+        out_specs=[whole(out)] + [whole(half)] * 2,
+        out_shape=[jax.ShapeDtypeStruct(out, BF16)] + [jax.ShapeDtypeStruct(half, BF16)] * 2,
         scratch_shapes=[pltpu.VMEM((rows, columns), F32)],
         cost_estimate=pl.CostEstimate(
             flops=2 * rows * features * columns,
@@ -119,7 +111,7 @@
         compiler_params=pltpu.CompilerParams(vmem_limit_bytes=32 * MIB),
         name="project",
     )(in_hbm(visual), *[in_hbm(key_weight)] * streams, in_hbm(value))
-    return out[0], out[1], out[2:]
+    return out
 
 
 def head_pair(ref, rows, start):
@@ -152,7 +144,7 @@
     for m in range(pieces):
         part = slice(m * rows, (m + 1) * rows)
         k_ref[part, :] = kv_refs[m][:, :width]
-        v_ref[part, :] = kv_refs[m][:, width : 2 * width]
+        v_ref[part, :] = kv_refs[m][:, width:]
     row = lax.broadcasted_iota(jnp.int32, (rows, pair), 0)
     for i in range(tiles):
         text = slice(i * TILE, (i + 1) * TILE)
@@ -282,7 +274,7 @@
     def values(self, gradients, weights):
         out = self.call(
             values_kernel,
-            0.03,
+            0.1,
             "values",
             grid=(KEY_HEADS, self.tiles),
             in_specs=[self.text_block, self.inner_block],
@@ -295,7 +287,7 @@
     def over_rows(self, inner, heads, name):
         return self.call(
             rows_kernel,
-            0.03,
+            0.1,
             name,
             grid=(KEY_HEADS, self.tiles),
             in_specs=[self.inner_block, self.head_block],
@@ -330,64 +322,74 @@
     return in_vmem(sum_kernel, name, [(half, F32), (half, BF16)], own, *came)
 
 
-def add_kernel(near_ref, far_ref, *refs):
-    value_refs, (own_ref, again_ref), near_refs = (
-        refs[: len(refs) // 2 - 1],
-        refs[len(refs) // 2 - 1 : len(refs) // 2 + 1],
-        refs[len(refs) // 2 + 1 :],
-    )
-    rows = own_ref.shape[0]
+def add_kernel(near_ref, far_ref, visual_ref, came_ref, own_ref, again_ref, sides_ref, *near_refs):
+    rows, columns = own_ref.shape
+    width = visual_ref.shape[1]
     total = (near_ref[...] + far_ref[...].astype(F32)).astype(BF16)
     own_ref[...] = total
     again_ref[...] = total
-    for ref, value_ref in zip(near_refs, value_refs):
-        ref[:rows, :] = total
-        ref[rows:, :] = value_ref[...]
-
-
-def add_far(near, far, values):
-    rows, width = far.shape
-    more = [((rows + v.shape[0], width), BF16) for v in values]
-    out = in_vmem(add_kernel, "key_grad", [(far.shape, BF16)] * 2 + more, near, far, *values)
-    return out[0], out[1], out[2:]
+    sides_ref[:rows, :] = visual_ref[:rows, :]
+    sides_ref[rows:, :] = came_ref[:rows, :]
+    for m, ref in enumerate(near_refs, 1):
+        part = slice(m * rows, (m + 1) * rows)
+        ref[:, :columns] = total
+        ref[:, columns : columns + width] = visual_ref[part, :]
+        ref[:, columns + width :] = came_ref[part, :]
+
+
+def add_far(near, far, visual_near, visual_came):
+    rows, columns = far.shape
+    width = visual_near.shape[1]
+    shapes = [(far.shape, BF16)] * 2 + [((2 * rows, width), BF16)]
+    shapes += [((rows, columns + 2 * width), BF16)] * (visual_near.shape[0] // rows - 1)
+    out = in_vmem(add_kernel, "key_grad", shapes, near, far, visual_near, visual_came)
+    return out[0], out[1], out[2], out[3:]
+
+
+def onward_kernel(far_ref, *refs):
+    value_refs, out_refs = refs[: len(refs) // 2], refs[len(refs) // 2 :]
+    rows, columns = far_ref.shape
+    for value_ref, ref in zip(value_refs, out_refs):
+        ref[:, :columns] = far_ref[...]
+        ref[:, columns : 2 * columns] = value_ref[:rows, :]
+        ref[:, 2 * columns :] = value_ref[rows:, :]
+
+
+def onward(far, values):
+    shape = (far.shape[0], 3 * far.shape[1])
+    return in_vmem(onward_kernel, "onward", [(shape, BF16)] * len(values), far, *values)
 
 
 def add_value_kernel(near_ref, far_ref, out_ref):
     out_ref[...] = (near_ref[...] + far_ref[...].astype(F32)).astype(BF16)
 
 
-def pack_kernel(own_ref, *refs):
-    came_refs, out_refs = refs[:-2], refs[-2:]
+def turn_kernel(columns, own_ref, *refs):
+    came_refs, out_ref = refs[:-1], refs[-1]
     rows, width = own_ref.shape[0] // 2, own_ref.shape[1]
-    for side, ref in enumerate(out_refs):
-        ref[:rows, :] = own_ref[side * rows : (side + 1) * rows, :]
-        for m, came_ref in enumerate(came_refs, 1):
-            first = came_ref.shape[1] - (2 - side) * width
-            ref[m * rows : (m + 1) * rows, :] = came_ref[:, first : first + width]
-
-
-def pack(own, came):
-    half = ((1 + len(came)) * own.shape[0] // 2, own.shape[1])
-    return in_vmem(pack_kernel, "pack_visual", [(half, BF16)] * 2, own, *came)
-
-
-def turn_kernel(near_ref, far_ref, out_ref):
-    out_ref[...] = jnp.concatenate([near_ref[...], far_ref[...]], axis=0).T
-
-
-def turn(near, far):
-    shape = (near.shape[1], 2 * near.shape[0])
-    return in_vmem(turn_kernel, "turn_visual", [(shape, BF16)], near, far)[0]
-
-
-def weight_kernel(order, core_ref, visual_ref, value_ref, *refs):
+    parts = []
+    for side in range(2):
+        parts.append(own_ref[side * rows : (side + 1) * rows, :])
+        first = columns + side * width
+        parts += [ref[:, first : first + width] for ref in came_refs]
+    out_ref[...] = jnp.concatenate(parts, axis=0).T
+
+
+def turn(columns, own, came):
+    rows, width = own.shape
+    shape = (width, (1 + len(came)) * rows)
+    kernel = functools.partial(turn_kernel, columns)
+    return in_vmem(kernel, "turn_visual", [(shape, BF16)], own, *came)[0]
+
+
+def weight_kernel(order, visual_ref, value_ref, *refs):
     pieces = len(order)
     kg_refs = [refs[order.index(m)] for m in range(pieces)]
     keep_ref, send_ref, near_ref, far_ref = refs[pieces:]
-    rows = near_ref.shape[0]
-    product = dot(visual_ref[...], jnp.concatenate([r[:rows, :] for r in kg_refs], axis=0))
+    rows, width = near_ref.shape
+    product = dot(visual_ref[...], jnp.concatenate([r[:, :width] for r in kg_refs], axis=0))
     count, share, _ = keep_ref.shape
-    core = core_ref[0] == 0
+    core = lax.axis_index("dp") % 2 == 0
     for n in range(count):
         even = product[2 * n * share : (2 * n + 1) * share]
         odd = product[(2 * n + 1) * share : (2 * n + 2) * share]
@@ -395,33 +397,24 @@
         send_ref[n] = jnp.where(core, odd, even).astype(BF16)
     for side, ref in enumerate((near_ref, far_ref)):
         total = value_ref[side * rows : (side + 1) * rows, :]
-        for kg_ref in kg_refs[1 : pieces // 2]:
-            total += kg_ref[(1 + side) * rows : (2 + side) * rows, :].astype(F32)
+        for kg_ref in kg_refs[pieces // 2 + 1 :]:
+            total += kg_ref[:, (1 + side) * width : (2 + side) * width].astype(F32)
         ref[...] = total.astype(ref.dtype)
 
 
-def weight_terms(samples, core, visual, value_own, key_grads):
+def weight_terms(samples, visual, value_own, key_grads):
     rows, width = key_grads[0].shape
-    half = (samples // 2, visual.shape[0] // samples, width)
     middle = len(key_grads) // 2
-    order = [0, *range(middle - 1, 0, -1), *range(middle + 1, 2 * middle), middle]
-    return pl.pallas_call(
-        functools.partial(weight_kernel, order),
-        in_specs=[pl.BlockSpec(memory_space=pltpu.SMEM)] + [VMEM] * (2 + len(key_grads)),
-        out_specs=[VMEM] * 4,
-        out_shape=[
-            jax.ShapeDtypeStruct(half, F32),
-            jax.ShapeDtypeStruct(half, BF16),
-            jax.ShapeDtypeStruct((rows, width), F32),
-            jax.ShapeDtypeStruct((rows, width), BF16),
-        ],
-        compiler_params=pltpu.CompilerParams(vmem_limit_bytes=32 * MIB),
-        name="weight_terms",
-    )(core, visual, value_own, *[key_grads[m] for m in order])
-
-
-def halve_kernel(bit_ref, kept_ref, came_ref, keep_ref, send_ref):
-    low = bit_ref[0] == 0
+    order = [0, *range(middle + 1, 2 * middle), *range(middle - 1, 0, -1), middle]
+    half = ((samples // 2, visual.shape[0] // samples, width), F32)
+    shapes = [half, (half[0], BF16), ((rows, width), F32), ((rows, width), BF16)]
+    kernel = functools.partial(weight_kernel, order)
+    ordered = [key_grads[m] for m in order]
+    return in_vmem(kernel, "weight_terms", shapes, visual, value_own, *ordered)
+
+
+def halve_kernel(bit, kept_ref, came_ref, keep_ref, send_ref):
+    low = (lax.axis_index("dp") >> bit) % 2 == 0
     for n in range(keep_ref.shape[0]):
         even = kept_ref[2 * n] + came_ref[2 * n].astype(F32)
         odd = kept_ref[2 * n + 1] + came_ref[2 * n + 1].astype(F32)
@@ -431,26 +424,17 @@
 
 def halve(bit, kept, came):
     half = (kept.shape[0] // 2, *kept.shape[1:])
-    return pl.pallas_call(
-        halve_kernel,
-        in_specs=[pl.BlockSpec(memory_space=pltpu.SMEM), VMEM, VMEM],
-        out_specs=[VMEM] * 2,
-        out_shape=[jax.ShapeDtypeStruct(half, F32), jax.ShapeDtypeStruct(half, BF16)],
-        compiler_params=pltpu.CompilerParams(vmem_limit_bytes=32 * MIB),
-        name="halve",
-    )(bit, kept, came)
+    kernel = functools.partial(halve_kernel, bit)
+    return in_vmem(kernel, "halve", [(half, F32), (half, BF16)], kept, came)
 
 
 def local(visual_rows, value_matrix, key_weight, queries, output_gradient, visual_len, frame_end):
     tie = lax.optimization_barrier
     blocks, samples = lax.axis_size("blk"), lax.axis_size("dp")
-    sample = lax.axis_index("dp").astype(jnp.int32)
     visual, half = visual_rows[0], blocks // 2
 
-    own, visual_own, near = project(blocks, visual, key_weight, value_matrix[0])
-    keys_values = gather(own, near)
-    keys_values[half + 1], visual_own = tie((keys_values[half + 1], visual_own))
-    visual_near, visual_far = pack(visual_own, keys_values[1:half])
+    own, visual_near, visual_far = project(blocks, visual, key_weight, value_matrix[0])
+    keys_values = gather(own)
     visual_far = swap(visual_far, "blk", half)
     attention = Attention(queries[0], blocks, visual.shape[0])
     inner, key_own, key_near = attention.scores(
@@ -463,26 +447,26 @@
     value_own, value_near = attention.values(output_gradient[0], weights)
     key_own, value_own = tie((key_own, value_own))
     key_sum, key_far = near_sums(key_own, key_near, "key_sums")
+    key_sum, dscores = tie((key_sum, dscores))
     key_far = swap(key_far, "blk", half)
-    key_grad, key_again, near = add_far(key_sum, key_far, value_near)
-    key_grads = gather(key_grad, near)
+    query_grad = attention.over_rows(dscores, keys, "query_grad")
+    key_sum, query_grad = tie((key_sum, query_grad))
+    key_grad, key_again, visual_own, near = add_far(key_sum, key_far, visual_near, visual_far)
+
+    key_grads = gather(key_grad, near, lambda far: onward(far, value_near))
     key_grads[0] = key_again
-    visual_columns = turn(visual_near, visual_far)
     attn_out = attention.over_rows(again, values, "output")
-    visual_columns, attn_out, dscores = tie((visual_columns, attn_out, dscores))
-    kept, sent, value_sum, value_far = weight_terms(
-        samples, (sample % 2)[None], visual_columns, value_own, key_grads
-    )
+    visual_columns = turn(key_grad.shape[1], visual_own, key_grads[1:half])
+    visual_columns, attn_out = tie((visual_columns, attn_out))
+    kept, sent, value_sum, value_far = weight_terms(samples, visual_columns, value_own, key_grads)
     value_far = swap(value_far, "blk", half)
-    query_grad = attention.over_rows(dscores, keys, "query_grad")
     came, bit = swap(sent, "dp", 1), 1
     while kept.shape[0] > 1:
-        kept, sent = halve(((sample >> bit) % 2)[None], kept, came)
+        kept, sent = halve(bit, kept, came)
         came, bit = swap(sent, "dp", 1 << bit), bit + 1
-    value_far, query_grad = tie((value_far, query_grad))
     shape = [(value_far.shape, BF16)]
     value_grad = in_vmem(add_value_kernel, "value_grad", shape, value_sum, value_far)[0]
-    came, query_grad, value_grad = tie((came, query_grad, value_grad))
+    came, value_grad = tie((came, value_grad))
     weight_grad = kept[0] + came[0].astype(F32)
     return attn_out[None], query_grad[None], value_grad[None], weight_grad
 

time: 74.9 us -> 60.7 us (0.81)
  local copies, waits for them, and re-layouts: 6.63 us -> 0.01 us
  waiting for transfers between devices: 13.6 us -> 8.49 us
  Pallas kernels: 19 us -> 17.6 us
  starting transfers between devices: 33 us -> 32.2 us
    unnamed x26 -> x6, local copies, waits for them, and re-layouts: 6.63 us -> 0.01 us
    ppermute x22, waiting for transfers between devices: 13.6 us -> 8.49 us  [swap(): return lax.ppermute(x, axis, [(i, i ^ mask) for i in range(size)])]
    pallas_call x5 -> x3, Pallas kernels: 9.04 us -> 7.98 us  [the longest x2 5.12 us: over_rows(): self.call(rows_kernel, 0.1, name, grid=(KEY_HEADS, self.tiles), in_specs=...]
    ppermute x22, starting transfers between devices: 33 us -> 32.2 us  [swap(): return lax.ppermute(x, axis, [(i, i ^ mask) for i in range(size)])]
    pallas_call x5 -> x7, Pallas kernels: 1.52 us -> 1.19 us  [in_vmem(): pl.pallas_call(kernel, in_specs=[VMEM] * len(arrays), out_specs=[VMEM] *...]
  transfers between devices with their start and end apart: 22 -> 22, of which waited for: 7 -> 7; matrix products, arithmetic and copies ran while one was open for 0% -> 0% of each run, Pallas kernels for 19% -> 23%
where the time goes in v11:
time: 60.7 us; the launch traced here: 60.5 us
  starting transfers between devices  32.2 us (53%)
  Pallas kernels  17.6 us (29%)
  waiting for transfers between devices  8.49 us (14%)
  between operations  1.46 us (2%)
  other arithmetic  0.73 us (1%)
    ppermute x22, starting transfers between devices, swap(): return lax.ppermute(x, axis, [(i, i ^ mask) for i in range(size)])  32.2 us
    ppermute x22, waiting for transfers between devices, swap(): return lax.ppermute(x, axis, [(i, i ^ mask) for i in range(size)])  8.49 us
    pallas_call x1, Pallas kernels, scores(): self.call(scores_kernel, 1.0, 'scores', in_specs=[smem, smem, VMEM, VMEM]...  5.47 us
    pallas_call x2, Pallas kernels, over_rows(): self.call(rows_kernel, 0.1, name, grid=(KEY_HEADS, self.tiles), in_specs=...  5.12 us
    pallas_call x1, Pallas kernels, project(): pl.pallas_call(functools.partial(project_kernel, streams), grid=(steps,),...  2.98 us
    pallas_call x1, Pallas kernels, values(): self.call(values_kernel, 0.1, 'values', grid=(KEY_HEADS, self.tiles), in_...  2.86 us
  transfers between devices with their start and end apart: 22, of which 7 were waited for; matrix products, arithmetic and copies ran while one was open for 0% of the time, Pallas kernels for 23%

profile of v11, /device:TPU:0, one launch (start us, length us, event | category | flops | bytes accessed | tf_op | source)
XLA Modules:
  0.0 60.5 jit_solution(8223780860921955076)
XLA Ops:
  0.7 3.0 %project.1 = (bf16[32,1024]{1,0:T(8,128)(2,1)S(1)}, bf16[128,512]{1,0:T(8,128)(2,1)S(1)}, bf16[128,512]{1,0:T(8,128)(2,1)S(1)}) custom-call(bf16[32,4096]{1,0:T(8,128)(2,1)} %bitcast.14, bf16[4096,512]{1,0:T(8,128)(2,1)} %refs_3_.1, bf16[4096,512]{1,0:T(8,128)(2,1)} %refs_3_.1, bf16[4096,512]{1,0:T(8,128)(2,1)} %refs_3_.1, bf16[4096,512]{1,0:T(8,128)(2,1)} %refs_3_.1, ...), custom_call_target="tpu_custom_call" | custom-call | flops 134217728 | bytes 4194304 | tf_op jit(solution)/shard_map/project/pallas_call | solution.py:94
  3.7 4.1 %collective-permute-start.3 = (bf16[32,1024]{1,0:T(8,128)(2,1)S(1)}, bf16[32,1024]{1,0:T(8,128)(2,1)S(1)}, u32[]{:S(2)}, u32[]{:S(2)}) collective-permute-start(bf16[32,1024]{1,0:T(8,128)(2,1)S(1)} %get-tuple-element.51.refs_0_), channel_id=1, source_target_pairs={{0,16},{4,20},{8,24},{12,28},{16,0},{20,4},{24,8},{28,12},{1,17},{... | collective-permute-start | bytes 196616 | tf_op jit(solution)/shard_map/ppermute | solution.py:28
  7.8 2.5 %collective-permute-start.2 = (bf16[32,1024]{1,0:T(8,128)(2,1)S(1)}, bf16[32,1024]{1,0:T(8,128)(2,1)S(1)}, u32[]{:S(2)}, u32[]{:S(2)}) collective-permute-start(bf16[32,1024]{1,0:T(8,128)(2,1)S(1)} %get-tuple-element.51.refs_0_), channel_id=1, source_target_pairs={{0,12},{4,8},{8,4},{12,0},{16,28},{20,24},{24,20},{28,16},{1,13},{... | collective-permute-start | bytes 196616 | tf_op jit(solution)/shard_map/ppermute | solution.py:28
  10.3 0.4 collective-permute-start.1
  10.7 0.5 collective-permute-start
  11.2 2.5 %collective-permute-start.6 = (bf16[32,1024]{1,0:T(8,128)(2,1)S(1)}, bf16[32,1024]{1,0:T(8,128)(2,1)S(1)}, u32[]{:S(2)}, u32[]{:S(2)}) collective-permute-start(bf16[32,1024]{1,0:T(8,128)(2,1)S(1)} %collective-permute-done.3.refs_4_), channel_id=1, source_target_pairs={{0,12},{4,8},{8,4},{12,0},{16,28},{20,24},{24,20},{28,16},{1,13},{... | collective-permute-start | bytes 196616 | tf_op jit(solution)/shard_map/ppermute | solution.py:28
  13.8 0.4 collective-permute-start.5
  14.2 0.9 %collective-permute-start.4 = (bf16[32,1024]{1,0:T(8,128)(2,1)S(1)}, bf16[32,1024]{1,0:T(8,128)(2,1)S(1)}, u32[]{:S(2)}, u32[]{:S(2)}) collective-permute-start(bf16[32,1024]{1,0:T(8,128)(2,1)S(1)} %collective-permute-done.3.refs_4_), channel_id=1, source_target_pairs={{0,4},{4,0},{8,12},{12,8},{16,20},{20,16},{24,28},{28,24},{1,5},{5... | collective-permute-start | bytes 196616 | tf_op jit(solution)/shard_map/ppermute | solution.py:28
  15.8 1.9 %collective-permute-start.7 = (bf16[128,512]{1,0:T(8,128)(2,1)S(1)}, bf16[128,512]{1,0:T(8,128)(2,1)S(1)}, u32[]{:S(2)}, u32[]{:S(2)}) collective-permute-start(bf16[128,512]{1,0:T(8,128)(2,1)S(1)} %get-tuple-element.59), channel_id=1, source_target_pairs={{0,16},{4,20},{8,24},{12,28},{16,0},{20,4},{24,8},{28,12},{1,17},{... | collective-permute-start | bytes 393224 | tf_op jit(solution)/shard_map/ppermute | solution.py:28
  17.7 1.8 %collective-permute-done.5.refs_6_ = bf16[32,1024]{1,0:T(8,128)(2,1)S(1)} collective-permute-done((bf16[32,1024]{1,0:T(8,128)(2,1)S(1)}, bf16[32,1024]{1,0:T(8,128)(2,1)S(1)}, u32[]{:S(2)}, u32[]{:S(2)}) %collective-permute-start.5) | collective-permute-done | bytes 65568 | tf_op jit(solution)/shard_map/ppermute | solution.py:28
  19.5 5.5 %scores.1 = (bf16[256,4096]{1,0:T(8,128)(2,1)S(1)}, bf16[256,4096]{1,0:T(8,128)(2,1)S(1)}, bf16[256,4096]{1,0:T(8,128)(2,1)S(1)}, bf16[256,512]{1,0:T(8,128)(2,1...) custom-call(s32[1]{0:T(128)S(6)} %copy.11.length_ref, ...), custom_call_target="tpu_custom_call" | custom-call | flops 1610612736 | bytes 4194304 | tf_op jit(solution)/shard_map/scores/pallas_call | solution.py:260
  25.0 1.7 %collective-permute-start.9 = (bf16[64,512]{1,0:T(8,128)(2,1)S(1)}, bf16[64,512]{1,0:T(8,128)(2,1)S(1)}, u32[]{:S(2)}, u32[]{:S(2)}) collective-permute-start(bf16[64,512]{1,0:T(8,128)(2,1)S(1)} %get-tuple-element.61), channel_id=1, source_target_pairs={{0,8},{4,12},{8,0},{12,4},{16,24},{20,28},{24,16},{28,20},{1,9},{5... | collective-permute-start | bytes 196616 | tf_op jit(solution)/shard_map/ppermute | solution.py:28
  26.7 1.8 %collective-permute-start.10 = (bf16[64,512]{1,0:T(8,128)(2,1)S(1)}, bf16[64,512]{1,0:T(8,128)(2,1)S(1)}, u32[]{:S(2)}, u32[]{:S(2)}) collective-permute-start(bf16[64,512]{1,0:T(8,128)(2,1)S(1)} %get-tuple-element.62), channel_id=1, source_target_pairs={{0,12},{4,8},{8,4},{12,0},{16,28},{20,24},{24,20},{28,16},{1,13},{... | collective-permute-start | bytes 196616 | tf_op jit(solution)/shard_map/ppermute | solution.py:28
  28.5 2.9 %values.1 = (f32[64,512]{1,0:T(8,128)S(1)}, bf16[64,512]{1,0:T(8,128)(2,1)S(1)}, bf16[64,512]{1,0:T(8,128)(2,1)S(1)}, bf16[64,512]{1,0:T(8,128)(2,1)S(1)}) custom-call(bf16[128,4096]{1,0:T(8,128)(2,1)} %bitcast.9, bf16[256,4096]{1,0:T(8,128)(2,1)S(1)} %get-tuple-element.53.w_ref), custom_call_target="tpu_custom_call" | custom-call | flops 161061280 | bytes 419430 | tf_op jit(solution)/shard_map/values/pallas_call | solution.py:275
  31.4 0.5 collective-permute-done.10.refs_2_
  31.9 2.3 %collective-permute-start.11 = (bf16[32,512]{1,0:T(8,128)(2,1)S(1)}, bf16[32,512]{1,0:T(8,128)(2,1)S(1)}, u32[]{:S(2)}, u32[]{:S(2)}) collective-permute-start(bf16[32,512]{1,0:T(8,128)(2,1)S(1)} %get-tuple-element.69), channel_id=1, source_target_pairs={{0,16},{4,20},{8,24},{12,28},{16,0},{20,4},{24,8},{28,12},{1,17},{... | collective-permute-start | bytes 98312 | tf_op jit(solution)/shard_map/ppermute | solution.py:28
  34.2 2.6 %query_grad.1 = bf16[128,4096]{1,0:T(8,128)(2,1)} custom-call(bf16[256,4096]{1,0:T(8,128)(2,1)S(1)} %get-tuple-element.66.inner_ref, bf16[256,512]{1,0:T(8,128)(2,1)S(1)} %get-tuple-element.67.head_ref), custom_call_target="tpu_custom_call" | custom-call | flops 161061280 | bytes 419430 | tf_op jit(solution)/shard_map/query_grad/pallas_call | solution.py:288
  37.0 1.5 %collective-permute-start.12 = (bf16[32,1536]{1,0:T(8,128)(2,1)S(1)}, bf16[32,1536]{1,0:T(8,128)(2,1)S(1)}, u32[]{:S(2)}, u32[]{:S(2)}) collective-permute-start(bf16[32,1536]{1,0:T(8,128)(2,1)S(1)} %get-tuple-element.73), channel_id=1, source_target_pairs={{0,4},{4,0},{8,12},{12,8},{16,20},{20,16},{24,28},{28,24},{1,5},{5... | collective-permute-start | bytes 294920 | tf_op jit(solution)/shard_map/ppermute | solution.py:28
  38.5 2.5 %collective-permute-start.15 = (bf16[32,512]{1,0:T(8,128)(2,1)S(1)}, bf16[32,512]{1,0:T(8,128)(2,1)S(1)}, u32[]{:S(2)}, u32[]{:S(2)}) collective-permute-start(bf16[32,512]{1,0:T(8,128)(2,1)S(1)} %get-tuple-element.83), channel_id=1, source_target_pairs={{0,16},{4,20},{8,24},{12,28},{16,0},{20,4},{24,8},{28,12},{1,17},{... | collective-permute-start | bytes 98312 | tf_op jit(solution)/shard_map/ppermute | solution.py:28
  41.2 1.4 %collective-permute-start.14 = (bf16[32,1536]{1,0:T(8,128)(2,1)S(1)}, bf16[32,1536]{1,0:T(8,128)(2,1)S(1)}, u32[]{:S(2)}, u32[]{:S(2)}) collective-permute-start(bf16[32,1536]{1,0:T(8,128)(2,1)S(1)} %get-tuple-element.75), channel_id=1, source_target_pairs={{0,12},{4,8},{8,4},{12,0},{16,28},{20,24},{24,20},{28,16},{1,13},{... | collective-permute-start | bytes 294920 | tf_op jit(solution)/shard_map/ppermute | solution.py:28
  42.6 1.0 %collective-permute-done.15.far_ref.refs_7_ = bf16[32,512]{1,0:T(8,128)(2,1)S(1)} collective-permute-done((bf16[32,512]{1,0:T(8,128)(2,1)S(1)}, bf16[32,512]{1,0:T(8,128)(2,1)S(1)}, u32[]{:S(2)}, u32[]{:S(2)}) %collective-permute-start.15) | collective-permute-done | bytes 32800 | tf_op jit(solution)/shard_map/ppermute | solution.py:28
  43.6 0.9 %collective-permute-start.16 = (bf16[32,1536]{1,0:T(8,128)(2,1)S(1)}, bf16[32,1536]{1,0:T(8,128)(2,1)S(1)}, u32[]{:S(2)}, u32[]{:S(2)}) collective-permute-start(bf16[32,1536]{1,0:T(8,128)(2,1)S(1)} %get-tuple-element.87), channel_id=1, source_target_pairs={{0,4},{4,0},{8,12},{12,8},{16,20},{20,16},{24,28},{28,24},{1,5},{5... | collective-permute-start | bytes 294920 | tf_op jit(solution)/shard_map/ppermute | solution.py:28
  44.8 2.4 %collective-permute-start.18 = (bf16[32,1536]{1,0:T(8,128)(2,1)S(1)}, bf16[32,1536]{1,0:T(8,128)(2,1)S(1)}, u32[]{:S(2)}, u32[]{:S(2)}) collective-permute-start(bf16[32,1536]{1,0:T(8,128)(2,1)S(1)} %get-tuple-element.89), channel_id=1, source_target_pairs={{0,12},{4,8},{8,4},{12,0},{16,28},{20,24},{24,20},{28,16},{1,13},{... | collective-permute-start | bytes 294920 | tf_op jit(solution)/shard_map/ppermute | solution.py:28
  47.2 2.6 %output.1 = bf16[128,4096]{1,0:T(8,128)(2,1)} custom-call(bf16[256,4096]{1,0:T(8,128)(2,1)S(1)} %get-tuple-element.76.inner_ref, bf16[256,512]{1,0:T(8,128)(2,1)S(1)} %get-tuple-element.77.head_ref), custom_call_target="tpu_custom_call" | custom-call | flops 161061280 | bytes 419430 | tf_op jit(solution)/shard_map/output/pallas_call | solution.py:288
  49.9 0.9 %collective-permute-done.18.refs_3_ = bf16[32,1536]{1,0:T(8,128)(2,1)S(1)} collective-permute-done((bf16[32,1536]{1,0:T(8,128)(2,1)S(1)}, bf16[32,1536]{1,0:T(8,128)(2,1)S(1)}, u32[]{:S(2)}, u32[]{:S(2)}) %collective-permute-start.18) | collective-permute-done | bytes 98336 | tf_op jit(solution)/shard_map/ppermute | solution.py:28
  50.8 0.3 weight_terms.1
  51.2 1.5 %collective-permute-done.19.came_ref = bf16[2,128,512]{2,1,0:T(8,128)(2,1)S(1)} collective-permute-done((bf16[2,128,512]{2,1,0:T(8,128)(2,1)S(1)}, bf16[2,128,512]{2,1,0:T(8,128)(2,1)S(1)}, u32[]{:S(2)}, u32[]{:S(2)}) %collective-permute-start.19) | collective-permute-done | bytes 262176 | tf_op jit(solution)/shard_map/ppermute | solution.py:28
  52.8 1.6 %collective-permute-start.20 = (bf16[1,128,512]{2,1,0:T(8,128)(2,1)S(1)}, bf16[1,128,512]{2,1,0:T(8,128)(2,1)S(1)}, u32[]{:S(2)}, u32[]{:S(2)}) collective-permute-start(bf16[1,128,512]{2,1,0:T(8,128)(2,1)S(1)} %get-tuple-element.92), channel_id=1, source_target_pairs={{0,2},{1,3},{2,0},{3,1},{4,6},{5,7},{6,4},{7,5},{8,10},{9,11},{10,... | collective-permute-start | bytes 393224 | tf_op jit(solution)/shard_map/ppermute | solution.py:28
  54.4 2.3 %collective-permute-start.21 = (bf16[32,512]{1,0:T(8,128)(2,1)S(1)}, bf16[32,512]{1,0:T(8,128)(2,1)S(1)}, u32[]{:S(2)}, u32[]{:S(2)}) collective-permute-start(bf16[32,512]{1,0:T(8,128)(2,1)S(1)} %get-tuple-element.94), channel_id=1, source_target_pairs={{0,16},{4,20},{8,24},{12,28},{16,0},{20,4},{24,8},{28,12},{1,17},{... | collective-permute-start | bytes 98312 | tf_op jit(solution)/shard_map/ppermute | solution.py:28
  56.7 2.5 %collective-permute-done.21.far_ref = bf16[32,512]{1,0:T(8,128)(2,1)S(1)} collective-permute-done((bf16[32,512]{1,0:T(8,128)(2,1)S(1)}, bf16[32,512]{1,0:T(8,128)(2,1)S(1)}, u32[]{:S(2)}, u32[]{:S(2)}) %collective-permute-start.21) | collective-permute-done | bytes 32800 | tf_op jit(solution)/shard_map/ppermute | solution.py:28
  59.2 0.6 %value_grad.1 = bf16[32,512]{1,0:T(8,128)(2,1)} custom-call(f32[32,512]{1,0:T(8,128)S(1)} %get-tuple-element.93.near_ref, bf16[32,512]{1,0:T(8,128)(2,1)S(1)} %collective-permute-done.21.far_ref), custom_call_target="tpu_custom_call" | custom-call | tf_op jit(solution)/shard_map/value_grad/pallas_call | solution.py:300
  59.8 0.7 %add_bitcast_fusion = f32[128,512]{1,0:T(8,128)} fusion(f32[1,128,512]{2,1,0:T(8,128)S(1)} %get-tuple-element.96, bf16[1,128,512]{2,1,0:T(8,128)(2,1)S(1)} %collective-permute-done.20), kind=kLoop, calls=%fused_computation | loop fusion | flops 131072 | bytes 655360 | tf_op jit(solution)/shard_map/add | solution.py:470
  (31 shorter events, 1.1 us)
Async XLA Ops:
  0.6 18.8 %copy-start = (bf16[1,128,4096]{2,1,0:T(8,128)(2,1)S(1)}, bf16[1,128,4096]{2,1,0:T(8,128)(2,1)}, u32[]{:S(2)}) copy-start(bf16[1,128,4096]{2,1,0:T(8,128)(2,1)} %param.11) | copy-start | bytes 3145732
  0.6 18.8 %copy-start.1 = (bf16[1,128,4096]{2,1,0:T(8,128)(2,1)S(1)}, bf16[1,128,4096]{2,1,0:T(8,128)(2,1)}, u32[]{:S(2)}) copy-start(bf16[1,128,4096]{2,1,0:T(8,128)(2,1)} %param.10) | copy-start | bytes 3145732
  0.7 18.8 %copy-start.2 = (s32[1,8]{1,0:T(1,128)S(1)}, s32[1,8]{1,0:T(1,128)}, u32[]{:S(2)}) copy-start(s32[1,8]{1,0:T(1,128)} %frame_ref.1) | copy-start | bytes 100
  3.7 7.6 %collective-permute-start.3 = (bf16[32,1024]{1,0:T(8,128)(2,1)S(1)}, bf16[32,1024]{1,0:T(8,128)(2,1)S(1)}, u32[]{:S(2)}, u32[]{:S(2)}) collective-permute-start(bf16[32,1024]{1,0:T(8,128)(2,1)S(1)} %get-tuple-element.51.refs_0_), channel_id=1, source_target_pairs={{0,16},{4,20},{8,24},{12,28},{16,0},{20,4},{24,8},{28,12},{1,17},{... | collective-permute-start | bytes 196616 | tf_op jit(solution)/shard_map/ppermute | solution.py:28
  7.8 6.5 %collective-permute-start.2 = (bf16[32,1024]{1,0:T(8,128)(2,1)S(1)}, bf16[32,1024]{1,0:T(8,128)(2,1)S(1)}, u32[]{:S(2)}, u32[]{:S(2)}) collective-permute-start(bf16[32,1024]{1,0:T(8,128)(2,1)S(1)} %get-tuple-element.51.refs_0_), channel_id=1, source_target_pairs={{0,12},{4,8},{8,4},{12,0},{16,28},{20,24},{24,20},{28,16},{1,13},{... | collective-permute-start | bytes 196616 | tf_op jit(solution)/shard_map/ppermute | solution.py:28
  10.3 5.5 %collective-permute-start.1 = (bf16[32,1024]{1,0:T(8,128)(2,1)S(1)}, bf16[32,1024]{1,0:T(8,128)(2,1)S(1)}, u32[]{:S(2)}, u32[]{:S(2)}) collective-permute-start(bf16[32,1024]{1,0:T(8,128)(2,1)S(1)} %get-tuple-element.51.refs_0_), channel_id=1, source_target_pairs={{0,8},{4,12},{8,0},{12,4},{16,24},{20,28},{24,16},{28,20},{1,9},{5... | collective-permute-start | bytes 196616 | tf_op jit(solution)/shard_map/ppermute | solution.py:28
  10.7 6.9 %collective-permute-start = (bf16[32,1024]{1,0:T(8,128)(2,1)S(1)}, bf16[32,1024]{1,0:T(8,128)(2,1)S(1)}, u32[]{:S(2)}, u32[]{:S(2)}) collective-permute-start(bf16[32,1024]{1,0:T(8,128)(2,1)S(1)} %get-tuple-element.51.refs_0_), channel_id=1, source_target_pairs={{0,4},{4,0},{8,12},{12,8},{16,20},{20,16},{24,28},{28,24},{1,5},{5... | collective-permute-start | bytes 196616 | tf_op jit(solution)/shard_map/ppermute | solution.py:28
  11.2 6.4 %collective-permute-start.6 = (bf16[32,1024]{1,0:T(8,128)(2,1)S(1)}, bf16[32,1024]{1,0:T(8,128)(2,1)S(1)}, u32[]{:S(2)}, u32[]{:S(2)}) collective-permute-start(bf16[32,1024]{1,0:T(8,128)(2,1)S(1)} %collective-permute-done.3.refs_4_), channel_id=1, source_target_pairs={{0,12},{4,8},{8,4},{12,0},{16,28},{20,24},{24,20},{28,16},{1,13},{... | collective-permute-start | bytes 196616 | tf_op jit(solution)/shard_map/ppermute | solution.py:28
  13.8 5.7 %collective-permute-start.5 = (bf16[32,1024]{1,0:T(8,128)(2,1)S(1)}, bf16[32,1024]{1,0:T(8,128)(2,1)S(1)}, u32[]{:S(2)}, u32[]{:S(2)}) collective-permute-start(bf16[32,1024]{1,0:T(8,128)(2,1)S(1)} %collective-permute-done.3.refs_4_), channel_id=1, source_target_pairs={{0,8},{4,12},{8,0},{12,4},{16,24},{20,28},{24,16},{28,20},{1,9},{5... | collective-permute-start | bytes 196616 | tf_op jit(solution)/shard_map/ppermute | solution.py:28
  14.2 5.2 %collective-permute-start.4 = (bf16[32,1024]{1,0:T(8,128)(2,1)S(1)}, bf16[32,1024]{1,0:T(8,128)(2,1)S(1)}, u32[]{:S(2)}, u32[]{:S(2)}) collective-permute-start(bf16[32,1024]{1,0:T(8,128)(2,1)S(1)} %collective-permute-done.3.refs_4_), channel_id=1, source_target_pairs={{0,4},{4,0},{8,12},{12,8},{16,20},{20,16},{24,28},{28,24},{1,5},{5... | collective-permute-start | bytes 196616 | tf_op jit(solution)/shard_map/ppermute | solution.py:28
  15.8 9.2 %collective-permute-start.7 = (bf16[128,512]{1,0:T(8,128)(2,1)S(1)}, bf16[128,512]{1,0:T(8,128)(2,1)S(1)}, u32[]{:S(2)}, u32[]{:S(2)}) collective-permute-start(bf16[128,512]{1,0:T(8,128)(2,1)S(1)} %get-tuple-element.59), channel_id=1, source_target_pairs={{0,16},{4,20},{8,24},{12,28},{16,0},{20,4},{24,8},{28,12},{1,17},{... | collective-permute-start | bytes 393224 | tf_op jit(solution)/shard_map/ppermute | solution.py:28
  25.0 6.4 %collective-permute-start.8 = (bf16[64,512]{1,0:T(8,128)(2,1)S(1)}, bf16[64,512]{1,0:T(8,128)(2,1)S(1)}, u32[]{:S(2)}, u32[]{:S(2)}) collective-permute-start(bf16[64,512]{1,0:T(8,128)(2,1)S(1)} %get-tuple-element.60), channel_id=1, source_target_pairs={{0,4},{4,0},{8,12},{12,8},{16,20},{20,16},{24,28},{28,24},{1,5},{5... | collective-permute-start | bytes 196616 | tf_op jit(solution)/shard_map/ppermute | solution.py:28
  25.0 6.4 %collective-permute-start.9 = (bf16[64,512]{1,0:T(8,128)(2,1)S(1)}, bf16[64,512]{1,0:T(8,128)(2,1)S(1)}, u32[]{:S(2)}, u32[]{:S(2)}) collective-permute-start(bf16[64,512]{1,0:T(8,128)(2,1)S(1)} %get-tuple-element.61), channel_id=1, source_target_pairs={{0,8},{4,12},{8,0},{12,4},{16,24},{20,28},{24,16},{28,20},{1,9},{5... | collective-permute-start | bytes 196616 | tf_op jit(solution)/shard_map/ppermute | solution.py:28
  26.7 5.2 %collective-permute-start.10 = (bf16[64,512]{1,0:T(8,128)(2,1)S(1)}, bf16[64,512]{1,0:T(8,128)(2,1)S(1)}, u32[]{:S(2)}, u32[]{:S(2)}) collective-permute-start(bf16[64,512]{1,0:T(8,128)(2,1)S(1)} %get-tuple-element.62), channel_id=1, source_target_pairs={{0,12},{4,8},{8,4},{12,0},{16,28},{20,24},{24,20},{28,16},{1,13},{... | collective-permute-start | bytes 196616 | tf_op jit(solution)/shard_map/ppermute | solution.py:28
  31.9 5.1 %collective-permute-start.11 = (bf16[32,512]{1,0:T(8,128)(2,1)S(1)}, bf16[32,512]{1,0:T(8,128)(2,1)S(1)}, u32[]{:S(2)}, u32[]{:S(2)}) collective-permute-start(bf16[32,512]{1,0:T(8,128)(2,1)S(1)} %get-tuple-element.69), channel_id=1, source_target_pairs={{0,16},{4,20},{8,24},{12,28},{16,0},{20,4},{24,8},{28,12},{1,17},{... | collective-permute-start | bytes 98312 | tf_op jit(solution)/shard_map/ppermute | solution.py:28
  37.0 7.7 %collective-permute-start.12 = (bf16[32,1536]{1,0:T(8,128)(2,1)S(1)}, bf16[32,1536]{1,0:T(8,128)(2,1)S(1)}, u32[]{:S(2)}, u32[]{:S(2)}) collective-permute-start(bf16[32,1536]{1,0:T(8,128)(2,1)S(1)} %get-tuple-element.73), channel_id=1, source_target_pairs={{0,4},{4,0},{8,12},{12,8},{16,20},{20,16},{24,28},{28,24},{1,5},{5... | collective-permute-start | bytes 294920 | tf_op jit(solution)/shard_map/ppermute | solution.py:28
  38.5 5.1 %collective-permute-start.15 = (bf16[32,512]{1,0:T(8,128)(2,1)S(1)}, bf16[32,512]{1,0:T(8,128)(2,1)S(1)}, u32[]{:S(2)}, u32[]{:S(2)}) collective-permute-start(bf16[32,512]{1,0:T(8,128)(2,1)S(1)} %get-tuple-element.83), channel_id=1, source_target_pairs={{0,16},{4,20},{8,24},{12,28},{16,0},{20,4},{24,8},{28,12},{1,17},{... | collective-permute-start | bytes 98312 | tf_op jit(solution)/shard_map/ppermute | solution.py:28
  41.0 8.8 %collective-permute-start.13 = (bf16[32,1536]{1,0:T(8,128)(2,1)S(1)}, bf16[32,1536]{1,0:T(8,128)(2,1)S(1)}, u32[]{:S(2)}, u32[]{:S(2)}) collective-permute-start(bf16[32,1536]{1,0:T(8,128)(2,1)S(1)} %get-tuple-element.74), channel_id=1, source_target_pairs={{0,8},{4,12},{8,0},{12,4},{16,24},{20,28},{24,16},{28,20},{1,9},{5... | collective-permute-start | bytes 294920 | tf_op jit(solution)/shard_map/ppermute | solution.py:28
  41.2 8.6 %collective-permute-start.14 = (bf16[32,1536]{1,0:T(8,128)(2,1)S(1)}, bf16[32,1536]{1,0:T(8,128)(2,1)S(1)}, u32[]{:S(2)}, u32[]{:S(2)}) collective-permute-start(bf16[32,1536]{1,0:T(8,128)(2,1)S(1)} %get-tuple-element.75), channel_id=1, source_target_pairs={{0,12},{4,8},{8,4},{12,0},{16,28},{20,24},{24,20},{28,16},{1,13},{... | collective-permute-start | bytes 294920 | tf_op jit(solution)/shard_map/ppermute | solution.py:28
  43.6 6.3 %collective-permute-start.16 = (bf16[32,1536]{1,0:T(8,128)(2,1)S(1)}, bf16[32,1536]{1,0:T(8,128)(2,1)S(1)}, u32[]{:S(2)}, u32[]{:S(2)}) collective-permute-start(bf16[32,1536]{1,0:T(8,128)(2,1)S(1)} %get-tuple-element.87), channel_id=1, source_target_pairs={{0,4},{4,0},{8,12},{12,8},{16,20},{20,16},{24,28},{28,24},{1,5},{5... | collective-permute-start | bytes 294920 | tf_op jit(solution)/shard_map/ppermute | solution.py:28
  44.6 5.3 %collective-permute-start.17 = (bf16[32,1536]{1,0:T(8,128)(2,1)S(1)}, bf16[32,1536]{1,0:T(8,128)(2,1)S(1)}, u32[]{:S(2)}, u32[]{:S(2)}) collective-permute-start(bf16[32,1536]{1,0:T(8,128)(2,1)S(1)} %get-tuple-element.88), channel_id=1, source_target_pairs={{0,8},{4,12},{8,0},{12,4},{16,24},{20,28},{24,16},{28,20},{1,9},{5... | collective-permute-start | bytes 294920 | tf_op jit(solution)/shard_map/ppermute | solution.py:28
  44.8 6.0 %collective-permute-start.18 = (bf16[32,1536]{1,0:T(8,128)(2,1)S(1)}, bf16[32,1536]{1,0:T(8,128)(2,1)S(1)}, u32[]{:S(2)}, u32[]{:S(2)}) collective-permute-start(bf16[32,1536]{1,0:T(8,128)(2,1)S(1)} %get-tuple-element.89), channel_id=1, source_target_pairs={{0,12},{4,8},{8,4},{12,0},{16,28},{20,24},{24,20},{28,16},{1,13},{... | collective-permute-start | bytes 294920 | tf_op jit(solution)/shard_map/ppermute | solution.py:28
  51.1 1.6 %collective-permute-start.19 = (bf16[2,128,512]{2,1,0:T(8,128)(2,1)S(1)}, bf16[2,128,512]{2,1,0:T(8,128)(2,1)S(1)}, u32[]{:S(2)}, u32[]{:S(2)}) collective-permute-start(bf16[2,128,512]{2,1,0:T(8,128)(2,1)S(1)} %get-tuple-element.91), channel_id=1, source_target_pairs={{0,1},{1,0},{2,3},{3,2},{4,5},{5,4},{6,7},{7,6},{8,9},{9,8},{10,11... | collective-permute-start | bytes 786440 | tf_op jit(solution)/shard_map/ppermute | solution.py:28
  52.8 7.0 %collective-permute-start.20 = (bf16[1,128,512]{2,1,0:T(8,128)(2,1)S(1)}, bf16[1,128,512]{2,1,0:T(8,128)(2,1)S(1)}, u32[]{:S(2)}, u32[]{:S(2)}) collective-permute-start(bf16[1,128,512]{2,1,0:T(8,128)(2,1)S(1)} %get-tuple-element.92), channel_id=1, source_target_pairs={{0,2},{1,3},{2,0},{3,1},{4,6},{5,7},{6,4},{7,5},{8,10},{9,11},{10,... | collective-permute-start | bytes 393224 | tf_op jit(solution)/shard_map/ppermute | solution.py:28
  54.4 4.8 %collective-permute-start.21 = (bf16[32,512]{1,0:T(8,128)(2,1)S(1)}, bf16[32,512]{1,0:T(8,128)(2,1)S(1)}, u32[]{:S(2)}, u32[]{:S(2)}) collective-permute-start(bf16[32,512]{1,0:T(8,128)(2,1)S(1)} %get-tuple-element.94), channel_id=1, source_target_pairs={{0,16},{4,20},{8,24},{12,28},{16,0},{20,4},{24,8},{28,12},{1,17},{... | collective-permute-start | bytes 98312 | tf_op jit(solution)/shard_map/ppermute | solution.py:28

commit v12 on v11

--- a/solution.py
+++ b/solution.py
@@ -39,9 +39,9 @@
     far = swap(own, "blk", half)
     pieces = {0: own, half: far}
     pieces.update({m: swap(near[m - 1] if near else own, "blk", m) for m in masks})
-    sent = onward(far) if onward else [far] * (half - 1)
+    kept, sent = onward(far) if onward else (None, [far] * (half - 1))
     pieces.update({m + half: swap(sent[m - 1], "blk", m) for m in masks})
-    return [pieces[m] for m in range(blocks)]
+    return [pieces[m] for m in range(blocks)], kept
 
 
 def near_exchange(pieces):
@@ -83,7 +83,7 @@
 def project(blocks, visual, key_weight, value):
     rows, features = visual.shape
     columns = key_weight.shape[1]
-    steps, streams = 2, 4
+    steps, streams = 4, 4
     slab = features // (steps * streams)
     out = (rows, columns + value.shape[1])
     half = (blocks // 2 * rows, features // blocks)
@@ -131,8 +131,8 @@
 
 
 def scores_kernel(pieces, length_ref, frame_ref, q_ref, g_ref, *refs):
-    kv_refs, (w_ref, again_ref, ds_ref, k_ref, v_ref) = refs[:pieces], refs[pieces : pieces + 5]
-    own_ref, near_refs, (kg_acc, bias_ref) = refs[pieces + 5], refs[pieces + 6 : -2], refs[-2:]
+    kv_refs, (w_ref, ds_ref, k_ref, v_ref) = refs[:pieces], refs[pieces : pieces + 4]
+    own_ref, near_refs, (kg_acc, bias_ref) = refs[pieces + 4], refs[pieces + 5 : -2], refs[-2:]
     block = lax.axis_index("blk")
     tiles = q_ref.shape[0] // TILE
     rows = kv_refs[0].shape[0]
@@ -145,7 +145,7 @@
         part = slice(m * rows, (m + 1) * rows)
         k_ref[part, :] = kv_refs[m][:, :width]
         v_ref[part, :] = kv_refs[m][:, width:]
-    row = lax.broadcasted_iota(jnp.int32, (rows, pair), 0)
+    row = lax.broadcasted_iota(jnp.int32, (rows, TILE), 0)
     for i in range(tiles):
         text = slice(i * TILE, (i + 1) * TILE)
         limit = jnp.minimum(length_ref[0], TILE * frame_ref[0, block * tiles + i])
@@ -170,20 +170,20 @@
             for p in range(pairs):
                 if p + 1 < pairs:
                     products(p + 1)
-                scores = raw.pop(p) + bias_ref[...]
-                peak = jnp.max(scores, axis=0, keepdims=True)
-                shifted = jnp.exp2((scores - peak) * (scale * LOG2_E))
-                terms = shifted * dprobs.pop(p)
-                inverse = 1.0 / jnp.sum(shifted, axis=0, keepdims=True)
-                slope = inverse * scale
-                offset = jnp.sum(terms, axis=0, keepdims=True) * inverse * slope
-                start = (i * KEY_HEADS + j) * span + p * pair
-                both = pl.ds(pl.multiple_of(start, HEAD_SIZE), pair)
-                weights = (shifted * inverse).astype(BF16)
-                w_ref[:, both] = weights
-                again_ref[:, both] = weights
-                ds_stack.append((terms * slope - shifted * offset).astype(BF16))
-                ds_ref[:, both] = ds_stack[p]
+                for h in range(2):
+                    one = slice(h * TILE, (h + 1) * TILE)
+                    scores = raw[p][:, one] + bias_ref[...]
+                    peak = jnp.max(scores, axis=0, keepdims=True)
+                    shifted = jnp.exp2((scores - peak) * (scale * LOG2_E))
+                    terms = shifted * dprobs[p][:, one]
+                    inverse = 1.0 / jnp.sum(shifted, axis=0, keepdims=True)
+                    slope = inverse * scale
+                    offset = jnp.sum(terms, axis=0, keepdims=True) * inverse * slope
+                    start = (i * KEY_HEADS + j) * span + p * pair + h * TILE
+                    columns = pl.ds(pl.multiple_of(start, HEAD_SIZE), TILE)
+                    w_ref[:, columns] = (shifted * inverse).astype(BF16)
+                    ds_stack.append((terms * slope - shifted * offset).astype(BF16))
+                    ds_ref[:, columns] = ds_stack[-1]
             kg = dot(jnp.concatenate(ds_stack, axis=1), jnp.concatenate(q_stack, axis=0))
             if i == 0:
                 kg_acc[:, head] = kg
@@ -193,10 +193,10 @@
     store_sides(own_ref, near_refs, kg_acc, slice(None))
 
 
-def values_kernel(pieces, g_ref, w_ref, own_ref, *refs):
-    near_refs, vg_acc = refs[:-1], refs[-1]
+def values_kernel(pieces, g_ref, w_ref, near_ref, far_ref, vg_acc):
     j, i = pl.program_id(0), pl.program_id(1)
     head = pl.ds(pl.multiple_of(j * HEAD_SIZE, HEAD_SIZE), HEAD_SIZE)
+    half = near_ref.shape[0]
     stack = [g_ref[:, h * HEAD_SIZE : (h + 1) * HEAD_SIZE] for h in range(HEADS_PER_KEY)]
     vg = dot(w_ref[...], jnp.concatenate(stack, axis=0))
 
@@ -210,7 +210,8 @@
 
     @pl.when(i == pl.num_programs(1) - 1)
     def _():
-        store_sides(own_ref, near_refs, vg_acc, head)
+        near_ref[:, head] = vg_acc[:half, :]
+        far_ref[:, head] = vg_acc[half:, :].astype(BF16)
 
 
 def store_rows(out_ref, left, inner_ref):
@@ -262,27 +263,27 @@
             1.0,
             "scores",
             in_specs=[smem, smem, VMEM, VMEM] + [VMEM] * self.pieces,
-            out_specs=[VMEM] * (5 + len(self.terms)),
-            out_shape=[self.inner] * 3 + [heads] * 2 + self.terms,
+            out_specs=[VMEM] * (4 + len(self.terms)),
+            out_shape=[self.inner] * 2 + [heads] * 2 + self.terms,
             scratch_shapes=[
                 pltpu.VMEM((self.all_rows, self.width), F32),
-                pltpu.VMEM((self.all_rows, 2 * TILE), F32),
+                pltpu.VMEM((self.all_rows, TILE), F32),
             ],
         )(length, frames, queries, gradients, *keys_values)
-        return out[:5], out[5], out[6:]
+        return out[:4], out[4], out[5:]
 
     def values(self, gradients, weights):
-        out = self.call(
+        half = (self.all_rows // 2, self.width)
+        return self.call(
             values_kernel,
             0.1,
             "values",
             grid=(KEY_HEADS, self.tiles),
             in_specs=[self.text_block, self.inner_block],
-            out_specs=[pl.BlockSpec(self.sides, lambda j, i: (0, 0))] * len(self.terms),
-            out_shape=self.terms,
+            out_specs=[pl.BlockSpec(half, lambda j, i: (0, 0))] * 2,
+            out_shape=[jax.ShapeDtypeStruct(half, F32), jax.ShapeDtypeStruct(half, BF16)],
             scratch_shapes=[pltpu.VMEM((self.all_rows, HEAD_SIZE), F32)],
         )(in_hbm(gradients), weights)
-        return out[0], out[1:]
 
     def over_rows(self, inner, heads, name):
         return self.call(
@@ -346,22 +347,24 @@
     return out[0], out[1], out[2], out[3:]
 
 
-def onward_kernel(far_ref, *refs):
-    value_refs, out_refs = refs[: len(refs) // 2], refs[len(refs) // 2 :]
+def onward_kernel(far_ref, value_ref, came_ref, own_ref, *refs):
     rows, columns = far_ref.shape
-    for value_ref, ref in zip(value_refs, out_refs):
-        ref[:, :columns] = far_ref[...]
-        ref[:, columns : 2 * columns] = value_ref[:rows, :]
-        ref[:, 2 * columns :] = value_ref[rows:, :]
-
-
-def onward(far, values):
-    shape = (far.shape[0], 3 * far.shape[1])
-    return in_vmem(onward_kernel, "onward", [(shape, BF16)] * len(values), far, *values)
-
-
-def add_value_kernel(near_ref, far_ref, out_ref):
-    out_ref[...] = (near_ref[...] + far_ref[...].astype(F32)).astype(BF16)
+    for m, ref in enumerate((own_ref, *refs)):
+        part = slice(m * rows, (m + 1) * rows)
+        total = value_ref[part, :] + came_ref[part, :].astype(F32)
+        if m == 0:
+            ref[...] = total
+        else:
+            ref[:, :columns] = far_ref[...]
+            ref[:, columns:] = total.astype(BF16)
+
+
+def onward(far, values, came):
+    rows, columns = far.shape
+    shapes = [((rows, columns), F32)]
+    shapes += [((rows, 2 * columns), BF16)] * (values.shape[0] // rows - 1)
+    out = in_vmem(onward_kernel, "onward", shapes, far, values, came)
+    return out[0], out[1:]
 
 
 def turn_kernel(columns, own_ref, *refs):
@@ -382,11 +385,9 @@
     return in_vmem(kernel, "turn_visual", [(shape, BF16)], own, *came)[0]
 
 
-def weight_kernel(order, visual_ref, value_ref, *refs):
-    pieces = len(order)
-    kg_refs = [refs[order.index(m)] for m in range(pieces)]
-    keep_ref, send_ref, near_ref, far_ref = refs[pieces:]
-    rows, width = near_ref.shape
+def weight_kernel(visual_ref, value_ref, *refs):
+    kg_refs, (keep_ref, send_ref, grad_ref) = refs[:-3], refs[-3:]
+    width = grad_ref.shape[1]
     product = dot(visual_ref[...], jnp.concatenate([r[:, :width] for r in kg_refs], axis=0))
     count, share, _ = keep_ref.shape
     core = lax.axis_index("dp") % 2 == 0
@@ -395,22 +396,17 @@
         odd = product[(2 * n + 1) * share : (2 * n + 2) * share]
         keep_ref[n] = jnp.where(core, even, odd)
         send_ref[n] = jnp.where(core, odd, even).astype(BF16)
-    for side, ref in enumerate((near_ref, far_ref)):
-        total = value_ref[side * rows : (side + 1) * rows, :]
-        for kg_ref in kg_refs[pieces // 2 + 1 :]:
-            total += kg_ref[:, (1 + side) * width : (2 + side) * width].astype(F32)
-        ref[...] = total.astype(ref.dtype)
+    total = value_ref[...]
+    for ref in kg_refs[len(kg_refs) // 2 + 1 :]:
+        total += ref[:, width:].astype(F32)
+    grad_ref[...] = total.astype(BF16)
 
 
 def weight_terms(samples, visual, value_own, key_grads):
     rows, width = key_grads[0].shape
-    middle = len(key_grads) // 2
-    order = [0, *range(middle + 1, 2 * middle), *range(middle - 1, 0, -1), middle]
     half = ((samples // 2, visual.shape[0] // samples, width), F32)
-    shapes = [half, (half[0], BF16), ((rows, width), F32), ((rows, width), BF16)]
-    kernel = functools.partial(weight_kernel, order)
-    ordered = [key_grads[m] for m in order]
-    return in_vmem(kernel, "weight_terms", shapes, visual, value_own, *ordered)
+    shapes = [half, (half[0], BF16), ((rows, width), BF16)]
+    return in_vmem(weight_kernel, "weight_terms", shapes, visual, value_own, *key_grads)
 
 
 def halve_kernel(bit, kept_ref, came_ref, keep_ref, send_ref):
@@ -434,18 +430,19 @@
     visual, half = visual_rows[0], blocks // 2
 
     own, visual_near, visual_far = project(blocks, visual, key_weight, value_matrix[0])
-    keys_values = gather(own)
+    keys_values, _ = gather(own)
     visual_far = swap(visual_far, "blk", half)
     attention = Attention(queries[0], blocks, visual.shape[0])
     inner, key_own, key_near = attention.scores(
         visual_len, frame_end, queries[0], output_gradient[0], keys_values
     )
-    weights, again, dscores, keys, values = inner
+    weights, dscores, keys, values = inner
     key_near, visual_far = tie((key_near, visual_far))
 
     key_near = near_exchange(key_near)
-    value_own, value_near = attention.values(output_gradient[0], weights)
-    key_own, value_own = tie((key_own, value_own))
+    value_near, value_far = attention.values(output_gradient[0], weights)
+    value_far = swap(value_far, "blk", half)
+    key_own, value_near = tie((key_own, value_near))
     key_sum, key_far = near_sums(key_own, key_near, "key_sums")
     key_sum, dscores = tie((key_sum, dscores))
     key_far = swap(key_far, "blk", half)
@@ -453,20 +450,16 @@
     key_sum, query_grad = tie((key_sum, query_grad))
     key_grad, key_again, visual_own, near = add_far(key_sum, key_far, visual_near, visual_far)
 
-    key_grads = gather(key_grad, near, lambda far: onward(far, value_near))
+    key_grads, value_own = gather(key_grad, near, lambda far: onward(far, value_near, value_far))
     key_grads[0] = key_again
-    attn_out = attention.over_rows(again, values, "output")
+    attn_out = attention.over_rows(weights, values, "output")
     visual_columns = turn(key_grad.shape[1], visual_own, key_grads[1:half])
     visual_columns, attn_out = tie((visual_columns, attn_out))
-    kept, sent, value_sum, value_far = weight_terms(samples, visual_columns, value_own, key_grads)
-    value_far = swap(value_far, "blk", half)
+    kept, sent, value_grad = weight_terms(samples, visual_columns, value_own, key_grads)
     came, bit = swap(sent, "dp", 1), 1
     while kept.shape[0] > 1:
         kept, sent = halve(bit, kept, came)
         came, bit = swap(sent, "dp", 1 << bit), bit + 1
-    shape = [(value_far.shape, BF16)]
-    value_grad = in_vmem(add_value_kernel, "value_grad", shape, value_sum, value_far)[0]
-    came, value_grad = tie((came, value_grad))
     weight_grad = kept[0] + came[0].astype(F32)
     return attn_out[None], query_grad[None], value_grad[None], weight_grad
 

time: 60.7 us -> 63.4 us (1.044)
  waiting for transfers between devices: 8.49 us -> 12.9 us
  starting transfers between devices: 32.2 us -> 29.6 us
  Pallas kernels: 17.6 us -> 18.6 us
    ppermute x22, waiting for transfers between devices: 8.49 us -> 12.9 us  [swap(): return lax.ppermute(x, axis, [(i, i ^ mask) for i in range(size)])]
    ppermute x22, starting transfers between devices: 32.2 us -> 29.6 us  [swap(): return lax.ppermute(x, axis, [(i, i ^ mask) for i in range(size)])]
    pallas_call x1, Pallas kernels: 2.98 us -> 3.79 us  [project(): pl.pallas_call(functools.partial(project_kernel, streams), grid=(steps,),...]
  transfers between devices with their start and end apart: 22 -> 22, of which waited for: 7 -> 6; matrix products, arithmetic and copies ran while one was open for 0% -> 0% of each run, Pallas kernels for 23% -> 22%
where the time goes in v12:
time: 63.4 us; the launch traced here: 63.2 us
  starting transfers between devices  29.6 us (47%)
  Pallas kernels  18.6 us (29%)
  waiting for transfers between devices  12.9 us (20%)
  between operations  1.42 us (2%)
  other arithmetic  0.74 us (1%)
    ppermute x22, starting transfers between devices, swap(): return lax.ppermute(x, axis, [(i, i ^ mask) for i in range(size)])  29.6 us
    ppermute x22, waiting for transfers between devices, swap(): return lax.ppermute(x, axis, [(i, i ^ mask) for i in range(size)])  12.9 us
    pallas_call x1, Pallas kernels, scores(): self.call(scores_kernel, 1.0, 'scores', in_specs=[smem, smem, VMEM, VMEM]...  5.66 us
    pallas_call x2, Pallas kernels, over_rows(): self.call(rows_kernel, 0.1, name, grid=(KEY_HEADS, self.tiles), in_specs=...  5.12 us
    pallas_call x1, Pallas kernels, project(): pl.pallas_call(functools.partial(project_kernel, streams), grid=(steps,),...  3.79 us
    pallas_call x1, Pallas kernels, values(): self.call(values_kernel, 0.1, 'values', grid=(KEY_HEADS, self.tiles), in_...  2.85 us
  transfers between devices with their start and end apart: 22, of which 6 were waited for; matrix products, arithmetic and copies ran while one was open for 0% of the time, Pallas kernels for 22%

profile of v12, /device:TPU:0, one launch (start us, length us, event | category | flops | bytes accessed | tf_op | source)
XLA Modules:
  0.0 63.2 jit_solution(14590228184362041181)
XLA Ops:
  0.7 3.8 %project.1 = (bf16[32,1024]{1,0:T(8,128)(2,1)S(1)}, bf16[128,512]{1,0:T(8,128)(2,1)S(1)}, bf16[128,512]{1,0:T(8,128)(2,1)S(1)}) custom-call(bf16[32,4096]{1,0:T(8,128)(2,1)} %bitcast.14, bf16[4096,512]{1,0:T(8,128)(2,1)} %refs_3_.1, bf16[4096,512]{1,0:T(8,128)(2,1)} %refs_3_.1, bf16[4096,512]{1,0:T(8,128)(2,1)} %refs_3_.1, bf16[4096,512]{1,0:T(8,128)(2,1)} %refs_3_.1, ...), custom_call_target="tpu_custom_call" | custom-call | flops 134217728 | bytes 4194304 | tf_op jit(solution)/shard_map/project/pallas_call | solution.py:94
  4.5 4.1 %collective-permute-start.3 = (bf16[32,1024]{1,0:T(8,128)(2,1)S(1)}, bf16[32,1024]{1,0:T(8,128)(2,1)S(1)}, u32[]{:S(2)}, u32[]{:S(2)}) collective-permute-start(bf16[32,1024]{1,0:T(8,128)(2,1)S(1)} %get-tuple-element.46.refs_0_), channel_id=1, source_target_pairs={{0,16},{4,20},{8,24},{12,28},{16,0},{20,4},{24,8},{28,12},{1,17},{... | collective-permute-start | bytes 196616 | tf_op jit(solution)/shard_map/ppermute | solution.py:28
  8.6 1.5 %collective-permute-start = (bf16[32,1024]{1,0:T(8,128)(2,1)S(1)}, bf16[32,1024]{1,0:T(8,128)(2,1)S(1)}, u32[]{:S(2)}, u32[]{:S(2)}) collective-permute-start(bf16[32,1024]{1,0:T(8,128)(2,1)S(1)} %get-tuple-element.46.refs_0_), channel_id=1, source_target_pairs={{0,4},{4,0},{8,12},{12,8},{16,20},{20,16},{24,28},{28,24},{1,5},{5... | collective-permute-start | bytes 196616 | tf_op jit(solution)/shard_map/ppermute | solution.py:28
  10.1 1.6 %collective-permute-start.1 = (bf16[32,1024]{1,0:T(8,128)(2,1)S(1)}, bf16[32,1024]{1,0:T(8,128)(2,1)S(1)}, u32[]{:S(2)}, u32[]{:S(2)}) collective-permute-start(bf16[32,1024]{1,0:T(8,128)(2,1)S(1)} %get-tuple-element.46.refs_0_), channel_id=1, source_target_pairs={{0,8},{4,12},{8,0},{12,4},{16,24},{20,28},{24,16},{28,20},{1,9},{5... | collective-permute-start | bytes 196616 | tf_op jit(solution)/shard_map/ppermute | solution.py:28
  11.7 0.4 collective-permute-start.2
  12.1 1.5 %collective-permute-start.4 = (bf16[32,1024]{1,0:T(8,128)(2,1)S(1)}, bf16[32,1024]{1,0:T(8,128)(2,1)S(1)}, u32[]{:S(2)}, u32[]{:S(2)}) collective-permute-start(bf16[32,1024]{1,0:T(8,128)(2,1)S(1)} %collective-permute-done.3.refs_4_), channel_id=1, source_target_pairs={{0,4},{4,0},{8,12},{12,8},{16,20},{20,16},{24,28},{28,24},{1,5},{5... | collective-permute-start | bytes 196616 | tf_op jit(solution)/shard_map/ppermute | solution.py:28
  13.6 1.6 %collective-permute-start.5 = (bf16[32,1024]{1,0:T(8,128)(2,1)S(1)}, bf16[32,1024]{1,0:T(8,128)(2,1)S(1)}, u32[]{:S(2)}, u32[]{:S(2)}) collective-permute-start(bf16[32,1024]{1,0:T(8,128)(2,1)S(1)} %collective-permute-done.3.refs_4_), channel_id=1, source_target_pairs={{0,8},{4,12},{8,0},{12,4},{16,24},{20,28},{24,16},{28,20},{1,9},{5... | collective-permute-start | bytes 196616 | tf_op jit(solution)/shard_map/ppermute | solution.py:28
  15.2 1.0 %collective-permute-start.6 = (bf16[32,1024]{1,0:T(8,128)(2,1)S(1)}, bf16[32,1024]{1,0:T(8,128)(2,1)S(1)}, u32[]{:S(2)}, u32[]{:S(2)}) collective-permute-start(bf16[32,1024]{1,0:T(8,128)(2,1)S(1)} %collective-permute-done.3.refs_4_), channel_id=1, source_target_pairs={{0,12},{4,8},{8,4},{12,0},{16,28},{20,24},{24,20},{28,16},{1,13},{... | collective-permute-start | bytes 196616 | tf_op jit(solution)/shard_map/ppermute | solution.py:28
  16.8 1.6 %collective-permute-start.7 = (bf16[128,512]{1,0:T(8,128)(2,1)S(1)}, bf16[128,512]{1,0:T(8,128)(2,1)S(1)}, u32[]{:S(2)}, u32[]{:S(2)}) collective-permute-start(bf16[128,512]{1,0:T(8,128)(2,1)S(1)} %get-tuple-element.54), channel_id=1, source_target_pairs={{0,16},{4,20},{8,24},{12,28},{16,0},{20,4},{24,8},{28,12},{1,17},{... | collective-permute-start | bytes 393224 | tf_op jit(solution)/shard_map/ppermute | solution.py:28
  18.5 2.8 %collective-permute-done.6.refs_7_ = bf16[32,1024]{1,0:T(8,128)(2,1)S(1)} collective-permute-done((bf16[32,1024]{1,0:T(8,128)(2,1)S(1)}, bf16[32,1024]{1,0:T(8,128)(2,1)S(1)}, u32[]{:S(2)}, u32[]{:S(2)}) %collective-permute-start.6) | collective-permute-done | bytes 65568 | tf_op jit(solution)/shard_map/ppermute | solution.py:28
  21.3 5.7 %scores.1 = (bf16[256,4096]{1,0:T(8,128)(2,1)S(1)}, bf16[256,4096]{1,0:T(8,128)(2,1)S(1)}, bf16[256,512]{1,0:T(8,128)(2,1)S(1)}, bf16[256,512]{1,0:T(8,128)(2,1)...) custom-call(s32[1]{0:T(128)S(6)} %copy.11.length_ref, ...), custom_call_target="tpu_custom_call" | custom-call | flops 1610612736 | bytes 4194304 | tf_op jit(solution)/shard_map/scores/pallas_call | solution.py:261
  26.9 0.8 %collective-permute-start.8 = (bf16[64,512]{1,0:T(8,128)(2,1)S(1)}, bf16[64,512]{1,0:T(8,128)(2,1)S(1)}, u32[]{:S(2)}, u32[]{:S(2)}) collective-permute-start(bf16[64,512]{1,0:T(8,128)(2,1)S(1)} %get-tuple-element.55), channel_id=1, source_target_pairs={{0,4},{4,0},{8,12},{12,8},{16,20},{20,16},{24,28},{28,24},{1,5},{5... | collective-permute-start | bytes 196616 | tf_op jit(solution)/shard_map/ppermute | solution.py:28
  28.1 2.4 %collective-permute-start.10 = (bf16[64,512]{1,0:T(8,128)(2,1)S(1)}, bf16[64,512]{1,0:T(8,128)(2,1)S(1)}, u32[]{:S(2)}, u32[]{:S(2)}) collective-permute-start(bf16[64,512]{1,0:T(8,128)(2,1)S(1)} %get-tuple-element.57), channel_id=1, source_target_pairs={{0,12},{4,8},{8,4},{12,0},{16,28},{20,24},{24,20},{28,16},{1,13},{... | collective-permute-start | bytes 196616 | tf_op jit(solution)/shard_map/ppermute | solution.py:28
  30.5 2.9 %values.1 = (f32[128,512]{1,0:T(8,128)S(1)}, bf16[128,512]{1,0:T(8,128)(2,1)S(1)}) custom-call(bf16[128,4096]{1,0:T(8,128)(2,1)} %bitcast.9, bf16[256,4096]{1,0:T(8,128)(2,1)S(1)} %get-tuple-element.48.w_ref.inner_ref), custom_call_target="tpu_custom_call" | custom-call | flops 161061280 | bytes 419430 | tf_op jit(solution)/shard_map/values/pallas_call | solution.py:277
  33.4 2.0 %collective-permute-start.16 = (bf16[128,512]{1,0:T(8,128)(2,1)S(1)}, bf16[128,512]{1,0:T(8,128)(2,1)S(1)}, u32[]{:S(2)}, u32[]{:S(2)}) collective-permute-start(bf16[128,512]{1,0:T(8,128)(2,1)S(1)} %get-tuple-element.77), channel_id=1, source_target_pairs={{0,16},{4,20},{8,24},{12,28},{16,0},{20,4},{24,8},{28,12},{1,17},{... | collective-permute-start | bytes 393224 | tf_op jit(solution)/shard_map/ppermute | solution.py:28
  35.4 1.1 %collective-permute-start.11 = (bf16[32,512]{1,0:T(8,128)(2,1)S(1)}, bf16[32,512]{1,0:T(8,128)(2,1)S(1)}, u32[]{:S(2)}, u32[]{:S(2)}) collective-permute-start(bf16[32,512]{1,0:T(8,128)(2,1)S(1)} %get-tuple-element.64), channel_id=1, source_target_pairs={{0,16},{4,20},{8,24},{12,28},{16,0},{20,4},{24,8},{28,12},{1,17},{... | collective-permute-start | bytes 98312 | tf_op jit(solution)/shard_map/ppermute | solution.py:28
  36.5 2.6 %query_grad.1 = bf16[128,4096]{1,0:T(8,128)(2,1)} custom-call(bf16[256,4096]{1,0:T(8,128)(2,1)S(1)} %get-tuple-element.61.inner_ref, bf16[256,512]{1,0:T(8,128)(2,1)S(1)} %get-tuple-element.62.head_ref), custom_call_target="tpu_custom_call" | custom-call | flops 161061280 | bytes 419430 | tf_op jit(solution)/shard_map/query_grad/pallas_call | solution.py:289
  39.0 2.2 %collective-permute-done.11.far_ref = bf16[32,512]{1,0:T(8,128)(2,1)S(1)} collective-permute-done((bf16[32,512]{1,0:T(8,128)(2,1)S(1)}, bf16[32,512]{1,0:T(8,128)(2,1)S(1)}, u32[]{:S(2)}, u32[]{:S(2)}) %collective-permute-start.11) | collective-permute-done | bytes 32800 | tf_op jit(solution)/shard_map/ppermute | solution.py:28
  41.2 0.9 %collective-permute-start.12 = (bf16[32,1536]{1,0:T(8,128)(2,1)S(1)}, bf16[32,1536]{1,0:T(8,128)(2,1)S(1)}, u32[]{:S(2)}, u32[]{:S(2)}) collective-permute-start(bf16[32,1536]{1,0:T(8,128)(2,1)S(1)} %get-tuple-element.68), channel_id=1, source_target_pairs={{0,4},{4,0},{8,12},{12,8},{16,20},{20,16},{24,28},{28,24},{1,5},{5... | collective-permute-start | bytes 294920 | tf_op jit(solution)/shard_map/ppermute | solution.py:28
  42.1 0.6 %collective-permute-start.15 = (bf16[32,512]{1,0:T(8,128)(2,1)S(1)}, bf16[32,512]{1,0:T(8,128)(2,1)S(1)}, u32[]{:S(2)}, u32[]{:S(2)}) collective-permute-start(bf16[32,512]{1,0:T(8,128)(2,1)S(1)} %get-tuple-element.75), channel_id=1, source_target_pairs={{0,16},{4,20},{8,24},{12,28},{16,0},{20,4},{24,8},{28,12},{1,17},{... | collective-permute-start | bytes 98312 | tf_op jit(solution)/shard_map/ppermute | solution.py:28
  42.8 2.9 %collective-permute-start.13 = (bf16[32,1536]{1,0:T(8,128)(2,1)S(1)}, bf16[32,1536]{1,0:T(8,128)(2,1)S(1)}, u32[]{:S(2)}, u32[]{:S(2)}) collective-permute-start(bf16[32,1536]{1,0:T(8,128)(2,1)S(1)} %get-tuple-element.69), channel_id=1, source_target_pairs={{0,8},{4,12},{8,0},{12,4},{16,24},{20,28},{24,16},{28,20},{1,9},{5... | collective-permute-start | bytes 294920 | tf_op jit(solution)/shard_map/ppermute | solution.py:28
  45.8 1.4 %collective-permute-done.15.far_ref.refs_4_ = bf16[32,512]{1,0:T(8,128)(2,1)S(1)} collective-permute-done((bf16[32,512]{1,0:T(8,128)(2,1)S(1)}, bf16[32,512]{1,0:T(8,128)(2,1)S(1)}, u32[]{:S(2)}, u32[]{:S(2)}) %collective-permute-start.15) | collective-permute-done | bytes 32800 | tf_op jit(solution)/shard_map/ppermute | solution.py:28
  47.2 1.0 %collective-permute-start.17 = (bf16[32,1024]{1,0:T(8,128)(2,1)S(1)}, bf16[32,1024]{1,0:T(8,128)(2,1)S(1)}, u32[]{:S(2)}, u32[]{:S(2)}) collective-permute-start(bf16[32,1024]{1,0:T(8,128)(2,1)S(1)} %get-tuple-element.80), channel_id=1, source_target_pairs={{0,4},{4,0},{8,12},{12,8},{16,20},{20,16},{24,28},{28,24},{1,5},{5... | collective-permute-start | bytes 196616 | tf_op jit(solution)/shard_map/ppermute | solution.py:28
  48.3 1.0 %collective-permute-start.18 = (bf16[32,1024]{1,0:T(8,128)(2,1)S(1)}, bf16[32,1024]{1,0:T(8,128)(2,1)S(1)}, u32[]{:S(2)}, u32[]{:S(2)}) collective-permute-start(bf16[32,1024]{1,0:T(8,128)(2,1)S(1)} %get-tuple-element.81), channel_id=1, source_target_pairs={{0,8},{4,12},{8,0},{12,4},{16,24},{20,28},{24,16},{28,20},{1,9},{5... | collective-permute-start | bytes 196616 | tf_op jit(solution)/shard_map/ppermute | solution.py:28
  49.3 1.5 %collective-permute-start.19 = (bf16[32,1024]{1,0:T(8,128)(2,1)S(1)}, bf16[32,1024]{1,0:T(8,128)(2,1)S(1)}, u32[]{:S(2)}, u32[]{:S(2)}) collective-permute-start(bf16[32,1024]{1,0:T(8,128)(2,1)S(1)} %get-tuple-element.82), channel_id=1, source_target_pairs={{0,12},{4,8},{8,4},{12,0},{16,28},{20,24},{24,20},{28,16},{1,13},{... | collective-permute-start | bytes 196616 | tf_op jit(solution)/shard_map/ppermute | solution.py:28
  50.8 2.6 %output.1 = bf16[128,4096]{1,0:T(8,128)(2,1)} custom-call(bf16[256,4096]{1,0:T(8,128)(2,1)S(1)} %get-tuple-element.48.w_ref.inner_ref, bf16[256,512]{1,0:T(8,128)(2,1)S(1)} %get-tuple-element.71.head_ref), custom_call_target="tpu_custom_call" | custom-call | flops 161061280 | bytes 419430 | tf_op jit(solution)/shard_map/output/pallas_call | solution.py:289
  53.5 0.9 %collective-permute-done.19.refs_7_ = bf16[32,1024]{1,0:T(8,128)(2,1)S(1)} collective-permute-done((bf16[32,1024]{1,0:T(8,128)(2,1)S(1)}, bf16[32,1024]{1,0:T(8,128)(2,1)S(1)}, u32[]{:S(2)}, u32[]{:S(2)}) %collective-permute-start.19) | collective-permute-done | bytes 65568 | tf_op jit(solution)/shard_map/ppermute | solution.py:28
  54.4 0.9 %weight_terms.1 = (f32[2,128,512]{2,1,0:T(8,128)S(1)}, bf16[2,128,512]{2,1,0:T(8,128)(2,1)S(1)}, bf16[32,512]{1,0:T(8,128)(2,1)}) custom-call(bf16[512,256]{1,0:T(8,128)(2,1)S(1)} %turn_visual.1.visual_ref, f32[32,512]{1,0:T(8,128)S(1)} %get-tuple-element.78.value_ref, bf16[32,512]{1,0:T(8,128)(2,1)S(1)} %get-tuple-element.79.refs_0_, ...), custom_call_target="tpu_custom_call" | custom-call | tf_op jit(solution)/shard_map/weight_terms/pallas_call | solution.py:301
  55.3 1.5 %collective-permute-done.20.came_ref = bf16[2,128,512]{2,1,0:T(8,128)(2,1)S(1)} collective-permute-done((bf16[2,128,512]{2,1,0:T(8,128)(2,1)S(1)}, bf16[2,128,512]{2,1,0:T(8,128)(2,1)S(1)}, u32[]{:S(2)}, u32[]{:S(2)}) %collective-permute-start.20) | collective-permute-done | bytes 262176 | tf_op jit(solution)/shard_map/ppermute | solution.py:28
  56.9 1.6 %collective-permute-start.21 = (bf16[1,128,512]{2,1,0:T(8,128)(2,1)S(1)}, bf16[1,128,512]{2,1,0:T(8,128)(2,1)S(1)}, u32[]{:S(2)}, u32[]{:S(2)}) collective-permute-start(bf16[1,128,512]{2,1,0:T(8,128)(2,1)S(1)} %get-tuple-element.87), channel_id=1, source_target_pairs={{0,2},{1,3},{2,0},{3,1},{4,6},{5,7},{6,4},{7,5},{8,10},{9,11},{10,... | collective-permute-start | bytes 393224 | tf_op jit(solution)/shard_map/ppermute | solution.py:28
  58.5 4.0 %collective-permute-done.21 = bf16[1,128,512]{2,1,0:T(8,128)(2,1)S(1)} collective-permute-done((bf16[1,128,512]{2,1,0:T(8,128)(2,1)S(1)}, bf16[1,128,512]{2,1,0:T(8,128)(2,1)S(1)}, u32[]{:S(2)}, u32[]{:S(2)}) %collective-permute-start.21) | collective-permute-done | bytes 131104 | tf_op jit(solution)/shard_map/ppermute | solution.py:28
  62.5 0.7 %add_bitcast_fusion = f32[128,512]{1,0:T(8,128)} fusion(f32[1,128,512]{2,1,0:T(8,128)S(1)} %get-tuple-element.86, bf16[1,128,512]{2,1,0:T(8,128)(2,1)S(1)} %collective-permute-done.21), kind=kLoop, calls=%fused_computation | loop fusion | flops 131072 | bytes 655360 | tf_op jit(solution)/shard_map/add | solution.py:463
  (30 shorter events, 0.8 us)
Async XLA Ops:
  0.6 20.6 %copy-start = (bf16[1,128,4096]{2,1,0:T(8,128)(2,1)S(1)}, bf16[1,128,4096]{2,1,0:T(8,128)(2,1)}, u32[]{:S(2)}) copy-start(bf16[1,128,4096]{2,1,0:T(8,128)(2,1)} %param.11) | copy-start | bytes 3145732
  0.6 20.6 %copy-start.1 = (bf16[1,128,4096]{2,1,0:T(8,128)(2,1)S(1)}, bf16[1,128,4096]{2,1,0:T(8,128)(2,1)}, u32[]{:S(2)}) copy-start(bf16[1,128,4096]{2,1,0:T(8,128)(2,1)} %param.10) | copy-start | bytes 3145732
  0.7 20.6 %copy-start.2 = (s32[1,8]{1,0:T(1,128)S(1)}, s32[1,8]{1,0:T(1,128)}, u32[]{:S(2)}) copy-start(s32[1,8]{1,0:T(1,128)} %frame_ref.1) | copy-start | bytes 100
  4.5 7.6 %collective-permute-start.3 = (bf16[32,1024]{1,0:T(8,128)(2,1)S(1)}, bf16[32,1024]{1,0:T(8,128)(2,1)S(1)}, u32[]{:S(2)}, u32[]{:S(2)}) collective-permute-start(bf16[32,1024]{1,0:T(8,128)(2,1)S(1)} %get-tuple-element.46.refs_0_), channel_id=1, source_target_pairs={{0,16},{4,20},{8,24},{12,28},{16,0},{20,4},{24,8},{28,12},{1,17},{... | collective-permute-start | bytes 196616 | tf_op jit(solution)/shard_map/ppermute | solution.py:28
  8.6 6.6 %collective-permute-start = (bf16[32,1024]{1,0:T(8,128)(2,1)S(1)}, bf16[32,1024]{1,0:T(8,128)(2,1)S(1)}, u32[]{:S(2)}, u32[]{:S(2)}) collective-permute-start(bf16[32,1024]{1,0:T(8,128)(2,1)S(1)} %get-tuple-element.46.refs_0_), channel_id=1, source_target_pairs={{0,4},{4,0},{8,12},{12,8},{16,20},{20,16},{24,28},{28,24},{1,5},{5... | collective-permute-start | bytes 196616 | tf_op jit(solution)/shard_map/ppermute | solution.py:28
  10.1 6.7 %collective-permute-start.1 = (bf16[32,1024]{1,0:T(8,128)(2,1)S(1)}, bf16[32,1024]{1,0:T(8,128)(2,1)S(1)}, u32[]{:S(2)}, u32[]{:S(2)}) collective-permute-start(bf16[32,1024]{1,0:T(8,128)(2,1)S(1)} %get-tuple-element.46.refs_0_), channel_id=1, source_target_pairs={{0,8},{4,12},{8,0},{12,4},{16,24},{20,28},{24,16},{28,20},{1,9},{5... | collective-permute-start | bytes 196616 | tf_op jit(solution)/shard_map/ppermute | solution.py:28
  11.7 6.8 %collective-permute-start.2 = (bf16[32,1024]{1,0:T(8,128)(2,1)S(1)}, bf16[32,1024]{1,0:T(8,128)(2,1)S(1)}, u32[]{:S(2)}, u32[]{:S(2)}) collective-permute-start(bf16[32,1024]{1,0:T(8,128)(2,1)S(1)} %get-tuple-element.46.refs_0_), channel_id=1, source_target_pairs={{0,12},{4,8},{8,4},{12,0},{16,28},{20,24},{24,20},{28,16},{1,13},{... | collective-permute-start | bytes 196616 | tf_op jit(solution)/shard_map/ppermute | solution.py:28
  12.1 6.4 %collective-permute-start.4 = (bf16[32,1024]{1,0:T(8,128)(2,1)S(1)}, bf16[32,1024]{1,0:T(8,128)(2,1)S(1)}, u32[]{:S(2)}, u32[]{:S(2)}) collective-permute-start(bf16[32,1024]{1,0:T(8,128)(2,1)S(1)} %collective-permute-done.3.refs_4_), channel_id=1, source_target_pairs={{0,4},{4,0},{8,12},{12,8},{16,20},{20,16},{24,28},{28,24},{1,5},{5... | collective-permute-start | bytes 196616 | tf_op jit(solution)/shard_map/ppermute | solution.py:28
  13.6 4.9 %collective-permute-start.5 = (bf16[32,1024]{1,0:T(8,128)(2,1)S(1)}, bf16[32,1024]{1,0:T(8,128)(2,1)S(1)}, u32[]{:S(2)}, u32[]{:S(2)}) collective-permute-start(bf16[32,1024]{1,0:T(8,128)(2,1)S(1)} %collective-permute-done.3.refs_4_), channel_id=1, source_target_pairs={{0,8},{4,12},{8,0},{12,4},{16,24},{20,28},{24,16},{28,20},{1,9},{5... | collective-permute-start | bytes 196616 | tf_op jit(solution)/shard_map/ppermute | solution.py:28
  15.2 6.1 %collective-permute-start.6 = (bf16[32,1024]{1,0:T(8,128)(2,1)S(1)}, bf16[32,1024]{1,0:T(8,128)(2,1)S(1)}, u32[]{:S(2)}, u32[]{:S(2)}) collective-permute-start(bf16[32,1024]{1,0:T(8,128)(2,1)S(1)} %collective-permute-done.3.refs_4_), channel_id=1, source_target_pairs={{0,12},{4,8},{8,4},{12,0},{16,28},{20,24},{24,20},{28,16},{1,13},{... | collective-permute-start | bytes 196616 | tf_op jit(solution)/shard_map/ppermute | solution.py:28
  16.8 10.1 %collective-permute-start.7 = (bf16[128,512]{1,0:T(8,128)(2,1)S(1)}, bf16[128,512]{1,0:T(8,128)(2,1)S(1)}, u32[]{:S(2)}, u32[]{:S(2)}) collective-permute-start(bf16[128,512]{1,0:T(8,128)(2,1)S(1)} %get-tuple-element.54), channel_id=1, source_target_pairs={{0,16},{4,20},{8,24},{12,28},{16,0},{20,4},{24,8},{28,12},{1,17},{... | collective-permute-start | bytes 393224 | tf_op jit(solution)/shard_map/ppermute | solution.py:28
  26.9 8.4 %collective-permute-start.8 = (bf16[64,512]{1,0:T(8,128)(2,1)S(1)}, bf16[64,512]{1,0:T(8,128)(2,1)S(1)}, u32[]{:S(2)}, u32[]{:S(2)}) collective-permute-start(bf16[64,512]{1,0:T(8,128)(2,1)S(1)} %get-tuple-element.55), channel_id=1, source_target_pairs={{0,4},{4,0},{8,12},{12,8},{16,20},{20,16},{24,28},{28,24},{1,5},{5... | collective-permute-start | bytes 196616 | tf_op jit(solution)/shard_map/ppermute | solution.py:28
  27.7 7.7 %collective-permute-start.9 = (bf16[64,512]{1,0:T(8,128)(2,1)S(1)}, bf16[64,512]{1,0:T(8,128)(2,1)S(1)}, u32[]{:S(2)}, u32[]{:S(2)}) collective-permute-start(bf16[64,512]{1,0:T(8,128)(2,1)S(1)} %get-tuple-element.56), channel_id=1, source_target_pairs={{0,8},{4,12},{8,0},{12,4},{16,24},{20,28},{24,16},{28,20},{1,9},{5... | collective-permute-start | bytes 196616 | tf_op jit(solution)/shard_map/ppermute | solution.py:28
  28.1 7.3 %collective-permute-start.10 = (bf16[64,512]{1,0:T(8,128)(2,1)S(1)}, bf16[64,512]{1,0:T(8,128)(2,1)S(1)}, u32[]{:S(2)}, u32[]{:S(2)}) collective-permute-start(bf16[64,512]{1,0:T(8,128)(2,1)S(1)} %get-tuple-element.57), channel_id=1, source_target_pairs={{0,12},{4,8},{8,4},{12,0},{16,28},{20,24},{24,20},{28,16},{1,13},{... | collective-permute-start | bytes 196616 | tf_op jit(solution)/shard_map/ppermute | solution.py:28
  33.4 13.8 %collective-permute-start.16 = (bf16[128,512]{1,0:T(8,128)(2,1)S(1)}, bf16[128,512]{1,0:T(8,128)(2,1)S(1)}, u32[]{:S(2)}, u32[]{:S(2)}) collective-permute-start(bf16[128,512]{1,0:T(8,128)(2,1)S(1)} %get-tuple-element.77), channel_id=1, source_target_pairs={{0,16},{4,20},{8,24},{12,28},{16,0},{20,4},{24,8},{28,12},{1,17},{... | collective-permute-start | bytes 393224 | tf_op jit(solution)/shard_map/ppermute | solution.py:28
  35.4 5.8 %collective-permute-start.11 = (bf16[32,512]{1,0:T(8,128)(2,1)S(1)}, bf16[32,512]{1,0:T(8,128)(2,1)S(1)}, u32[]{:S(2)}, u32[]{:S(2)}) collective-permute-start(bf16[32,512]{1,0:T(8,128)(2,1)S(1)} %get-tuple-element.64), channel_id=1, source_target_pairs={{0,16},{4,20},{8,24},{12,28},{16,0},{20,4},{24,8},{28,12},{1,17},{... | collective-permute-start | bytes 98312 | tf_op jit(solution)/shard_map/ppermute | solution.py:28
  41.2 8.0 %collective-permute-start.12 = (bf16[32,1536]{1,0:T(8,128)(2,1)S(1)}, bf16[32,1536]{1,0:T(8,128)(2,1)S(1)}, u32[]{:S(2)}, u32[]{:S(2)}) collective-permute-start(bf16[32,1536]{1,0:T(8,128)(2,1)S(1)} %get-tuple-element.68), channel_id=1, source_target_pairs={{0,4},{4,0},{8,12},{12,8},{16,20},{20,16},{24,28},{28,24},{1,5},{5... | collective-permute-start | bytes 294920 | tf_op jit(solution)/shard_map/ppermute | solution.py:28
  42.1 5.1 %collective-permute-start.15 = (bf16[32,512]{1,0:T(8,128)(2,1)S(1)}, bf16[32,512]{1,0:T(8,128)(2,1)S(1)}, u32[]{:S(2)}, u32[]{:S(2)}) collective-permute-start(bf16[32,512]{1,0:T(8,128)(2,1)S(1)} %get-tuple-element.75), channel_id=1, source_target_pairs={{0,16},{4,20},{8,24},{12,28},{16,0},{20,4},{24,8},{28,12},{1,17},{... | collective-permute-start | bytes 98312 | tf_op jit(solution)/shard_map/ppermute | solution.py:28
  42.8 10.6 %collective-permute-start.13 = (bf16[32,1536]{1,0:T(8,128)(2,1)S(1)}, bf16[32,1536]{1,0:T(8,128)(2,1)S(1)}, u32[]{:S(2)}, u32[]{:S(2)}) collective-permute-start(bf16[32,1536]{1,0:T(8,128)(2,1)S(1)} %get-tuple-element.69), channel_id=1, source_target_pairs={{0,8},{4,12},{8,0},{12,4},{16,24},{20,28},{24,16},{28,20},{1,9},{5... | collective-permute-start | bytes 294920 | tf_op jit(solution)/shard_map/ppermute | solution.py:28
  45.7 7.7 %collective-permute-start.14 = (bf16[32,1536]{1,0:T(8,128)(2,1)S(1)}, bf16[32,1536]{1,0:T(8,128)(2,1)S(1)}, u32[]{:S(2)}, u32[]{:S(2)}) collective-permute-start(bf16[32,1536]{1,0:T(8,128)(2,1)S(1)} %get-tuple-element.70), channel_id=1, source_target_pairs={{0,12},{4,8},{8,4},{12,0},{16,28},{20,24},{24,20},{28,16},{1,13},{... | collective-permute-start | bytes 294920 | tf_op jit(solution)/shard_map/ppermute | solution.py:28
  47.2 6.3 %collective-permute-start.17 = (bf16[32,1024]{1,0:T(8,128)(2,1)S(1)}, bf16[32,1024]{1,0:T(8,128)(2,1)S(1)}, u32[]{:S(2)}, u32[]{:S(2)}) collective-permute-start(bf16[32,1024]{1,0:T(8,128)(2,1)S(1)} %get-tuple-element.80), channel_id=1, source_target_pairs={{0,4},{4,0},{8,12},{12,8},{16,20},{20,16},{24,28},{28,24},{1,5},{5... | collective-permute-start | bytes 196616 | tf_op jit(solution)/shard_map/ppermute | solution.py:28
  48.3 5.2 %collective-permute-start.18 = (bf16[32,1024]{1,0:T(8,128)(2,1)S(1)}, bf16[32,1024]{1,0:T(8,128)(2,1)S(1)}, u32[]{:S(2)}, u32[]{:S(2)}) collective-permute-start(bf16[32,1024]{1,0:T(8,128)(2,1)S(1)} %get-tuple-element.81), channel_id=1, source_target_pairs={{0,8},{4,12},{8,0},{12,4},{16,24},{20,28},{24,16},{28,20},{1,9},{5... | collective-permute-start | bytes 196616 | tf_op jit(solution)/shard_map/ppermute | solution.py:28
  49.3 5.2 %collective-permute-start.19 = (bf16[32,1024]{1,0:T(8,128)(2,1)S(1)}, bf16[32,1024]{1,0:T(8,128)(2,1)S(1)}, u32[]{:S(2)}, u32[]{:S(2)}) collective-permute-start(bf16[32,1024]{1,0:T(8,128)(2,1)S(1)} %get-tuple-element.82), channel_id=1, source_target_pairs={{0,12},{4,8},{8,4},{12,0},{16,28},{20,24},{24,20},{28,16},{1,13},{... | collective-permute-start | bytes 196616 | tf_op jit(solution)/shard_map/ppermute | solution.py:28
  55.3 1.5 %collective-permute-start.20 = (bf16[2,128,512]{2,1,0:T(8,128)(2,1)S(1)}, bf16[2,128,512]{2,1,0:T(8,128)(2,1)S(1)}, u32[]{:S(2)}, u32[]{:S(2)}) collective-permute-start(bf16[2,128,512]{2,1,0:T(8,128)(2,1)S(1)} %get-tuple-element.85), channel_id=1, source_target_pairs={{0,1},{1,0},{2,3},{3,2},{4,5},{5,4},{6,7},{7,6},{8,9},{9,8},{10,11... | collective-permute-start | bytes 786440 | tf_op jit(solution)/shard_map/ppermute | solution.py:28
  56.9 5.6 %collective-permute-start.21 = (bf16[1,128,512]{2,1,0:T(8,128)(2,1)S(1)}, bf16[1,128,512]{2,1,0:T(8,128)(2,1)S(1)}, u32[]{:S(2)}, u32[]{:S(2)}) collective-permute-start(bf16[1,128,512]{2,1,0:T(8,128)(2,1)S(1)} %get-tuple-element.87), channel_id=1, source_target_pairs={{0,2},{1,3},{2,0},{3,1},{4,6},{5,7},{6,4},{7,5},{8,10},{9,11},{10,... | collective-permute-start | bytes 393224 | tf_op jit(solution)/shard_map/ppermute | solution.py:28

commit v13 on v11

--- a/solution.py
+++ b/solution.py
@@ -131,8 +131,9 @@
 
 
 def scores_kernel(pieces, length_ref, frame_ref, q_ref, g_ref, *refs):
-    kv_refs, (w_ref, again_ref, ds_ref, k_ref, v_ref) = refs[:pieces], refs[pieces : pieces + 5]
-    own_ref, near_refs, (kg_acc, bias_ref) = refs[pieces + 5], refs[pieces + 6 : -2], refs[-2:]
+    kv_refs, (w_ref, ds_ref, k_ref, v_ref) = refs[:pieces], refs[pieces : pieces + 4]
+    kv_refs = (kv_refs[0], *kv_refs[:0:-1])
+    own_ref, near_refs, (kg_acc, bias_ref) = refs[pieces + 4], refs[pieces + 5 : -2], refs[-2:]
     block = lax.axis_index("blk")
     tiles = q_ref.shape[0] // TILE
     rows = kv_refs[0].shape[0]
@@ -179,9 +180,7 @@
                 offset = jnp.sum(terms, axis=0, keepdims=True) * inverse * slope
                 start = (i * KEY_HEADS + j) * span + p * pair
                 both = pl.ds(pl.multiple_of(start, HEAD_SIZE), pair)
-                weights = (shifted * inverse).astype(BF16)
-                w_ref[:, both] = weights
-                again_ref[:, both] = weights
+                w_ref[:, both] = (shifted * inverse).astype(BF16)
                 ds_stack.append((terms * slope - shifted * offset).astype(BF16))
                 ds_ref[:, both] = ds_stack[p]
             kg = dot(jnp.concatenate(ds_stack, axis=1), jnp.concatenate(q_stack, axis=0))
@@ -262,14 +261,14 @@
             1.0,
             "scores",
             in_specs=[smem, smem, VMEM, VMEM] + [VMEM] * self.pieces,
-            out_specs=[VMEM] * (5 + len(self.terms)),
-            out_shape=[self.inner] * 3 + [heads] * 2 + self.terms,
+            out_specs=[VMEM] * (4 + len(self.terms)),
+            out_shape=[self.inner] * 2 + [heads] * 2 + self.terms,
             scratch_shapes=[
                 pltpu.VMEM((self.all_rows, self.width), F32),
                 pltpu.VMEM((self.all_rows, 2 * TILE), F32),
             ],
-        )(length, frames, queries, gradients, *keys_values)
-        return out[:5], out[5], out[6:]
+        )(length, frames, queries, gradients, keys_values[0], *keys_values[:0:-1])
+        return out[:4], out[4], out[5:]
 
     def values(self, gradients, weights):
         out = self.call(
@@ -296,9 +295,10 @@
         )(inner, heads)
 
 
-def in_vmem(kernel, name, out_shape, *arrays):
+def in_vmem(kernel, name, out_shape, *arrays, cost=None):
     return pl.pallas_call(
         kernel,
+        cost_estimate=cost,
         in_specs=[VMEM] * len(arrays),
         out_specs=[VMEM] * len(out_shape),
         out_shape=[jax.ShapeDtypeStruct(*shape) for shape in out_shape],
@@ -405,7 +405,7 @@
 def weight_terms(samples, visual, value_own, key_grads):
     rows, width = key_grads[0].shape
     middle = len(key_grads) // 2
-    order = [0, *range(middle + 1, 2 * middle), *range(middle - 1, 0, -1), middle]
+    order = [0, *range(2 * middle - 1, middle, -1), *range(middle - 1, 0, -1), middle]
     half = ((samples // 2, visual.shape[0] // samples, width), F32)
     shapes = [half, (half[0], BF16), ((rows, width), F32), ((rows, width), BF16)]
     kernel = functools.partial(weight_kernel, order)
@@ -440,13 +440,13 @@
     inner, key_own, key_near = attention.scores(
         visual_len, frame_end, queries[0], output_gradient[0], keys_values
     )
-    weights, again, dscores, keys, values = inner
+    weights, dscores, keys, values = inner
     key_near, visual_far = tie((key_near, visual_far))
 
     key_near = near_exchange(key_near)
     value_own, value_near = attention.values(output_gradient[0], weights)
     key_own, value_own = tie((key_own, value_own))
-    key_sum, key_far = near_sums(key_own, key_near, "key_sums")
+    key_sum, key_far = near_sums(key_own, key_near[::-1], "key_sums")
     key_sum, dscores = tie((key_sum, dscores))
     key_far = swap(key_far, "blk", half)
     query_grad = attention.over_rows(dscores, keys, "query_grad")
@@ -455,7 +455,7 @@
 
     key_grads = gather(key_grad, near, lambda far: onward(far, value_near))
     key_grads[0] = key_again
-    attn_out = attention.over_rows(again, values, "output")
+    attn_out = attention.over_rows(weights, values, "output")
     visual_columns = turn(key_grad.shape[1], visual_own, key_grads[1:half])
     visual_columns, attn_out = tie((visual_columns, attn_out))
     kept, sent, value_sum, value_far = weight_terms(samples, visual_columns, value_own, key_grads)
@@ -465,7 +465,10 @@
         kept, sent = halve(bit, kept, came)
         came, bit = swap(sent, "dp", 1 << bit), bit + 1
     shape = [(value_far.shape, BF16)]
-    value_grad = in_vmem(add_value_kernel, "value_grad", shape, value_sum, value_far)[0]
+    cost = pl.CostEstimate(flops=4 * 10**9, bytes_accessed=2**24, transcendentals=0)
+    value_grad = in_vmem(
+        add_value_kernel, "value_grad", shape, value_sum, value_far, cost=cost
+    )[0]
     came, value_grad = tie((came, value_grad))
     weight_grad = kept[0] + came[0].astype(F32)
     return attn_out[None], query_grad[None], value_grad[None], weight_grad

time: 60.7 us -> 58.5 us (0.964)
  waiting for transfers between devices: 8.49 us -> 7.36 us
  starting transfers between devices: 32.2 us -> 31.4 us
    ppermute x22, waiting for transfers between devices: 8.49 us -> 7.36 us  [swap(): return lax.ppermute(x, axis, [(i, i ^ mask) for i in range(size)])]
    ppermute x22, starting transfers between devices: 32.2 us -> 31.4 us  [swap(): return lax.ppermute(x, axis, [(i, i ^ mask) for i in range(size)])]
  transfers between devices with their start and end apart: 22 -> 22, of which waited for: 7 -> 6; matrix products, arithmetic and copies ran while one was open for 0% -> 0% of each run, Pallas kernels for 23% -> 24%
where the time goes in v13:
time: 58.5 us; the launch traced here: 58.4 us
  starting transfers between devices  31.4 us (54%)
  Pallas kernels  17.4 us (30%)
  waiting for transfers between devices  7.36 us (13%)
  between operations  1.46 us (2%)
  other arithmetic  0.73 us (1%)
    ppermute x22, starting transfers between devices, swap(): return lax.ppermute(x, axis, [(i, i ^ mask) for i in range(size)])  31.4 us
    ppermute x22, waiting for transfers between devices, swap(): return lax.ppermute(x, axis, [(i, i ^ mask) for i in range(size)])  7.36 us
    pallas_call x1, Pallas kernels, scores(): self.call(scores_kernel, 1.0, 'scores', in_specs=[smem, smem, VMEM, VMEM]...  5.23 us
    pallas_call x2, Pallas kernels, over_rows(): self.call(rows_kernel, 0.1, name, grid=(KEY_HEADS, self.tiles), in_specs=...  5.12 us
    pallas_call x1, Pallas kernels, project(): pl.pallas_call(functools.partial(project_kernel, streams), grid=(steps,),...  2.98 us
    pallas_call x1, Pallas kernels, values(): self.call(values_kernel, 0.1, 'values', grid=(KEY_HEADS, self.tiles), in_...  2.85 us
    pallas_call x7, Pallas kernels, in_vmem(): pl.pallas_call(kernel, cost_estimate=cost, in_specs=[VMEM] * len(arrays),...  1.2 us
  transfers between devices with their start and end apart: 22, of which 6 were waited for; matrix products, arithmetic and copies ran while one was open for 0% of the time, Pallas kernels for 24%

profile of v13, /device:TPU:0, one launch (start us, length us, event | category | flops | bytes accessed | tf_op | source)
XLA Modules:
  0.0 58.4 jit_solution(5710604618324697311)
XLA Ops:
  0.7 3.0 %project.1 = (bf16[32,1024]{1,0:T(8,128)(2,1)S(1)}, bf16[128,512]{1,0:T(8,128)(2,1)S(1)}, bf16[128,512]{1,0:T(8,128)(2,1)S(1)}) custom-call(bf16[32,4096]{1,0:T(8,128)(2,1)} %bitcast.14, bf16[4096,512]{1,0:T(8,128)(2,1)} %refs_3_.1, bf16[4096,512]{1,0:T(8,128)(2,1)} %refs_3_.1, bf16[4096,512]{1,0:T(8,128)(2,1)} %refs_3_.1, bf16[4096,512]{1,0:T(8,128)(2,1)} %refs_3_.1, ...), custom_call_target="tpu_custom_call" | custom-call | flops 134217728 | bytes 4194304 | tf_op jit(solution)/shard_map/project/pallas_call | solution.py:94
  3.7 4.1 %collective-permute-start = (bf16[32,1024]{1,0:T(8,128)(2,1)S(1)}, bf16[32,1024]{1,0:T(8,128)(2,1)S(1)}, u32[]{:S(2)}, u32[]{:S(2)}) collective-permute-start(bf16[32,1024]{1,0:T(8,128)(2,1)S(1)} %get-tuple-element.50.refs_0_), channel_id=1, source_target_pairs={{0,16},{4,20},{8,24},{12,28},{16,0},{20,4},{24,8},{28,12},{1,17},{... | collective-permute-start | bytes 196616 | tf_op jit(solution)/shard_map/ppermute | solution.py:28
  7.8 2.5 %collective-permute-start.4 = (bf16[32,1024]{1,0:T(8,128)(2,1)S(1)}, bf16[32,1024]{1,0:T(8,128)(2,1)S(1)}, u32[]{:S(2)}, u32[]{:S(2)}) collective-permute-start(bf16[32,1024]{1,0:T(8,128)(2,1)S(1)} %get-tuple-element.50.refs_0_), channel_id=1, source_target_pairs={{0,12},{4,8},{8,4},{12,0},{16,28},{20,24},{24,20},{28,16},{1,13},{... | collective-permute-start | bytes 196616 | tf_op jit(solution)/shard_map/ppermute | solution.py:28
  10.3 0.4 collective-permute-start.5
  10.7 0.5 collective-permute-start.6
  11.2 2.5 %collective-permute-start.1 = (bf16[32,1024]{1,0:T(8,128)(2,1)S(1)}, bf16[32,1024]{1,0:T(8,128)(2,1)S(1)}, u32[]{:S(2)}, u32[]{:S(2)}) collective-permute-start(bf16[32,1024]{1,0:T(8,128)(2,1)S(1)} %collective-permute-done.refs_4_), channel_id=1, source_target_pairs={{0,12},{4,8},{8,4},{12,0},{16,28},{20,24},{24,20},{28,16},{1,13},{... | collective-permute-start | bytes 196616 | tf_op jit(solution)/shard_map/ppermute | solution.py:28
  13.8 0.4 collective-permute-start.2
  14.2 0.9 %collective-permute-start.3 = (bf16[32,1024]{1,0:T(8,128)(2,1)S(1)}, bf16[32,1024]{1,0:T(8,128)(2,1)S(1)}, u32[]{:S(2)}, u32[]{:S(2)}) collective-permute-start(bf16[32,1024]{1,0:T(8,128)(2,1)S(1)} %collective-permute-done.refs_4_), channel_id=1, source_target_pairs={{0,4},{4,0},{8,12},{12,8},{16,20},{20,16},{24,28},{28,24},{1,5},{5... | collective-permute-start | bytes 196616 | tf_op jit(solution)/shard_map/ppermute | solution.py:28
  15.8 1.9 %collective-permute-start.7 = (bf16[128,512]{1,0:T(8,128)(2,1)S(1)}, bf16[128,512]{1,0:T(8,128)(2,1)S(1)}, u32[]{:S(2)}, u32[]{:S(2)}) collective-permute-start(bf16[128,512]{1,0:T(8,128)(2,1)S(1)} %get-tuple-element.58), channel_id=1, source_target_pairs={{0,16},{4,20},{8,24},{12,28},{16,0},{20,4},{24,8},{28,12},{1,17},{... | collective-permute-start | bytes 393224 | tf_op jit(solution)/shard_map/ppermute | solution.py:28
  17.7 1.8 %collective-permute-done.2.refs_2_ = bf16[32,1024]{1,0:T(8,128)(2,1)S(1)} collective-permute-done((bf16[32,1024]{1,0:T(8,128)(2,1)S(1)}, bf16[32,1024]{1,0:T(8,128)(2,1)S(1)}, u32[]{:S(2)}, u32[]{:S(2)}) %collective-permute-start.2) | collective-permute-done | bytes 65568 | tf_op jit(solution)/shard_map/ppermute | solution.py:28
  19.5 5.2 %scores.1 = (bf16[256,4096]{1,0:T(8,128)(2,1)S(1)}, bf16[256,4096]{1,0:T(8,128)(2,1)S(1)}, bf16[256,512]{1,0:T(8,128)(2,1)S(1)}, bf16[256,512]{1,0:T(8,128)(2,1)...) custom-call(s32[1]{0:T(128)S(6)} %copy.11.length_ref, ...), custom_call_target="tpu_custom_call" | custom-call | flops 1610612736 | bytes 4194304 | tf_op jit(solution)/shard_map/scores/pallas_call | solution.py:259
  24.7 1.2 %collective-permute-start.8 = (bf16[64,512]{1,0:T(8,128)(2,1)S(1)}, bf16[64,512]{1,0:T(8,128)(2,1)S(1)}, u32[]{:S(2)}, u32[]{:S(2)}) collective-permute-start(bf16[64,512]{1,0:T(8,128)(2,1)S(1)} %get-tuple-element.59), channel_id=1, source_target_pairs={{0,12},{4,8},{8,4},{12,0},{16,28},{20,24},{24,20},{28,16},{1,13},{... | collective-permute-start | bytes 196616 | tf_op jit(solution)/shard_map/ppermute | solution.py:28
  26.3 2.0 %collective-permute-start.10 = (bf16[64,512]{1,0:T(8,128)(2,1)S(1)}, bf16[64,512]{1,0:T(8,128)(2,1)S(1)}, u32[]{:S(2)}, u32[]{:S(2)}) collective-permute-start(bf16[64,512]{1,0:T(8,128)(2,1)S(1)} %get-tuple-element.61), channel_id=1, source_target_pairs={{0,4},{4,0},{8,12},{12,8},{16,20},{20,16},{24,28},{28,24},{1,5},{5... | collective-permute-start | bytes 196616 | tf_op jit(solution)/shard_map/ppermute | solution.py:28
  28.3 2.9 %values.1 = (f32[64,512]{1,0:T(8,128)S(1)}, bf16[64,512]{1,0:T(8,128)(2,1)S(1)}, bf16[64,512]{1,0:T(8,128)(2,1)S(1)}, bf16[64,512]{1,0:T(8,128)(2,1)S(1)}) custom-call(bf16[128,4096]{1,0:T(8,128)(2,1)} %bitcast.9, bf16[256,4096]{1,0:T(8,128)(2,1)S(1)} %get-tuple-element.52.w_ref.inner_ref), custom_call_target="tpu_custom_call" | custom-call | flops 161061280 | bytes 419430 | tf_op jit(solution)/shard_map/values/pallas_call | solution.py:274
  31.2 2.0 %collective-permute-start.11 = (bf16[32,512]{1,0:T(8,128)(2,1)S(1)}, bf16[32,512]{1,0:T(8,128)(2,1)S(1)}, u32[]{:S(2)}, u32[]{:S(2)}) collective-permute-start(bf16[32,512]{1,0:T(8,128)(2,1)S(1)} %get-tuple-element.68), channel_id=1, source_target_pairs={{0,16},{4,20},{8,24},{12,28},{16,0},{20,4},{24,8},{28,12},{1,17},{... | collective-permute-start | bytes 98312 | tf_op jit(solution)/shard_map/ppermute | solution.py:28
  33.2 2.6 %query_grad.1 = bf16[128,4096]{1,0:T(8,128)(2,1)} custom-call(bf16[256,4096]{1,0:T(8,128)(2,1)S(1)} %get-tuple-element.65.inner_ref, bf16[256,512]{1,0:T(8,128)(2,1)S(1)} %get-tuple-element.66.head_ref), custom_call_target="tpu_custom_call" | custom-call | flops 161061280 | bytes 419430 | tf_op jit(solution)/shard_map/query_grad/pallas_call | solution.py:287
  36.1 1.8 %collective-permute-start.12 = (bf16[32,1536]{1,0:T(8,128)(2,1)S(1)}, bf16[32,1536]{1,0:T(8,128)(2,1)S(1)}, u32[]{:S(2)}, u32[]{:S(2)}) collective-permute-start(bf16[32,1536]{1,0:T(8,128)(2,1)S(1)} %get-tuple-element.72), channel_id=1, source_target_pairs={{0,4},{4,0},{8,12},{12,8},{16,20},{20,16},{24,28},{28,24},{1,5},{5... | collective-permute-start | bytes 294920 | tf_op jit(solution)/shard_map/ppermute | solution.py:28
  37.9 1.7 %collective-permute-start.15 = (bf16[32,512]{1,0:T(8,128)(2,1)S(1)}, bf16[32,512]{1,0:T(8,128)(2,1)S(1)}, u32[]{:S(2)}, u32[]{:S(2)}) collective-permute-start(bf16[32,512]{1,0:T(8,128)(2,1)S(1)} %get-tuple-element.81), channel_id=1, source_target_pairs={{0,16},{4,20},{8,24},{12,28},{16,0},{20,4},{24,8},{28,12},{1,17},{... | collective-permute-start | bytes 98312 | tf_op jit(solution)/shard_map/ppermute | solution.py:28
  39.6 1.5 %collective-permute-start.13 = (bf16[32,1536]{1,0:T(8,128)(2,1)S(1)}, bf16[32,1536]{1,0:T(8,128)(2,1)S(1)}, u32[]{:S(2)}, u32[]{:S(2)}) collective-permute-start(bf16[32,1536]{1,0:T(8,128)(2,1)S(1)} %get-tuple-element.73), channel_id=1, source_target_pairs={{0,8},{4,12},{8,0},{12,4},{16,24},{20,28},{24,16},{28,20},{1,9},{5... | collective-permute-start | bytes 294920 | tf_op jit(solution)/shard_map/ppermute | solution.py:28
  41.1 0.6 %collective-permute-start.14 = (bf16[32,1536]{1,0:T(8,128)(2,1)S(1)}, bf16[32,1536]{1,0:T(8,128)(2,1)S(1)}, u32[]{:S(2)}, u32[]{:S(2)}) collective-permute-start(bf16[32,1536]{1,0:T(8,128)(2,1)S(1)} %get-tuple-element.74), channel_id=1, source_target_pairs={{0,12},{4,8},{8,4},{12,0},{16,28},{20,24},{24,20},{28,16},{1,13},{... | collective-permute-start | bytes 294920 | tf_op jit(solution)/shard_map/ppermute | solution.py:28
  41.7 1.4 %collective-permute-done.15.far_ref.refs_7_ = bf16[32,512]{1,0:T(8,128)(2,1)S(1)} collective-permute-done((bf16[32,512]{1,0:T(8,128)(2,1)S(1)}, bf16[32,512]{1,0:T(8,128)(2,1)S(1)}, u32[]{:S(2)}, u32[]{:S(2)}) %collective-permute-start.15) | collective-permute-done | bytes 32800 | tf_op jit(solution)/shard_map/ppermute | solution.py:28
  43.1 1.0 %collective-permute-start.16 = (bf16[32,1536]{1,0:T(8,128)(2,1)S(1)}, bf16[32,1536]{1,0:T(8,128)(2,1)S(1)}, u32[]{:S(2)}, u32[]{:S(2)}) collective-permute-start(bf16[32,1536]{1,0:T(8,128)(2,1)S(1)} %get-tuple-element.85), channel_id=1, source_target_pairs={{0,12},{4,8},{8,4},{12,0},{16,28},{20,24},{24,20},{28,16},{1,13},{... | collective-permute-start | bytes 294920 | tf_op jit(solution)/shard_map/ppermute | solution.py:28
  44.1 0.6 collective-permute-start.17
  44.7 2.0 %collective-permute-start.18 = (bf16[32,1536]{1,0:T(8,128)(2,1)S(1)}, bf16[32,1536]{1,0:T(8,128)(2,1)S(1)}, u32[]{:S(2)}, u32[]{:S(2)}) collective-permute-start(bf16[32,1536]{1,0:T(8,128)(2,1)S(1)} %get-tuple-element.87), channel_id=1, source_target_pairs={{0,4},{4,0},{8,12},{12,8},{16,20},{20,16},{24,28},{28,24},{1,5},{5... | collective-permute-start | bytes 294920 | tf_op jit(solution)/shard_map/ppermute | solution.py:28
  46.7 2.6 %output.1 = bf16[128,4096]{1,0:T(8,128)(2,1)} custom-call(bf16[256,4096]{1,0:T(8,128)(2,1)S(1)} %get-tuple-element.52.w_ref.inner_ref, bf16[256,512]{1,0:T(8,128)(2,1)S(1)} %get-tuple-element.75.head_ref), custom_call_target="tpu_custom_call" | custom-call | flops 161061280 | bytes 419430 | tf_op jit(solution)/shard_map/output/pallas_call | solution.py:287
  49.4 0.4 collective-permute-done.18.refs_3_
  50.1 1.8 %collective-permute-start.21 = (bf16[32,512]{1,0:T(8,128)(2,1)S(1)}, bf16[32,512]{1,0:T(8,128)(2,1)S(1)}, u32[]{:S(2)}, u32[]{:S(2)}) collective-permute-start(bf16[32,512]{1,0:T(8,128)(2,1)S(1)} %get-tuple-element.92), channel_id=1, source_target_pairs={{0,16},{4,20},{8,24},{12,28},{16,0},{20,4},{24,8},{28,12},{1,17},{... | collective-permute-start | bytes 98312 | tf_op jit(solution)/shard_map/ppermute | solution.py:28
  52.0 1.6 %collective-permute-start.20 = (bf16[1,128,512]{2,1,0:T(8,128)(2,1)S(1)}, bf16[1,128,512]{2,1,0:T(8,128)(2,1)S(1)}, u32[]{:S(2)}, u32[]{:S(2)}) collective-permute-start(bf16[1,128,512]{2,1,0:T(8,128)(2,1)S(1)} %get-tuple-element.90), channel_id=1, source_target_pairs={{0,2},{1,3},{2,0},{3,1},{4,6},{5,7},{6,4},{7,5},{8,10},{9,11},{10,... | collective-permute-start | bytes 393224 | tf_op jit(solution)/shard_map/ppermute | solution.py:28
  53.6 2.1 %collective-permute-done.21.far_ref = bf16[32,512]{1,0:T(8,128)(2,1)S(1)} collective-permute-done((bf16[32,512]{1,0:T(8,128)(2,1)S(1)}, bf16[32,512]{1,0:T(8,128)(2,1)S(1)}, u32[]{:S(2)}, u32[]{:S(2)}) %collective-permute-start.21) | collective-permute-done | bytes 32800 | tf_op jit(solution)/shard_map/ppermute | solution.py:28
  55.6 0.6 %value_grad.1 = bf16[32,512]{1,0:T(8,128)(2,1)} custom-call(f32[32,512]{1,0:T(8,128)S(1)} %get-tuple-element.91.near_ref, bf16[32,512]{1,0:T(8,128)(2,1)S(1)} %collective-permute-done.21.far_ref), custom_call_target="tpu_custom_call" | custom-call | flops 4000000000 | bytes 16777216 | tf_op jit(solution)/shard_map/value_grad/pallas_call | solution.py:299
  56.3 1.4 %collective-permute-done.20 = bf16[1,128,512]{2,1,0:T(8,128)(2,1)S(1)} collective-permute-done((bf16[1,128,512]{2,1,0:T(8,128)(2,1)S(1)}, bf16[1,128,512]{2,1,0:T(8,128)(2,1)S(1)}, u32[]{:S(2)}, u32[]{:S(2)}) %collective-permute-start.20) | collective-permute-done | bytes 131104 | tf_op jit(solution)/shard_map/ppermute | solution.py:28
  57.6 0.7 %add_bitcast_fusion = f32[128,512]{1,0:T(8,128)} fusion(f32[1,128,512]{2,1,0:T(8,128)S(1)} %get-tuple-element.94, bf16[1,128,512]{2,1,0:T(8,128)(2,1)S(1)} %collective-permute-done.20), kind=kLoop, calls=%fused_computation | loop fusion | flops 131072 | bytes 655360 | tf_op jit(solution)/shard_map/add | solution.py:473
  (31 shorter events, 1.4 us)
Async XLA Ops:
  0.6 18.8 %copy-start = (bf16[1,128,4096]{2,1,0:T(8,128)(2,1)S(1)}, bf16[1,128,4096]{2,1,0:T(8,128)(2,1)}, u32[]{:S(2)}) copy-start(bf16[1,128,4096]{2,1,0:T(8,128)(2,1)} %param.11) | copy-start | bytes 3145732
  0.6 18.8 %copy-start.1 = (bf16[1,128,4096]{2,1,0:T(8,128)(2,1)S(1)}, bf16[1,128,4096]{2,1,0:T(8,128)(2,1)}, u32[]{:S(2)}) copy-start(bf16[1,128,4096]{2,1,0:T(8,128)(2,1)} %param.10) | copy-start | bytes 3145732
  0.7 18.8 %copy-start.2 = (s32[1,8]{1,0:T(1,128)S(1)}, s32[1,8]{1,0:T(1,128)}, u32[]{:S(2)}) copy-start(s32[1,8]{1,0:T(1,128)} %frame_ref.1) | copy-start | bytes 100
  3.7 7.6 %collective-permute-start = (bf16[32,1024]{1,0:T(8,128)(2,1)S(1)}, bf16[32,1024]{1,0:T(8,128)(2,1)S(1)}, u32[]{:S(2)}, u32[]{:S(2)}) collective-permute-start(bf16[32,1024]{1,0:T(8,128)(2,1)S(1)} %get-tuple-element.50.refs_0_), channel_id=1, source_target_pairs={{0,16},{4,20},{8,24},{12,28},{16,0},{20,4},{24,8},{28,12},{1,17},{... | collective-permute-start | bytes 196616 | tf_op jit(solution)/shard_map/ppermute | solution.py:28
  7.8 6.5 %collective-permute-start.4 = (bf16[32,1024]{1,0:T(8,128)(2,1)S(1)}, bf16[32,1024]{1,0:T(8,128)(2,1)S(1)}, u32[]{:S(2)}, u32[]{:S(2)}) collective-permute-start(bf16[32,1024]{1,0:T(8,128)(2,1)S(1)} %get-tuple-element.50.refs_0_), channel_id=1, source_target_pairs={{0,12},{4,8},{8,4},{12,0},{16,28},{20,24},{24,20},{28,16},{1,13},{... | collective-permute-start | bytes 196616 | tf_op jit(solution)/shard_map/ppermute | solution.py:28
  10.3 5.5 %collective-permute-start.5 = (bf16[32,1024]{1,0:T(8,128)(2,1)S(1)}, bf16[32,1024]{1,0:T(8,128)(2,1)S(1)}, u32[]{:S(2)}, u32[]{:S(2)}) collective-permute-start(bf16[32,1024]{1,0:T(8,128)(2,1)S(1)} %get-tuple-element.50.refs_0_), channel_id=1, source_target_pairs={{0,8},{4,12},{8,0},{12,4},{16,24},{20,28},{24,16},{28,20},{1,9},{5... | collective-permute-start | bytes 196616 | tf_op jit(solution)/shard_map/ppermute | solution.py:28
  10.7 6.9 %collective-permute-start.6 = (bf16[32,1024]{1,0:T(8,128)(2,1)S(1)}, bf16[32,1024]{1,0:T(8,128)(2,1)S(1)}, u32[]{:S(2)}, u32[]{:S(2)}) collective-permute-start(bf16[32,1024]{1,0:T(8,128)(2,1)S(1)} %get-tuple-element.50.refs_0_), channel_id=1, source_target_pairs={{0,4},{4,0},{8,12},{12,8},{16,20},{20,16},{24,28},{28,24},{1,5},{5... | collective-permute-start | bytes 196616 | tf_op jit(solution)/shard_map/ppermute | solution.py:28
  11.2 6.4 %collective-permute-start.1 = (bf16[32,1024]{1,0:T(8,128)(2,1)S(1)}, bf16[32,1024]{1,0:T(8,128)(2,1)S(1)}, u32[]{:S(2)}, u32[]{:S(2)}) collective-permute-start(bf16[32,1024]{1,0:T(8,128)(2,1)S(1)} %collective-permute-done.refs_4_), channel_id=1, source_target_pairs={{0,12},{4,8},{8,4},{12,0},{16,28},{20,24},{24,20},{28,16},{1,13},{... | collective-permute-start | bytes 196616 | tf_op jit(solution)/shard_map/ppermute | solution.py:28
  13.8 5.7 %collective-permute-start.2 = (bf16[32,1024]{1,0:T(8,128)(2,1)S(1)}, bf16[32,1024]{1,0:T(8,128)(2,1)S(1)}, u32[]{:S(2)}, u32[]{:S(2)}) collective-permute-start(bf16[32,1024]{1,0:T(8,128)(2,1)S(1)} %collective-permute-done.refs_4_), channel_id=1, source_target_pairs={{0,8},{4,12},{8,0},{12,4},{16,24},{20,28},{24,16},{28,20},{1,9},{5... | collective-permute-start | bytes 196616 | tf_op jit(solution)/shard_map/ppermute | solution.py:28
  14.2 5.2 %collective-permute-start.3 = (bf16[32,1024]{1,0:T(8,128)(2,1)S(1)}, bf16[32,1024]{1,0:T(8,128)(2,1)S(1)}, u32[]{:S(2)}, u32[]{:S(2)}) collective-permute-start(bf16[32,1024]{1,0:T(8,128)(2,1)S(1)} %collective-permute-done.refs_4_), channel_id=1, source_target_pairs={{0,4},{4,0},{8,12},{12,8},{16,20},{20,16},{24,28},{28,24},{1,5},{5... | collective-permute-start | bytes 196616 | tf_op jit(solution)/shard_map/ppermute | solution.py:28
  15.8 8.9 %collective-permute-start.7 = (bf16[128,512]{1,0:T(8,128)(2,1)S(1)}, bf16[128,512]{1,0:T(8,128)(2,1)S(1)}, u32[]{:S(2)}, u32[]{:S(2)}) collective-permute-start(bf16[128,512]{1,0:T(8,128)(2,1)S(1)} %get-tuple-element.58), channel_id=1, source_target_pairs={{0,16},{4,20},{8,24},{12,28},{16,0},{20,4},{24,8},{28,12},{1,17},{... | collective-permute-start | bytes 393224 | tf_op jit(solution)/shard_map/ppermute | solution.py:28
  24.7 6.4 %collective-permute-start.8 = (bf16[64,512]{1,0:T(8,128)(2,1)S(1)}, bf16[64,512]{1,0:T(8,128)(2,1)S(1)}, u32[]{:S(2)}, u32[]{:S(2)}) collective-permute-start(bf16[64,512]{1,0:T(8,128)(2,1)S(1)} %get-tuple-element.59), channel_id=1, source_target_pairs={{0,12},{4,8},{8,4},{12,0},{16,28},{20,24},{24,20},{28,16},{1,13},{... | collective-permute-start | bytes 196616 | tf_op jit(solution)/shard_map/ppermute | solution.py:28
  25.9 5.2 %collective-permute-start.9 = (bf16[64,512]{1,0:T(8,128)(2,1)S(1)}, bf16[64,512]{1,0:T(8,128)(2,1)S(1)}, u32[]{:S(2)}, u32[]{:S(2)}) collective-permute-start(bf16[64,512]{1,0:T(8,128)(2,1)S(1)} %get-tuple-element.60), channel_id=1, source_target_pairs={{0,8},{4,12},{8,0},{12,4},{16,24},{20,28},{24,16},{28,20},{1,9},{5... | collective-permute-start | bytes 196616 | tf_op jit(solution)/shard_map/ppermute | solution.py:28
  26.3 4.9 %collective-permute-start.10 = (bf16[64,512]{1,0:T(8,128)(2,1)S(1)}, bf16[64,512]{1,0:T(8,128)(2,1)S(1)}, u32[]{:S(2)}, u32[]{:S(2)}) collective-permute-start(bf16[64,512]{1,0:T(8,128)(2,1)S(1)} %get-tuple-element.61), channel_id=1, source_target_pairs={{0,4},{4,0},{8,12},{12,8},{16,20},{20,16},{24,28},{28,24},{1,5},{5... | collective-permute-start | bytes 196616 | tf_op jit(solution)/shard_map/ppermute | solution.py:28
  31.2 4.9 %collective-permute-start.11 = (bf16[32,512]{1,0:T(8,128)(2,1)S(1)}, bf16[32,512]{1,0:T(8,128)(2,1)S(1)}, u32[]{:S(2)}, u32[]{:S(2)}) collective-permute-start(bf16[32,512]{1,0:T(8,128)(2,1)S(1)} %get-tuple-element.68), channel_id=1, source_target_pairs={{0,16},{4,20},{8,24},{12,28},{16,0},{20,4},{24,8},{28,12},{1,17},{... | collective-permute-start | bytes 98312 | tf_op jit(solution)/shard_map/ppermute | solution.py:28
  36.1 8.5 %collective-permute-start.12 = (bf16[32,1536]{1,0:T(8,128)(2,1)S(1)}, bf16[32,1536]{1,0:T(8,128)(2,1)S(1)}, u32[]{:S(2)}, u32[]{:S(2)}) collective-permute-start(bf16[32,1536]{1,0:T(8,128)(2,1)S(1)} %get-tuple-element.72), channel_id=1, source_target_pairs={{0,4},{4,0},{8,12},{12,8},{16,20},{20,16},{24,28},{28,24},{1,5},{5... | collective-permute-start | bytes 294920 | tf_op jit(solution)/shard_map/ppermute | solution.py:28
  37.9 5.2 %collective-permute-start.15 = (bf16[32,512]{1,0:T(8,128)(2,1)S(1)}, bf16[32,512]{1,0:T(8,128)(2,1)S(1)}, u32[]{:S(2)}, u32[]{:S(2)}) collective-permute-start(bf16[32,512]{1,0:T(8,128)(2,1)S(1)} %get-tuple-element.81), channel_id=1, source_target_pairs={{0,16},{4,20},{8,24},{12,28},{16,0},{20,4},{24,8},{28,12},{1,17},{... | collective-permute-start | bytes 98312 | tf_op jit(solution)/shard_map/ppermute | solution.py:28
  39.6 9.7 %collective-permute-start.13 = (bf16[32,1536]{1,0:T(8,128)(2,1)S(1)}, bf16[32,1536]{1,0:T(8,128)(2,1)S(1)}, u32[]{:S(2)}, u32[]{:S(2)}) collective-permute-start(bf16[32,1536]{1,0:T(8,128)(2,1)S(1)} %get-tuple-element.73), channel_id=1, source_target_pairs={{0,8},{4,12},{8,0},{12,4},{16,24},{20,28},{24,16},{28,20},{1,9},{5... | collective-permute-start | bytes 294920 | tf_op jit(solution)/shard_map/ppermute | solution.py:28
  41.1 8.1 %collective-permute-start.14 = (bf16[32,1536]{1,0:T(8,128)(2,1)S(1)}, bf16[32,1536]{1,0:T(8,128)(2,1)S(1)}, u32[]{:S(2)}, u32[]{:S(2)}) collective-permute-start(bf16[32,1536]{1,0:T(8,128)(2,1)S(1)} %get-tuple-element.74), channel_id=1, source_target_pairs={{0,12},{4,8},{8,4},{12,0},{16,28},{20,24},{24,20},{28,16},{1,13},{... | collective-permute-start | bytes 294920 | tf_op jit(solution)/shard_map/ppermute | solution.py:28
  43.1 6.3 %collective-permute-start.16 = (bf16[32,1536]{1,0:T(8,128)(2,1)S(1)}, bf16[32,1536]{1,0:T(8,128)(2,1)S(1)}, u32[]{:S(2)}, u32[]{:S(2)}) collective-permute-start(bf16[32,1536]{1,0:T(8,128)(2,1)S(1)} %get-tuple-element.85), channel_id=1, source_target_pairs={{0,12},{4,8},{8,4},{12,0},{16,28},{20,24},{24,20},{28,16},{1,13},{... | collective-permute-start | bytes 294920 | tf_op jit(solution)/shard_map/ppermute | solution.py:28
  44.1 5.3 %collective-permute-start.17 = (bf16[32,1536]{1,0:T(8,128)(2,1)S(1)}, bf16[32,1536]{1,0:T(8,128)(2,1)S(1)}, u32[]{:S(2)}, u32[]{:S(2)}) collective-permute-start(bf16[32,1536]{1,0:T(8,128)(2,1)S(1)} %get-tuple-element.86), channel_id=1, source_target_pairs={{0,8},{4,12},{8,0},{12,4},{16,24},{20,28},{24,16},{28,20},{1,9},{5... | collective-permute-start | bytes 294920 | tf_op jit(solution)/shard_map/ppermute | solution.py:28
  44.7 5.1 %collective-permute-start.18 = (bf16[32,1536]{1,0:T(8,128)(2,1)S(1)}, bf16[32,1536]{1,0:T(8,128)(2,1)S(1)}, u32[]{:S(2)}, u32[]{:S(2)}) collective-permute-start(bf16[32,1536]{1,0:T(8,128)(2,1)S(1)} %get-tuple-element.87), channel_id=1, source_target_pairs={{0,4},{4,0},{8,12},{12,8},{16,20},{20,16},{24,28},{28,24},{1,5},{5... | collective-permute-start | bytes 294920 | tf_op jit(solution)/shard_map/ppermute | solution.py:28
  50.1 1.9 %collective-permute-start.19 = (bf16[2,128,512]{2,1,0:T(8,128)(2,1)S(1)}, bf16[2,128,512]{2,1,0:T(8,128)(2,1)S(1)}, u32[]{:S(2)}, u32[]{:S(2)}) collective-permute-start(bf16[2,128,512]{2,1,0:T(8,128)(2,1)S(1)} %get-tuple-element.89), channel_id=1, source_target_pairs={{0,1},{1,0},{2,3},{3,2},{4,5},{5,4},{6,7},{7,6},{8,9},{9,8},{10,11... | collective-permute-start | bytes 786440 | tf_op jit(solution)/shard_map/ppermute | solution.py:28
  50.1 5.5 %collective-permute-start.21 = (bf16[32,512]{1,0:T(8,128)(2,1)S(1)}, bf16[32,512]{1,0:T(8,128)(2,1)S(1)}, u32[]{:S(2)}, u32[]{:S(2)}) collective-permute-start(bf16[32,512]{1,0:T(8,128)(2,1)S(1)} %get-tuple-element.92), channel_id=1, source_target_pairs={{0,16},{4,20},{8,24},{12,28},{16,0},{20,4},{24,8},{28,12},{1,17},{... | collective-permute-start | bytes 98312 | tf_op jit(solution)/shard_map/ppermute | solution.py:28
  52.0 5.6 %collective-permute-start.20 = (bf16[1,128,512]{2,1,0:T(8,128)(2,1)S(1)}, bf16[1,128,512]{2,1,0:T(8,128)(2,1)S(1)}, u32[]{:S(2)}, u32[]{:S(2)}) collective-permute-start(bf16[1,128,512]{2,1,0:T(8,128)(2,1)S(1)} %get-tuple-element.90), channel_id=1, source_target_pairs={{0,2},{1,3},{2,0},{3,1},{4,6},{5,7},{6,4},{7,5},{8,10},{9,11},{10,... | collective-permute-start | bytes 393224 | tf_op jit(solution)/shard_map/ppermute | solution.py:28

commit v14 on v13

--- a/solution.py
+++ b/solution.py
@@ -48,61 +48,54 @@
     return [swap(piece, "blk", m) for m, piece in enumerate(pieces, 1)]
 
 
-def project_kernel(streams, visual_ref, *refs):
-    weight_refs, value_ref = refs[:streams], refs[streams]
-    out_ref, near_ref, far_ref, acc_ref = refs[streams + 1 :]
-    step = pl.program_id(0)
-    slab = weight_refs[0].shape[0]
-    part = 0.0
-    for p in range(streams):
-        start = pl.multiple_of((step * streams + p) * slab, HEAD_SIZE)
-        part += dot(visual_ref[:, pl.ds(start, slab)], weight_refs[p][...])
-
-    @pl.when(step == 0)
-    def _():
-        acc_ref[...] = part
-        block = lax.axis_index("blk")
-        rows, width = visual_ref.shape[0], near_ref.shape[1]
-        half = near_ref.shape[0] // rows
-        for side, ref in enumerate((near_ref, far_ref)):
-            for m in range(half):
-                start = pl.multiple_of((block ^ (m + side * half)) * width, HEAD_SIZE)
-                ref[m * rows : (m + 1) * rows, :] = visual_ref[:, pl.ds(start, width)]
-
-    @pl.when(step > 0)
-    def _():
-        acc_ref[...] += part
-
-    @pl.when(step == pl.num_programs(0) - 1)
-    def _():
-        columns = acc_ref.shape[1]
-        out_ref[:, :columns] = acc_ref[...].astype(BF16)
-        out_ref[:, columns:] = value_ref[...]
+def project_kernel(chunks, weight_hbm, visual_hbm, value_hbm, *refs):
+    out_ref, near_ref, far_ref, weight, visual_ref, value_ref, sems = refs
+    slab = weight.shape[0] // chunks
+    copies = [
+        pltpu.make_async_copy(visual_hbm, visual_ref, sems.at[chunks]),
+        pltpu.make_async_copy(value_hbm, value_ref, sems.at[chunks + 1]),
+    ]
+    for c in range(chunks):
+        part = pl.ds(c * slab, slab)
+        copies.append(pltpu.make_async_copy(weight_hbm.at[part], weight.at[part], sems.at[c]))
+    for copy in copies:
+        copy.start()
+    copies[0].wait()
+    copies[1].wait()
+    block = lax.axis_index("blk")
+    rows, width = visual_ref.shape[0], near_ref.shape[1]
+    half = near_ref.shape[0] // rows
+    for side, ref in enumerate((near_ref, far_ref)):
+        for m in range(half):
+            start = pl.multiple_of((block ^ (m + side * half)) * width, HEAD_SIZE)
+            ref[m * rows : (m + 1) * rows, :] = visual_ref[:, pl.ds(start, width)]
+    columns = weight.shape[1]
+    out_ref[:, columns:] = value_ref[...]
+    keys = jnp.zeros((rows, columns), F32)
+    for c in range(chunks):
+        copies[2 + c].wait()
+        part = slice(c * slab, (c + 1) * slab)
+        keys += dot(visual_ref[:, part], weight[part, :])
+    out_ref[:, :columns] = keys.astype(BF16)
 
 
 def project(blocks, visual, key_weight, value):
     rows, features = visual.shape
     columns = key_weight.shape[1]
-    steps, streams = 2, 4
-    slab = features // (steps * streams)
-    out = (rows, columns + value.shape[1])
+    chunks = 4
     half = (blocks // 2 * rows, features // blocks)
-
-    def whole(shape):
-        return pl.BlockSpec(shape, lambda k: (0, 0))
-
-    out = pl.pallas_call(
-        functools.partial(project_kernel, streams),
-        grid=(steps,),
-        in_specs=[whole(visual.shape)]
-        + [
-            pl.BlockSpec((slab, columns), lambda k, p=p: (k * streams + p, 0))
-            for p in range(streams)
-        ]
-        + [whole(value.shape)],
-        out_specs=[whole(out)] + [whole(half)] * 2,
-        out_shape=[jax.ShapeDtypeStruct(out, BF16)] + [jax.ShapeDtypeStruct(half, BF16)] * 2,
-        scratch_shapes=[pltpu.VMEM((rows, columns), F32)],
+    shapes = [(rows, columns + value.shape[1]), half, half]
+    return pl.pallas_call(
+        functools.partial(project_kernel, chunks),
+        in_specs=[pl.BlockSpec(memory_space=pltpu.HBM)] * 3,
+        out_specs=[VMEM] * 3,
+        out_shape=[jax.ShapeDtypeStruct(shape, BF16) for shape in shapes],
+        scratch_shapes=[
+            pltpu.VMEM(key_weight.shape, BF16),
+            pltpu.VMEM(visual.shape, BF16),
+            pltpu.VMEM(value.shape, BF16),
+            pltpu.SemaphoreType.DMA((chunks + 2,)),
+        ],
         cost_estimate=pl.CostEstimate(
             flops=2 * rows * features * columns,
             bytes_accessed=2 * features * columns,
@@ -110,8 +103,7 @@
         ),
         compiler_params=pltpu.CompilerParams(vmem_limit_bytes=32 * MIB),
         name="project",
-    )(in_hbm(visual), *[in_hbm(key_weight)] * streams, in_hbm(value))
-    return out
+    )(in_hbm(key_weight), in_hbm(visual), in_hbm(value))
 
 
 def head_pair(ref, rows, start):
@@ -154,7 +146,7 @@
             live = row + (block ^ m) * rows < limit
             bias_ref[m * rows : (m + 1) * rows, :] = jnp.where(live, 0.0, NEGATIVE_FILLER)
 
-        @pl.loop(0, KEY_HEADS)
+        @pl.loop(0, KEY_HEADS, unroll=True)
         def _(j, i=i, text=text):
             head = pl.ds(pl.multiple_of(j * HEAD_SIZE, HEAD_SIZE), HEAD_SIZE)
             keys, values = k_ref[:, head], v_ref[:, head]

time: 58.5 us -> 57.3 us (0.979)
  Pallas kernels: 17.4 us -> 16.4 us
    pallas_call x1, Pallas kernels: 5.23 us -> 4.51 us  [scores(): self.call(scores_kernel, 1.0, 'scores', in_specs=[smem, smem, VMEM, VMEM]...]
  transfers between devices with their start and end apart: 22 -> 22, of which waited for: 6 -> 7; matrix products, arithmetic and copies ran while one was open for 0% -> 0% of each run, Pallas kernels for 24% -> 23%
where the time goes in v14:
time: 57.3 us; the launch traced here: 57.1 us
  starting transfers between devices  30.9 us (54%)
  Pallas kernels  16.4 us (29%)
  waiting for transfers between devices  7.62 us (13%)
  between operations  1.45 us (3%)
  other arithmetic  0.73 us (1%)
    ppermute x22, starting transfers between devices, swap(): return lax.ppermute(x, axis, [(i, i ^ mask) for i in range(size)])  30.9 us
    ppermute x22, waiting for transfers between devices, swap(): return lax.ppermute(x, axis, [(i, i ^ mask) for i in range(size)])  7.62 us
    pallas_call x2, Pallas kernels, over_rows(): self.call(rows_kernel, 0.1, name, grid=(KEY_HEADS, self.tiles), in_specs=...  5.12 us
    pallas_call x1, Pallas kernels, scores(): self.call(scores_kernel, 1.0, 'scores', in_specs=[smem, smem, VMEM, VMEM]...  4.51 us
    pallas_call x1, Pallas kernels, values(): self.call(values_kernel, 0.1, 'values', grid=(KEY_HEADS, self.tiles), in_...  2.86 us
    pallas_call x1, Pallas kernels, project(): pl.pallas_call(functools.partial(project_kernel, chunks), in_specs=[pl.Bl...  2.75 us
    pallas_call x7, Pallas kernels, in_vmem(): pl.pallas_call(kernel, cost_estimate=cost, in_specs=[VMEM] * len(arrays),...  1.19 us
  transfers between devices with their start and end apart: 22, of which 7 were waited for; matrix products, arithmetic and copies ran while one was open for 0% of the time, Pallas kernels for 23%

profile of v14, /device:TPU:0, one launch (start us, length us, event | category | flops | bytes accessed | tf_op | source)
XLA Modules:
  0.0 57.1 jit_solution(4013577453145851453)
XLA Ops:
  0.7 2.8 %project.1 = (bf16[32,1024]{1,0:T(8,128)(2,1)S(1)}, bf16[128,512]{1,0:T(8,128)(2,1)S(1)}, bf16[128,512]{1,0:T(8,128)(2,1)S(1)}) custom-call(bf16[4096,512]{1,0:T(8,128)(2,1)} %weight_hbm.1, bf16[32,4096]{1,0:T(8,128)(2,1)} %bitcast.14, bf16[32,512]{1,0:T(8,128)(2,1)} %bitcast.15), custom_call_target="tpu_custom_call" | custom-call | flops 134217728 | bytes 4194304 | tf_op jit(solution)/shard_map/project/pallas_call | solution.py:88
  3.4 4.1 %collective-permute-start = (bf16[32,1024]{1,0:T(8,128)(2,1)S(1)}, bf16[32,1024]{1,0:T(8,128)(2,1)S(1)}, u32[]{:S(2)}, u32[]{:S(2)}) collective-permute-start(bf16[32,1024]{1,0:T(8,128)(2,1)S(1)} %get-tuple-element.50.refs_0_), channel_id=1, source_target_pairs={{0,16},{4,20},{8,24},{12,28},{16,0},{20,4},{24,8},{28,12},{1,17},{... | collective-permute-start | bytes 196616 | tf_op jit(solution)/shard_map/ppermute | solution.py:28
  7.5 2.5 %collective-permute-start.4 = (bf16[32,1024]{1,0:T(8,128)(2,1)S(1)}, bf16[32,1024]{1,0:T(8,128)(2,1)S(1)}, u32[]{:S(2)}, u32[]{:S(2)}) collective-permute-start(bf16[32,1024]{1,0:T(8,128)(2,1)S(1)} %get-tuple-element.50.refs_0_), channel_id=1, source_target_pairs={{0,12},{4,8},{8,4},{12,0},{16,28},{20,24},{24,20},{28,16},{1,13},{... | collective-permute-start | bytes 196616 | tf_op jit(solution)/shard_map/ppermute | solution.py:28
  10.1 0.5 collective-permute-start.5
  10.5 0.5 collective-permute-start.6
  11.0 2.5 %collective-permute-start.1 = (bf16[32,1024]{1,0:T(8,128)(2,1)S(1)}, bf16[32,1024]{1,0:T(8,128)(2,1)S(1)}, u32[]{:S(2)}, u32[]{:S(2)}) collective-permute-start(bf16[32,1024]{1,0:T(8,128)(2,1)S(1)} %collective-permute-done.refs_4_), channel_id=1, source_target_pairs={{0,12},{4,8},{8,4},{12,0},{16,28},{20,24},{24,20},{28,16},{1,13},{... | collective-permute-start | bytes 196616 | tf_op jit(solution)/shard_map/ppermute | solution.py:28
  13.6 0.5 collective-permute-start.2
  14.0 0.9 %collective-permute-start.3 = (bf16[32,1024]{1,0:T(8,128)(2,1)S(1)}, bf16[32,1024]{1,0:T(8,128)(2,1)S(1)}, u32[]{:S(2)}, u32[]{:S(2)}) collective-permute-start(bf16[32,1024]{1,0:T(8,128)(2,1)S(1)} %collective-permute-done.refs_4_), channel_id=1, source_target_pairs={{0,4},{4,0},{8,12},{12,8},{16,20},{20,16},{24,28},{28,24},{1,5},{5... | collective-permute-start | bytes 196616 | tf_op jit(solution)/shard_map/ppermute | solution.py:28
  15.6 1.9 %collective-permute-start.7 = (bf16[128,512]{1,0:T(8,128)(2,1)S(1)}, bf16[128,512]{1,0:T(8,128)(2,1)S(1)}, u32[]{:S(2)}, u32[]{:S(2)}) collective-permute-start(bf16[128,512]{1,0:T(8,128)(2,1)S(1)} %get-tuple-element.58), channel_id=1, source_target_pairs={{0,16},{4,20},{8,24},{12,28},{16,0},{20,4},{24,8},{28,12},{1,17},{... | collective-permute-start | bytes 393224 | tf_op jit(solution)/shard_map/ppermute | solution.py:28
  17.4 1.8 %collective-permute-done.2.refs_2_ = bf16[32,1024]{1,0:T(8,128)(2,1)S(1)} collective-permute-done((bf16[32,1024]{1,0:T(8,128)(2,1)S(1)}, bf16[32,1024]{1,0:T(8,128)(2,1)S(1)}, u32[]{:S(2)}, u32[]{:S(2)}) %collective-permute-start.2) | collective-permute-done | bytes 65568 | tf_op jit(solution)/shard_map/ppermute | solution.py:28
  19.2 4.5 %scores.1 = (bf16[256,4096]{1,0:T(8,128)(2,1)S(1)}, bf16[256,4096]{1,0:T(8,128)(2,1)S(1)}, bf16[256,512]{1,0:T(8,128)(2,1)S(1)}, bf16[256,512]{1,0:T(8,128)(2,1)...) custom-call(s32[1]{0:T(128)S(6)} %copy.11.length_ref, ...), custom_call_target="tpu_custom_call" | custom-call | flops 1610612736 | bytes 4194304 | tf_op jit(solution)/shard_map/scores/pallas_call | solution.py:251
  23.8 1.2 %collective-permute-start.8 = (bf16[64,512]{1,0:T(8,128)(2,1)S(1)}, bf16[64,512]{1,0:T(8,128)(2,1)S(1)}, u32[]{:S(2)}, u32[]{:S(2)}) collective-permute-start(bf16[64,512]{1,0:T(8,128)(2,1)S(1)} %get-tuple-element.59), channel_id=1, source_target_pairs={{0,12},{4,8},{8,4},{12,0},{16,28},{20,24},{24,20},{28,16},{1,13},{... | collective-permute-start | bytes 196616 | tf_op jit(solution)/shard_map/ppermute | solution.py:28
  25.0 1.1 %collective-permute-start.9 = (bf16[64,512]{1,0:T(8,128)(2,1)S(1)}, bf16[64,512]{1,0:T(8,128)(2,1)S(1)}, u32[]{:S(2)}, u32[]{:S(2)}) collective-permute-start(bf16[64,512]{1,0:T(8,128)(2,1)S(1)} %get-tuple-element.60), channel_id=1, source_target_pairs={{0,8},{4,12},{8,0},{12,4},{16,24},{20,28},{24,16},{28,20},{1,9},{5... | collective-permute-start | bytes 196616 | tf_op jit(solution)/shard_map/ppermute | solution.py:28
  26.1 1.3 %collective-permute-start.10 = (bf16[64,512]{1,0:T(8,128)(2,1)S(1)}, bf16[64,512]{1,0:T(8,128)(2,1)S(1)}, u32[]{:S(2)}, u32[]{:S(2)}) collective-permute-start(bf16[64,512]{1,0:T(8,128)(2,1)S(1)} %get-tuple-element.61), channel_id=1, source_target_pairs={{0,4},{4,0},{8,12},{12,8},{16,20},{20,16},{24,28},{28,24},{1,5},{5... | collective-permute-start | bytes 196616 | tf_op jit(solution)/shard_map/ppermute | solution.py:28
  27.3 2.9 %values.1 = (f32[64,512]{1,0:T(8,128)S(1)}, bf16[64,512]{1,0:T(8,128)(2,1)S(1)}, bf16[64,512]{1,0:T(8,128)(2,1)S(1)}, bf16[64,512]{1,0:T(8,128)(2,1)S(1)}) custom-call(bf16[128,4096]{1,0:T(8,128)(2,1)} %bitcast.9, bf16[256,4096]{1,0:T(8,128)(2,1)S(1)} %get-tuple-element.52.w_ref.inner_ref), custom_call_target="tpu_custom_call" | custom-call | flops 161061280 | bytes 419430 | tf_op jit(solution)/shard_map/values/pallas_call | solution.py:266
  30.4 1.9 %collective-permute-start.11 = (bf16[32,512]{1,0:T(8,128)(2,1)S(1)}, bf16[32,512]{1,0:T(8,128)(2,1)S(1)}, u32[]{:S(2)}, u32[]{:S(2)}) collective-permute-start(bf16[32,512]{1,0:T(8,128)(2,1)S(1)} %get-tuple-element.68), channel_id=1, source_target_pairs={{0,16},{4,20},{8,24},{12,28},{16,0},{20,4},{24,8},{28,12},{1,17},{... | collective-permute-start | bytes 98312 | tf_op jit(solution)/shard_map/ppermute | solution.py:28
  32.3 2.6 %query_grad.1 = bf16[128,4096]{1,0:T(8,128)(2,1)} custom-call(bf16[256,4096]{1,0:T(8,128)(2,1)S(1)} %get-tuple-element.65.inner_ref, bf16[256,512]{1,0:T(8,128)(2,1)S(1)} %get-tuple-element.66.head_ref), custom_call_target="tpu_custom_call" | custom-call | flops 161061280 | bytes 419430 | tf_op jit(solution)/shard_map/query_grad/pallas_call | solution.py:279
  34.8 0.4 collective-permute-done.11.far_ref
  35.3 1.7 %collective-permute-start.12 = (bf16[32,1536]{1,0:T(8,128)(2,1)S(1)}, bf16[32,1536]{1,0:T(8,128)(2,1)S(1)}, u32[]{:S(2)}, u32[]{:S(2)}) collective-permute-start(bf16[32,1536]{1,0:T(8,128)(2,1)S(1)} %get-tuple-element.72), channel_id=1, source_target_pairs={{0,4},{4,0},{8,12},{12,8},{16,20},{20,16},{24,28},{28,24},{1,5},{5... | collective-permute-start | bytes 294920 | tf_op jit(solution)/shard_map/ppermute | solution.py:28
  37.0 1.7 %collective-permute-start.15 = (bf16[32,512]{1,0:T(8,128)(2,1)S(1)}, bf16[32,512]{1,0:T(8,128)(2,1)S(1)}, u32[]{:S(2)}, u32[]{:S(2)}) collective-permute-start(bf16[32,512]{1,0:T(8,128)(2,1)S(1)} %get-tuple-element.81), channel_id=1, source_target_pairs={{0,16},{4,20},{8,24},{12,28},{16,0},{20,4},{24,8},{28,12},{1,17},{... | collective-permute-start | bytes 98312 | tf_op jit(solution)/shard_map/ppermute | solution.py:28
  38.6 1.5 %collective-permute-start.13 = (bf16[32,1536]{1,0:T(8,128)(2,1)S(1)}, bf16[32,1536]{1,0:T(8,128)(2,1)S(1)}, u32[]{:S(2)}, u32[]{:S(2)}) collective-permute-start(bf16[32,1536]{1,0:T(8,128)(2,1)S(1)} %get-tuple-element.73), channel_id=1, source_target_pairs={{0,8},{4,12},{8,0},{12,4},{16,24},{20,28},{24,16},{28,20},{1,9},{5... | collective-permute-start | bytes 294920 | tf_op jit(solution)/shard_map/ppermute | solution.py:28
  40.2 0.5 collective-permute-start.14
  40.7 1.4 %collective-permute-done.15.far_ref.refs_7_ = bf16[32,512]{1,0:T(8,128)(2,1)S(1)} collective-permute-done((bf16[32,512]{1,0:T(8,128)(2,1)S(1)}, bf16[32,512]{1,0:T(8,128)(2,1)S(1)}, u32[]{:S(2)}, u32[]{:S(2)}) %collective-permute-start.15) | collective-permute-done | bytes 32800 | tf_op jit(solution)/shard_map/ppermute | solution.py:28
  42.1 1.4 %collective-permute-start.16 = (bf16[32,1536]{1,0:T(8,128)(2,1)S(1)}, bf16[32,1536]{1,0:T(8,128)(2,1)S(1)}, u32[]{:S(2)}, u32[]{:S(2)}) collective-permute-start(bf16[32,1536]{1,0:T(8,128)(2,1)S(1)} %get-tuple-element.85), channel_id=1, source_target_pairs={{0,12},{4,8},{8,4},{12,0},{16,28},{20,24},{24,20},{28,16},{1,13},{... | collective-permute-start | bytes 294920 | tf_op jit(solution)/shard_map/ppermute | solution.py:28
  43.9 1.9 %collective-permute-start.18 = (bf16[32,1536]{1,0:T(8,128)(2,1)S(1)}, bf16[32,1536]{1,0:T(8,128)(2,1)S(1)}, u32[]{:S(2)}, u32[]{:S(2)}) collective-permute-start(bf16[32,1536]{1,0:T(8,128)(2,1)S(1)} %get-tuple-element.87), channel_id=1, source_target_pairs={{0,4},{4,0},{8,12},{12,8},{16,20},{20,16},{24,28},{28,24},{1,5},{5... | collective-permute-start | bytes 294920 | tf_op jit(solution)/shard_map/ppermute | solution.py:28
  45.7 2.6 %output.1 = bf16[128,4096]{1,0:T(8,128)(2,1)} custom-call(bf16[256,4096]{1,0:T(8,128)(2,1)S(1)} %get-tuple-element.52.w_ref.inner_ref, bf16[256,512]{1,0:T(8,128)(2,1)S(1)} %get-tuple-element.75.head_ref), custom_call_target="tpu_custom_call" | custom-call | flops 161061280 | bytes 419430 | tf_op jit(solution)/shard_map/output/pallas_call | solution.py:279
  49.2 1.5 %collective-permute-start.21 = (bf16[32,512]{1,0:T(8,128)(2,1)S(1)}, bf16[32,512]{1,0:T(8,128)(2,1)S(1)}, u32[]{:S(2)}, u32[]{:S(2)}) collective-permute-start(bf16[32,512]{1,0:T(8,128)(2,1)S(1)} %get-tuple-element.92), channel_id=1, source_target_pairs={{0,16},{4,20},{8,24},{12,28},{16,0},{20,4},{24,8},{28,12},{1,17},{... | collective-permute-start | bytes 98312 | tf_op jit(solution)/shard_map/ppermute | solution.py:28
  50.8 1.6 %collective-permute-start.20 = (bf16[1,128,512]{2,1,0:T(8,128)(2,1)S(1)}, bf16[1,128,512]{2,1,0:T(8,128)(2,1)S(1)}, u32[]{:S(2)}, u32[]{:S(2)}) collective-permute-start(bf16[1,128,512]{2,1,0:T(8,128)(2,1)S(1)} %get-tuple-element.90), channel_id=1, source_target_pairs={{0,2},{1,3},{2,0},{3,1},{4,6},{5,7},{6,4},{7,5},{8,10},{9,11},{10,... | collective-permute-start | bytes 393224 | tf_op jit(solution)/shard_map/ppermute | solution.py:28
  52.4 1.7 %collective-permute-done.21.far_ref = bf16[32,512]{1,0:T(8,128)(2,1)S(1)} collective-permute-done((bf16[32,512]{1,0:T(8,128)(2,1)S(1)}, bf16[32,512]{1,0:T(8,128)(2,1)S(1)}, u32[]{:S(2)}, u32[]{:S(2)}) %collective-permute-start.21) | collective-permute-done | bytes 32800 | tf_op jit(solution)/shard_map/ppermute | solution.py:28
  54.1 0.6 %value_grad.1 = bf16[32,512]{1,0:T(8,128)(2,1)} custom-call(f32[32,512]{1,0:T(8,128)S(1)} %get-tuple-element.91.near_ref, bf16[32,512]{1,0:T(8,128)(2,1)S(1)} %collective-permute-done.21.far_ref), custom_call_target="tpu_custom_call" | custom-call | flops 4000000000 | bytes 16777216 | tf_op jit(solution)/shard_map/value_grad/pallas_call | solution.py:291
  54.7 1.7 %collective-permute-done.20 = bf16[1,128,512]{2,1,0:T(8,128)(2,1)S(1)} collective-permute-done((bf16[1,128,512]{2,1,0:T(8,128)(2,1)S(1)}, bf16[1,128,512]{2,1,0:T(8,128)(2,1)S(1)}, u32[]{:S(2)}, u32[]{:S(2)}) %collective-permute-start.20) | collective-permute-done | bytes 131104 | tf_op jit(solution)/shard_map/ppermute | solution.py:28
  56.4 0.7 %add_bitcast_fusion = f32[128,512]{1,0:T(8,128)} fusion(f32[1,128,512]{2,1,0:T(8,128)S(1)} %get-tuple-element.94, bf16[1,128,512]{2,1,0:T(8,128)(2,1)S(1)} %collective-permute-done.20), kind=kLoop, calls=%fused_computation | loop fusion | flops 131072 | bytes 655360 | tf_op jit(solution)/shard_map/add | solution.py:465
  (31 shorter events, 1.5 us)
Async XLA Ops:
  0.6 18.6 %copy-start = (bf16[1,128,4096]{2,1,0:T(8,128)(2,1)S(1)}, bf16[1,128,4096]{2,1,0:T(8,128)(2,1)}, u32[]{:S(2)}) copy-start(bf16[1,128,4096]{2,1,0:T(8,128)(2,1)} %param.11) | copy-start | bytes 3145732
  0.6 18.6 %copy-start.1 = (bf16[1,128,4096]{2,1,0:T(8,128)(2,1)S(1)}, bf16[1,128,4096]{2,1,0:T(8,128)(2,1)}, u32[]{:S(2)}) copy-start(bf16[1,128,4096]{2,1,0:T(8,128)(2,1)} %param.10) | copy-start | bytes 3145732
  0.7 18.6 %copy-start.2 = (s32[1,8]{1,0:T(1,128)S(1)}, s32[1,8]{1,0:T(1,128)}, u32[]{:S(2)}) copy-start(s32[1,8]{1,0:T(1,128)} %frame_ref.1) | copy-start | bytes 100
  3.4 7.6 %collective-permute-start = (bf16[32,1024]{1,0:T(8,128)(2,1)S(1)}, bf16[32,1024]{1,0:T(8,128)(2,1)S(1)}, u32[]{:S(2)}, u32[]{:S(2)}) collective-permute-start(bf16[32,1024]{1,0:T(8,128)(2,1)S(1)} %get-tuple-element.50.refs_0_), channel_id=1, source_target_pairs={{0,16},{4,20},{8,24},{12,28},{16,0},{20,4},{24,8},{28,12},{1,17},{... | collective-permute-start | bytes 196616 | tf_op jit(solution)/shard_map/ppermute | solution.py:28
  7.5 6.5 %collective-permute-start.4 = (bf16[32,1024]{1,0:T(8,128)(2,1)S(1)}, bf16[32,1024]{1,0:T(8,128)(2,1)S(1)}, u32[]{:S(2)}, u32[]{:S(2)}) collective-permute-start(bf16[32,1024]{1,0:T(8,128)(2,1)S(1)} %get-tuple-element.50.refs_0_), channel_id=1, source_target_pairs={{0,12},{4,8},{8,4},{12,0},{16,28},{20,24},{24,20},{28,16},{1,13},{... | collective-permute-start | bytes 196616 | tf_op jit(solution)/shard_map/ppermute | solution.py:28
  10.1 5.5 %collective-permute-start.5 = (bf16[32,1024]{1,0:T(8,128)(2,1)S(1)}, bf16[32,1024]{1,0:T(8,128)(2,1)S(1)}, u32[]{:S(2)}, u32[]{:S(2)}) collective-permute-start(bf16[32,1024]{1,0:T(8,128)(2,1)S(1)} %get-tuple-element.50.refs_0_), channel_id=1, source_target_pairs={{0,8},{4,12},{8,0},{12,4},{16,24},{20,28},{24,16},{28,20},{1,9},{5... | collective-permute-start | bytes 196616 | tf_op jit(solution)/shard_map/ppermute | solution.py:28
  10.5 6.9 %collective-permute-start.6 = (bf16[32,1024]{1,0:T(8,128)(2,1)S(1)}, bf16[32,1024]{1,0:T(8,128)(2,1)S(1)}, u32[]{:S(2)}, u32[]{:S(2)}) collective-permute-start(bf16[32,1024]{1,0:T(8,128)(2,1)S(1)} %get-tuple-element.50.refs_0_), channel_id=1, source_target_pairs={{0,4},{4,0},{8,12},{12,8},{16,20},{20,16},{24,28},{28,24},{1,5},{5... | collective-permute-start | bytes 196616 | tf_op jit(solution)/shard_map/ppermute | solution.py:28
  11.0 6.4 %collective-permute-start.1 = (bf16[32,1024]{1,0:T(8,128)(2,1)S(1)}, bf16[32,1024]{1,0:T(8,128)(2,1)S(1)}, u32[]{:S(2)}, u32[]{:S(2)}) collective-permute-start(bf16[32,1024]{1,0:T(8,128)(2,1)S(1)} %collective-permute-done.refs_4_), channel_id=1, source_target_pairs={{0,12},{4,8},{8,4},{12,0},{16,28},{20,24},{24,20},{28,16},{1,13},{... | collective-permute-start | bytes 196616 | tf_op jit(solution)/shard_map/ppermute | solution.py:28
  13.6 5.7 %collective-permute-start.2 = (bf16[32,1024]{1,0:T(8,128)(2,1)S(1)}, bf16[32,1024]{1,0:T(8,128)(2,1)S(1)}, u32[]{:S(2)}, u32[]{:S(2)}) collective-permute-start(bf16[32,1024]{1,0:T(8,128)(2,1)S(1)} %collective-permute-done.refs_4_), channel_id=1, source_target_pairs={{0,8},{4,12},{8,0},{12,4},{16,24},{20,28},{24,16},{28,20},{1,9},{5... | collective-permute-start | bytes 196616 | tf_op jit(solution)/shard_map/ppermute | solution.py:28
  14.0 5.2 %collective-permute-start.3 = (bf16[32,1024]{1,0:T(8,128)(2,1)S(1)}, bf16[32,1024]{1,0:T(8,128)(2,1)S(1)}, u32[]{:S(2)}, u32[]{:S(2)}) collective-permute-start(bf16[32,1024]{1,0:T(8,128)(2,1)S(1)} %collective-permute-done.refs_4_), channel_id=1, source_target_pairs={{0,4},{4,0},{8,12},{12,8},{16,20},{20,16},{24,28},{28,24},{1,5},{5... | collective-permute-start | bytes 196616 | tf_op jit(solution)/shard_map/ppermute | solution.py:28
  15.6 8.2 %collective-permute-start.7 = (bf16[128,512]{1,0:T(8,128)(2,1)S(1)}, bf16[128,512]{1,0:T(8,128)(2,1)S(1)}, u32[]{:S(2)}, u32[]{:S(2)}) collective-permute-start(bf16[128,512]{1,0:T(8,128)(2,1)S(1)} %get-tuple-element.58), channel_id=1, source_target_pairs={{0,16},{4,20},{8,24},{12,28},{16,0},{20,4},{24,8},{28,12},{1,17},{... | collective-permute-start | bytes 393224 | tf_op jit(solution)/shard_map/ppermute | solution.py:28
  23.8 6.4 %collective-permute-start.8 = (bf16[64,512]{1,0:T(8,128)(2,1)S(1)}, bf16[64,512]{1,0:T(8,128)(2,1)S(1)}, u32[]{:S(2)}, u32[]{:S(2)}) collective-permute-start(bf16[64,512]{1,0:T(8,128)(2,1)S(1)} %get-tuple-element.59), channel_id=1, source_target_pairs={{0,12},{4,8},{8,4},{12,0},{16,28},{20,24},{24,20},{28,16},{1,13},{... | collective-permute-start | bytes 196616 | tf_op jit(solution)/shard_map/ppermute | solution.py:28
  25.0 5.2 %collective-permute-start.9 = (bf16[64,512]{1,0:T(8,128)(2,1)S(1)}, bf16[64,512]{1,0:T(8,128)(2,1)S(1)}, u32[]{:S(2)}, u32[]{:S(2)}) collective-permute-start(bf16[64,512]{1,0:T(8,128)(2,1)S(1)} %get-tuple-element.60), channel_id=1, source_target_pairs={{0,8},{4,12},{8,0},{12,4},{16,24},{20,28},{24,16},{28,20},{1,9},{5... | collective-permute-start | bytes 196616 | tf_op jit(solution)/shard_map/ppermute | solution.py:28
  26.1 4.3 %collective-permute-start.10 = (bf16[64,512]{1,0:T(8,128)(2,1)S(1)}, bf16[64,512]{1,0:T(8,128)(2,1)S(1)}, u32[]{:S(2)}, u32[]{:S(2)}) collective-permute-start(bf16[64,512]{1,0:T(8,128)(2,1)S(1)} %get-tuple-element.61), channel_id=1, source_target_pairs={{0,4},{4,0},{8,12},{12,8},{16,20},{20,16},{24,28},{28,24},{1,5},{5... | collective-permute-start | bytes 196616 | tf_op jit(solution)/shard_map/ppermute | solution.py:28
  30.4 4.9 %collective-permute-start.11 = (bf16[32,512]{1,0:T(8,128)(2,1)S(1)}, bf16[32,512]{1,0:T(8,128)(2,1)S(1)}, u32[]{:S(2)}, u32[]{:S(2)}) collective-permute-start(bf16[32,512]{1,0:T(8,128)(2,1)S(1)} %get-tuple-element.68), channel_id=1, source_target_pairs={{0,16},{4,20},{8,24},{12,28},{16,0},{20,4},{24,8},{28,12},{1,17},{... | collective-permute-start | bytes 98312 | tf_op jit(solution)/shard_map/ppermute | solution.py:28
  35.3 8.6 %collective-permute-start.12 = (bf16[32,1536]{1,0:T(8,128)(2,1)S(1)}, bf16[32,1536]{1,0:T(8,128)(2,1)S(1)}, u32[]{:S(2)}, u32[]{:S(2)}) collective-permute-start(bf16[32,1536]{1,0:T(8,128)(2,1)S(1)} %get-tuple-element.72), channel_id=1, source_target_pairs={{0,4},{4,0},{8,12},{12,8},{16,20},{20,16},{24,28},{28,24},{1,5},{5... | collective-permute-start | bytes 294920 | tf_op jit(solution)/shard_map/ppermute | solution.py:28
  37.0 5.2 %collective-permute-start.15 = (bf16[32,512]{1,0:T(8,128)(2,1)S(1)}, bf16[32,512]{1,0:T(8,128)(2,1)S(1)}, u32[]{:S(2)}, u32[]{:S(2)}) collective-permute-start(bf16[32,512]{1,0:T(8,128)(2,1)S(1)} %get-tuple-element.81), channel_id=1, source_target_pairs={{0,16},{4,20},{8,24},{12,28},{16,0},{20,4},{24,8},{28,12},{1,17},{... | collective-permute-start | bytes 98312 | tf_op jit(solution)/shard_map/ppermute | solution.py:28
  38.6 9.6 %collective-permute-start.13 = (bf16[32,1536]{1,0:T(8,128)(2,1)S(1)}, bf16[32,1536]{1,0:T(8,128)(2,1)S(1)}, u32[]{:S(2)}, u32[]{:S(2)}) collective-permute-start(bf16[32,1536]{1,0:T(8,128)(2,1)S(1)} %get-tuple-element.73), channel_id=1, source_target_pairs={{0,8},{4,12},{8,0},{12,4},{16,24},{20,28},{24,16},{28,20},{1,9},{5... | collective-permute-start | bytes 294920 | tf_op jit(solution)/shard_map/ppermute | solution.py:28
  40.2 8.1 %collective-permute-start.14 = (bf16[32,1536]{1,0:T(8,128)(2,1)S(1)}, bf16[32,1536]{1,0:T(8,128)(2,1)S(1)}, u32[]{:S(2)}, u32[]{:S(2)}) collective-permute-start(bf16[32,1536]{1,0:T(8,128)(2,1)S(1)} %get-tuple-element.74), channel_id=1, source_target_pairs={{0,12},{4,8},{8,4},{12,0},{16,28},{20,24},{24,20},{28,16},{1,13},{... | collective-permute-start | bytes 294920 | tf_op jit(solution)/shard_map/ppermute | solution.py:28
  42.1 6.3 %collective-permute-start.16 = (bf16[32,1536]{1,0:T(8,128)(2,1)S(1)}, bf16[32,1536]{1,0:T(8,128)(2,1)S(1)}, u32[]{:S(2)}, u32[]{:S(2)}) collective-permute-start(bf16[32,1536]{1,0:T(8,128)(2,1)S(1)} %get-tuple-element.85), channel_id=1, source_target_pairs={{0,12},{4,8},{8,4},{12,0},{16,28},{20,24},{24,20},{28,16},{1,13},{... | collective-permute-start | bytes 294920 | tf_op jit(solution)/shard_map/ppermute | solution.py:28
  43.5 4.9 %collective-permute-start.17 = (bf16[32,1536]{1,0:T(8,128)(2,1)S(1)}, bf16[32,1536]{1,0:T(8,128)(2,1)S(1)}, u32[]{:S(2)}, u32[]{:S(2)}) collective-permute-start(bf16[32,1536]{1,0:T(8,128)(2,1)S(1)} %get-tuple-element.86), channel_id=1, source_target_pairs={{0,8},{4,12},{8,0},{12,4},{16,24},{20,28},{24,16},{28,20},{1,9},{5... | collective-permute-start | bytes 294920 | tf_op jit(solution)/shard_map/ppermute | solution.py:28
  43.9 4.9 %collective-permute-start.18 = (bf16[32,1536]{1,0:T(8,128)(2,1)S(1)}, bf16[32,1536]{1,0:T(8,128)(2,1)S(1)}, u32[]{:S(2)}, u32[]{:S(2)}) collective-permute-start(bf16[32,1536]{1,0:T(8,128)(2,1)S(1)} %get-tuple-element.87), channel_id=1, source_target_pairs={{0,4},{4,0},{8,12},{12,8},{16,20},{20,16},{24,28},{28,24},{1,5},{5... | collective-permute-start | bytes 294920 | tf_op jit(solution)/shard_map/ppermute | solution.py:28
  49.1 1.6 %collective-permute-start.19 = (bf16[2,128,512]{2,1,0:T(8,128)(2,1)S(1)}, bf16[2,128,512]{2,1,0:T(8,128)(2,1)S(1)}, u32[]{:S(2)}, u32[]{:S(2)}) collective-permute-start(bf16[2,128,512]{2,1,0:T(8,128)(2,1)S(1)} %get-tuple-element.89), channel_id=1, source_target_pairs={{0,1},{1,0},{2,3},{3,2},{4,5},{5,4},{6,7},{7,6},{8,9},{9,8},{10,11... | collective-permute-start | bytes 786440 | tf_op jit(solution)/shard_map/ppermute | solution.py:28
  49.2 4.9 %collective-permute-start.21 = (bf16[32,512]{1,0:T(8,128)(2,1)S(1)}, bf16[32,512]{1,0:T(8,128)(2,1)S(1)}, u32[]{:S(2)}, u32[]{:S(2)}) collective-permute-start(bf16[32,512]{1,0:T(8,128)(2,1)S(1)} %get-tuple-element.92), channel_id=1, source_target_pairs={{0,16},{4,20},{8,24},{12,28},{16,0},{20,4},{24,8},{28,12},{1,17},{... | collective-permute-start | bytes 98312 | tf_op jit(solution)/shard_map/ppermute | solution.py:28
  50.8 5.6 %collective-permute-start.20 = (bf16[1,128,512]{2,1,0:T(8,128)(2,1)S(1)}, bf16[1,128,512]{2,1,0:T(8,128)(2,1)S(1)}, u32[]{:S(2)}, u32[]{:S(2)}) collective-permute-start(bf16[1,128,512]{2,1,0:T(8,128)(2,1)S(1)} %get-tuple-element.90), channel_id=1, source_target_pairs={{0,2},{1,3},{2,0},{3,1},{4,6},{5,7},{6,4},{7,5},{8,10},{9,11},{10,... | collective-permute-start | bytes 393224 | tf_op jit(solution)/shard_map/ppermute | solution.py:28

commit v15 on v14

--- a/solution.py
+++ b/solution.py
@@ -166,16 +166,16 @@
                 scores = raw.pop(p) + bias_ref[...]
                 peak = jnp.max(scores, axis=0, keepdims=True)
                 shifted = jnp.exp2((scores - peak) * (scale * LOG2_E))
-                terms = shifted * dprobs.pop(p)
                 inverse = 1.0 / jnp.sum(shifted, axis=0, keepdims=True)
-                slope = inverse * scale
-                offset = jnp.sum(terms, axis=0, keepdims=True) * inverse * slope
+                change = dprobs.pop(p)
+                delta = jnp.sum(shifted * change, axis=0, keepdims=True) * inverse
+                probs = shifted * inverse
                 start = (i * KEY_HEADS + j) * span + p * pair
                 both = pl.ds(pl.multiple_of(start, HEAD_SIZE), pair)
-                w_ref[:, both] = (shifted * inverse).astype(BF16)
-                ds_stack.append((terms * slope - shifted * offset).astype(BF16))
+                w_ref[:, both] = probs.astype(BF16)
+                ds_stack.append((probs * (change - delta)).astype(BF16))
                 ds_ref[:, both] = ds_stack[p]
-            kg = dot(jnp.concatenate(ds_stack, axis=1), jnp.concatenate(q_stack, axis=0))
+            kg = dot(jnp.concatenate(ds_stack, axis=1), jnp.concatenate(q_stack, axis=0)) * scale
             if i == 0:
                 kg_acc[:, head] = kg
             else:
@@ -184,36 +184,29 @@
     store_sides(own_ref, near_refs, kg_acc, slice(None))
 
 
-def values_kernel(pieces, g_ref, w_ref, own_ref, *refs):
-    near_refs, vg_acc = refs[:-1], refs[-1]
-    j, i = pl.program_id(0), pl.program_id(1)
-    head = pl.ds(pl.multiple_of(j * HEAD_SIZE, HEAD_SIZE), HEAD_SIZE)
-    stack = [g_ref[:, h * HEAD_SIZE : (h + 1) * HEAD_SIZE] for h in range(HEADS_PER_KEY)]
-    vg = dot(w_ref[...], jnp.concatenate(stack, axis=0))
-
-    @pl.when(i == 0)
-    def _():
-        vg_acc[...] = vg
-
-    @pl.when(i > 0)
-    def _():
-        vg_acc[...] += vg
-
-    @pl.when(i == pl.num_programs(1) - 1)
-    def _():
-        store_sides(own_ref, near_refs, vg_acc, head)
-
-
-def store_rows(out_ref, left, inner_ref):
+def values_kernel(pieces, g_ref, w_ref, own_ref, *near_refs):
+    span = HEADS_PER_KEY * HEAD_SIZE
+    for j in range(KEY_HEADS):
+        total = 0.0
+        for i in range(g_ref.shape[0] // TILE):
+            text = slice(i * TILE, (i + 1) * TILE)
+            starts = range(j * span, (j + 1) * span, HEAD_SIZE)
+            stack = [g_ref[text, start : start + HEAD_SIZE] for start in starts]
+            first = (i * KEY_HEADS + j) * span
+            total += dot(w_ref[:, first : first + span], jnp.concatenate(stack, axis=0))
+        store_sides(own_ref, near_refs, total, slice(j * HEAD_SIZE, (j + 1) * HEAD_SIZE))
+
+
+def rows_kernel(factor, pieces, inner_ref, head_ref, out_ref):
+    left = head_ref[...].T
     pair = 2 * TILE
     for p in range(HEADS_PER_KEY // 2):
-        out = dot(left, inner_ref[:, p * pair : (p + 1) * pair]).T.astype(BF16)
+        out = dot(left, inner_ref[:, p * pair : (p + 1) * pair])
+        if factor is not None:
+            out *= factor
+        out = out.T.astype(BF16)
         out_ref[:, p * pair : p * pair + HEAD_SIZE] = out[:TILE]
         out_ref[:, p * pair + HEAD_SIZE : (p + 1) * pair] = out[TILE:]
-
-
-def rows_kernel(pieces, inner_ref, head_ref, out_ref):
-    store_rows(out_ref, head_ref[...].T, inner_ref)
 
 
 class Attention:
@@ -267,17 +260,15 @@
             values_kernel,
             0.1,
             "values",
-            grid=(KEY_HEADS, self.tiles),
-            in_specs=[self.text_block, self.inner_block],
-            out_specs=[pl.BlockSpec(self.sides, lambda j, i: (0, 0))] * len(self.terms),
+            in_specs=[VMEM] * 2,
+            out_specs=[VMEM] * len(self.terms),
             out_shape=self.terms,
-            scratch_shapes=[pltpu.VMEM((self.all_rows, HEAD_SIZE), F32)],
-        )(in_hbm(gradients), weights)
+        )(gradients, weights)
         return out[0], out[1:]
 
-    def over_rows(self, inner, heads, name):
+    def over_rows(self, inner, heads, name, factor=None):
         return self.call(
-            rows_kernel,
+            functools.partial(rows_kernel, factor),
             0.1,
             name,
             grid=(KEY_HEADS, self.tiles),
@@ -441,7 +432,7 @@
     key_sum, key_far = near_sums(key_own, key_near[::-1], "key_sums")
     key_sum, dscores = tie((key_sum, dscores))
     key_far = swap(key_far, "blk", half)
-    query_grad = attention.over_rows(dscores, keys, "query_grad")
+    query_grad = attention.over_rows(dscores, keys, "query_grad", HEAD_SIZE**-0.5)
     key_sum, query_grad = tie((key_sum, query_grad))
     key_grad, key_again, visual_own, near = add_far(key_sum, key_far, visual_near, visual_far)
 

time: 57.3 us -> 57.3 us (level)
  Pallas kernels: 16.4 us -> 13.6 us
  waiting for transfers between devices: 7.62 us -> 10.3 us
    ppermute x22, waiting for transfers between devices: 7.62 us -> 10.3 us  [swap(): return lax.ppermute(x, axis, [(i, i ^ mask) for i in range(size)])]
    pallas_call x3, Pallas kernels: 7.98 us -> 5.82 us  [the longest x2 5.12 us: over_rows(): self.call(functools.partial(rows_kernel, factor), 0.1, name, grid=(KEY_HE...]
    pallas_call x1, Pallas kernels: 4.51 us -> 3.86 us  [scores(): self.call(scores_kernel, 1.0, 'scores', in_specs=[smem, smem, VMEM, VMEM]...]
  transfers between devices with their start and end apart: 22 -> 22, of which waited for: 7 -> 11; matrix products, arithmetic and copies ran while one was open for 0% -> 0% of each run, Pallas kernels for 23% -> 18%
where the time goes in v15:
time: 57.3 us; the launch traced here: 57.2 us
  starting transfers between devices  31.1 us (54%)
  Pallas kernels  13.6 us (24%)
  waiting for transfers between devices  10.3 us (18%)
  between operations  1.41 us (2%)
  other arithmetic  0.73 us (1%)
    ppermute x22, starting transfers between devices, swap(): return lax.ppermute(x, axis, [(i, i ^ mask) for i in range(size)])  31.1 us
    ppermute x22, waiting for transfers between devices, swap(): return lax.ppermute(x, axis, [(i, i ^ mask) for i in range(size)])  10.3 us
    pallas_call x2, Pallas kernels, over_rows(): self.call(functools.partial(rows_kernel, factor), 0.1, name, grid=(KEY_HE...  5.12 us
    pallas_call x1, Pallas kernels, scores(): self.call(scores_kernel, 1.0, 'scores', in_specs=[smem, smem, VMEM, VMEM]...  3.86 us
    pallas_call x1, Pallas kernels, project(): pl.pallas_call(functools.partial(project_kernel, chunks), in_specs=[pl.Bl...  2.75 us
    pallas_call x7, Pallas kernels, in_vmem(): pl.pallas_call(kernel, cost_estimate=cost, in_specs=[VMEM] * len(arrays),...  1.19 us
  transfers between devices with their start and end apart: 22, of which 11 were waited for; matrix products, arithmetic and copies ran while one was open for 0% of the time, Pallas kernels for 18%

profile of v15, /device:TPU:0, one launch (start us, length us, event | category | flops | bytes accessed | tf_op | source)
XLA Modules:
  0.0 57.2 jit_solution(7926758353136113992)
XLA Ops:
  0.7 2.8 %project.1 = (bf16[32,1024]{1,0:T(8,128)(2,1)S(1)}, bf16[128,512]{1,0:T(8,128)(2,1)S(1)}, bf16[128,512]{1,0:T(8,128)(2,1)S(1)}) custom-call(bf16[4096,512]{1,0:T(8,128)(2,1)} %weight_hbm.1, bf16[32,4096]{1,0:T(8,128)(2,1)} %bitcast.14, bf16[32,512]{1,0:T(8,128)(2,1)} %bitcast.15), custom_call_target="tpu_custom_call" | custom-call | flops 134217728 | bytes 4194304 | tf_op jit(solution)/shard_map/project/pallas_call | solution.py:88
  3.4 4.1 %collective-permute-start = (bf16[32,1024]{1,0:T(8,128)(2,1)S(1)}, bf16[32,1024]{1,0:T(8,128)(2,1)S(1)}, u32[]{:S(2)}, u32[]{:S(2)}) collective-permute-start(bf16[32,1024]{1,0:T(8,128)(2,1)S(1)} %get-tuple-element.50.refs_0_), channel_id=1, source_target_pairs={{0,16},{4,20},{8,24},{12,28},{16,0},{20,4},{24,8},{28,12},{1,17},{... | collective-permute-start | bytes 196616 | tf_op jit(solution)/shard_map/ppermute | solution.py:28
  7.5 2.5 %collective-permute-start.4 = (bf16[32,1024]{1,0:T(8,128)(2,1)S(1)}, bf16[32,1024]{1,0:T(8,128)(2,1)S(1)}, u32[]{:S(2)}, u32[]{:S(2)}) collective-permute-start(bf16[32,1024]{1,0:T(8,128)(2,1)S(1)} %get-tuple-element.50.refs_0_), channel_id=1, source_target_pairs={{0,12},{4,8},{8,4},{12,0},{16,28},{20,24},{24,20},{28,16},{1,13},{... | collective-permute-start | bytes 196616 | tf_op jit(solution)/shard_map/ppermute | solution.py:28
  11.0 2.5 %collective-permute-start.1 = (bf16[32,1024]{1,0:T(8,128)(2,1)S(1)}, bf16[32,1024]{1,0:T(8,128)(2,1)S(1)}, u32[]{:S(2)}, u32[]{:S(2)}) collective-permute-start(bf16[32,1024]{1,0:T(8,128)(2,1)S(1)} %collective-permute-done.refs_4_), channel_id=1, source_target_pairs={{0,12},{4,8},{8,4},{12,0},{16,28},{20,24},{24,20},{28,16},{1,13},{... | collective-permute-start | bytes 196616 | tf_op jit(solution)/shard_map/ppermute | solution.py:28
  14.0 0.9 %collective-permute-start.3 = (bf16[32,1024]{1,0:T(8,128)(2,1)S(1)}, bf16[32,1024]{1,0:T(8,128)(2,1)S(1)}, u32[]{:S(2)}, u32[]{:S(2)}) collective-permute-start(bf16[32,1024]{1,0:T(8,128)(2,1)S(1)} %collective-permute-done.refs_4_), channel_id=1, source_target_pairs={{0,4},{4,0},{8,12},{12,8},{16,20},{20,16},{24,28},{28,24},{1,5},{5... | collective-permute-start | bytes 196616 | tf_op jit(solution)/shard_map/ppermute | solution.py:28
  15.6 1.9 %collective-permute-start.7 = (bf16[128,512]{1,0:T(8,128)(2,1)S(1)}, bf16[128,512]{1,0:T(8,128)(2,1)S(1)}, u32[]{:S(2)}, u32[]{:S(2)}) collective-permute-start(bf16[128,512]{1,0:T(8,128)(2,1)S(1)} %get-tuple-element.58), channel_id=1, source_target_pairs={{0,16},{4,20},{8,24},{12,28},{16,0},{20,4},{24,8},{28,12},{1,17},{... | collective-permute-start | bytes 393224 | tf_op jit(solution)/shard_map/ppermute | solution.py:28
  17.4 1.8 %collective-permute-done.2.refs_2_ = bf16[32,1024]{1,0:T(8,128)(2,1)S(1)} collective-permute-done((bf16[32,1024]{1,0:T(8,128)(2,1)S(1)}, bf16[32,1024]{1,0:T(8,128)(2,1)S(1)}, u32[]{:S(2)}, u32[]{:S(2)}) %collective-permute-start.2) | collective-permute-done | bytes 65568 | tf_op jit(solution)/shard_map/ppermute | solution.py:28
  19.2 3.9 %scores.1 = (bf16[256,4096]{1,0:T(8,128)(2,1)S(1)}, bf16[256,4096]{1,0:T(8,128)(2,1)S(1)}, bf16[256,512]{1,0:T(8,128)(2,1)S(1)}, bf16[256,512]{1,0:T(8,128)(2,1)...) custom-call(s32[1]{0:T(128)S(6)} %copy.11.length_ref, ...), custom_call_target="tpu_custom_call" | custom-call | flops 1610612736 | bytes 4194304 | tf_op jit(solution)/shard_map/scores/pallas_call | solution.py:244
  23.3 1.2 %collective-permute-start.8 = (bf16[64,512]{1,0:T(8,128)(2,1)S(1)}, bf16[64,512]{1,0:T(8,128)(2,1)S(1)}, u32[]{:S(2)}, u32[]{:S(2)}) collective-permute-start(bf16[64,512]{1,0:T(8,128)(2,1)S(1)} %get-tuple-element.59), channel_id=1, source_target_pairs={{0,12},{4,8},{8,4},{12,0},{16,28},{20,24},{24,20},{28,16},{1,13},{... | collective-permute-start | bytes 196616 | tf_op jit(solution)/shard_map/ppermute | solution.py:28
  24.5 1.6 %collective-permute-start.9 = (bf16[64,512]{1,0:T(8,128)(2,1)S(1)}, bf16[64,512]{1,0:T(8,128)(2,1)S(1)}, u32[]{:S(2)}, u32[]{:S(2)}) collective-permute-start(bf16[64,512]{1,0:T(8,128)(2,1)S(1)} %get-tuple-element.60), channel_id=1, source_target_pairs={{0,8},{4,12},{8,0},{12,4},{16,24},{20,28},{24,16},{28,20},{1,9},{5... | collective-permute-start | bytes 196616 | tf_op jit(solution)/shard_map/ppermute | solution.py:28
  26.1 0.7 %collective-permute-start.10 = (bf16[64,512]{1,0:T(8,128)(2,1)S(1)}, bf16[64,512]{1,0:T(8,128)(2,1)S(1)}, u32[]{:S(2)}, u32[]{:S(2)}) collective-permute-start(bf16[64,512]{1,0:T(8,128)(2,1)S(1)} %get-tuple-element.61), channel_id=1, source_target_pairs={{0,4},{4,0},{8,12},{12,8},{16,20},{20,16},{24,28},{28,24},{1,5},{5... | collective-permute-start | bytes 196616 | tf_op jit(solution)/shard_map/ppermute | solution.py:28
  26.8 0.7 %values.1 = (f32[64,512]{1,0:T(8,128)S(1)}, bf16[64,512]{1,0:T(8,128)(2,1)S(1)}, bf16[64,512]{1,0:T(8,128)(2,1)S(1)}, bf16[64,512]{1,0:T(8,128)(2,1)S(1)}) custom-call(bf16[128,4096]{1,0:T(8,128)(2,1)S(1)} %bitcast.10, bf16[256,4096]{1,0:T(8,128)(2,1)S(1)} %get-tuple-element.52.w_ref.inner_ref), custom_call_target="tpu_custom_call" | custom-call | flops 161061280 | bytes 419430 | tf_op jit(solution)/shard_map/values/pallas_call | solution.py:259
  27.5 1.0 %collective-permute-done.8.refs_0_ = bf16[64,512]{1,0:T(8,128)(2,1)S(1)} collective-permute-done((bf16[64,512]{1,0:T(8,128)(2,1)S(1)}, bf16[64,512]{1,0:T(8,128)(2,1)S(1)}, u32[]{:S(2)}, u32[]{:S(2)}) %collective-permute-start.8) | collective-permute-done | bytes 65568 | tf_op jit(solution)/shard_map/ppermute | solution.py:28
  28.5 0.5 collective-permute-done.9.refs_1_
  29.0 1.3 %collective-permute-done.10.refs_2_ = bf16[64,512]{1,0:T(8,128)(2,1)S(1)} collective-permute-done((bf16[64,512]{1,0:T(8,128)(2,1)S(1)}, bf16[64,512]{1,0:T(8,128)(2,1)S(1)}, u32[]{:S(2)}, u32[]{:S(2)}) %collective-permute-start.10) | collective-permute-done | bytes 65568 | tf_op jit(solution)/shard_map/ppermute | solution.py:28
  30.4 1.9 %collective-permute-start.11 = (bf16[32,512]{1,0:T(8,128)(2,1)S(1)}, bf16[32,512]{1,0:T(8,128)(2,1)S(1)}, u32[]{:S(2)}, u32[]{:S(2)}) collective-permute-start(bf16[32,512]{1,0:T(8,128)(2,1)S(1)} %get-tuple-element.68), channel_id=1, source_target_pairs={{0,16},{4,20},{8,24},{12,28},{16,0},{20,4},{24,8},{28,12},{1,17},{... | collective-permute-start | bytes 98312 | tf_op jit(solution)/shard_map/ppermute | solution.py:28
  32.2 2.6 %query_grad.1 = bf16[128,4096]{1,0:T(8,128)(2,1)} custom-call(bf16[256,4096]{1,0:T(8,128)(2,1)S(1)} %get-tuple-element.65.inner_ref, bf16[256,512]{1,0:T(8,128)(2,1)S(1)} %get-tuple-element.66.head_ref), custom_call_target="tpu_custom_call" | custom-call | flops 161061280 | bytes 419430 | tf_op jit(solution)/shard_map/query_grad/pallas_call | solution.py:270
  35.3 1.1 %collective-permute-start.12 = (bf16[32,1536]{1,0:T(8,128)(2,1)S(1)}, bf16[32,1536]{1,0:T(8,128)(2,1)S(1)}, u32[]{:S(2)}, u32[]{:S(2)}) collective-permute-start(bf16[32,1536]{1,0:T(8,128)(2,1)S(1)} %get-tuple-element.72), channel_id=1, source_target_pairs={{0,4},{4,0},{8,12},{12,8},{16,20},{20,16},{24,28},{28,24},{1,5},{5... | collective-permute-start | bytes 294920 | tf_op jit(solution)/shard_map/ppermute | solution.py:28
  36.4 1.5 %collective-permute-start.15 = (bf16[32,512]{1,0:T(8,128)(2,1)S(1)}, bf16[32,512]{1,0:T(8,128)(2,1)S(1)}, u32[]{:S(2)}, u32[]{:S(2)}) collective-permute-start(bf16[32,512]{1,0:T(8,128)(2,1)S(1)} %get-tuple-element.81), channel_id=1, source_target_pairs={{0,16},{4,20},{8,24},{12,28},{16,0},{20,4},{24,8},{28,12},{1,17},{... | collective-permute-start | bytes 98312 | tf_op jit(solution)/shard_map/ppermute | solution.py:28
  37.9 1.9 %collective-permute-start.13 = (bf16[32,1536]{1,0:T(8,128)(2,1)S(1)}, bf16[32,1536]{1,0:T(8,128)(2,1)S(1)}, u32[]{:S(2)}, u32[]{:S(2)}) collective-permute-start(bf16[32,1536]{1,0:T(8,128)(2,1)S(1)} %get-tuple-element.73), channel_id=1, source_target_pairs={{0,8},{4,12},{8,0},{12,4},{16,24},{20,28},{24,16},{28,20},{1,9},{5... | collective-permute-start | bytes 294920 | tf_op jit(solution)/shard_map/ppermute | solution.py:28
  39.8 0.9 %collective-permute-start.14 = (bf16[32,1536]{1,0:T(8,128)(2,1)S(1)}, bf16[32,1536]{1,0:T(8,128)(2,1)S(1)}, u32[]{:S(2)}, u32[]{:S(2)}) collective-permute-start(bf16[32,1536]{1,0:T(8,128)(2,1)S(1)} %get-tuple-element.74), channel_id=1, source_target_pairs={{0,12},{4,8},{8,4},{12,0},{16,28},{20,24},{24,20},{28,16},{1,13},{... | collective-permute-start | bytes 294920 | tf_op jit(solution)/shard_map/ppermute | solution.py:28
  40.6 0.7 %collective-permute-done.15.far_ref.refs_7_ = bf16[32,512]{1,0:T(8,128)(2,1)S(1)} collective-permute-done((bf16[32,512]{1,0:T(8,128)(2,1)S(1)}, bf16[32,512]{1,0:T(8,128)(2,1)S(1)}, u32[]{:S(2)}, u32[]{:S(2)}) %collective-permute-start.15) | collective-permute-done | bytes 32800 | tf_op jit(solution)/shard_map/ppermute | solution.py:28
  41.4 2.3 %collective-permute-start.16 = (bf16[32,1536]{1,0:T(8,128)(2,1)S(1)}, bf16[32,1536]{1,0:T(8,128)(2,1)S(1)}, u32[]{:S(2)}, u32[]{:S(2)}) collective-permute-start(bf16[32,1536]{1,0:T(8,128)(2,1)S(1)} %get-tuple-element.85), channel_id=1, source_target_pairs={{0,12},{4,8},{8,4},{12,0},{16,28},{20,24},{24,20},{28,16},{1,13},{... | collective-permute-start | bytes 294920 | tf_op jit(solution)/shard_map/ppermute | solution.py:28
  43.9 1.1 %collective-permute-start.18 = (bf16[32,1536]{1,0:T(8,128)(2,1)S(1)}, bf16[32,1536]{1,0:T(8,128)(2,1)S(1)}, u32[]{:S(2)}, u32[]{:S(2)}) collective-permute-start(bf16[32,1536]{1,0:T(8,128)(2,1)S(1)} %get-tuple-element.87), channel_id=1, source_target_pairs={{0,4},{4,0},{8,12},{12,8},{16,20},{20,16},{24,28},{28,24},{1,5},{5... | collective-permute-start | bytes 294920 | tf_op jit(solution)/shard_map/ppermute | solution.py:28
  44.9 2.6 %output.1 = bf16[128,4096]{1,0:T(8,128)(2,1)} custom-call(bf16[256,4096]{1,0:T(8,128)(2,1)S(1)} %get-tuple-element.52.w_ref.inner_ref, bf16[256,512]{1,0:T(8,128)(2,1)S(1)} %get-tuple-element.75.head_ref), custom_call_target="tpu_custom_call" | custom-call | flops 161061280 | bytes 419430 | tf_op jit(solution)/shard_map/output/pallas_call | solution.py:270
  47.6 0.7 %collective-permute-done.17.refs_2_ = bf16[32,1536]{1,0:T(8,128)(2,1)S(1)} collective-permute-done((bf16[32,1536]{1,0:T(8,128)(2,1)S(1)}, bf16[32,1536]{1,0:T(8,128)(2,1)S(1)}, u32[]{:S(2)}, u32[]{:S(2)}) %collective-permute-start.17) | collective-permute-done | bytes 98336 | tf_op jit(solution)/shard_map/ppermute | solution.py:28
  48.9 1.9 %collective-permute-start.21 = (bf16[32,512]{1,0:T(8,128)(2,1)S(1)}, bf16[32,512]{1,0:T(8,128)(2,1)S(1)}, u32[]{:S(2)}, u32[]{:S(2)}) collective-permute-start(bf16[32,512]{1,0:T(8,128)(2,1)S(1)} %get-tuple-element.92), channel_id=1, source_target_pairs={{0,16},{4,20},{8,24},{12,28},{16,0},{20,4},{24,8},{28,12},{1,17},{... | collective-permute-start | bytes 98312 | tf_op jit(solution)/shard_map/ppermute | solution.py:28
  50.8 1.5 %collective-permute-start.20 = (bf16[1,128,512]{2,1,0:T(8,128)(2,1)S(1)}, bf16[1,128,512]{2,1,0:T(8,128)(2,1)S(1)}, u32[]{:S(2)}, u32[]{:S(2)}) collective-permute-start(bf16[1,128,512]{2,1,0:T(8,128)(2,1)S(1)} %get-tuple-element.90), channel_id=1, source_target_pairs={{0,2},{1,3},{2,0},{3,1},{4,6},{5,7},{6,4},{7,5},{8,10},{9,11},{10,... | collective-permute-start | bytes 393224 | tf_op jit(solution)/shard_map/ppermute | solution.py:28
  52.3 1.4 %collective-permute-done.21.far_ref = bf16[32,512]{1,0:T(8,128)(2,1)S(1)} collective-permute-done((bf16[32,512]{1,0:T(8,128)(2,1)S(1)}, bf16[32,512]{1,0:T(8,128)(2,1)S(1)}, u32[]{:S(2)}, u32[]{:S(2)}) %collective-permute-start.21) | collective-permute-done | bytes 32800 | tf_op jit(solution)/shard_map/ppermute | solution.py:28
  53.7 0.6 %value_grad.1 = bf16[32,512]{1,0:T(8,128)(2,1)} custom-call(f32[32,512]{1,0:T(8,128)S(1)} %get-tuple-element.91.near_ref, bf16[32,512]{1,0:T(8,128)(2,1)S(1)} %collective-permute-done.21.far_ref), custom_call_target="tpu_custom_call" | custom-call | flops 4000000000 | bytes 16777216 | tf_op jit(solution)/shard_map/value_grad/pallas_call | solution.py:282
  54.4 2.1 %collective-permute-done.20 = bf16[1,128,512]{2,1,0:T(8,128)(2,1)S(1)} collective-permute-done((bf16[1,128,512]{2,1,0:T(8,128)(2,1)S(1)}, bf16[1,128,512]{2,1,0:T(8,128)(2,1)S(1)}, u32[]{:S(2)}, u32[]{:S(2)}) %collective-permute-start.20) | collective-permute-done | bytes 131104 | tf_op jit(solution)/shard_map/ppermute | solution.py:28
  56.4 0.7 %add_bitcast_fusion = f32[128,512]{1,0:T(8,128)} fusion(f32[1,128,512]{2,1,0:T(8,128)S(1)} %get-tuple-element.94, bf16[1,128,512]{2,1,0:T(8,128)(2,1)S(1)} %collective-permute-done.20), kind=kLoop, calls=%fused_computation | loop fusion | flops 131072 | bytes 655360 | tf_op jit(solution)/shard_map/add | solution.py:456
  (31 shorter events, 3.0 us)
Async XLA Ops:
  0.6 18.6 %copy-start = (bf16[1,128,4096]{2,1,0:T(8,128)(2,1)S(1)}, bf16[1,128,4096]{2,1,0:T(8,128)(2,1)}, u32[]{:S(2)}) copy-start(bf16[1,128,4096]{2,1,0:T(8,128)(2,1)} %param.11) | copy-start | bytes 3145732
  0.6 18.6 %copy-start.1 = (bf16[1,128,4096]{2,1,0:T(8,128)(2,1)S(1)}, bf16[1,128,4096]{2,1,0:T(8,128)(2,1)}, u32[]{:S(2)}) copy-start(bf16[1,128,4096]{2,1,0:T(8,128)(2,1)} %param.10) | copy-start | bytes 3145732
  0.7 18.6 %copy-start.2 = (s32[1,8]{1,0:T(1,128)S(1)}, s32[1,8]{1,0:T(1,128)}, u32[]{:S(2)}) copy-start(s32[1,8]{1,0:T(1,128)} %frame_ref.1) | copy-start | bytes 100
  3.4 7.6 %collective-permute-start = (bf16[32,1024]{1,0:T(8,128)(2,1)S(1)}, bf16[32,1024]{1,0:T(8,128)(2,1)S(1)}, u32[]{:S(2)}, u32[]{:S(2)}) collective-permute-start(bf16[32,1024]{1,0:T(8,128)(2,1)S(1)} %get-tuple-element.50.refs_0_), channel_id=1, source_target_pairs={{0,16},{4,20},{8,24},{12,28},{16,0},{20,4},{24,8},{28,12},{1,17},{... | collective-permute-start | bytes 196616 | tf_op jit(solution)/shard_map/ppermute | solution.py:28
  7.5 6.5 %collective-permute-start.4 = (bf16[32,1024]{1,0:T(8,128)(2,1)S(1)}, bf16[32,1024]{1,0:T(8,128)(2,1)S(1)}, u32[]{:S(2)}, u32[]{:S(2)}) collective-permute-start(bf16[32,1024]{1,0:T(8,128)(2,1)S(1)} %get-tuple-element.50.refs_0_), channel_id=1, source_target_pairs={{0,12},{4,8},{8,4},{12,0},{16,28},{20,24},{24,20},{28,16},{1,13},{... | collective-permute-start | bytes 196616 | tf_op jit(solution)/shard_map/ppermute | solution.py:28
  10.1 5.5 %collective-permute-start.5 = (bf16[32,1024]{1,0:T(8,128)(2,1)S(1)}, bf16[32,1024]{1,0:T(8,128)(2,1)S(1)}, u32[]{:S(2)}, u32[]{:S(2)}) collective-permute-start(bf16[32,1024]{1,0:T(8,128)(2,1)S(1)} %get-tuple-element.50.refs_0_), channel_id=1, source_target_pairs={{0,8},{4,12},{8,0},{12,4},{16,24},{20,28},{24,16},{28,20},{1,9},{5... | collective-permute-start | bytes 196616 | tf_op jit(solution)/shard_map/ppermute | solution.py:28
  10.5 6.9 %collective-permute-start.6 = (bf16[32,1024]{1,0:T(8,128)(2,1)S(1)}, bf16[32,1024]{1,0:T(8,128)(2,1)S(1)}, u32[]{:S(2)}, u32[]{:S(2)}) collective-permute-start(bf16[32,1024]{1,0:T(8,128)(2,1)S(1)} %get-tuple-element.50.refs_0_), channel_id=1, source_target_pairs={{0,4},{4,0},{8,12},{12,8},{16,20},{20,16},{24,28},{28,24},{1,5},{5... | collective-permute-start | bytes 196616 | tf_op jit(solution)/shard_map/ppermute | solution.py:28
  11.0 6.4 %collective-permute-start.1 = (bf16[32,1024]{1,0:T(8,128)(2,1)S(1)}, bf16[32,1024]{1,0:T(8,128)(2,1)S(1)}, u32[]{:S(2)}, u32[]{:S(2)}) collective-permute-start(bf16[32,1024]{1,0:T(8,128)(2,1)S(1)} %collective-permute-done.refs_4_), channel_id=1, source_target_pairs={{0,12},{4,8},{8,4},{12,0},{16,28},{20,24},{24,20},{28,16},{1,13},{... | collective-permute-start | bytes 196616 | tf_op jit(solution)/shard_map/ppermute | solution.py:28
  13.5 5.7 %collective-permute-start.2 = (bf16[32,1024]{1,0:T(8,128)(2,1)S(1)}, bf16[32,1024]{1,0:T(8,128)(2,1)S(1)}, u32[]{:S(2)}, u32[]{:S(2)}) collective-permute-start(bf16[32,1024]{1,0:T(8,128)(2,1)S(1)} %collective-permute-done.refs_4_), channel_id=1, source_target_pairs={{0,8},{4,12},{8,0},{12,4},{16,24},{20,28},{24,16},{28,20},{1,9},{5... | collective-permute-start | bytes 196616 | tf_op jit(solution)/shard_map/ppermute | solution.py:28
  14.0 5.2 %collective-permute-start.3 = (bf16[32,1024]{1,0:T(8,128)(2,1)S(1)}, bf16[32,1024]{1,0:T(8,128)(2,1)S(1)}, u32[]{:S(2)}, u32[]{:S(2)}) collective-permute-start(bf16[32,1024]{1,0:T(8,128)(2,1)S(1)} %collective-permute-done.refs_4_), channel_id=1, source_target_pairs={{0,4},{4,0},{8,12},{12,8},{16,20},{20,16},{24,28},{28,24},{1,5},{5... | collective-permute-start | bytes 196616 | tf_op jit(solution)/shard_map/ppermute | solution.py:28
  15.6 7.7 %collective-permute-start.7 = (bf16[128,512]{1,0:T(8,128)(2,1)S(1)}, bf16[128,512]{1,0:T(8,128)(2,1)S(1)}, u32[]{:S(2)}, u32[]{:S(2)}) collective-permute-start(bf16[128,512]{1,0:T(8,128)(2,1)S(1)} %get-tuple-element.58), channel_id=1, source_target_pairs={{0,16},{4,20},{8,24},{12,28},{16,0},{20,4},{24,8},{28,12},{1,17},{... | collective-permute-start | bytes 393224 | tf_op jit(solution)/shard_map/ppermute | solution.py:28
  23.3 5.2 %collective-permute-start.8 = (bf16[64,512]{1,0:T(8,128)(2,1)S(1)}, bf16[64,512]{1,0:T(8,128)(2,1)S(1)}, u32[]{:S(2)}, u32[]{:S(2)}) collective-permute-start(bf16[64,512]{1,0:T(8,128)(2,1)S(1)} %get-tuple-element.59), channel_id=1, source_target_pairs={{0,12},{4,8},{8,4},{12,0},{16,28},{20,24},{24,20},{28,16},{1,13},{... | collective-permute-start | bytes 196616 | tf_op jit(solution)/shard_map/ppermute | solution.py:28
  24.5 4.5 %collective-permute-start.9 = (bf16[64,512]{1,0:T(8,128)(2,1)S(1)}, bf16[64,512]{1,0:T(8,128)(2,1)S(1)}, u32[]{:S(2)}, u32[]{:S(2)}) collective-permute-start(bf16[64,512]{1,0:T(8,128)(2,1)S(1)} %get-tuple-element.60), channel_id=1, source_target_pairs={{0,8},{4,12},{8,0},{12,4},{16,24},{20,28},{24,16},{28,20},{1,9},{5... | collective-permute-start | bytes 196616 | tf_op jit(solution)/shard_map/ppermute | solution.py:28
  26.1 4.3 %collective-permute-start.10 = (bf16[64,512]{1,0:T(8,128)(2,1)S(1)}, bf16[64,512]{1,0:T(8,128)(2,1)S(1)}, u32[]{:S(2)}, u32[]{:S(2)}) collective-permute-start(bf16[64,512]{1,0:T(8,128)(2,1)S(1)} %get-tuple-element.61), channel_id=1, source_target_pairs={{0,4},{4,0},{8,12},{12,8},{16,20},{20,16},{24,28},{28,24},{1,5},{5... | collective-permute-start | bytes 196616 | tf_op jit(solution)/shard_map/ppermute | solution.py:28
  30.4 4.9 %collective-permute-start.11 = (bf16[32,512]{1,0:T(8,128)(2,1)S(1)}, bf16[32,512]{1,0:T(8,128)(2,1)S(1)}, u32[]{:S(2)}, u32[]{:S(2)}) collective-permute-start(bf16[32,512]{1,0:T(8,128)(2,1)S(1)} %get-tuple-element.68), channel_id=1, source_target_pairs={{0,16},{4,20},{8,24},{12,28},{16,0},{20,4},{24,8},{28,12},{1,17},{... | collective-permute-start | bytes 98312 | tf_op jit(solution)/shard_map/ppermute | solution.py:28
  35.3 8.6 %collective-permute-start.12 = (bf16[32,1536]{1,0:T(8,128)(2,1)S(1)}, bf16[32,1536]{1,0:T(8,128)(2,1)S(1)}, u32[]{:S(2)}, u32[]{:S(2)}) collective-permute-start(bf16[32,1536]{1,0:T(8,128)(2,1)S(1)} %get-tuple-element.72), channel_id=1, source_target_pairs={{0,4},{4,0},{8,12},{12,8},{16,20},{20,16},{24,28},{28,24},{1,5},{5... | collective-permute-start | bytes 294920 | tf_op jit(solution)/shard_map/ppermute | solution.py:28
  36.4 4.9 %collective-permute-start.15 = (bf16[32,512]{1,0:T(8,128)(2,1)S(1)}, bf16[32,512]{1,0:T(8,128)(2,1)S(1)}, u32[]{:S(2)}, u32[]{:S(2)}) collective-permute-start(bf16[32,512]{1,0:T(8,128)(2,1)S(1)} %get-tuple-element.81), channel_id=1, source_target_pairs={{0,16},{4,20},{8,24},{12,28},{16,0},{20,4},{24,8},{28,12},{1,17},{... | collective-permute-start | bytes 98312 | tf_op jit(solution)/shard_map/ppermute | solution.py:28
  37.9 9.6 %collective-permute-start.13 = (bf16[32,1536]{1,0:T(8,128)(2,1)S(1)}, bf16[32,1536]{1,0:T(8,128)(2,1)S(1)}, u32[]{:S(2)}, u32[]{:S(2)}) collective-permute-start(bf16[32,1536]{1,0:T(8,128)(2,1)S(1)} %get-tuple-element.73), channel_id=1, source_target_pairs={{0,8},{4,12},{8,0},{12,4},{16,24},{20,28},{24,16},{28,20},{1,9},{5... | collective-permute-start | bytes 294920 | tf_op jit(solution)/shard_map/ppermute | solution.py:28
  39.8 7.7 %collective-permute-start.14 = (bf16[32,1536]{1,0:T(8,128)(2,1)S(1)}, bf16[32,1536]{1,0:T(8,128)(2,1)S(1)}, u32[]{:S(2)}, u32[]{:S(2)}) collective-permute-start(bf16[32,1536]{1,0:T(8,128)(2,1)S(1)} %get-tuple-element.74), channel_id=1, source_target_pairs={{0,12},{4,8},{8,4},{12,0},{16,28},{20,24},{24,20},{28,16},{1,13},{... | collective-permute-start | bytes 294920 | tf_op jit(solution)/shard_map/ppermute | solution.py:28
  41.4 6.3 %collective-permute-start.16 = (bf16[32,1536]{1,0:T(8,128)(2,1)S(1)}, bf16[32,1536]{1,0:T(8,128)(2,1)S(1)}, u32[]{:S(2)}, u32[]{:S(2)}) collective-permute-start(bf16[32,1536]{1,0:T(8,128)(2,1)S(1)} %get-tuple-element.85), channel_id=1, source_target_pairs={{0,12},{4,8},{8,4},{12,0},{16,28},{20,24},{24,20},{28,16},{1,13},{... | collective-permute-start | bytes 294920 | tf_op jit(solution)/shard_map/ppermute | solution.py:28
  43.7 4.6 %collective-permute-start.17 = (bf16[32,1536]{1,0:T(8,128)(2,1)S(1)}, bf16[32,1536]{1,0:T(8,128)(2,1)S(1)}, u32[]{:S(2)}, u32[]{:S(2)}) collective-permute-start(bf16[32,1536]{1,0:T(8,128)(2,1)S(1)} %get-tuple-element.86), channel_id=1, source_target_pairs={{0,8},{4,12},{8,0},{12,4},{16,24},{20,28},{24,16},{28,20},{1,9},{5... | collective-permute-start | bytes 294920 | tf_op jit(solution)/shard_map/ppermute | solution.py:28
  43.9 4.6 %collective-permute-start.18 = (bf16[32,1536]{1,0:T(8,128)(2,1)S(1)}, bf16[32,1536]{1,0:T(8,128)(2,1)S(1)}, u32[]{:S(2)}, u32[]{:S(2)}) collective-permute-start(bf16[32,1536]{1,0:T(8,128)(2,1)S(1)} %get-tuple-element.87), channel_id=1, source_target_pairs={{0,4},{4,0},{8,12},{12,8},{16,20},{20,16},{24,28},{28,24},{1,5},{5... | collective-permute-start | bytes 294920 | tf_op jit(solution)/shard_map/ppermute | solution.py:28
  48.8 1.9 %collective-permute-start.19 = (bf16[2,128,512]{2,1,0:T(8,128)(2,1)S(1)}, bf16[2,128,512]{2,1,0:T(8,128)(2,1)S(1)}, u32[]{:S(2)}, u32[]{:S(2)}) collective-permute-start(bf16[2,128,512]{2,1,0:T(8,128)(2,1)S(1)} %get-tuple-element.89), channel_id=1, source_target_pairs={{0,1},{1,0},{2,3},{3,2},{4,5},{5,4},{6,7},{7,6},{8,9},{9,8},{10,11... | collective-permute-start | bytes 786440 | tf_op jit(solution)/shard_map/ppermute | solution.py:28
  48.9 4.9 %collective-permute-start.21 = (bf16[32,512]{1,0:T(8,128)(2,1)S(1)}, bf16[32,512]{1,0:T(8,128)(2,1)S(1)}, u32[]{:S(2)}, u32[]{:S(2)}) collective-permute-start(bf16[32,512]{1,0:T(8,128)(2,1)S(1)} %get-tuple-element.92), channel_id=1, source_target_pairs={{0,16},{4,20},{8,24},{12,28},{16,0},{20,4},{24,8},{28,12},{1,17},{... | collective-permute-start | bytes 98312 | tf_op jit(solution)/shard_map/ppermute | solution.py:28
  50.8 5.6 %collective-permute-start.20 = (bf16[1,128,512]{2,1,0:T(8,128)(2,1)S(1)}, bf16[1,128,512]{2,1,0:T(8,128)(2,1)S(1)}, u32[]{:S(2)}, u32[]{:S(2)}) collective-permute-start(bf16[1,128,512]{2,1,0:T(8,128)(2,1)S(1)} %get-tuple-element.90), channel_id=1, source_target_pairs={{0,2},{1,3},{2,0},{3,1},{4,6},{5,7},{6,4},{7,5},{8,10},{9,11},{10,... | collective-permute-start | bytes 393224 | tf_op jit(solution)/shard_map/ppermute | solution.py:28

commit v16 on v15

--- a/solution.py
+++ b/solution.py
@@ -424,11 +424,10 @@
         visual_len, frame_end, queries[0], output_gradient[0], keys_values
     )
     weights, dscores, keys, values = inner
-    key_near, visual_far = tie((key_near, visual_far))
 
     key_near = near_exchange(key_near)
     value_own, value_near = attention.values(output_gradient[0], weights)
-    key_own, value_own = tie((key_own, value_own))
+    key_own, value_own, visual_far = tie((key_own, value_own, visual_far))
     key_sum, key_far = near_sums(key_own, key_near[::-1], "key_sums")
     key_sum, dscores = tie((key_sum, dscores))
     key_far = swap(key_far, "blk", half)

time: 57.3 us -> 57 us (level)
  waiting for transfers between devices: 10.3 us -> 8.94 us
  starting transfers between devices: 31.1 us -> 32.1 us
    ppermute x22, waiting for transfers between devices: 10.3 us -> 8.94 us  [swap(): return lax.ppermute(x, axis, [(i, i ^ mask) for i in range(size)])]
    ppermute x22, starting transfers between devices: 31.1 us -> 32.1 us  [swap(): return lax.ppermute(x, axis, [(i, i ^ mask) for i in range(size)])]
  transfers between devices with their start and end apart: 22 -> 22, of which waited for: 11 -> 9; matrix products, arithmetic and copies ran while one was open for 0% -> 0% of each run, Pallas kernels for 18% -> 18%
where the time goes in v16:
time: 57 us; the launch traced here: 56.8 us
  starting transfers between devices  32.1 us (56%)
  Pallas kernels  13.6 us (24%)
  waiting for transfers between devices  8.94 us (16%)
  between operations  1.43 us (3%)
  other arithmetic  0.73 us (1%)
    ppermute x22, starting transfers between devices, swap(): return lax.ppermute(x, axis, [(i, i ^ mask) for i in range(size)])  32.1 us
    ppermute x22, waiting for transfers between devices, swap(): return lax.ppermute(x, axis, [(i, i ^ mask) for i in range(size)])  8.94 us
    pallas_call x2, Pallas kernels, over_rows(): self.call(functools.partial(rows_kernel, factor), 0.1, name, grid=(KEY_HE...  5.13 us
    pallas_call x1, Pallas kernels, scores(): self.call(scores_kernel, 1.0, 'scores', in_specs=[smem, smem, VMEM, VMEM]...  3.86 us
    pallas_call x1, Pallas kernels, project(): pl.pallas_call(functools.partial(project_kernel, chunks), in_specs=[pl.Bl...  2.75 us
    pallas_call x7, Pallas kernels, in_vmem(): pl.pallas_call(kernel, cost_estimate=cost, in_specs=[VMEM] * len(arrays),...  1.19 us
  transfers between devices with their start and end apart: 22, of which 9 were waited for; matrix products, arithmetic and copies ran while one was open for 0% of the time, Pallas kernels for 18%

profile of v16, /device:TPU:0, one launch (start us, length us, event | category | flops | bytes accessed | tf_op | source)
XLA Modules:
  0.0 56.8 jit_solution(16947899942632001021)
XLA Ops:
  0.7 2.8 %project.1 = (bf16[32,1024]{1,0:T(8,128)(2,1)S(1)}, bf16[128,512]{1,0:T(8,128)(2,1)S(1)}, bf16[128,512]{1,0:T(8,128)(2,1)S(1)}) custom-call(bf16[4096,512]{1,0:T(8,128)(2,1)} %weight_hbm.1, bf16[32,4096]{1,0:T(8,128)(2,1)} %bitcast.14, bf16[32,512]{1,0:T(8,128)(2,1)} %bitcast.15), custom_call_target="tpu_custom_call" | custom-call | flops 134217728 | bytes 4194304 | tf_op jit(solution)/shard_map/project/pallas_call | solution.py:88
  3.4 4.1 %collective-permute-start = (bf16[32,1024]{1,0:T(8,128)(2,1)S(1)}, bf16[32,1024]{1,0:T(8,128)(2,1)S(1)}, u32[]{:S(2)}, u32[]{:S(2)}) collective-permute-start(bf16[32,1024]{1,0:T(8,128)(2,1)S(1)} %get-tuple-element.47.refs_0_), channel_id=1, source_target_pairs={{0,16},{4,20},{8,24},{12,28},{16,0},{20,4},{24,8},{28,12},{1,17},{... | collective-permute-start | bytes 196616 | tf_op jit(solution)/shard_map/ppermute | solution.py:28
  7.5 2.5 %collective-permute-start.4 = (bf16[32,1024]{1,0:T(8,128)(2,1)S(1)}, bf16[32,1024]{1,0:T(8,128)(2,1)S(1)}, u32[]{:S(2)}, u32[]{:S(2)}) collective-permute-start(bf16[32,1024]{1,0:T(8,128)(2,1)S(1)} %get-tuple-element.47.refs_0_), channel_id=1, source_target_pairs={{0,12},{4,8},{8,4},{12,0},{16,28},{20,24},{24,20},{28,16},{1,13},{... | collective-permute-start | bytes 196616 | tf_op jit(solution)/shard_map/ppermute | solution.py:28
  10.1 0.4 collective-permute-start.5
  10.5 0.5 collective-permute-start.6
  11.0 2.5 %collective-permute-start.1 = (bf16[32,1024]{1,0:T(8,128)(2,1)S(1)}, bf16[32,1024]{1,0:T(8,128)(2,1)S(1)}, u32[]{:S(2)}, u32[]{:S(2)}) collective-permute-start(bf16[32,1024]{1,0:T(8,128)(2,1)S(1)} %collective-permute-done.refs_4_), channel_id=1, source_target_pairs={{0,12},{4,8},{8,4},{12,0},{16,28},{20,24},{24,20},{28,16},{1,13},{... | collective-permute-start | bytes 196616 | tf_op jit(solution)/shard_map/ppermute | solution.py:28
  13.5 0.4 collective-permute-start.2
  14.0 0.9 %collective-permute-start.3 = (bf16[32,1024]{1,0:T(8,128)(2,1)S(1)}, bf16[32,1024]{1,0:T(8,128)(2,1)S(1)}, u32[]{:S(2)}, u32[]{:S(2)}) collective-permute-start(bf16[32,1024]{1,0:T(8,128)(2,1)S(1)} %collective-permute-done.refs_4_), channel_id=1, source_target_pairs={{0,4},{4,0},{8,12},{12,8},{16,20},{20,16},{24,28},{28,24},{1,5},{5... | collective-permute-start | bytes 196616 | tf_op jit(solution)/shard_map/ppermute | solution.py:28
  15.6 1.9 %collective-permute-start.7 = (bf16[128,512]{1,0:T(8,128)(2,1)S(1)}, bf16[128,512]{1,0:T(8,128)(2,1)S(1)}, u32[]{:S(2)}, u32[]{:S(2)}) collective-permute-start(bf16[128,512]{1,0:T(8,128)(2,1)S(1)} %get-tuple-element.51), channel_id=1, source_target_pairs={{0,16},{4,20},{8,24},{12,28},{16,0},{20,4},{24,8},{28,12},{1,17},{... | collective-permute-start | bytes 393224 | tf_op jit(solution)/shard_map/ppermute | solution.py:28
  17.4 1.8 %collective-permute-done.2.refs_2_ = bf16[32,1024]{1,0:T(8,128)(2,1)S(1)} collective-permute-done((bf16[32,1024]{1,0:T(8,128)(2,1)S(1)}, bf16[32,1024]{1,0:T(8,128)(2,1)S(1)}, u32[]{:S(2)}, u32[]{:S(2)}) %collective-permute-start.2) | collective-permute-done | bytes 65568 | tf_op jit(solution)/shard_map/ppermute | solution.py:28
  19.2 3.9 %scores.1 = (bf16[256,4096]{1,0:T(8,128)(2,1)S(1)}, bf16[256,4096]{1,0:T(8,128)(2,1)S(1)}, bf16[256,512]{1,0:T(8,128)(2,1)S(1)}, bf16[256,512]{1,0:T(8,128)(2,1)...) custom-call(s32[1]{0:T(128)S(6)} %copy.11.length_ref, ...), custom_call_target="tpu_custom_call" | custom-call | flops 1610612736 | bytes 4194304 | tf_op jit(solution)/shard_map/scores/pallas_call | solution.py:244
  23.1 1.2 %collective-permute-start.8 = (bf16[64,512]{1,0:T(8,128)(2,1)S(1)}, bf16[64,512]{1,0:T(8,128)(2,1)S(1)}, u32[]{:S(2)}, u32[]{:S(2)}) collective-permute-start(bf16[64,512]{1,0:T(8,128)(2,1)S(1)} %get-tuple-element.53), channel_id=1, source_target_pairs={{0,12},{4,8},{8,4},{12,0},{16,28},{20,24},{24,20},{28,16},{1,13},{... | collective-permute-start | bytes 196616 | tf_op jit(solution)/shard_map/ppermute | solution.py:28
  24.6 2.1 %collective-permute-start.10 = (bf16[64,512]{1,0:T(8,128)(2,1)S(1)}, bf16[64,512]{1,0:T(8,128)(2,1)S(1)}, u32[]{:S(2)}, u32[]{:S(2)}) collective-permute-start(bf16[64,512]{1,0:T(8,128)(2,1)S(1)} %get-tuple-element.55), channel_id=1, source_target_pairs={{0,4},{4,0},{8,12},{12,8},{16,20},{20,16},{24,28},{28,24},{1,5},{5... | collective-permute-start | bytes 196616 | tf_op jit(solution)/shard_map/ppermute | solution.py:28
  26.7 0.7 %values.1 = (f32[64,512]{1,0:T(8,128)S(1)}, bf16[64,512]{1,0:T(8,128)(2,1)S(1)}, bf16[64,512]{1,0:T(8,128)(2,1)S(1)}, bf16[64,512]{1,0:T(8,128)(2,1)S(1)}) custom-call(bf16[128,4096]{1,0:T(8,128)(2,1)S(1)} %bitcast.10, bf16[256,4096]{1,0:T(8,128)(2,1)S(1)} %get-tuple-element.49.w_ref.inner_ref), custom_call_target="tpu_custom_call" | custom-call | flops 161061280 | bytes 419430 | tf_op jit(solution)/shard_map/values/pallas_call | solution.py:259
  27.4 1.0 %collective-permute-done.8.refs_0_ = bf16[64,512]{1,0:T(8,128)(2,1)S(1)} collective-permute-done((bf16[64,512]{1,0:T(8,128)(2,1)S(1)}, bf16[64,512]{1,0:T(8,128)(2,1)S(1)}, u32[]{:S(2)}, u32[]{:S(2)}) %collective-permute-start.8) | collective-permute-done | bytes 65568 | tf_op jit(solution)/shard_map/ppermute | solution.py:28
  28.6 0.4 collective-permute-done.10.refs_2_
  29.1 2.2 %collective-permute-start.11 = (bf16[32,512]{1,0:T(8,128)(2,1)S(1)}, bf16[32,512]{1,0:T(8,128)(2,1)S(1)}, u32[]{:S(2)}, u32[]{:S(2)}) collective-permute-start(bf16[32,512]{1,0:T(8,128)(2,1)S(1)} %get-tuple-element.62), channel_id=1, source_target_pairs={{0,16},{4,20},{8,24},{12,28},{16,0},{20,4},{24,8},{28,12},{1,17},{... | collective-permute-start | bytes 98312 | tf_op jit(solution)/shard_map/ppermute | solution.py:28
  31.2 2.6 %query_grad.1 = bf16[128,4096]{1,0:T(8,128)(2,1)} custom-call(bf16[256,4096]{1,0:T(8,128)(2,1)S(1)} %get-tuple-element.59.inner_ref, bf16[256,512]{1,0:T(8,128)(2,1)S(1)} %get-tuple-element.60.head_ref), custom_call_target="tpu_custom_call" | custom-call | flops 161061280 | bytes 419430 | tf_op jit(solution)/shard_map/query_grad/pallas_call | solution.py:270
  34.0 2.5 %collective-permute-start.12 = (bf16[32,1536]{1,0:T(8,128)(2,1)S(1)}, bf16[32,1536]{1,0:T(8,128)(2,1)S(1)}, u32[]{:S(2)}, u32[]{:S(2)}) collective-permute-start(bf16[32,1536]{1,0:T(8,128)(2,1)S(1)} %get-tuple-element.66), channel_id=1, source_target_pairs={{0,4},{4,0},{8,12},{12,8},{16,20},{20,16},{24,28},{28,24},{1,5},{5... | collective-permute-start | bytes 294920 | tf_op jit(solution)/shard_map/ppermute | solution.py:28
  36.5 1.5 %collective-permute-start.15 = (bf16[32,512]{1,0:T(8,128)(2,1)S(1)}, bf16[32,512]{1,0:T(8,128)(2,1)S(1)}, u32[]{:S(2)}, u32[]{:S(2)}) collective-permute-start(bf16[32,512]{1,0:T(8,128)(2,1)S(1)} %get-tuple-element.75), channel_id=1, source_target_pairs={{0,16},{4,20},{8,24},{12,28},{16,0},{20,4},{24,8},{28,12},{1,17},{... | collective-permute-start | bytes 98312 | tf_op jit(solution)/shard_map/ppermute | solution.py:28
  38.0 2.2 %collective-permute-start.13 = (bf16[32,1536]{1,0:T(8,128)(2,1)S(1)}, bf16[32,1536]{1,0:T(8,128)(2,1)S(1)}, u32[]{:S(2)}, u32[]{:S(2)}) collective-permute-start(bf16[32,1536]{1,0:T(8,128)(2,1)S(1)} %get-tuple-element.67), channel_id=1, source_target_pairs={{0,8},{4,12},{8,0},{12,4},{16,24},{20,28},{24,16},{28,20},{1,9},{5... | collective-permute-start | bytes 294920 | tf_op jit(solution)/shard_map/ppermute | solution.py:28
  40.2 1.5 %collective-permute-done.15.far_ref.refs_7_ = bf16[32,512]{1,0:T(8,128)(2,1)S(1)} collective-permute-done((bf16[32,512]{1,0:T(8,128)(2,1)S(1)}, bf16[32,512]{1,0:T(8,128)(2,1)S(1)}, u32[]{:S(2)}, u32[]{:S(2)}) %collective-permute-start.15) | collective-permute-done | bytes 32800 | tf_op jit(solution)/shard_map/ppermute | solution.py:28
  41.7 1.5 %collective-permute-start.16 = (bf16[32,1536]{1,0:T(8,128)(2,1)S(1)}, bf16[32,1536]{1,0:T(8,128)(2,1)S(1)}, u32[]{:S(2)}, u32[]{:S(2)}) collective-permute-start(bf16[32,1536]{1,0:T(8,128)(2,1)S(1)} %get-tuple-element.79), channel_id=1, source_target_pairs={{0,12},{4,8},{8,4},{12,0},{16,28},{20,24},{24,20},{28,16},{1,13},{... | collective-permute-start | bytes 294920 | tf_op jit(solution)/shard_map/ppermute | solution.py:28
  43.2 2.0 %collective-permute-start.18 = (bf16[32,1536]{1,0:T(8,128)(2,1)S(1)}, bf16[32,1536]{1,0:T(8,128)(2,1)S(1)}, u32[]{:S(2)}, u32[]{:S(2)}) collective-permute-start(bf16[32,1536]{1,0:T(8,128)(2,1)S(1)} %get-tuple-element.81), channel_id=1, source_target_pairs={{0,4},{4,0},{8,12},{12,8},{16,20},{20,16},{24,28},{28,24},{1,5},{5... | collective-permute-start | bytes 294920 | tf_op jit(solution)/shard_map/ppermute | solution.py:28
  45.3 2.6 %output.1 = bf16[128,4096]{1,0:T(8,128)(2,1)} custom-call(bf16[256,4096]{1,0:T(8,128)(2,1)S(1)} %get-tuple-element.49.w_ref.inner_ref, bf16[256,512]{1,0:T(8,128)(2,1)S(1)} %get-tuple-element.69.head_ref), custom_call_target="tpu_custom_call" | custom-call | flops 161061280 | bytes 419430 | tf_op jit(solution)/shard_map/output/pallas_call | solution.py:270
  48.0 0.4 collective-permute-done.18.refs_3_
  48.7 1.7 %collective-permute-start.21 = (bf16[32,512]{1,0:T(8,128)(2,1)S(1)}, bf16[32,512]{1,0:T(8,128)(2,1)S(1)}, u32[]{:S(2)}, u32[]{:S(2)}) collective-permute-start(bf16[32,512]{1,0:T(8,128)(2,1)S(1)} %get-tuple-element.86), channel_id=1, source_target_pairs={{0,16},{4,20},{8,24},{12,28},{16,0},{20,4},{24,8},{28,12},{1,17},{... | collective-permute-start | bytes 98312 | tf_op jit(solution)/shard_map/ppermute | solution.py:28
  50.5 1.6 %collective-permute-start.20 = (bf16[1,128,512]{2,1,0:T(8,128)(2,1)S(1)}, bf16[1,128,512]{2,1,0:T(8,128)(2,1)S(1)}, u32[]{:S(2)}, u32[]{:S(2)}) collective-permute-start(bf16[1,128,512]{2,1,0:T(8,128)(2,1)S(1)} %get-tuple-element.84), channel_id=1, source_target_pairs={{0,2},{1,3},{2,0},{3,1},{4,6},{5,7},{6,4},{7,5},{8,10},{9,11},{10,... | collective-permute-start | bytes 393224 | tf_op jit(solution)/shard_map/ppermute | solution.py:28
  52.0 1.6 %collective-permute-done.21.far_ref = bf16[32,512]{1,0:T(8,128)(2,1)S(1)} collective-permute-done((bf16[32,512]{1,0:T(8,128)(2,1)S(1)}, bf16[32,512]{1,0:T(8,128)(2,1)S(1)}, u32[]{:S(2)}, u32[]{:S(2)}) %collective-permute-start.21) | collective-permute-done | bytes 32800 | tf_op jit(solution)/shard_map/ppermute | solution.py:28
  53.6 0.6 %value_grad.1 = bf16[32,512]{1,0:T(8,128)(2,1)} custom-call(f32[32,512]{1,0:T(8,128)S(1)} %get-tuple-element.85.near_ref, bf16[32,512]{1,0:T(8,128)(2,1)S(1)} %collective-permute-done.21.far_ref), custom_call_target="tpu_custom_call" | custom-call | flops 4000000000 | bytes 16777216 | tf_op jit(solution)/shard_map/value_grad/pallas_call | solution.py:282
  54.2 1.9 %collective-permute-done.20 = bf16[1,128,512]{2,1,0:T(8,128)(2,1)S(1)} collective-permute-done((bf16[1,128,512]{2,1,0:T(8,128)(2,1)S(1)}, bf16[1,128,512]{2,1,0:T(8,128)(2,1)S(1)}, u32[]{:S(2)}, u32[]{:S(2)}) %collective-permute-start.20) | collective-permute-done | bytes 131104 | tf_op jit(solution)/shard_map/ppermute | solution.py:28
  56.1 0.7 %add_bitcast_fusion = f32[128,512]{1,0:T(8,128)} fusion(f32[1,128,512]{2,1,0:T(8,128)S(1)} %get-tuple-element.88, bf16[1,128,512]{2,1,0:T(8,128)(2,1)S(1)} %collective-permute-done.20), kind=kLoop, calls=%fused_computation | loop fusion | flops 131072 | bytes 655360 | tf_op jit(solution)/shard_map/add | solution.py:455
  (31 shorter events, 1.3 us)
Async XLA Ops:
  0.6 18.6 %copy-start = (bf16[1,128,4096]{2,1,0:T(8,128)(2,1)S(1)}, bf16[1,128,4096]{2,1,0:T(8,128)(2,1)}, u32[]{:S(2)}) copy-start(bf16[1,128,4096]{2,1,0:T(8,128)(2,1)} %param.11) | copy-start | bytes 3145732
  0.6 18.6 %copy-start.1 = (bf16[1,128,4096]{2,1,0:T(8,128)(2,1)S(1)}, bf16[1,128,4096]{2,1,0:T(8,128)(2,1)}, u32[]{:S(2)}) copy-start(bf16[1,128,4096]{2,1,0:T(8,128)(2,1)} %param.10) | copy-start | bytes 3145732
  0.7 18.6 %copy-start.2 = (s32[1,8]{1,0:T(1,128)S(1)}, s32[1,8]{1,0:T(1,128)}, u32[]{:S(2)}) copy-start(s32[1,8]{1,0:T(1,128)} %frame_ref.1) | copy-start | bytes 100
  3.4 7.6 %collective-permute-start = (bf16[32,1024]{1,0:T(8,128)(2,1)S(1)}, bf16[32,1024]{1,0:T(8,128)(2,1)S(1)}, u32[]{:S(2)}, u32[]{:S(2)}) collective-permute-start(bf16[32,1024]{1,0:T(8,128)(2,1)S(1)} %get-tuple-element.47.refs_0_), channel_id=1, source_target_pairs={{0,16},{4,20},{8,24},{12,28},{16,0},{20,4},{24,8},{28,12},{1,17},{... | collective-permute-start | bytes 196616 | tf_op jit(solution)/shard_map/ppermute | solution.py:28
  7.5 6.5 %collective-permute-start.4 = (bf16[32,1024]{1,0:T(8,128)(2,1)S(1)}, bf16[32,1024]{1,0:T(8,128)(2,1)S(1)}, u32[]{:S(2)}, u32[]{:S(2)}) collective-permute-start(bf16[32,1024]{1,0:T(8,128)(2,1)S(1)} %get-tuple-element.47.refs_0_), channel_id=1, source_target_pairs={{0,12},{4,8},{8,4},{12,0},{16,28},{20,24},{24,20},{28,16},{1,13},{... | collective-permute-start | bytes 196616 | tf_op jit(solution)/shard_map/ppermute | solution.py:28
  10.1 5.5 %collective-permute-start.5 = (bf16[32,1024]{1,0:T(8,128)(2,1)S(1)}, bf16[32,1024]{1,0:T(8,128)(2,1)S(1)}, u32[]{:S(2)}, u32[]{:S(2)}) collective-permute-start(bf16[32,1024]{1,0:T(8,128)(2,1)S(1)} %get-tuple-element.47.refs_0_), channel_id=1, source_target_pairs={{0,8},{4,12},{8,0},{12,4},{16,24},{20,28},{24,16},{28,20},{1,9},{5... | collective-permute-start | bytes 196616 | tf_op jit(solution)/shard_map/ppermute | solution.py:28
  10.5 6.9 %collective-permute-start.6 = (bf16[32,1024]{1,0:T(8,128)(2,1)S(1)}, bf16[32,1024]{1,0:T(8,128)(2,1)S(1)}, u32[]{:S(2)}, u32[]{:S(2)}) collective-permute-start(bf16[32,1024]{1,0:T(8,128)(2,1)S(1)} %get-tuple-element.47.refs_0_), channel_id=1, source_target_pairs={{0,4},{4,0},{8,12},{12,8},{16,20},{20,16},{24,28},{28,24},{1,5},{5... | collective-permute-start | bytes 196616 | tf_op jit(solution)/shard_map/ppermute | solution.py:28
  11.0 6.4 %collective-permute-start.1 = (bf16[32,1024]{1,0:T(8,128)(2,1)S(1)}, bf16[32,1024]{1,0:T(8,128)(2,1)S(1)}, u32[]{:S(2)}, u32[]{:S(2)}) collective-permute-start(bf16[32,1024]{1,0:T(8,128)(2,1)S(1)} %collective-permute-done.refs_4_), channel_id=1, source_target_pairs={{0,12},{4,8},{8,4},{12,0},{16,28},{20,24},{24,20},{28,16},{1,13},{... | collective-permute-start | bytes 196616 | tf_op jit(solution)/shard_map/ppermute | solution.py:28
  13.5 5.7 %collective-permute-start.2 = (bf16[32,1024]{1,0:T(8,128)(2,1)S(1)}, bf16[32,1024]{1,0:T(8,128)(2,1)S(1)}, u32[]{:S(2)}, u32[]{:S(2)}) collective-permute-start(bf16[32,1024]{1,0:T(8,128)(2,1)S(1)} %collective-permute-done.refs_4_), channel_id=1, source_target_pairs={{0,8},{4,12},{8,0},{12,4},{16,24},{20,28},{24,16},{28,20},{1,9},{5... | collective-permute-start | bytes 196616 | tf_op jit(solution)/shard_map/ppermute | solution.py:28
  14.0 5.2 %collective-permute-start.3 = (bf16[32,1024]{1,0:T(8,128)(2,1)S(1)}, bf16[32,1024]{1,0:T(8,128)(2,1)S(1)}, u32[]{:S(2)}, u32[]{:S(2)}) collective-permute-start(bf16[32,1024]{1,0:T(8,128)(2,1)S(1)} %collective-permute-done.refs_4_), channel_id=1, source_target_pairs={{0,4},{4,0},{8,12},{12,8},{16,20},{20,16},{24,28},{28,24},{1,5},{5... | collective-permute-start | bytes 196616 | tf_op jit(solution)/shard_map/ppermute | solution.py:28
  15.6 11.8 %collective-permute-start.7 = (bf16[128,512]{1,0:T(8,128)(2,1)S(1)}, bf16[128,512]{1,0:T(8,128)(2,1)S(1)}, u32[]{:S(2)}, u32[]{:S(2)}) collective-permute-start(bf16[128,512]{1,0:T(8,128)(2,1)S(1)} %get-tuple-element.51), channel_id=1, source_target_pairs={{0,16},{4,20},{8,24},{12,28},{16,0},{20,4},{24,8},{28,12},{1,17},{... | collective-permute-start | bytes 393224 | tf_op jit(solution)/shard_map/ppermute | solution.py:28
  23.1 5.2 %collective-permute-start.8 = (bf16[64,512]{1,0:T(8,128)(2,1)S(1)}, bf16[64,512]{1,0:T(8,128)(2,1)S(1)}, u32[]{:S(2)}, u32[]{:S(2)}) collective-permute-start(bf16[64,512]{1,0:T(8,128)(2,1)S(1)} %get-tuple-element.53), channel_id=1, source_target_pairs={{0,12},{4,8},{8,4},{12,0},{16,28},{20,24},{24,20},{28,16},{1,13},{... | collective-permute-start | bytes 196616 | tf_op jit(solution)/shard_map/ppermute | solution.py:28
  24.3 4.3 %collective-permute-start.9 = (bf16[64,512]{1,0:T(8,128)(2,1)S(1)}, bf16[64,512]{1,0:T(8,128)(2,1)S(1)}, u32[]{:S(2)}, u32[]{:S(2)}) collective-permute-start(bf16[64,512]{1,0:T(8,128)(2,1)S(1)} %get-tuple-element.54), channel_id=1, source_target_pairs={{0,8},{4,12},{8,0},{12,4},{16,24},{20,28},{24,16},{28,20},{1,9},{5... | collective-permute-start | bytes 196616 | tf_op jit(solution)/shard_map/ppermute | solution.py:28
  24.6 4.5 %collective-permute-start.10 = (bf16[64,512]{1,0:T(8,128)(2,1)S(1)}, bf16[64,512]{1,0:T(8,128)(2,1)S(1)}, u32[]{:S(2)}, u32[]{:S(2)}) collective-permute-start(bf16[64,512]{1,0:T(8,128)(2,1)S(1)} %get-tuple-element.55), channel_id=1, source_target_pairs={{0,4},{4,0},{8,12},{12,8},{16,20},{20,16},{24,28},{28,24},{1,5},{5... | collective-permute-start | bytes 196616 | tf_op jit(solution)/shard_map/ppermute | solution.py:28
  29.1 4.9 %collective-permute-start.11 = (bf16[32,512]{1,0:T(8,128)(2,1)S(1)}, bf16[32,512]{1,0:T(8,128)(2,1)S(1)}, u32[]{:S(2)}, u32[]{:S(2)}) collective-permute-start(bf16[32,512]{1,0:T(8,128)(2,1)S(1)} %get-tuple-element.62), channel_id=1, source_target_pairs={{0,16},{4,20},{8,24},{12,28},{16,0},{20,4},{24,8},{28,12},{1,17},{... | collective-permute-start | bytes 98312 | tf_op jit(solution)/shard_map/ppermute | solution.py:28
  34.0 9.2 %collective-permute-start.12 = (bf16[32,1536]{1,0:T(8,128)(2,1)S(1)}, bf16[32,1536]{1,0:T(8,128)(2,1)S(1)}, u32[]{:S(2)}, u32[]{:S(2)}) collective-permute-start(bf16[32,1536]{1,0:T(8,128)(2,1)S(1)} %get-tuple-element.66), channel_id=1, source_target_pairs={{0,4},{4,0},{8,12},{12,8},{16,20},{20,16},{24,28},{28,24},{1,5},{5... | collective-permute-start | bytes 294920 | tf_op jit(solution)/shard_map/ppermute | solution.py:28
  36.5 5.2 %collective-permute-start.15 = (bf16[32,512]{1,0:T(8,128)(2,1)S(1)}, bf16[32,512]{1,0:T(8,128)(2,1)S(1)}, u32[]{:S(2)}, u32[]{:S(2)}) collective-permute-start(bf16[32,512]{1,0:T(8,128)(2,1)S(1)} %get-tuple-element.75), channel_id=1, source_target_pairs={{0,16},{4,20},{8,24},{12,28},{16,0},{20,4},{24,8},{28,12},{1,17},{... | collective-permute-start | bytes 98312 | tf_op jit(solution)/shard_map/ppermute | solution.py:28
  38.0 9.8 %collective-permute-start.13 = (bf16[32,1536]{1,0:T(8,128)(2,1)S(1)}, bf16[32,1536]{1,0:T(8,128)(2,1)S(1)}, u32[]{:S(2)}, u32[]{:S(2)}) collective-permute-start(bf16[32,1536]{1,0:T(8,128)(2,1)S(1)} %get-tuple-element.67), channel_id=1, source_target_pairs={{0,8},{4,12},{8,0},{12,4},{16,24},{20,28},{24,16},{28,20},{1,9},{5... | collective-permute-start | bytes 294920 | tf_op jit(solution)/shard_map/ppermute | solution.py:28
  40.2 7.6 %collective-permute-start.14 = (bf16[32,1536]{1,0:T(8,128)(2,1)S(1)}, bf16[32,1536]{1,0:T(8,128)(2,1)S(1)}, u32[]{:S(2)}, u32[]{:S(2)}) collective-permute-start(bf16[32,1536]{1,0:T(8,128)(2,1)S(1)} %get-tuple-element.68), channel_id=1, source_target_pairs={{0,12},{4,8},{8,4},{12,0},{16,28},{20,24},{24,20},{28,16},{1,13},{... | collective-permute-start | bytes 294920 | tf_op jit(solution)/shard_map/ppermute | solution.py:28
  41.7 6.3 %collective-permute-start.16 = (bf16[32,1536]{1,0:T(8,128)(2,1)S(1)}, bf16[32,1536]{1,0:T(8,128)(2,1)S(1)}, u32[]{:S(2)}, u32[]{:S(2)}) collective-permute-start(bf16[32,1536]{1,0:T(8,128)(2,1)S(1)} %get-tuple-element.79), channel_id=1, source_target_pairs={{0,12},{4,8},{8,4},{12,0},{16,28},{20,24},{24,20},{28,16},{1,13},{... | collective-permute-start | bytes 294920 | tf_op jit(solution)/shard_map/ppermute | solution.py:28
  43.2 4.8 %collective-permute-start.17 = (bf16[32,1536]{1,0:T(8,128)(2,1)S(1)}, bf16[32,1536]{1,0:T(8,128)(2,1)S(1)}, u32[]{:S(2)}, u32[]{:S(2)}) collective-permute-start(bf16[32,1536]{1,0:T(8,128)(2,1)S(1)} %get-tuple-element.80), channel_id=1, source_target_pairs={{0,8},{4,12},{8,0},{12,4},{16,24},{20,28},{24,16},{28,20},{1,9},{5... | collective-permute-start | bytes 294920 | tf_op jit(solution)/shard_map/ppermute | solution.py:28
  43.2 5.1 %collective-permute-start.18 = (bf16[32,1536]{1,0:T(8,128)(2,1)S(1)}, bf16[32,1536]{1,0:T(8,128)(2,1)S(1)}, u32[]{:S(2)}, u32[]{:S(2)}) collective-permute-start(bf16[32,1536]{1,0:T(8,128)(2,1)S(1)} %get-tuple-element.81), channel_id=1, source_target_pairs={{0,4},{4,0},{8,12},{12,8},{16,20},{20,16},{24,28},{28,24},{1,5},{5... | collective-permute-start | bytes 294920 | tf_op jit(solution)/shard_map/ppermute | solution.py:28
  48.6 1.8 %collective-permute-start.19 = (bf16[2,128,512]{2,1,0:T(8,128)(2,1)S(1)}, bf16[2,128,512]{2,1,0:T(8,128)(2,1)S(1)}, u32[]{:S(2)}, u32[]{:S(2)}) collective-permute-start(bf16[2,128,512]{2,1,0:T(8,128)(2,1)S(1)} %get-tuple-element.83), channel_id=1, source_target_pairs={{0,1},{1,0},{2,3},{3,2},{4,5},{5,4},{6,7},{7,6},{8,9},{9,8},{10,11... | collective-permute-start | bytes 786440 | tf_op jit(solution)/shard_map/ppermute | solution.py:28
  48.7 4.9 %collective-permute-start.21 = (bf16[32,512]{1,0:T(8,128)(2,1)S(1)}, bf16[32,512]{1,0:T(8,128)(2,1)S(1)}, u32[]{:S(2)}, u32[]{:S(2)}) collective-permute-start(bf16[32,512]{1,0:T(8,128)(2,1)S(1)} %get-tuple-element.86), channel_id=1, source_target_pairs={{0,16},{4,20},{8,24},{12,28},{16,0},{20,4},{24,8},{28,12},{1,17},{... | collective-permute-start | bytes 98312 | tf_op jit(solution)/shard_map/ppermute | solution.py:28
  50.5 5.6 %collective-permute-start.20 = (bf16[1,128,512]{2,1,0:T(8,128)(2,1)S(1)}, bf16[1,128,512]{2,1,0:T(8,128)(2,1)S(1)}, u32[]{:S(2)}, u32[]{:S(2)}) collective-permute-start(bf16[1,128,512]{2,1,0:T(8,128)(2,1)S(1)} %get-tuple-element.84), channel_id=1, source_target_pairs={{0,2},{1,3},{2,0},{3,1},{4,6},{5,7},{6,4},{7,5},{8,10},{9,11},{10,... | collective-permute-start | bytes 393224 | tf_op jit(solution)/shard_map/ppermute | solution.py:28

commit v17 on v16

--- a/solution.py
+++ b/solution.py
@@ -159,10 +159,11 @@
                 dprobs[p] = dot(values, head_pair(g_ref, text, start), ((1,), (1,)))
 
             products(0)
+            products(1)
             ds_stack = []
             for p in range(pairs):
-                if p + 1 < pairs:
-                    products(p + 1)
+                if p + 2 < pairs:
+                    products(p + 2)
                 scores = raw.pop(p) + bias_ref[...]
                 peak = jnp.max(scores, axis=0, keepdims=True)
                 shifted = jnp.exp2((scores - peak) * (scale * LOG2_E))

time: 57 us -> 57 us (level)
  transfers between devices with their start and end apart: 22 -> 22, of which waited for: 9 -> 9; matrix products, arithmetic and copies ran while one was open for 0% -> 0% of each run, Pallas kernels for 18% -> 19%
where the time goes in v17:
time: 57 us; the launch traced here: 56.9 us
  starting transfers between devices  32.1 us (56%)
  Pallas kernels  13.7 us (24%)
  waiting for transfers between devices  8.94 us (16%)
  between operations  1.43 us (3%)
  other arithmetic  0.73 us (1%)
    ppermute x22, starting transfers between devices, swap(): return lax.ppermute(x, axis, [(i, i ^ mask) for i in range(size)])  32.1 us
    ppermute x22, waiting for transfers between devices, swap(): return lax.ppermute(x, axis, [(i, i ^ mask) for i in range(size)])  8.94 us
    pallas_call x2, Pallas kernels, over_rows(): self.call(functools.partial(rows_kernel, factor), 0.1, name, grid=(KEY_HE...  5.12 us
    pallas_call x1, Pallas kernels, scores(): self.call(scores_kernel, 1.0, 'scores', in_specs=[smem, smem, VMEM, VMEM]...  3.9 us
    pallas_call x1, Pallas kernels, project(): pl.pallas_call(functools.partial(project_kernel, chunks), in_specs=[pl.Bl...  2.75 us
    pallas_call x7, Pallas kernels, in_vmem(): pl.pallas_call(kernel, cost_estimate=cost, in_specs=[VMEM] * len(arrays),...  1.19 us
  transfers between devices with their start and end apart: 22, of which 9 were waited for; matrix products, arithmetic and copies ran while one was open for 0% of the time, Pallas kernels for 19%

profile of v17, /device:TPU:0, one launch (start us, length us, event | category | flops | bytes accessed | tf_op | source)
XLA Modules:
  0.0 56.9 jit_solution(15628635993135013604)
XLA Ops:
  0.7 2.8 %project.1 = (bf16[32,1024]{1,0:T(8,128)(2,1)S(1)}, bf16[128,512]{1,0:T(8,128)(2,1)S(1)}, bf16[128,512]{1,0:T(8,128)(2,1)S(1)}) custom-call(bf16[4096,512]{1,0:T(8,128)(2,1)} %weight_hbm.1, bf16[32,4096]{1,0:T(8,128)(2,1)} %bitcast.14, bf16[32,512]{1,0:T(8,128)(2,1)} %bitcast.15), custom_call_target="tpu_custom_call" | custom-call | flops 134217728 | bytes 4194304 | tf_op jit(solution)/shard_map/project/pallas_call | solution.py:88
  3.4 4.1 %collective-permute-start = (bf16[32,1024]{1,0:T(8,128)(2,1)S(1)}, bf16[32,1024]{1,0:T(8,128)(2,1)S(1)}, u32[]{:S(2)}, u32[]{:S(2)}) collective-permute-start(bf16[32,1024]{1,0:T(8,128)(2,1)S(1)} %get-tuple-element.47.refs_0_), channel_id=1, source_target_pairs={{0,16},{4,20},{8,24},{12,28},{16,0},{20,4},{24,8},{28,12},{1,17},{... | collective-permute-start | bytes 196616 | tf_op jit(solution)/shard_map/ppermute | solution.py:28
  7.5 2.5 %collective-permute-start.4 = (bf16[32,1024]{1,0:T(8,128)(2,1)S(1)}, bf16[32,1024]{1,0:T(8,128)(2,1)S(1)}, u32[]{:S(2)}, u32[]{:S(2)}) collective-permute-start(bf16[32,1024]{1,0:T(8,128)(2,1)S(1)} %get-tuple-element.47.refs_0_), channel_id=1, source_target_pairs={{0,12},{4,8},{8,4},{12,0},{16,28},{20,24},{24,20},{28,16},{1,13},{... | collective-permute-start | bytes 196616 | tf_op jit(solution)/shard_map/ppermute | solution.py:28
  10.1 0.4 collective-permute-start.5
  10.5 0.5 collective-permute-start.6
  11.0 2.5 %collective-permute-start.1 = (bf16[32,1024]{1,0:T(8,128)(2,1)S(1)}, bf16[32,1024]{1,0:T(8,128)(2,1)S(1)}, u32[]{:S(2)}, u32[]{:S(2)}) collective-permute-start(bf16[32,1024]{1,0:T(8,128)(2,1)S(1)} %collective-permute-done.refs_4_), channel_id=1, source_target_pairs={{0,12},{4,8},{8,4},{12,0},{16,28},{20,24},{24,20},{28,16},{1,13},{... | collective-permute-start | bytes 196616 | tf_op jit(solution)/shard_map/ppermute | solution.py:28
  13.5 0.4 collective-permute-start.2
  14.0 0.9 %collective-permute-start.3 = (bf16[32,1024]{1,0:T(8,128)(2,1)S(1)}, bf16[32,1024]{1,0:T(8,128)(2,1)S(1)}, u32[]{:S(2)}, u32[]{:S(2)}) collective-permute-start(bf16[32,1024]{1,0:T(8,128)(2,1)S(1)} %collective-permute-done.refs_4_), channel_id=1, source_target_pairs={{0,4},{4,0},{8,12},{12,8},{16,20},{20,16},{24,28},{28,24},{1,5},{5... | collective-permute-start | bytes 196616 | tf_op jit(solution)/shard_map/ppermute | solution.py:28
  15.6 1.9 %collective-permute-start.7 = (bf16[128,512]{1,0:T(8,128)(2,1)S(1)}, bf16[128,512]{1,0:T(8,128)(2,1)S(1)}, u32[]{:S(2)}, u32[]{:S(2)}) collective-permute-start(bf16[128,512]{1,0:T(8,128)(2,1)S(1)} %get-tuple-element.51), channel_id=1, source_target_pairs={{0,16},{4,20},{8,24},{12,28},{16,0},{20,4},{24,8},{28,12},{1,17},{... | collective-permute-start | bytes 393224 | tf_op jit(solution)/shard_map/ppermute | solution.py:28
  17.4 1.8 %collective-permute-done.2.refs_2_ = bf16[32,1024]{1,0:T(8,128)(2,1)S(1)} collective-permute-done((bf16[32,1024]{1,0:T(8,128)(2,1)S(1)}, bf16[32,1024]{1,0:T(8,128)(2,1)S(1)}, u32[]{:S(2)}, u32[]{:S(2)}) %collective-permute-start.2) | collective-permute-done | bytes 65568 | tf_op jit(solution)/shard_map/ppermute | solution.py:28
  19.2 3.9 %scores.1 = (bf16[256,4096]{1,0:T(8,128)(2,1)S(1)}, bf16[256,4096]{1,0:T(8,128)(2,1)S(1)}, bf16[256,512]{1,0:T(8,128)(2,1)S(1)}, bf16[256,512]{1,0:T(8,128)(2,1)...) custom-call(s32[1]{0:T(128)S(6)} %copy.11.length_ref, ...), custom_call_target="tpu_custom_call" | custom-call | flops 1610612736 | bytes 4194304 | tf_op jit(solution)/shard_map/scores/pallas_call | solution.py:245
  23.1 1.2 %collective-permute-start.8 = (bf16[64,512]{1,0:T(8,128)(2,1)S(1)}, bf16[64,512]{1,0:T(8,128)(2,1)S(1)}, u32[]{:S(2)}, u32[]{:S(2)}) collective-permute-start(bf16[64,512]{1,0:T(8,128)(2,1)S(1)} %get-tuple-element.53), channel_id=1, source_target_pairs={{0,12},{4,8},{8,4},{12,0},{16,28},{20,24},{24,20},{28,16},{1,13},{... | collective-permute-start | bytes 196616 | tf_op jit(solution)/shard_map/ppermute | solution.py:28
  24.6 2.1 %collective-permute-start.10 = (bf16[64,512]{1,0:T(8,128)(2,1)S(1)}, bf16[64,512]{1,0:T(8,128)(2,1)S(1)}, u32[]{:S(2)}, u32[]{:S(2)}) collective-permute-start(bf16[64,512]{1,0:T(8,128)(2,1)S(1)} %get-tuple-element.55), channel_id=1, source_target_pairs={{0,4},{4,0},{8,12},{12,8},{16,20},{20,16},{24,28},{28,24},{1,5},{5... | collective-permute-start | bytes 196616 | tf_op jit(solution)/shard_map/ppermute | solution.py:28
  26.7 0.7 %values.1 = (f32[64,512]{1,0:T(8,128)S(1)}, bf16[64,512]{1,0:T(8,128)(2,1)S(1)}, bf16[64,512]{1,0:T(8,128)(2,1)S(1)}, bf16[64,512]{1,0:T(8,128)(2,1)S(1)}) custom-call(bf16[128,4096]{1,0:T(8,128)(2,1)S(1)} %bitcast.10, bf16[256,4096]{1,0:T(8,128)(2,1)S(1)} %get-tuple-element.49.w_ref.inner_ref), custom_call_target="tpu_custom_call" | custom-call | flops 161061280 | bytes 419430 | tf_op jit(solution)/shard_map/values/pallas_call | solution.py:260
  27.4 1.0 %collective-permute-done.8.refs_0_ = bf16[64,512]{1,0:T(8,128)(2,1)S(1)} collective-permute-done((bf16[64,512]{1,0:T(8,128)(2,1)S(1)}, bf16[64,512]{1,0:T(8,128)(2,1)S(1)}, u32[]{:S(2)}, u32[]{:S(2)}) %collective-permute-start.8) | collective-permute-done | bytes 65568 | tf_op jit(solution)/shard_map/ppermute | solution.py:28
  28.6 0.4 collective-permute-done.10.refs_2_
  29.1 2.2 %collective-permute-start.11 = (bf16[32,512]{1,0:T(8,128)(2,1)S(1)}, bf16[32,512]{1,0:T(8,128)(2,1)S(1)}, u32[]{:S(2)}, u32[]{:S(2)}) collective-permute-start(bf16[32,512]{1,0:T(8,128)(2,1)S(1)} %get-tuple-element.62), channel_id=1, source_target_pairs={{0,16},{4,20},{8,24},{12,28},{16,0},{20,4},{24,8},{28,12},{1,17},{... | collective-permute-start | bytes 98312 | tf_op jit(solution)/shard_map/ppermute | solution.py:28
  31.3 2.6 %query_grad.1 = bf16[128,4096]{1,0:T(8,128)(2,1)} custom-call(bf16[256,4096]{1,0:T(8,128)(2,1)S(1)} %get-tuple-element.59.inner_ref, bf16[256,512]{1,0:T(8,128)(2,1)S(1)} %get-tuple-element.60.head_ref), custom_call_target="tpu_custom_call" | custom-call | flops 161061280 | bytes 419430 | tf_op jit(solution)/shard_map/query_grad/pallas_call | solution.py:271
  34.0 2.5 %collective-permute-start.12 = (bf16[32,1536]{1,0:T(8,128)(2,1)S(1)}, bf16[32,1536]{1,0:T(8,128)(2,1)S(1)}, u32[]{:S(2)}, u32[]{:S(2)}) collective-permute-start(bf16[32,1536]{1,0:T(8,128)(2,1)S(1)} %get-tuple-element.66), channel_id=1, source_target_pairs={{0,4},{4,0},{8,12},{12,8},{16,20},{20,16},{24,28},{28,24},{1,5},{5... | collective-permute-start | bytes 294920 | tf_op jit(solution)/shard_map/ppermute | solution.py:28
  36.6 1.5 %collective-permute-start.15 = (bf16[32,512]{1,0:T(8,128)(2,1)S(1)}, bf16[32,512]{1,0:T(8,128)(2,1)S(1)}, u32[]{:S(2)}, u32[]{:S(2)}) collective-permute-start(bf16[32,512]{1,0:T(8,128)(2,1)S(1)} %get-tuple-element.75), channel_id=1, source_target_pairs={{0,16},{4,20},{8,24},{12,28},{16,0},{20,4},{24,8},{28,12},{1,17},{... | collective-permute-start | bytes 98312 | tf_op jit(solution)/shard_map/ppermute | solution.py:28
  38.1 2.2 %collective-permute-start.13 = (bf16[32,1536]{1,0:T(8,128)(2,1)S(1)}, bf16[32,1536]{1,0:T(8,128)(2,1)S(1)}, u32[]{:S(2)}, u32[]{:S(2)}) collective-permute-start(bf16[32,1536]{1,0:T(8,128)(2,1)S(1)} %get-tuple-element.67), channel_id=1, source_target_pairs={{0,8},{4,12},{8,0},{12,4},{16,24},{20,28},{24,16},{28,20},{1,9},{5... | collective-permute-start | bytes 294920 | tf_op jit(solution)/shard_map/ppermute | solution.py:28
  40.3 1.5 %collective-permute-done.15.far_ref.refs_7_ = bf16[32,512]{1,0:T(8,128)(2,1)S(1)} collective-permute-done((bf16[32,512]{1,0:T(8,128)(2,1)S(1)}, bf16[32,512]{1,0:T(8,128)(2,1)S(1)}, u32[]{:S(2)}, u32[]{:S(2)}) %collective-permute-start.15) | collective-permute-done | bytes 32800 | tf_op jit(solution)/shard_map/ppermute | solution.py:28
  41.8 1.5 %collective-permute-start.16 = (bf16[32,1536]{1,0:T(8,128)(2,1)S(1)}, bf16[32,1536]{1,0:T(8,128)(2,1)S(1)}, u32[]{:S(2)}, u32[]{:S(2)}) collective-permute-start(bf16[32,1536]{1,0:T(8,128)(2,1)S(1)} %get-tuple-element.79), channel_id=1, source_target_pairs={{0,12},{4,8},{8,4},{12,0},{16,28},{20,24},{24,20},{28,16},{1,13},{... | collective-permute-start | bytes 294920 | tf_op jit(solution)/shard_map/ppermute | solution.py:28
  43.3 2.0 %collective-permute-start.18 = (bf16[32,1536]{1,0:T(8,128)(2,1)S(1)}, bf16[32,1536]{1,0:T(8,128)(2,1)S(1)}, u32[]{:S(2)}, u32[]{:S(2)}) collective-permute-start(bf16[32,1536]{1,0:T(8,128)(2,1)S(1)} %get-tuple-element.81), channel_id=1, source_target_pairs={{0,4},{4,0},{8,12},{12,8},{16,20},{20,16},{24,28},{28,24},{1,5},{5... | collective-permute-start | bytes 294920 | tf_op jit(solution)/shard_map/ppermute | solution.py:28
  45.3 2.6 %output.1 = bf16[128,4096]{1,0:T(8,128)(2,1)} custom-call(bf16[256,4096]{1,0:T(8,128)(2,1)S(1)} %get-tuple-element.49.w_ref.inner_ref, bf16[256,512]{1,0:T(8,128)(2,1)S(1)} %get-tuple-element.69.head_ref), custom_call_target="tpu_custom_call" | custom-call | flops 161061280 | bytes 419430 | tf_op jit(solution)/shard_map/output/pallas_call | solution.py:271
  48.0 0.4 collective-permute-done.18.refs_3_
  48.8 1.7 %collective-permute-start.21 = (bf16[32,512]{1,0:T(8,128)(2,1)S(1)}, bf16[32,512]{1,0:T(8,128)(2,1)S(1)}, u32[]{:S(2)}, u32[]{:S(2)}) collective-permute-start(bf16[32,512]{1,0:T(8,128)(2,1)S(1)} %get-tuple-element.86), channel_id=1, source_target_pairs={{0,16},{4,20},{8,24},{12,28},{16,0},{20,4},{24,8},{28,12},{1,17},{... | collective-permute-start | bytes 98312 | tf_op jit(solution)/shard_map/ppermute | solution.py:28
  50.5 1.5 %collective-permute-start.20 = (bf16[1,128,512]{2,1,0:T(8,128)(2,1)S(1)}, bf16[1,128,512]{2,1,0:T(8,128)(2,1)S(1)}, u32[]{:S(2)}, u32[]{:S(2)}) collective-permute-start(bf16[1,128,512]{2,1,0:T(8,128)(2,1)S(1)} %get-tuple-element.84), channel_id=1, source_target_pairs={{0,2},{1,3},{2,0},{3,1},{4,6},{5,7},{6,4},{7,5},{8,10},{9,11},{10,... | collective-permute-start | bytes 393224 | tf_op jit(solution)/shard_map/ppermute | solution.py:28
  52.1 1.6 %collective-permute-done.21.far_ref = bf16[32,512]{1,0:T(8,128)(2,1)S(1)} collective-permute-done((bf16[32,512]{1,0:T(8,128)(2,1)S(1)}, bf16[32,512]{1,0:T(8,128)(2,1)S(1)}, u32[]{:S(2)}, u32[]{:S(2)}) %collective-permute-start.21) | collective-permute-done | bytes 32800 | tf_op jit(solution)/shard_map/ppermute | solution.py:28
  53.6 0.6 %value_grad.1 = bf16[32,512]{1,0:T(8,128)(2,1)} custom-call(f32[32,512]{1,0:T(8,128)S(1)} %get-tuple-element.85.near_ref, bf16[32,512]{1,0:T(8,128)(2,1)S(1)} %collective-permute-done.21.far_ref), custom_call_target="tpu_custom_call" | custom-call | flops 4000000000 | bytes 16777216 | tf_op jit(solution)/shard_map/value_grad/pallas_call | solution.py:283
  54.3 1.9 %collective-permute-done.20 = bf16[1,128,512]{2,1,0:T(8,128)(2,1)S(1)} collective-permute-done((bf16[1,128,512]{2,1,0:T(8,128)(2,1)S(1)}, bf16[1,128,512]{2,1,0:T(8,128)(2,1)S(1)}, u32[]{:S(2)}, u32[]{:S(2)}) %collective-permute-start.20) | collective-permute-done | bytes 131104 | tf_op jit(solution)/shard_map/ppermute | solution.py:28
  56.1 0.7 %add_bitcast_fusion = f32[128,512]{1,0:T(8,128)} fusion(f32[1,128,512]{2,1,0:T(8,128)S(1)} %get-tuple-element.88, bf16[1,128,512]{2,1,0:T(8,128)(2,1)S(1)} %collective-permute-done.20), kind=kLoop, calls=%fused_computation | loop fusion | flops 131072 | bytes 655360 | tf_op jit(solution)/shard_map/add | solution.py:456
  (31 shorter events, 1.3 us)
Async XLA Ops:
  0.6 18.6 %copy-start = (bf16[1,128,4096]{2,1,0:T(8,128)(2,1)S(1)}, bf16[1,128,4096]{2,1,0:T(8,128)(2,1)}, u32[]{:S(2)}) copy-start(bf16[1,128,4096]{2,1,0:T(8,128)(2,1)} %param.11) | copy-start | bytes 3145732
  0.6 18.6 %copy-start.1 = (bf16[1,128,4096]{2,1,0:T(8,128)(2,1)S(1)}, bf16[1,128,4096]{2,1,0:T(8,128)(2,1)}, u32[]{:S(2)}) copy-start(bf16[1,128,4096]{2,1,0:T(8,128)(2,1)} %param.10) | copy-start | bytes 3145732
  0.7 18.6 %copy-start.2 = (s32[1,8]{1,0:T(1,128)S(1)}, s32[1,8]{1,0:T(1,128)}, u32[]{:S(2)}) copy-start(s32[1,8]{1,0:T(1,128)} %frame_ref.1) | copy-start | bytes 100
  3.4 7.6 %collective-permute-start = (bf16[32,1024]{1,0:T(8,128)(2,1)S(1)}, bf16[32,1024]{1,0:T(8,128)(2,1)S(1)}, u32[]{:S(2)}, u32[]{:S(2)}) collective-permute-start(bf16[32,1024]{1,0:T(8,128)(2,1)S(1)} %get-tuple-element.47.refs_0_), channel_id=1, source_target_pairs={{0,16},{4,20},{8,24},{12,28},{16,0},{20,4},{24,8},{28,12},{1,17},{... | collective-permute-start | bytes 196616 | tf_op jit(solution)/shard_map/ppermute | solution.py:28
  7.5 6.5 %collective-permute-start.4 = (bf16[32,1024]{1,0:T(8,128)(2,1)S(1)}, bf16[32,1024]{1,0:T(8,128)(2,1)S(1)}, u32[]{:S(2)}, u32[]{:S(2)}) collective-permute-start(bf16[32,1024]{1,0:T(8,128)(2,1)S(1)} %get-tuple-element.47.refs_0_), channel_id=1, source_target_pairs={{0,12},{4,8},{8,4},{12,0},{16,28},{20,24},{24,20},{28,16},{1,13},{... | collective-permute-start | bytes 196616 | tf_op jit(solution)/shard_map/ppermute | solution.py:28
  10.1 5.5 %collective-permute-start.5 = (bf16[32,1024]{1,0:T(8,128)(2,1)S(1)}, bf16[32,1024]{1,0:T(8,128)(2,1)S(1)}, u32[]{:S(2)}, u32[]{:S(2)}) collective-permute-start(bf16[32,1024]{1,0:T(8,128)(2,1)S(1)} %get-tuple-element.47.refs_0_), channel_id=1, source_target_pairs={{0,8},{4,12},{8,0},{12,4},{16,24},{20,28},{24,16},{28,20},{1,9},{5... | collective-permute-start | bytes 196616 | tf_op jit(solution)/shard_map/ppermute | solution.py:28
  10.5 6.9 %collective-permute-start.6 = (bf16[32,1024]{1,0:T(8,128)(2,1)S(1)}, bf16[32,1024]{1,0:T(8,128)(2,1)S(1)}, u32[]{:S(2)}, u32[]{:S(2)}) collective-permute-start(bf16[32,1024]{1,0:T(8,128)(2,1)S(1)} %get-tuple-element.47.refs_0_), channel_id=1, source_target_pairs={{0,4},{4,0},{8,12},{12,8},{16,20},{20,16},{24,28},{28,24},{1,5},{5... | collective-permute-start | bytes 196616 | tf_op jit(solution)/shard_map/ppermute | solution.py:28
  11.0 6.4 %collective-permute-start.1 = (bf16[32,1024]{1,0:T(8,128)(2,1)S(1)}, bf16[32,1024]{1,0:T(8,128)(2,1)S(1)}, u32[]{:S(2)}, u32[]{:S(2)}) collective-permute-start(bf16[32,1024]{1,0:T(8,128)(2,1)S(1)} %collective-permute-done.refs_4_), channel_id=1, source_target_pairs={{0,12},{4,8},{8,4},{12,0},{16,28},{20,24},{24,20},{28,16},{1,13},{... | collective-permute-start | bytes 196616 | tf_op jit(solution)/shard_map/ppermute | solution.py:28
  13.5 5.7 %collective-permute-start.2 = (bf16[32,1024]{1,0:T(8,128)(2,1)S(1)}, bf16[32,1024]{1,0:T(8,128)(2,1)S(1)}, u32[]{:S(2)}, u32[]{:S(2)}) collective-permute-start(bf16[32,1024]{1,0:T(8,128)(2,1)S(1)} %collective-permute-done.refs_4_), channel_id=1, source_target_pairs={{0,8},{4,12},{8,0},{12,4},{16,24},{20,28},{24,16},{28,20},{1,9},{5... | collective-permute-start | bytes 196616 | tf_op jit(solution)/shard_map/ppermute | solution.py:28
  14.0 5.2 %collective-permute-start.3 = (bf16[32,1024]{1,0:T(8,128)(2,1)S(1)}, bf16[32,1024]{1,0:T(8,128)(2,1)S(1)}, u32[]{:S(2)}, u32[]{:S(2)}) collective-permute-start(bf16[32,1024]{1,0:T(8,128)(2,1)S(1)} %collective-permute-done.refs_4_), channel_id=1, source_target_pairs={{0,4},{4,0},{8,12},{12,8},{16,20},{20,16},{24,28},{28,24},{1,5},{5... | collective-permute-start | bytes 196616 | tf_op jit(solution)/shard_map/ppermute | solution.py:28
  15.6 11.8 %collective-permute-start.7 = (bf16[128,512]{1,0:T(8,128)(2,1)S(1)}, bf16[128,512]{1,0:T(8,128)(2,1)S(1)}, u32[]{:S(2)}, u32[]{:S(2)}) collective-permute-start(bf16[128,512]{1,0:T(8,128)(2,1)S(1)} %get-tuple-element.51), channel_id=1, source_target_pairs={{0,16},{4,20},{8,24},{12,28},{16,0},{20,4},{24,8},{28,12},{1,17},{... | collective-permute-start | bytes 393224 | tf_op jit(solution)/shard_map/ppermute | solution.py:28
  23.1 5.2 %collective-permute-start.8 = (bf16[64,512]{1,0:T(8,128)(2,1)S(1)}, bf16[64,512]{1,0:T(8,128)(2,1)S(1)}, u32[]{:S(2)}, u32[]{:S(2)}) collective-permute-start(bf16[64,512]{1,0:T(8,128)(2,1)S(1)} %get-tuple-element.53), channel_id=1, source_target_pairs={{0,12},{4,8},{8,4},{12,0},{16,28},{20,24},{24,20},{28,16},{1,13},{... | collective-permute-start | bytes 196616 | tf_op jit(solution)/shard_map/ppermute | solution.py:28
  24.4 4.3 %collective-permute-start.9 = (bf16[64,512]{1,0:T(8,128)(2,1)S(1)}, bf16[64,512]{1,0:T(8,128)(2,1)S(1)}, u32[]{:S(2)}, u32[]{:S(2)}) collective-permute-start(bf16[64,512]{1,0:T(8,128)(2,1)S(1)} %get-tuple-element.54), channel_id=1, source_target_pairs={{0,8},{4,12},{8,0},{12,4},{16,24},{20,28},{24,16},{28,20},{1,9},{5... | collective-permute-start | bytes 196616 | tf_op jit(solution)/shard_map/ppermute | solution.py:28
  24.6 4.5 %collective-permute-start.10 = (bf16[64,512]{1,0:T(8,128)(2,1)S(1)}, bf16[64,512]{1,0:T(8,128)(2,1)S(1)}, u32[]{:S(2)}, u32[]{:S(2)}) collective-permute-start(bf16[64,512]{1,0:T(8,128)(2,1)S(1)} %get-tuple-element.55), channel_id=1, source_target_pairs={{0,4},{4,0},{8,12},{12,8},{16,20},{20,16},{24,28},{28,24},{1,5},{5... | collective-permute-start | bytes 196616 | tf_op jit(solution)/shard_map/ppermute | solution.py:28
  29.1 4.9 %collective-permute-start.11 = (bf16[32,512]{1,0:T(8,128)(2,1)S(1)}, bf16[32,512]{1,0:T(8,128)(2,1)S(1)}, u32[]{:S(2)}, u32[]{:S(2)}) collective-permute-start(bf16[32,512]{1,0:T(8,128)(2,1)S(1)} %get-tuple-element.62), channel_id=1, source_target_pairs={{0,16},{4,20},{8,24},{12,28},{16,0},{20,4},{24,8},{28,12},{1,17},{... | collective-permute-start | bytes 98312 | tf_op jit(solution)/shard_map/ppermute | solution.py:28
  34.0 9.2 %collective-permute-start.12 = (bf16[32,1536]{1,0:T(8,128)(2,1)S(1)}, bf16[32,1536]{1,0:T(8,128)(2,1)S(1)}, u32[]{:S(2)}, u32[]{:S(2)}) collective-permute-start(bf16[32,1536]{1,0:T(8,128)(2,1)S(1)} %get-tuple-element.66), channel_id=1, source_target_pairs={{0,4},{4,0},{8,12},{12,8},{16,20},{20,16},{24,28},{28,24},{1,5},{5... | collective-permute-start | bytes 294920 | tf_op jit(solution)/shard_map/ppermute | solution.py:28
  36.6 5.2 %collective-permute-start.15 = (bf16[32,512]{1,0:T(8,128)(2,1)S(1)}, bf16[32,512]{1,0:T(8,128)(2,1)S(1)}, u32[]{:S(2)}, u32[]{:S(2)}) collective-permute-start(bf16[32,512]{1,0:T(8,128)(2,1)S(1)} %get-tuple-element.75), channel_id=1, source_target_pairs={{0,16},{4,20},{8,24},{12,28},{16,0},{20,4},{24,8},{28,12},{1,17},{... | collective-permute-start | bytes 98312 | tf_op jit(solution)/shard_map/ppermute | solution.py:28
  38.1 9.8 %collective-permute-start.13 = (bf16[32,1536]{1,0:T(8,128)(2,1)S(1)}, bf16[32,1536]{1,0:T(8,128)(2,1)S(1)}, u32[]{:S(2)}, u32[]{:S(2)}) collective-permute-start(bf16[32,1536]{1,0:T(8,128)(2,1)S(1)} %get-tuple-element.67), channel_id=1, source_target_pairs={{0,8},{4,12},{8,0},{12,4},{16,24},{20,28},{24,16},{28,20},{1,9},{5... | collective-permute-start | bytes 294920 | tf_op jit(solution)/shard_map/ppermute | solution.py:28
  40.2 7.6 %collective-permute-start.14 = (bf16[32,1536]{1,0:T(8,128)(2,1)S(1)}, bf16[32,1536]{1,0:T(8,128)(2,1)S(1)}, u32[]{:S(2)}, u32[]{:S(2)}) collective-permute-start(bf16[32,1536]{1,0:T(8,128)(2,1)S(1)} %get-tuple-element.68), channel_id=1, source_target_pairs={{0,12},{4,8},{8,4},{12,0},{16,28},{20,24},{24,20},{28,16},{1,13},{... | collective-permute-start | bytes 294920 | tf_op jit(solution)/shard_map/ppermute | solution.py:28
  41.8 6.3 %collective-permute-start.16 = (bf16[32,1536]{1,0:T(8,128)(2,1)S(1)}, bf16[32,1536]{1,0:T(8,128)(2,1)S(1)}, u32[]{:S(2)}, u32[]{:S(2)}) collective-permute-start(bf16[32,1536]{1,0:T(8,128)(2,1)S(1)} %get-tuple-element.79), channel_id=1, source_target_pairs={{0,12},{4,8},{8,4},{12,0},{16,28},{20,24},{24,20},{28,16},{1,13},{... | collective-permute-start | bytes 294920 | tf_op jit(solution)/shard_map/ppermute | solution.py:28
  43.3 4.7 %collective-permute-start.17 = (bf16[32,1536]{1,0:T(8,128)(2,1)S(1)}, bf16[32,1536]{1,0:T(8,128)(2,1)S(1)}, u32[]{:S(2)}, u32[]{:S(2)}) collective-permute-start(bf16[32,1536]{1,0:T(8,128)(2,1)S(1)} %get-tuple-element.80), channel_id=1, source_target_pairs={{0,8},{4,12},{8,0},{12,4},{16,24},{20,28},{24,16},{28,20},{1,9},{5... | collective-permute-start | bytes 294920 | tf_op jit(solution)/shard_map/ppermute | solution.py:28
  43.3 5.1 %collective-permute-start.18 = (bf16[32,1536]{1,0:T(8,128)(2,1)S(1)}, bf16[32,1536]{1,0:T(8,128)(2,1)S(1)}, u32[]{:S(2)}, u32[]{:S(2)}) collective-permute-start(bf16[32,1536]{1,0:T(8,128)(2,1)S(1)} %get-tuple-element.81), channel_id=1, source_target_pairs={{0,4},{4,0},{8,12},{12,8},{16,20},{20,16},{24,28},{28,24},{1,5},{5... | collective-permute-start | bytes 294920 | tf_op jit(solution)/shard_map/ppermute | solution.py:28
  48.7 1.8 %collective-permute-start.19 = (bf16[2,128,512]{2,1,0:T(8,128)(2,1)S(1)}, bf16[2,128,512]{2,1,0:T(8,128)(2,1)S(1)}, u32[]{:S(2)}, u32[]{:S(2)}) collective-permute-start(bf16[2,128,512]{2,1,0:T(8,128)(2,1)S(1)} %get-tuple-element.83), channel_id=1, source_target_pairs={{0,1},{1,0},{2,3},{3,2},{4,5},{5,4},{6,7},{7,6},{8,9},{9,8},{10,11... | collective-permute-start | bytes 786440 | tf_op jit(solution)/shard_map/ppermute | solution.py:28
  48.8 4.9 %collective-permute-start.21 = (bf16[32,512]{1,0:T(8,128)(2,1)S(1)}, bf16[32,512]{1,0:T(8,128)(2,1)S(1)}, u32[]{:S(2)}, u32[]{:S(2)}) collective-permute-start(bf16[32,512]{1,0:T(8,128)(2,1)S(1)} %get-tuple-element.86), channel_id=1, source_target_pairs={{0,16},{4,20},{8,24},{12,28},{16,0},{20,4},{24,8},{28,12},{1,17},{... | collective-permute-start | bytes 98312 | tf_op jit(solution)/shard_map/ppermute | solution.py:28
  50.5 5.6 %collective-permute-start.20 = (bf16[1,128,512]{2,1,0:T(8,128)(2,1)S(1)}, bf16[1,128,512]{2,1,0:T(8,128)(2,1)S(1)}, u32[]{:S(2)}, u32[]{:S(2)}) collective-permute-start(bf16[1,128,512]{2,1,0:T(8,128)(2,1)S(1)} %get-tuple-element.84), channel_id=1, source_target_pairs={{0,2},{1,3},{2,0},{3,1},{4,6},{5,7},{6,4},{7,5},{8,10},{9,11},{10,... | collective-permute-start | bytes 393224 | tf_op jit(solution)/shard_map/ppermute | solution.py:28
